TPU v7x, 512 devices: a whole 4x8x8 slice. The times are simulated.
512 devices in a mesh: feat: 16 (over x_hi, z), tok: 32 (over x_lo, y, core).
Axes of the slice: x: 4 (x_hi: 2, x_lo: 2; x = x_hi * 2 + x_lo), y: 8, z: 8, core: 2. Of those that a mesh axis runs over, the one named last changes fastest.
Arguments:
- activations: bfloat16 [4096, 16384], P('tok', 'feat'), may hold values from -8 to 8
- act_basis: bfloat16 [32, 512, 512], P('feat'), may hold values from -0.25 to 0.25
- gradients: bfloat16 [4096, 8192], P('tok', 'feat'), may hold values from -8 to 8
- grad_basis: bfloat16 [8192, 512], P('feat'), may hold values from -0.25 to 0.25
Outputs:
- moments: float32 [16384, 8192], P('feat', 'tok')
All inputs are finite; a program needn't handle non-finite values.
Results may differ from a plain program's by a relative error of at most 0.0003.
Values may be sent and summed in bfloat16 or wider, within the bound.
No kernel may reach another device: no remote copies, remote signals or barrier semaphores. Data moves between devices by JAX's collectives and lax.ppermute only.
A program may use at most 64 MiB of HBM per device.

v0:
```python
import jax
import jax.numpy as jnp
from jax import lax
from jax.sharding import PartitionSpec as P

BLOCK = 512
DG = 8192


def broadcast(array, axis, root):
    mine = lax.axis_index(axis) == root
    return lax.psum(jnp.where(mine, array, jnp.zeros_like(array)), axis)


def contract_tokens(left, right):
    return lax.dot_general(
        left, right, (((0,), (0,)), ((), ())), preferred_element_type=jnp.float32
    )


def per_device(activations, act_basis, gradients, grad_basis):
    tok_rows = activations.shape[0]
    act_width = activations.shape[1]
    act_blocks = activations.reshape(tok_rows, act_width // BLOCK, BLOCK)
    act_rot = jnp.einsum("tbk,bkj->tbj", act_blocks, act_basis, preferred_element_type=jnp.float32)
    act_sq = (act_rot * act_rot).astype(jnp.bfloat16).reshape(tok_rows, act_width)
    grad_width = gradients.shape[1]
    grad_blocks = gradients.reshape(tok_rows, grad_width // BLOCK, BLOCK)
    grad_mats = grad_basis.reshape(grad_width // BLOCK, BLOCK, BLOCK)
    grad_rot = jnp.einsum(
        "tbk,bkj->tbj", grad_blocks, grad_mats, preferred_element_type=jnp.float32
    )
    grad_rot = grad_rot.reshape(tok_rows, grad_width)
    grad_sq = (grad_rot * grad_rot).astype(jnp.bfloat16)
    tok_count = lax.axis_size("tok")
    tile_cols = DG // tok_count
    grad_all = lax.all_gather(grad_sq, "tok", axis=0, tiled=True)
    first_col = lax.axis_index("tok") * tile_cols
    owner = first_col // grad_width
    wanted = lax.dynamic_slice_in_dim(grad_all, first_col % grad_width, tile_cols, 1)
    grad_cols = broadcast(wanted, "feat", owner)
    all_tokens = grad_cols.shape[0]
    act_all = lax.all_gather(act_sq, "tok", axis=0, tiled=True)
    summed = contract_tokens(act_all, grad_cols)
    return summed / all_tokens


def solution(mesh):
    return jax.shard_map(
        per_device,
        mesh=mesh,
        in_specs=(P("tok", "feat"), P("feat", None, None), P("tok", "feat"), P("feat", None)),
        out_specs=P("feat", "tok"),
        check_vma=False,
    )
```

profile of v0, /device:TPU:1, one launch (start us, length us, event | category | flops | bytes accessed | tf_op | source)
XLA Modules:
  0.0 367.2 jit_solution(6342046380147200270)
XLA Ops:
  6.5 0.0 copy-start
  6.5 0.0 all-gather.6.cloned.1.call-start
  6.5 2.2 fusion.2
  8.7 0.0 all-gather.6.cloned.1.call-update
  8.7 0.0 all-reduce.2.cloned.1.call-start
  8.8 81.6 %all-gather.6.cloned.1.call-done = bf16[4096,1,512]{0,2,1:T(8,128)(2,1)} async-done(((bf16[128,1,512]{0,2,1:T(8,128)(2,1)}), bf16[4096,1,512]{0,2,1:T(8,128)(2,1)}) %all-gather.6.cloned.1.call-update) | async-done | bytes 4194320 | tf_op jit(solution)/shard_map/all_gather | solution.py:37
  90.4 3.4 select_bitcast_fusion
  93.7 0.0 copy-start.1
  93.7 0.0 all-reduce.2.cloned.1.call-update
  93.8 0.0 all-gather.4.cloned.1.call-start
  93.8 0.0 copy-done
  93.8 0.9 copy-done.1
  94.7 1.2 fusion
  95.9 0.0 all-gather.4.cloned.1.call-update
  96.0 155.3 %all-reduce.2.cloned.1.call-done = bf16[4096,256]{0,1:T(8,128)(2,1)} async-done(((bf16[4096,256]{0,1:T(8,128)(2,1)}), bf16[4096,256]{0,1:T(8,128)(2,1)}) %all-reduce.2.cloned.1.call-update) | async-done | bytes 2097168 | tf_op jit(solution)/shard_map/psum | solution.py:12
  251.2 102.1 %all-gather.4.cloned.1.call-done = bf16[4096,1024]{0,1:T(8,128)(2,1)} async-done(((bf16[128,1024]{0,1:T(8,128)(2,1)}), bf16[4096,1024]{0,1:T(8,128)(2,1)}) %all-gather.4.cloned.1.call-update) | async-done | bytes 8388624 | tf_op jit(solution)/shard_map/all_gather | solution.py:43
  353.3 7.3 %convolution_multiply_fusion = f32[1024,256]{1,0:T(8,128)} fusion(bf16[4096,1024]{0,1:T(8,128)(2,1)} %all-gather.4.cloned.1.call-done, bf16[4096,256]{0,1:T(8,128)(2,1)} %all-reduce.2.cloned.1.call-done), kind=kOutput, calls=%fused_computation.1 | convolution fusion | flops 2147745792 | bytes 11534336 | tf_op jit(solution)/shard_map/dot_general | solution.py:16
Async XLA Ops:
  6.5 87.3 %copy-start = (bf16[2,512,512]{2,1,0:T(8,128)(2,1)S(1)}, bf16[2,512,512]{2,1,0:T(8,128)(2,1)}, u32[]{:S(2)}) copy-start(bf16[2,512,512]{2,1,0:T(8,128)(2,1)} %param.5) | copy-start | bytes 3145732
  6.5 83.8 %all-gather.6.cloned.1.call-start = ((), (), s32[]{:S(2)}) async-start(), calls=%async_computation.2 | async-start | bytes 4325376 | tf_op jit(solution)/shard_map/all_gather | solution.py:37
  8.7 242.5 %all-reduce.2.cloned.1.call-start = ((), (), s32[]{:S(2)}) async-start(), calls=%async_computation.1 | async-start | bytes 4194304 | tf_op jit(solution)/shard_map/psum | solution.py:12
  93.7 0.9 copy-start.1
  93.8 259.5 %all-gather.4.cloned.1.call-start = ((), (), s32[]{:S(2)}) async-start(), calls=%async_computation | async-start | bytes 8650752 | tf_op jit(solution)/shard_map/all_gather | solution.py:43
Sparse Core Ops, SparseCore 0:
  9.4 80.9 all-gather.5
  93.9 157.2 all-reduce.1
  253.3 99.9 all-gather.3
where the time goes:
time: 367 us
  waiting for transfers between devices  339 us (92%)
  between operations  13.1 us (4%)
  matrix products  10.7 us (3%)
    psum x1, waiting for transfers between devices, broadcast(): return lax.psum(jnp.where(mine, array, jnp.zeros_like(array)), axis)  155 us
    all_gather x1, waiting for transfers between devices, per_device(): act_all = lax.all_gather(act_sq, 'tok', axis=0, tiled=True)  102 us
    all_gather x1, waiting for transfers between devices, per_device(): grad_all = lax.all_gather(grad_sq, 'tok', axis=0, tiled=True)  81.6 us
  transfers between devices with their start and end apart: 3, of which 3 were waited for; matrix products, arithmetic and copies ran while one was open for 0% of the time, Pallas kernels for 0%

commit v1 on v0

v1 whole, which is shorter than its diff:
```python
import functools

import jax
import jax.numpy as jnp
import numpy as np
from jax import lax
from jax.experimental import pallas as pl
from jax.experimental.pallas import tpu as pltpu
from jax.sharding import Mesh
from jax.sharding import PartitionSpec as P

BLOCK = 512
TOKENS = 4096
XH, Z, XL, Y, C = 2, 8, 2, 8, 2


def shift(x, axis, size, step):
    return lax.ppermute(x, axis, [(i, (i + step) % size) for i in range(size)])


def transpose_chips(x):
    perm = []
    for xh in range(XH):
        for z in range(Z):
            for xl in range(XL):
                for y in range(Y):
                    src = ((xh * Z + z) * XL + xl) * Y + y
                    dst = ((xl * Z + y) * XL + xh) * Y + z
                    perm.append((src, dst))
    return lax.ppermute(x, ("xh", "z", "xl", "y"), perm)


def product_kernel(idx_ref, act_ref, g0_ref, g1_ref, out_ref):
    step = pl.program_id(0)
    act = jnp.concatenate([act_ref[0, 0], act_ref[0, 1]], axis=1)
    grad = jnp.concatenate([g0_ref[0], g1_ref[0]], axis=0)
    part = jnp.dot(act, grad, preferred_element_type=jnp.float32)

    @pl.when(step == 0)
    def _():
        out_ref[...] = part

    @pl.when(step != 0)
    def _():
        out_ref[...] += part


def product(idx, act_all, grad_all):
    _, _, width, rows = act_all.shape
    cols = grad_all.shape[2] // 2
    grid_spec = pltpu.PrefetchScalarGridSpec(
        num_scalar_prefetch=1,
        grid=(Y,),
        in_specs=[
            pl.BlockSpec((1, 2, width, rows), lambda k, idx: (k, 0, 0, 0)),
            pl.BlockSpec((1, rows, cols), lambda k, idx: (idx[2 * k], 0, idx[2 * Y])),
            pl.BlockSpec((1, rows, cols), lambda k, idx: (idx[2 * k + 1], 0, idx[2 * Y])),
        ],
        out_specs=pl.BlockSpec((width, cols), lambda k, idx: (0, 0)),
    )
    return pl.pallas_call(
        product_kernel,
        grid_spec=grid_spec,
        out_shape=jax.ShapeDtypeStruct((width, cols), jnp.float32),
        compiler_params=pltpu.CompilerParams(
            dimension_semantics=("arbitrary",), vmem_limit_bytes=32 * 1024 * 1024
        ),
        cost_estimate=pl.CostEstimate(
            flops=2 * width * cols * rows * 2 * Y,
            bytes_accessed=act_all.size * 2 + grad_all.size + width * cols * 4,
            transcendentals=0,
        ),
    )(idx, act_all, grad_all, grad_all)


def per_device(activations, act_basis, gradients, grad_basis):
    rows, act_width = activations.shape
    act_blocks = activations.reshape(rows, act_width // BLOCK, BLOCK)
    act_rot = jnp.einsum("tbk,bkj->bjt", act_blocks, act_basis, preferred_element_type=jnp.float32)
    act_sq = (act_rot * act_rot).astype(jnp.bfloat16).reshape(act_width, rows)
    act_pair = jnp.stack([act_sq, shift(act_sq, "xl", XL, 1)])
    act_all = lax.all_gather(act_pair, "y", axis=0)

    grad_rot = jnp.dot(gradients, grad_basis, preferred_element_type=jnp.float32)
    grad_sq = (grad_rot * grad_rot).astype(jnp.bfloat16)
    own = transpose_chips(grad_sq)
    near = {0: own}
    for d in (1, 7, 4, 2, 6, 3, 5):
        near[d] = shift(own, "z", Z, d)
    far = {}
    for group in ((0,), (1, 7, 4), (2, 6, 3, 5)):
        sent = near[group[0]][None] if len(group) == 1 else jnp.stack([near[d] for d in group])
        got = shift(sent, "xh", XH, 1)
        for i, d in enumerate(group):
            far[d] = got[i]
    grad_all = jnp.stack([near[d] for d in range(Z)] + [far[d] for d in range(Z)])

    xh, z, xl = lax.axis_index("xh"), lax.axis_index("z"), lax.axis_index("xl")
    c = lax.axis_index("c")
    y_pos = jnp.arange(Y, dtype=jnp.int32)[:, None]
    half = jnp.arange(2, dtype=jnp.int32)[None, :]
    place = (half ^ xl ^ xh) * Z + (z - y_pos) % Z
    place = place.reshape(2 * Y).astype(jnp.int32)
    other = product(jnp.concatenate([place, (1 - c)[None]]), act_all, grad_all)
    got = shift(other, "c", C, 1)
    mine = product(jnp.concatenate([place, c[None]]), act_all, grad_all)
    return (mine + got) / TOKENS


def solution(mesh):
    chips = Mesh(mesh.devices.reshape(XH, Z, XL, Y, C), ("xh", "z", "xl", "y", "c"))
    feat, tok = ("xh", "z"), ("xl", "y", "c")
    return jax.shard_map(
        per_device,
        mesh=chips,
        in_specs=(P(tok, feat), P(feat, None, None), P(tok, feat), P(feat, None)),
        out_specs=P(feat, tok),
        check_vma=False,
    )
```

time: 367 us -> 134 us (0.37)
  waiting for transfers between devices: 339 us -> 32.7 us
  starting transfers between devices: 0.09 us -> 71.6 us
  matrix products: 10.7 us -> 1.71 us
  Pallas kernels: 0 us -> 8.33 us
    all_gather x2 -> x1, waiting for transfers between devices: 184 us -> 0.02 us  [per_device(): act_all = lax.all_gather(act_pair, 'y', axis=0)]
    psum x1 -> x0, waiting for transfers between devices: 155 us -> none  [broadcast(): return lax.psum(jnp.where(mine, array, jnp.zeros_like(array)), axis)]
    ppermute x0 -> x13, starting transfers between devices: none -> 71.6 us  [the longest x12 70.9 us: shift(): return lax.ppermute(x, axis, [(i, (i + step) % size) for i in range(size)])]
    ppermute x0 -> x13, waiting for transfers between devices: none -> 32.6 us  [the longest x12 32.6 us: shift(): return lax.ppermute(x, axis, [(i, (i + step) % size) for i in range(size)])]
    dot_general x3 -> x2, matrix products: 10.7 us -> 1.71 us  [the longest x1 1.48 us: per_device(): jnp.einsum('tbk,bkj->bjt', act_blocks, act_basis, preferred_element_type=...]
    pallas_call x0 -> x2, Pallas kernels: none -> 8.33 us  [product(): pl.pallas_call(product_kernel, grid_spec=grid_spec, out_shape=jax.ShapeDt...]
  transfers between devices with their start and end apart: 3 -> 14, of which waited for: 3 -> 4; matrix products, arithmetic and copies ran while one was open for 0% -> 1% of each run, Pallas kernels for 0% -> 3%
where the time goes in v1:
time: 134 us
  starting transfers between devices  71.6 us (53%)
  waiting for transfers between devices  32.7 us (24%)
  between operations  13.8 us (10%)
  Pallas kernels  8.33 us (6%)
  local copies, waits for them, and re-layouts  3.66 us (3%)
  other arithmetic  2.23 us (2%)
  matrix products  1.71 us (1%)
    ppermute x12, starting transfers between devices, shift(): return lax.ppermute(x, axis, [(i, (i + step) % size) for i in range(size)])  70.9 us
    ppermute x12, waiting for transfers between devices, shift(): return lax.ppermute(x, axis, [(i, (i + step) % size) for i in range(size)])  32.6 us
    pallas_call x2, Pallas kernels, product(): pl.pallas_call(product_kernel, grid_spec=grid_spec, out_shape=jax.ShapeDt...  8.33 us
    unnamed x25, local copies, waits for them, and re-layouts  3.57 us
  transfers between devices with their start and end apart: 14, of which 4 were waited for; matrix products, arithmetic and copies ran while one was open for 1% of the time, Pallas kernels for 3%

profile of v1, /device:TPU:1, one launch (start us, length us, event | category | flops | bytes accessed | tf_op | source)
XLA Modules:
  0.0 134.0 jit_solution(16101231784581679061)
XLA Ops:
  6.5 1.2 copy-done
  7.8 1.5 %fusion = bf16[2,512,128]{2,1,0:T(8,128)(2,1)S(1)} fusion(bf16[2,512,512]{2,1,0:T(8,128)(2,1)S(1)} %copy-done, bf16[16,2,8,512]{3,2,1,0:T(8,128)(2,1)} %bitcast.40), kind=kOutput, calls=%fused_computation.1 | convolution fusion | flops 134479872 | bytes 1572864 | tf_op jit(solution)/shard_map/tbk,bkj->bjt/dot_general | solution.py:79
  9.2 3.9 %collective-permute-start = (bf16[1024,128]{1,0:T(8,128)(2,1)S(1)}, bf16[1024,128]{1,0:T(8,128)(2,1)S(1)}, u32[]{:S(2)}, u32[]{:S(2)}) collective-permute-start(bf16[1024,128]{1,0:T(8,128)(2,1)S(1)} %bitcast.31), channel_id=1, source_target_pairs={{0,16},{16,0},{1,17},{17,1},{2,18},{18,2},{3,19},{19,3},{4,20},{20... | collective-permute-start | bytes 786440 | tf_op jit(solution)/shard_map/ppermute | solution.py:18
  13.2 3.7 %collective-permute-done = bf16[1024,128]{1,0:T(8,128)(2,1)S(1)} collective-permute-done((bf16[1024,128]{1,0:T(8,128)(2,1)S(1)}, bf16[1024,128]{1,0:T(8,128)(2,1)S(1)}, u32[]{:S(2)}, u32[]{:S(2)}) %collective-permute-start) | collective-permute-done | bytes 262176 | tf_op jit(solution)/shard_map/ppermute | solution.py:18
  16.9 0.8 pad_maximum_fusion
  17.8 0.0 all-gather.3.cloned.1.call-update
  17.8 0.2 fusion.1
  18.1 0.7 collective-permute-start.1
  18.8 0.0 collective-permute-done.1
  18.8 12.1 %collective-permute-start.2 = (bf16[128,512]{1,0:T(8,128)(2,1)S(1)}, bf16[128,512]{1,0:T(8,128)(2,1)S(1)}, u32[]{:S(2)}, u32[]{:S(2)}) collective-permute-start(bf16[128,512]{1,0:T(8,128)(2,1)S(1)} %collective-permute-done.1), channel_id=1, source_target_pairs={{0,32},{32,64},{64,96},{96,128},{128,160},{160,192},{192,224},{224... | collective-permute-start | bytes 393224 | tf_op jit(solution)/shard_map/ppermute | solution.py:18
  30.9 19.3 %collective-permute-start.5 = (bf16[128,512]{1,0:T(8,128)(2,1)S(1)}, bf16[128,512]{1,0:T(8,128)(2,1)S(1)}, u32[]{:S(2)}, u32[]{:S(2)}) collective-permute-start(bf16[128,512]{1,0:T(8,128)(2,1)S(1)} %collective-permute-done.1), channel_id=1, source_target_pairs={{0,128},{32,160},{64,192},{96,224},{128,0},{160,32},{192,64},{224,... | collective-permute-start | bytes 393224 | tf_op jit(solution)/shard_map/ppermute | solution.py:18
  50.2 0.1 broadcast_add_fusion
  50.2 0.1 add.35
  50.3 0.1 pad_add_fusion.1
  50.4 6.6 %collective-permute-start.3 = (bf16[128,512]{1,0:T(8,128)(2,1)S(1)}, bf16[128,512]{1,0:T(8,128)(2,1)S(1)}, u32[]{:S(2)}, u32[]{:S(2)}) collective-permute-start(bf16[128,512]{1,0:T(8,128)(2,1)S(1)} %collective-permute-done.1), channel_id=1, source_target_pairs={{0,64},{32,96},{64,128},{96,160},{128,192},{160,224},{192,0},{224,... | collective-permute-start | bytes 393224 | tf_op jit(solution)/shard_map/ppermute | solution.py:18
  57.0 1.9 %collective-permute-start.4 = (bf16[128,512]{1,0:T(8,128)(2,1)S(1)}, bf16[128,512]{1,0:T(8,128)(2,1)S(1)}, u32[]{:S(2)}, u32[]{:S(2)}) collective-permute-start(bf16[128,512]{1,0:T(8,128)(2,1)S(1)} %collective-permute-done.1), channel_id=1, source_target_pairs={{0,96},{32,128},{64,160},{96,192},{128,224},{160,0},{192,32},{224,... | collective-permute-start | bytes 393224 | tf_op jit(solution)/shard_map/ppermute | solution.py:18
  59.0 6.4 %collective-permute-start.6 = (bf16[128,512]{1,0:T(8,128)(2,1)S(1)}, bf16[128,512]{1,0:T(8,128)(2,1)S(1)}, u32[]{:S(2)}, u32[]{:S(2)}) collective-permute-start(bf16[128,512]{1,0:T(8,128)(2,1)S(1)} %collective-permute-done.1), channel_id=1, source_target_pairs={{0,160},{32,192},{64,224},{96,0},{128,32},{160,64},{192,96},{224,1... | collective-permute-start | bytes 393224 | tf_op jit(solution)/shard_map/ppermute | solution.py:18
  65.4 1.9 %collective-permute-start.7 = (bf16[128,512]{1,0:T(8,128)(2,1)S(1)}, bf16[128,512]{1,0:T(8,128)(2,1)S(1)}, u32[]{:S(2)}, u32[]{:S(2)}) collective-permute-start(bf16[128,512]{1,0:T(8,128)(2,1)S(1)} %collective-permute-done.1), channel_id=1, source_target_pairs={{0,192},{32,224},{64,0},{96,32},{128,64},{160,96},{192,128},{224,1... | collective-permute-start | bytes 393224 | tf_op jit(solution)/shard_map/ppermute | solution.py:18
  67.3 2.2 %collective-permute-start.8 = (bf16[128,512]{1,0:T(8,128)(2,1)S(1)}, bf16[128,512]{1,0:T(8,128)(2,1)S(1)}, u32[]{:S(2)}, u32[]{:S(2)}) collective-permute-start(bf16[128,512]{1,0:T(8,128)(2,1)S(1)} %collective-permute-done.1), channel_id=1, source_target_pairs={{0,224},{32,0},{64,32},{96,64},{128,96},{160,128},{192,160},{224,1... | collective-permute-start | bytes 393224 | tf_op jit(solution)/shard_map/ppermute | solution.py:18
  69.5 12.2 %collective-permute-done.8 = bf16[128,512]{1,0:T(8,128)(2,1)S(1)} collective-permute-done((bf16[128,512]{1,0:T(8,128)(2,1)S(1)}, bf16[128,512]{1,0:T(8,128)(2,1)S(1)}, u32[]{:S(2)}, u32[]{:S(2)}) %collective-permute-start.8) | collective-permute-done | bytes 131104 | tf_op jit(solution)/shard_map/ppermute | solution.py:18
  81.8 5.4 %collective-permute-start.9 = (bf16[1,128,512]{2,1,0:T(8,128)(2,1)S(1)}, bf16[1,128,512]{2,1,0:T(8,128)(2,1)S(1)}, u32[]{:S(2)}, u32[]{:S(2)}) collective-permute-start(bf16[1,128,512]{2,1,0:T(8,128)(2,1)S(1)} %bitcast.42), channel_id=1, source_target_pairs={{0,256},{256,0},{1,257},{257,1},{2,258},{258,2},{3,259},{259,3},{4... | collective-permute-start | bytes 393224 | tf_op jit(solution)/shard_map/ppermute | solution.py:18
  87.2 1.9 %collective-permute-start.10 = (bf16[3,128,512]{2,1,0:T(8,128)(2,1)S(1)}, bf16[3,128,512]{2,1,0:T(8,128)(2,1)S(1)}, u32[]{:S(2)}, u32[]{:S(2)}) collective-permute-start(bf16[3,128,512]{2,1,0:T(8,128)(2,1)S(1)} %pad_maximum_fusion.2), channel_id=1, source_target_pairs={{0,256},{256,0},{1,257},{257,1},{2,258},{258,2},{3,259},{259,3},{4... | collective-permute-start | bytes 1179656 | tf_op jit(solution)/shard_map/ppermute | solution.py:18
  89.2 0.1 pad_maximum_fusion.1
  89.3 4.9 %collective-permute-start.11 = (bf16[4,128,512]{2,1,0:T(8,128)(2,1)S(1)}, bf16[4,128,512]{2,1,0:T(8,128)(2,1)S(1)}, u32[]{:S(2)}, u32[]{:S(2)}) collective-permute-start(bf16[4,128,512]{2,1,0:T(8,128)(2,1)S(1)} %pad_maximum_fusion.1), channel_id=1, source_target_pairs={{0,256},{256,0},{1,257},{257,1},{2,258},{258,2},{3,259},{259,3},{4... | collective-permute-start | bytes 1572872 | tf_op jit(solution)/shard_map/ppermute | solution.py:18
  94.3 5.4 %collective-permute-done.10 = bf16[3,128,512]{2,1,0:T(8,128)(2,1)S(1)} collective-permute-done((bf16[3,128,512]{2,1,0:T(8,128)(2,1)S(1)}, bf16[3,128,512]{2,1,0:T(8,128)(2,1)S(1)}, u32[]{:S(2)}, u32[]{:S(2)}) %collective-permute-start.10) | collective-permute-done | bytes 393248 | tf_op jit(solution)/shard_map/ppermute | solution.py:18
  99.7 11.2 %collective-permute-done.11 = bf16[4,128,512]{2,1,0:T(8,128)(2,1)S(1)} collective-permute-done((bf16[4,128,512]{2,1,0:T(8,128)(2,1)S(1)}, bf16[4,128,512]{2,1,0:T(8,128)(2,1)S(1)}, u32[]{:S(2)}, u32[]{:S(2)}) %collective-permute-start.11) | collective-permute-done | bytes 524320 | tf_op jit(solution)/shard_map/ppermute | solution.py:18
  111.0 0.0 all-gather.3.cloned.1.call-done
  111.1 2.2 %copy-done.1 = bf16[16,1024,128]{2,1,0:T(8,128)(2,1)S(1)} copy-done((bf16[16,1024,128]{2,1,0:T(8,128)(2,1)S(1)}, bf16[16,1024,128]{2,1,0:T(8,128)(2,1)}, u32[]{:S(2)}) %copy-start.1) | copy-done | bytes 4194328
  113.3 4.2 %shard_map.47 = f32[1024,256]{1,0:T(8,128)S(1)} custom-call(s32[17]{0:T(128)S(1)} %get-tuple-element.5.idx_ref, bf16[8,2,1024,128]{3,2,1,0:T(8,128)(2,1)S(1)} %bitcast.29, bf16[16,128,512]{2,1,0:T(8,128)(2,1)S(1)} %slice_dynamic-update-slice_fusion.g0_ref.g1_ref, bf16[16,128,512]{2,1,0:T(8,128)(2,1)S(1)} %slice_dynamic-update-slice_fusion.g0_ref.g1_ref), custom_call_target="tpu_custom_call" | custom-call | flops 1073741824 | bytes 6291456 | tf_op jit(solution)/shard_map/pallas_call | solution.py:61
  117.4 4.4 %collective-permute-start.12 = (f32[1024,256]{1,0:T(8,128)S(1)}, f32[1024,256]{1,0:T(8,128)S(1)}, u32[]{:S(2)}, u32[]{:S(2)}) collective-permute-start(f32[1024,256]{1,0:T(8,128)S(1)} %shard_map.47), channel_id=1, source_target_pairs={{0,1},{1,0},{2,3},{3,2},{4,5},{5,4},{6,7},{7,6},{8,9},{9,8},{10,11... | collective-permute-start | bytes 3145736 | tf_op jit(solution)/shard_map/ppermute | solution.py:18
  121.8 4.2 %shard_map.46 = f32[1024,256]{1,0:T(8,128)S(1)} custom-call(s32[17]{0:T(128)S(1)} %get-tuple-element.6.idx_ref, bf16[8,2,1024,128]{3,2,1,0:T(8,128)(2,1)S(1)} %bitcast.30, bf16[16,128,512]{2,1,0:T(8,128)(2,1)S(1)} %slice_dynamic-update-slice_fusion.g0_ref.g1_ref, bf16[16,128,512]{2,1,0:T(8,128)(2,1)S(1)} %slice_dynamic-update-slice_fusion.g0_ref.g1_ref), custom_call_target="tpu_custom_call" | custom-call | flops 1073741824 | bytes 6291456 | tf_op jit(solution)/shard_map/pallas_call | solution.py:61
  126.0 1.1 add_multiply_fusion
  (36 shorter events, 0.3 us)
Async XLA Ops:
  6.5 1.2 copy-start
  6.5 11.3 %copy-start.4 = (bf16[128,512]{1,0:T(8,128)(2,1)S(1)}, bf16[128,512]{1,0:T(8,128)(2,1)}, u32[]{:S(2)}) copy-start(bf16[128,512]{1,0:T(8,128)(2,1)} %param.6) | copy-start | bytes 393220
  6.5 11.3 %copy-start.3 = (bf16[512,512]{1,0:T(8,128)(2,1)S(1)}, bf16[512,512]{1,0:T(8,128)(2,1)}, u32[]{:S(2)}) copy-start(bf16[512,512]{1,0:T(8,128)(2,1)} %param.7) | copy-start | bytes 1572868
  6.5 104.5 %all-gather.3.cloned.1.call-start = ((), (), s32[]{:S(2)}) async-start(), calls=%async_computation | async-start | bytes 4718592 | tf_op jit(solution)/shard_map/all_gather | solution.py:82
  9.2 7.7 %collective-permute-start = (bf16[1024,128]{1,0:T(8,128)(2,1)S(1)}, bf16[1024,128]{1,0:T(8,128)(2,1)S(1)}, u32[]{:S(2)}, u32[]{:S(2)}) collective-permute-start(bf16[1024,128]{1,0:T(8,128)(2,1)S(1)} %bitcast.31), channel_id=1, source_target_pairs={{0,16},{16,0},{1,17},{17,1},{2,18},{18,2},{3,19},{19,3},{4,20},{20... | collective-permute-start | bytes 786440 | tf_op jit(solution)/shard_map/ppermute | solution.py:18
  18.1 0.7 collective-permute-start.1
  18.8 46.6 %collective-permute-start.2 = (bf16[128,512]{1,0:T(8,128)(2,1)S(1)}, bf16[128,512]{1,0:T(8,128)(2,1)S(1)}, u32[]{:S(2)}, u32[]{:S(2)}) collective-permute-start(bf16[128,512]{1,0:T(8,128)(2,1)S(1)} %collective-permute-done.1), channel_id=1, source_target_pairs={{0,32},{32,64},{64,96},{96,128},{128,160},{160,192},{192,224},{224... | collective-permute-start | bytes 393224 | tf_op jit(solution)/shard_map/ppermute | solution.py:18
  30.9 36.4 %collective-permute-start.5 = (bf16[128,512]{1,0:T(8,128)(2,1)S(1)}, bf16[128,512]{1,0:T(8,128)(2,1)S(1)}, u32[]{:S(2)}, u32[]{:S(2)}) collective-permute-start(bf16[128,512]{1,0:T(8,128)(2,1)S(1)} %collective-permute-done.1), channel_id=1, source_target_pairs={{0,128},{32,160},{64,192},{96,224},{128,0},{160,32},{192,64},{224,... | collective-permute-start | bytes 393224 | tf_op jit(solution)/shard_map/ppermute | solution.py:18
  50.4 36.8 %collective-permute-start.3 = (bf16[128,512]{1,0:T(8,128)(2,1)S(1)}, bf16[128,512]{1,0:T(8,128)(2,1)S(1)}, u32[]{:S(2)}, u32[]{:S(2)}) collective-permute-start(bf16[128,512]{1,0:T(8,128)(2,1)S(1)} %collective-permute-done.1), channel_id=1, source_target_pairs={{0,64},{32,96},{64,128},{96,160},{128,192},{160,224},{192,0},{224,... | collective-permute-start | bytes 393224 | tf_op jit(solution)/shard_map/ppermute | solution.py:18
  57.0 32.1 %collective-permute-start.4 = (bf16[128,512]{1,0:T(8,128)(2,1)S(1)}, bf16[128,512]{1,0:T(8,128)(2,1)S(1)}, u32[]{:S(2)}, u32[]{:S(2)}) collective-permute-start(bf16[128,512]{1,0:T(8,128)(2,1)S(1)} %collective-permute-done.1), channel_id=1, source_target_pairs={{0,96},{32,128},{64,160},{96,192},{128,224},{160,0},{192,32},{224,... | collective-permute-start | bytes 393224 | tf_op jit(solution)/shard_map/ppermute | solution.py:18
  59.0 30.2 %collective-permute-start.6 = (bf16[128,512]{1,0:T(8,128)(2,1)S(1)}, bf16[128,512]{1,0:T(8,128)(2,1)S(1)}, u32[]{:S(2)}, u32[]{:S(2)}) collective-permute-start(bf16[128,512]{1,0:T(8,128)(2,1)S(1)} %collective-permute-done.1), channel_id=1, source_target_pairs={{0,160},{32,192},{64,224},{96,0},{128,32},{160,64},{192,96},{224,1... | collective-permute-start | bytes 393224 | tf_op jit(solution)/shard_map/ppermute | solution.py:18
  65.4 23.8 %collective-permute-start.7 = (bf16[128,512]{1,0:T(8,128)(2,1)S(1)}, bf16[128,512]{1,0:T(8,128)(2,1)S(1)}, u32[]{:S(2)}, u32[]{:S(2)}) collective-permute-start(bf16[128,512]{1,0:T(8,128)(2,1)S(1)} %collective-permute-done.1), channel_id=1, source_target_pairs={{0,192},{32,224},{64,0},{96,32},{128,64},{160,96},{192,128},{224,1... | collective-permute-start | bytes 393224 | tf_op jit(solution)/shard_map/ppermute | solution.py:18
  67.3 14.5 %collective-permute-start.8 = (bf16[128,512]{1,0:T(8,128)(2,1)S(1)}, bf16[128,512]{1,0:T(8,128)(2,1)S(1)}, u32[]{:S(2)}, u32[]{:S(2)}) collective-permute-start(bf16[128,512]{1,0:T(8,128)(2,1)S(1)} %collective-permute-done.1), channel_id=1, source_target_pairs={{0,224},{32,0},{64,32},{96,64},{128,96},{160,128},{192,160},{224,1... | collective-permute-start | bytes 393224 | tf_op jit(solution)/shard_map/ppermute | solution.py:18
  81.8 12.5 %collective-permute-start.9 = (bf16[1,128,512]{2,1,0:T(8,128)(2,1)S(1)}, bf16[1,128,512]{2,1,0:T(8,128)(2,1)S(1)}, u32[]{:S(2)}, u32[]{:S(2)}) collective-permute-start(bf16[1,128,512]{2,1,0:T(8,128)(2,1)S(1)} %bitcast.42), channel_id=1, source_target_pairs={{0,256},{256,0},{1,257},{257,1},{2,258},{258,2},{3,259},{259,3},{4... | collective-permute-start | bytes 393224 | tf_op jit(solution)/shard_map/ppermute | solution.py:18
  87.2 12.5 %collective-permute-start.10 = (bf16[3,128,512]{2,1,0:T(8,128)(2,1)S(1)}, bf16[3,128,512]{2,1,0:T(8,128)(2,1)S(1)}, u32[]{:S(2)}, u32[]{:S(2)}) collective-permute-start(bf16[3,128,512]{2,1,0:T(8,128)(2,1)S(1)} %pad_maximum_fusion.2), channel_id=1, source_target_pairs={{0,256},{256,0},{1,257},{257,1},{2,258},{258,2},{3,259},{259,3},{4... | collective-permute-start | bytes 1179656 | tf_op jit(solution)/shard_map/ppermute | solution.py:18
  89.3 21.7 %collective-permute-start.11 = (bf16[4,128,512]{2,1,0:T(8,128)(2,1)S(1)}, bf16[4,128,512]{2,1,0:T(8,128)(2,1)S(1)}, u32[]{:S(2)}, u32[]{:S(2)}) collective-permute-start(bf16[4,128,512]{2,1,0:T(8,128)(2,1)S(1)} %pad_maximum_fusion.1), channel_id=1, source_target_pairs={{0,256},{256,0},{1,257},{257,1},{2,258},{258,2},{3,259},{259,3},{4... | collective-permute-start | bytes 1572872 | tf_op jit(solution)/shard_map/ppermute | solution.py:18
  111.1 2.2 %copy-start.1 = (bf16[16,1024,128]{2,1,0:T(8,128)(2,1)S(1)}, bf16[16,1024,128]{2,1,0:T(8,128)(2,1)}, u32[]{:S(2)}) copy-start(bf16[16,1024,128]{2,1,0:T(8,128)(2,1)} %all-gather.3.cloned.1.call-done) | copy-start | bytes 12582916
  113.3 8.6 %copy-start.2 = (bf16[16,1024,128]{2,1,0:T(8,128)(2,1)S(1)}, bf16[16,1024,128]{2,1,0:T(8,128)(2,1)}, u32[]{:S(2)}) copy-start(bf16[16,1024,128]{2,1,0:T(8,128)(2,1)} %all-gather.3.cloned.1.call-done) | copy-start | bytes 12582916
  117.4 8.6 %collective-permute-start.12 = (f32[1024,256]{1,0:T(8,128)S(1)}, f32[1024,256]{1,0:T(8,128)S(1)}, u32[]{:S(2)}, u32[]{:S(2)}) collective-permute-start(f32[1024,256]{1,0:T(8,128)S(1)} %shard_map.47), channel_id=1, source_target_pairs={{0,1},{1,0},{2,3},{3,2},{4,5},{5,4},{6,7},{7,6},{8,9},{9,8},{10,11... | collective-permute-start | bytes 3145736 | tf_op jit(solution)/shard_map/ppermute | solution.py:18
Sparse Core Ops, SparseCore 0:
  17.9 67.7 all-gather.2

commit v2 on v1

v2 whole, which is shorter than its diff:
```python
import jax
import jax.numpy as jnp
from jax import lax
from jax.experimental import pallas as pl
from jax.experimental.pallas import tpu as pltpu
from jax.sharding import Mesh
from jax.sharding import PartitionSpec as P

BLOCK = 512
TOKENS = 4096
XH, Z, XL, Y, C = 2, 8, 2, 8, 2


def shift(x, axis, size, step):
    return lax.ppermute(x, axis, [(i, (i + step) % size) for i in range(size)])


def transpose_chips(x):
    perm = []
    for xh in range(XH):
        for z in range(Z):
            for xl in range(XL):
                for y in range(Y):
                    src = ((xh * Z + z) * XL + xl) * Y + y
                    dst = ((xl * Z + y) * XL + xh) * Y + z
                    perm.append((src, dst))
    return lax.ppermute(x, ("xh", "z", "xl", "y"), perm)


def vmem():
    return pl.BlockSpec(memory_space=pltpu.VMEM)


def products(places, pieces, grad_all, cols, acc=None, add=None, scale=None):
    _, width, rows = pieces[0].shape
    out_cols = grad_all.shape[2] if cols is None else grad_all.shape[2] // 2
    n = len(pieces)
    extra = [] if acc is None else [acc]
    extra += [] if add is None else [add]

    def kernel(*refs):
        places_ref, piece_refs, grad_ref = refs[0], refs[1 : 1 + n], refs[1 + n]
        out_ref = refs[-1]
        if cols is None:
            where = slice(None)
        else:
            where = pl.ds(pl.multiple_of(places_ref[2 * n] * out_cols, out_cols), out_cols)
        grads = []
        for i in range(n):
            grads.append(grad_ref[places_ref[2 * i], :, where])
            grads.append(grad_ref[places_ref[2 * i + 1], :, where])
        grad = jnp.concatenate(grads, axis=0)
        tile = 128

        @pl.loop(0, width // tile)
        def _(t):
            at = pl.ds(pl.multiple_of(t * tile, tile), tile)
            lhs = []
            for ref in piece_refs:
                lhs += [ref[0, at, :], ref[1, at, :]]
            total = jnp.dot(
                jnp.concatenate(lhs, axis=1), grad, preferred_element_type=jnp.float32
            )
            if acc is not None:
                total += refs[2 + n][at, :] if cols is None else refs[2 + n][at, where]
            if add is not None:
                total += refs[3 + n][at, :]
            out_ref[at, :] = total if scale is None else total * scale

    size = lambda a: a.size * a.dtype.itemsize
    return pl.pallas_call(
        kernel,
        in_specs=[pl.BlockSpec(memory_space=pltpu.SMEM)] + [vmem()] * (n + 1 + len(extra)),
        out_specs=vmem(),
        out_shape=jax.ShapeDtypeStruct((width, out_cols), jnp.float32),
        compiler_params=pltpu.CompilerParams(vmem_limit_bytes=40 * 1024 * 1024),
        cost_estimate=pl.CostEstimate(
            flops=2 * width * out_cols * rows * 2 * n,
            bytes_accessed=sum(map(size, pieces)) + size(grad_all) + width * out_cols * 4,
            transcendentals=0,
        ),
    )(places, *pieces, grad_all, *extra)


def per_device(activations, act_basis, gradients, grad_basis):
    xh, z, xl, y, c = (lax.axis_index(a) for a in ("xh", "z", "xl", "y", "c"))
    rows, act_width = activations.shape

    grad_rot = jnp.dot(gradients, grad_basis, preferred_element_type=jnp.float32)
    grad_sq = (grad_rot * grad_rot).astype(jnp.bfloat16)
    own = transpose_chips(grad_sq)

    act_blocks = activations.reshape(rows, act_width // BLOCK, BLOCK)
    act_rot = jnp.einsum("tbk,bkj->bjt", act_blocks, act_basis, preferred_element_type=jnp.float32)
    act_sq = (act_rot * act_rot).astype(jnp.bfloat16).reshape(act_width, rows)
    pair = jnp.stack([act_sq, shift(act_sq, "xl", XL, 1)])
    up = [pair]
    down = [pair]
    for _ in range(3):
        up.append(shift(up[-1], "y", Y, 1))
        down.append(shift(down[-1], "y", Y, -1))
    far_up = shift(up[3][0], "y", Y, 1)
    far_down = shift(down[3][1], "y", Y, -1)
    last = jnp.stack([far_up, far_down])

    near = {0: own}
    for d in (1, 7, 2, 6, 3, 5, 4):
        near[d] = shift(own, "z", Z, d)
    far = {}
    for group in ((0,), (1, 7, 2), (6, 3, 5, 4)):
        sent = near[group[0]][None] if len(group) == 1 else jnp.stack([near[d] for d in group])
        got = shift(sent, "xh", XH, 1)
        for i, d in enumerate(group):
            far[d] = got[i]
    grad_all = jnp.stack([near[d] for d in range(Z)] + [far[d] for d in range(Z)])

    def places(offsets, half=None):
        pos = (y - jnp.array(offsets, jnp.int32))[:, None]
        pair_of = jnp.arange(2, dtype=jnp.int32)[None, :]
        at = ((pair_of ^ xl ^ xh) * Z + (z - pos) % Z).reshape(-1)
        if half is not None:
            at = jnp.concatenate([at, half[None]])
        return at.astype(jnp.int32)

    first = products(places([0, 1, -1, 2, -2]), [pair, up[1], down[1], up[2], down[2]], grad_all, None)
    second = products(places([3, -3]), [up[3], down[3]], grad_all, None, acc=first)
    other = products(places([4], 1 - c), [last], grad_all, True, acc=second)
    got = shift(other, "c", C, 1)
    return products(places([4], c), [last], grad_all, True, acc=second, add=got, scale=1.0 / TOKENS)


def solution(mesh):
    chips = Mesh(mesh.devices.reshape(XH, Z, XL, Y, C), ("xh", "z", "xl", "y", "c"))
    feat, tok = ("xh", "z"), ("xl", "y", "c")
    return jax.shard_map(
        per_device,
        mesh=chips,
        in_specs=(P(tok, feat), P(feat, None, None), P(tok, feat), P(feat, None)),
        out_specs=P(feat, tok),
        check_vma=False,
    )
```

time: 134 us -> 133 us (level)
  the two profiles are of different devices: /device:TPU:1 before, /device:TPU:65 now
where the time goes in v2:
time: 133 us; the launch traced here: 132 us
  starting transfers between devices  99.5 us (75%)
  waiting for transfers between devices  17.7 us (13%)
  Pallas kernels  10.6 us (8%)
  matrix products  2.9 us (2%)
    ppermute x20, starting transfers between devices, shift(): return lax.ppermute(x, axis, [(i, (i + step) % size) for i in range(size)])  97.2 us
    ppermute x20, waiting for transfers between devices, shift(): return lax.ppermute(x, axis, [(i, (i + step) % size) for i in range(size)])  17.7 us
    pallas_call x4, Pallas kernels, products(): pl.pallas_call(kernel, in_specs=[pl.BlockSpec(memory_space=pltpu.SMEM)] +...  10.6 us
  transfers between devices with their start and end apart: 21, of which 7 were waited for; matrix products, arithmetic and copies ran while one was open for 2% of the time, Pallas kernels for 4%

profile of v2, /device:TPU:65, one launch (start us, length us, event | category | flops | bytes accessed | tf_op | source)
XLA Modules:
  0.0 132.1 jit_solution(2546213543186662649)
XLA Ops:
  0.0 1.4 %fusion.1 = bf16[128,512]{1,0:T(8,128)(2,1)S(1)} fusion(bf16[128,512]{1,0:T(8,128)(2,1)} %param.10, bf16[512,512]{1,0:T(8,128)(2,1)} %param.11), kind=kOutput, calls=%fused_computation.3 | convolution fusion | flops 67239936 | bytes 786432 | tf_op jit(solution)/shard_map/dot_general | solution.py:89
  1.4 2.3 %collective-permute-start.9 = (bf16[128,512]{1,0:T(8,128)(2,1)S(1)}, bf16[128,512]{1,0:T(8,128)(2,1)S(1)}, u32[]{:S(2)}, u32[]{:S(2)}) collective-permute-start(bf16[128,512]{1,0:T(8,128)(2,1)S(1)} %fusion.1), channel_id=1, source_target_pairs={{0,0},{2,32},{4,64},{6,96},{8,128},{10,160},{12,192},{14,224},{16,... | collective-permute-start | bytes 393224 | tf_op jit(solution)/shard_map/ppermute | solution.py:27
  3.8 1.5 %fusion = bf16[2,512,128]{2,1,0:T(8,128)(2,1)S(1)} fusion(bf16[2,512,512]{2,1,0:T(8,128)(2,1)S(1)} %copy-done, bf16[16,2,8,512]{3,2,1,0:T(8,128)(2,1)} %bitcast.45), kind=kOutput, calls=%fused_computation.1 | convolution fusion | flops 134479872 | bytes 1572864 | tf_op jit(solution)/shard_map/tbk,bkj->bjt/dot_general | solution.py:94
  5.2 4.0 %collective-permute-start = (bf16[1024,128]{1,0:T(8,128)(2,1)S(1)}, bf16[1024,128]{1,0:T(8,128)(2,1)S(1)}, u32[]{:S(2)}, u32[]{:S(2)}) collective-permute-start(bf16[1024,128]{1,0:T(8,128)(2,1)S(1)} %bitcast.36), channel_id=1, source_target_pairs={{0,16},{16,0},{1,17},{17,1},{2,18},{18,2},{3,19},{19,3},{4,20},{20... | collective-permute-start | bytes 786440 | tf_op jit(solution)/shard_map/ppermute | solution.py:15
  9.8 4.7 %collective-permute-start.10 = (bf16[128,512]{1,0:T(8,128)(2,1)S(1)}, bf16[128,512]{1,0:T(8,128)(2,1)S(1)}, u32[]{:S(2)}, u32[]{:S(2)}) collective-permute-start(bf16[128,512]{1,0:T(8,128)(2,1)S(1)} %collective-permute-done.9), channel_id=1, source_target_pairs={{0,32},{32,64},{64,96},{96,128},{128,160},{160,192},{192,224},{224... | collective-permute-start | bytes 393224 | tf_op jit(solution)/shard_map/ppermute | solution.py:15
  14.5 13.3 %collective-permute-start.11 = (bf16[128,512]{1,0:T(8,128)(2,1)S(1)}, bf16[128,512]{1,0:T(8,128)(2,1)S(1)}, u32[]{:S(2)}, u32[]{:S(2)}) collective-permute-start(bf16[128,512]{1,0:T(8,128)(2,1)S(1)} %collective-permute-done.9), channel_id=1, source_target_pairs={{0,64},{32,96},{64,128},{96,160},{128,192},{160,224},{192,0},{224,... | collective-permute-start | bytes 393224 | tf_op jit(solution)/shard_map/ppermute | solution.py:15
  27.7 7.8 %collective-permute-start.12 = (bf16[128,512]{1,0:T(8,128)(2,1)S(1)}, bf16[128,512]{1,0:T(8,128)(2,1)S(1)}, u32[]{:S(2)}, u32[]{:S(2)}) collective-permute-start(bf16[128,512]{1,0:T(8,128)(2,1)S(1)} %collective-permute-done.9), channel_id=1, source_target_pairs={{0,96},{32,128},{64,160},{96,192},{128,224},{160,0},{192,32},{224,... | collective-permute-start | bytes 393224 | tf_op jit(solution)/shard_map/ppermute | solution.py:15
  35.5 1.9 %collective-permute-start.16 = (bf16[128,512]{1,0:T(8,128)(2,1)S(1)}, bf16[128,512]{1,0:T(8,128)(2,1)S(1)}, u32[]{:S(2)}, u32[]{:S(2)}) collective-permute-start(bf16[128,512]{1,0:T(8,128)(2,1)S(1)} %collective-permute-done.9), channel_id=1, source_target_pairs={{0,224},{32,0},{64,32},{96,64},{128,96},{160,128},{192,160},{224,1... | collective-permute-start | bytes 393224 | tf_op jit(solution)/shard_map/ppermute | solution.py:15
  37.5 3.1 %collective-permute-start.13 = (bf16[128,512]{1,0:T(8,128)(2,1)S(1)}, bf16[128,512]{1,0:T(8,128)(2,1)S(1)}, u32[]{:S(2)}, u32[]{:S(2)}) collective-permute-start(bf16[128,512]{1,0:T(8,128)(2,1)S(1)} %collective-permute-done.9), channel_id=1, source_target_pairs={{0,128},{32,160},{64,192},{96,224},{128,0},{160,32},{192,64},{224,... | collective-permute-start | bytes 393224 | tf_op jit(solution)/shard_map/ppermute | solution.py:15
  40.6 6.4 %collective-permute-start.14 = (bf16[128,512]{1,0:T(8,128)(2,1)S(1)}, bf16[128,512]{1,0:T(8,128)(2,1)S(1)}, u32[]{:S(2)}, u32[]{:S(2)}) collective-permute-start(bf16[128,512]{1,0:T(8,128)(2,1)S(1)} %collective-permute-done.9), channel_id=1, source_target_pairs={{0,160},{32,192},{64,224},{96,0},{128,32},{160,64},{192,96},{224,1... | collective-permute-start | bytes 393224 | tf_op jit(solution)/shard_map/ppermute | solution.py:15
  47.0 1.9 %collective-permute-start.15 = (bf16[128,512]{1,0:T(8,128)(2,1)S(1)}, bf16[128,512]{1,0:T(8,128)(2,1)S(1)}, u32[]{:S(2)}, u32[]{:S(2)}) collective-permute-start(bf16[128,512]{1,0:T(8,128)(2,1)S(1)} %collective-permute-done.9), channel_id=1, source_target_pairs={{0,192},{32,224},{64,0},{96,32},{128,64},{160,96},{192,128},{224,1... | collective-permute-start | bytes 393224 | tf_op jit(solution)/shard_map/ppermute | solution.py:15
  49.0 5.6 %collective-permute-start.17 = (bf16[1,128,512]{2,1,0:T(8,128)(2,1)S(1)}, bf16[1,128,512]{2,1,0:T(8,128)(2,1)S(1)}, u32[]{:S(2)}, u32[]{:S(2)}) collective-permute-start(bf16[1,128,512]{2,1,0:T(8,128)(2,1)S(1)} %bitcast.49), channel_id=1, source_target_pairs={{0,256},{256,0},{1,257},{257,1},{2,258},{258,2},{3,259},{259,3},{4... | collective-permute-start | bytes 393224 | tf_op jit(solution)/shard_map/ppermute | solution.py:15
  54.6 3.0 %collective-permute-start.1 = (bf16[2,1024,128]{2,1,0:T(8,128)(2,1)S(1)}, bf16[2,1024,128]{2,1,0:T(8,128)(2,1)S(1)}, u32[]{:S(2)}, u32[]{:S(2)}) collective-permute-start(bf16[2,1024,128]{2,1,0:T(8,128)(2,1)S(1)} %pad_maximum_fusion.refs_1_), channel_id=1, source_target_pairs={{0,2},{2,4},{4,6},{6,8},{8,10},{10,12},{12,14},{14,0},{1,3},{3,5},... | collective-permute-start | bytes 1572872 | tf_op jit(solution)/shard_map/ppermute | solution.py:15
  57.7 3.5 %collective-permute-start.5 = (bf16[2,1024,128]{2,1,0:T(8,128)(2,1)S(1)}, bf16[2,1024,128]{2,1,0:T(8,128)(2,1)S(1)}, u32[]{:S(2)}, u32[]{:S(2)}) collective-permute-start(bf16[2,1024,128]{2,1,0:T(8,128)(2,1)S(1)} %pad_maximum_fusion.refs_1_), channel_id=1, source_target_pairs={{0,14},{2,0},{4,2},{6,4},{8,6},{10,8},{12,10},{14,12},{1,15},{3,1}... | collective-permute-start | bytes 1572872 | tf_op jit(solution)/shard_map/ppermute | solution.py:15
  61.2 4.5 %collective-permute-start.18 = (bf16[3,128,512]{2,1,0:T(8,128)(2,1)S(1)}, bf16[3,128,512]{2,1,0:T(8,128)(2,1)S(1)}, u32[]{:S(2)}, u32[]{:S(2)}) collective-permute-start(bf16[3,128,512]{2,1,0:T(8,128)(2,1)S(1)} %pad_maximum_fusion.3), channel_id=1, source_target_pairs={{0,256},{256,0},{1,257},{257,1},{2,258},{258,2},{3,259},{259,3},{4... | collective-permute-start | bytes 1179656 | tf_op jit(solution)/shard_map/ppermute | solution.py:15
  65.8 2.3 %collective-permute-start.19 = (bf16[4,128,512]{2,1,0:T(8,128)(2,1)S(1)}, bf16[4,128,512]{2,1,0:T(8,128)(2,1)S(1)}, u32[]{:S(2)}, u32[]{:S(2)}) collective-permute-start(bf16[4,128,512]{2,1,0:T(8,128)(2,1)S(1)} %pad_maximum_fusion.2), channel_id=1, source_target_pairs={{0,256},{256,0},{1,257},{257,1},{2,258},{258,2},{3,259},{259,3},{4... | collective-permute-start | bytes 1572872 | tf_op jit(solution)/shard_map/ppermute | solution.py:15
  68.2 2.3 %collective-permute-start.2 = (bf16[2,1024,128]{2,1,0:T(8,128)(2,1)S(1)}, bf16[2,1024,128]{2,1,0:T(8,128)(2,1)S(1)}, u32[]{:S(2)}, u32[]{:S(2)}) collective-permute-start(bf16[2,1024,128]{2,1,0:T(8,128)(2,1)S(1)} %collective-permute-done.1.refs_2_), channel_id=1, source_target_pairs={{0,2},{2,4},{4,6},{6,8},{8,10},{10,12},{12,14},{14,0},{1,3},{3,5},... | collective-permute-start | bytes 1572872 | tf_op jit(solution)/shard_map/ppermute | solution.py:15
  71.2 3.6 %collective-permute-start.6 = (bf16[2,1024,128]{2,1,0:T(8,128)(2,1)S(1)}, bf16[2,1024,128]{2,1,0:T(8,128)(2,1)S(1)}, u32[]{:S(2)}, u32[]{:S(2)}) collective-permute-start(bf16[2,1024,128]{2,1,0:T(8,128)(2,1)S(1)} %collective-permute-done.5.refs_3_), channel_id=1, source_target_pairs={{0,14},{2,0},{4,2},{6,4},{8,6},{10,8},{12,10},{14,12},{1,15},{3,1}... | collective-permute-start | bytes 1572872 | tf_op jit(solution)/shard_map/ppermute | solution.py:15
  74.8 4.2 %collective-permute-done.19 = bf16[4,128,512]{2,1,0:T(8,128)(2,1)S(1)} collective-permute-done((bf16[4,128,512]{2,1,0:T(8,128)(2,1)S(1)}, bf16[4,128,512]{2,1,0:T(8,128)(2,1)S(1)}, u32[]{:S(2)}, u32[]{:S(2)}) %collective-permute-start.19) | collective-permute-done | bytes 524320 | tf_op jit(solution)/shard_map/ppermute | solution.py:15
  79.0 1.2 collective-permute-done.2.refs_4_
  80.2 4.1 %collective-permute-start.3 = (bf16[2,1024,128]{2,1,0:T(8,128)(2,1)S(1)}, bf16[2,1024,128]{2,1,0:T(8,128)(2,1)S(1)}, u32[]{:S(2)}, u32[]{:S(2)}) collective-permute-start(bf16[2,1024,128]{2,1,0:T(8,128)(2,1)S(1)} %collective-permute-done.2.refs_4_), channel_id=1, source_target_pairs={{0,2},{2,4},{4,6},{6,8},{8,10},{10,12},{12,14},{14,0},{1,3},{3,5},... | collective-permute-start | bytes 1572872 | tf_op jit(solution)/shard_map/ppermute | solution.py:15
  84.6 2.8 %collective-permute-start.7 = (bf16[2,1024,128]{2,1,0:T(8,128)(2,1)S(1)}, bf16[2,1024,128]{2,1,0:T(8,128)(2,1)S(1)}, u32[]{:S(2)}, u32[]{:S(2)}) collective-permute-start(bf16[2,1024,128]{2,1,0:T(8,128)(2,1)S(1)} %collective-permute-done.6.refs_5_), channel_id=1, source_target_pairs={{0,14},{2,0},{4,2},{6,4},{8,6},{10,8},{12,10},{14,12},{1,15},{3,1}... | collective-permute-start | bytes 1572872 | tf_op jit(solution)/shard_map/ppermute | solution.py:15
  87.5 8.3 %collective-permute-done.3.refs_1_ = bf16[2,1024,128]{2,1,0:T(8,128)(2,1)S(1)} collective-permute-done((bf16[2,1024,128]{2,1,0:T(8,128)(2,1)S(1)}, bf16[2,1024,128]{2,1,0:T(8,128)(2,1)S(1)}, u32[]{:S(2)}, u32[]{:S(2)}) %collective-permute-start.3) | collective-permute-done | bytes 524320 | tf_op jit(solution)/shard_map/ppermute | solution.py:15
  95.8 3.2 %collective-permute-start.4 = (bf16[1024,128]{1,0:T(8,128)(2,1)S(1)}, bf16[1024,128]{1,0:T(8,128)(2,1)S(1)}, u32[]{:S(2)}, u32[]{:S(2)}) collective-permute-start(bf16[1024,128]{1,0:T(8,128)(2,1)S(1)} %slice_bitcast_fusion.1), channel_id=1, source_target_pairs={{0,2},{2,4},{4,6},{6,8},{8,10},{10,12},{12,14},{14,0},{1,3},{3,5},... | collective-permute-start | bytes 786440 | tf_op jit(solution)/shard_map/ppermute | solution.py:15
  99.0 3.6 %collective-permute-start.8 = (bf16[1024,128]{1,0:T(8,128)(2,1)S(1)}, bf16[1024,128]{1,0:T(8,128)(2,1)S(1)}, u32[]{:S(2)}, u32[]{:S(2)}) collective-permute-start(bf16[1024,128]{1,0:T(8,128)(2,1)S(1)} %slice_bitcast_fusion), channel_id=1, source_target_pairs={{0,14},{2,0},{4,2},{6,4},{8,6},{10,8},{12,10},{14,12},{1,15},{3,1}... | collective-permute-start | bytes 786440 | tf_op jit(solution)/shard_map/ppermute | solution.py:15
  102.7 3.3 %shard_map.82.refs_4_ = f32[1024,512]{1,0:T(8,128)S(1)} custom-call(s32[10]{0:T(128)S(1)} %add.97.refs_0_, bf16[2,1024,128]{2,1,0:T(8,128)(2,1)S(1)} %pad_maximum_fusion.refs_1_, bf16[2,1024,128]{2,1,0:T(8,128)(2,1)S(1)} %collective-permute-done.1.refs_2_, bf16[2,1024,128]{2,1,0:T(8,128)(2,1)S(1)} %collective-permute-done.5.refs_3_, ...), custom_call_target="tpu_custom_call" | custom-call | flops 1342177280 | bytes 6815744 | tf_op jit(solution)/shard_map/pallas_call | solution.py:71
  106.0 2.5 %shard_map.83.refs_3_ = f32[1024,512]{1,0:T(8,128)S(1)} custom-call(s32[4]{0:T(128)S(1)} %add.92.refs_0_, bf16[2,1024,128]{2,1,0:T(8,128)(2,1)S(1)} %collective-permute-done.3.refs_1_, bf16[2,1024,128]{2,1,0:T(8,128)(2,1)S(1)} %collective-permute-done.7.refs_2_, bf16[16,128,512]{2,1,0:T(8,128)(2,1)S(1)} %slice_dynamic-update-slice_fusion.refs_6_.refs_3_.refs_2_, ...), custom_call_target="tpu_custom_call" | custom-call | flops 536870912 | bytes 5242880 | tf_op jit(solution)/shard_map/pallas_call | solution.py:71
  108.5 0.8 collective-permute-done.8
  109.3 1.9 %shard_map.84 = f32[1024,256]{1,0:T(8,128)S(1)} custom-call(s32[3]{0:T(128)S(1)} %get-tuple-element.7.refs_0_, bf16[2,1024,128]{2,1,0:T(8,128)(2,1)S(1)} %pad_maximum_fusion.1.refs_1_, bf16[16,128,512]{2,1,0:T(8,128)(2,1)S(1)} %slice_dynamic-update-slice_fusion.refs_6_.refs_3_.refs_2_, f32[1024,512]{1,0:T(8,128)S(1)} %shard_map.83.refs_3_), custom_call_target="tpu_custom_call" | custom-call | flops 134217728 | bytes 3670016 | tf_op jit(solution)/shard_map/pallas_call | solution.py:71
  111.2 15.7 %collective-permute-start.20 = (f32[1024,256]{1,0:T(8,128)S(1)}, f32[1024,256]{1,0:T(8,128)S(1)}, u32[]{:S(2)}, u32[]{:S(2)}) collective-permute-start(f32[1024,256]{1,0:T(8,128)S(1)} %shard_map.84), channel_id=1, source_target_pairs={{0,1},{1,0},{2,3},{3,2},{4,5},{5,4},{6,7},{7,6},{8,9},{9,8},{10,11... | collective-permute-start | bytes 3145736 | tf_op jit(solution)/shard_map/ppermute | solution.py:15
  126.9 2.3 %collective-permute-done.20.refs_4_ = f32[1024,256]{1,0:T(8,128)S(1)} collective-permute-done((f32[1024,256]{1,0:T(8,128)S(1)}, f32[1024,256]{1,0:T(8,128)S(1)}, u32[]{:S(2)}, u32[]{:S(2)}) %collective-permute-start.20) | collective-permute-done | bytes 1048608 | tf_op jit(solution)/shard_map/ppermute | solution.py:15
  129.2 2.9 %shard_map.85 = f32[1024,256]{1,0:T(8,128)} custom-call(s32[3]{0:T(128)S(1)} %get-tuple-element.8.refs_0_, bf16[2,1024,128]{2,1,0:T(8,128)(2,1)S(1)} %pad_maximum_fusion.1.refs_1_, bf16[16,128,512]{2,1,0:T(8,128)(2,1)S(1)} %slice_dynamic-update-slice_fusion.refs_6_.refs_3_.refs_2_, f32[1024,512]{1,0:T(8,128)S(1)} %shard_map.83.refs_3_, ...), custom_call_target="tpu_custom_call" | custom-call | flops 134217728 | bytes 3670016 | tf_op jit(solution)/shard_map/pallas_call | solution.py:71
  (51 shorter events, 1.9 us)
Async XLA Ops:
  0.0 3.7 %copy-start = (bf16[2,512,512]{2,1,0:T(8,128)(2,1)S(1)}, bf16[2,512,512]{2,1,0:T(8,128)(2,1)}, u32[]{:S(2)}) copy-start(bf16[2,512,512]{2,1,0:T(8,128)(2,1)} %param.9) | copy-start | bytes 3145732
  0.0 9.3 %copy-start.2 = (s32[5]{0:T(128)S(1)}, s32[5]{0:T(128)}, u32[]{:S(2)}) copy-start(s32[5]{0:T(128)} %constant.80) | copy-start | bytes 64
  0.0 9.4 %copy-start.1 = (s32[2]{0:T(128)S(1)}, s32[2]{0:T(128)}, u32[]{:S(2)}) copy-start(s32[2]{0:T(128)} %constant.79) | copy-start | bytes 28
  1.4 8.3 %collective-permute-start.9 = (bf16[128,512]{1,0:T(8,128)(2,1)S(1)}, bf16[128,512]{1,0:T(8,128)(2,1)S(1)}, u32[]{:S(2)}, u32[]{:S(2)}) collective-permute-start(bf16[128,512]{1,0:T(8,128)(2,1)S(1)} %fusion.1), channel_id=1, source_target_pairs={{0,0},{2,32},{4,64},{6,96},{8,128},{10,160},{12,192},{14,224},{16,... | collective-permute-start | bytes 393224 | tf_op jit(solution)/shard_map/ppermute | solution.py:27
  5.2 43.7 %collective-permute-start = (bf16[1024,128]{1,0:T(8,128)(2,1)S(1)}, bf16[1024,128]{1,0:T(8,128)(2,1)S(1)}, u32[]{:S(2)}, u32[]{:S(2)}) collective-permute-start(bf16[1024,128]{1,0:T(8,128)(2,1)S(1)} %bitcast.36), channel_id=1, source_target_pairs={{0,16},{16,0},{1,17},{17,1},{2,18},{18,2},{3,19},{19,3},{4,20},{20... | collective-permute-start | bytes 786440 | tf_op jit(solution)/shard_map/ppermute | solution.py:15
  9.8 27.7 %collective-permute-start.10 = (bf16[128,512]{1,0:T(8,128)(2,1)S(1)}, bf16[128,512]{1,0:T(8,128)(2,1)S(1)}, u32[]{:S(2)}, u32[]{:S(2)}) collective-permute-start(bf16[128,512]{1,0:T(8,128)(2,1)S(1)} %collective-permute-done.9), channel_id=1, source_target_pairs={{0,32},{32,64},{64,96},{96,128},{128,160},{160,192},{192,224},{224... | collective-permute-start | bytes 393224 | tf_op jit(solution)/shard_map/ppermute | solution.py:15
  14.5 26.1 %collective-permute-start.11 = (bf16[128,512]{1,0:T(8,128)(2,1)S(1)}, bf16[128,512]{1,0:T(8,128)(2,1)S(1)}, u32[]{:S(2)}, u32[]{:S(2)}) collective-permute-start(bf16[128,512]{1,0:T(8,128)(2,1)S(1)} %collective-permute-done.9), channel_id=1, source_target_pairs={{0,64},{32,96},{64,128},{96,160},{128,192},{160,224},{192,0},{224,... | collective-permute-start | bytes 393224 | tf_op jit(solution)/shard_map/ppermute | solution.py:15
  27.7 26.9 %collective-permute-start.12 = (bf16[128,512]{1,0:T(8,128)(2,1)S(1)}, bf16[128,512]{1,0:T(8,128)(2,1)S(1)}, u32[]{:S(2)}, u32[]{:S(2)}) collective-permute-start(bf16[128,512]{1,0:T(8,128)(2,1)S(1)} %collective-permute-done.9), channel_id=1, source_target_pairs={{0,96},{32,128},{64,160},{96,192},{128,224},{160,0},{192,32},{224,... | collective-permute-start | bytes 393224 | tf_op jit(solution)/shard_map/ppermute | solution.py:15
  35.5 11.4 %collective-permute-start.16 = (bf16[128,512]{1,0:T(8,128)(2,1)S(1)}, bf16[128,512]{1,0:T(8,128)(2,1)S(1)}, u32[]{:S(2)}, u32[]{:S(2)}) collective-permute-start(bf16[128,512]{1,0:T(8,128)(2,1)S(1)} %collective-permute-done.9), channel_id=1, source_target_pairs={{0,224},{32,0},{64,32},{96,64},{128,96},{160,128},{192,160},{224,1... | collective-permute-start | bytes 393224 | tf_op jit(solution)/shard_map/ppermute | solution.py:15
  37.5 20.2 %collective-permute-start.13 = (bf16[128,512]{1,0:T(8,128)(2,1)S(1)}, bf16[128,512]{1,0:T(8,128)(2,1)S(1)}, u32[]{:S(2)}, u32[]{:S(2)}) collective-permute-start(bf16[128,512]{1,0:T(8,128)(2,1)S(1)} %collective-permute-done.9), channel_id=1, source_target_pairs={{0,128},{32,160},{64,192},{96,224},{128,0},{160,32},{192,64},{224,... | collective-permute-start | bytes 393224 | tf_op jit(solution)/shard_map/ppermute | solution.py:15
  40.6 20.5 %collective-permute-start.14 = (bf16[128,512]{1,0:T(8,128)(2,1)S(1)}, bf16[128,512]{1,0:T(8,128)(2,1)S(1)}, u32[]{:S(2)}, u32[]{:S(2)}) collective-permute-start(bf16[128,512]{1,0:T(8,128)(2,1)S(1)} %collective-permute-done.9), channel_id=1, source_target_pairs={{0,160},{32,192},{64,224},{96,0},{128,32},{160,64},{192,96},{224,1... | collective-permute-start | bytes 393224 | tf_op jit(solution)/shard_map/ppermute | solution.py:15
  47.0 18.7 %collective-permute-start.15 = (bf16[128,512]{1,0:T(8,128)(2,1)S(1)}, bf16[128,512]{1,0:T(8,128)(2,1)S(1)}, u32[]{:S(2)}, u32[]{:S(2)}) collective-permute-start(bf16[128,512]{1,0:T(8,128)(2,1)S(1)} %collective-permute-done.9), channel_id=1, source_target_pairs={{0,192},{32,224},{64,0},{96,32},{128,64},{160,96},{192,128},{224,1... | collective-permute-start | bytes 393224 | tf_op jit(solution)/shard_map/ppermute | solution.py:15
  49.0 19.2 %collective-permute-start.17 = (bf16[1,128,512]{2,1,0:T(8,128)(2,1)S(1)}, bf16[1,128,512]{2,1,0:T(8,128)(2,1)S(1)}, u32[]{:S(2)}, u32[]{:S(2)}) collective-permute-start(bf16[1,128,512]{2,1,0:T(8,128)(2,1)S(1)} %bitcast.49), channel_id=1, source_target_pairs={{0,256},{256,0},{1,257},{257,1},{2,258},{258,2},{3,259},{259,3},{4... | collective-permute-start | bytes 393224 | tf_op jit(solution)/shard_map/ppermute | solution.py:15
  54.6 13.6 %collective-permute-start.1 = (bf16[2,1024,128]{2,1,0:T(8,128)(2,1)S(1)}, bf16[2,1024,128]{2,1,0:T(8,128)(2,1)S(1)}, u32[]{:S(2)}, u32[]{:S(2)}) collective-permute-start(bf16[2,1024,128]{2,1,0:T(8,128)(2,1)S(1)} %pad_maximum_fusion.refs_1_), channel_id=1, source_target_pairs={{0,2},{2,4},{4,6},{6,8},{8,10},{10,12},{12,14},{14,0},{1,3},{3,5},... | collective-permute-start | bytes 1572872 | tf_op jit(solution)/shard_map/ppermute | solution.py:15
  57.7 13.5 %collective-permute-start.5 = (bf16[2,1024,128]{2,1,0:T(8,128)(2,1)S(1)}, bf16[2,1024,128]{2,1,0:T(8,128)(2,1)S(1)}, u32[]{:S(2)}, u32[]{:S(2)}) collective-permute-start(bf16[2,1024,128]{2,1,0:T(8,128)(2,1)S(1)} %pad_maximum_fusion.refs_1_), channel_id=1, source_target_pairs={{0,14},{2,0},{4,2},{6,4},{8,6},{10,8},{12,10},{14,12},{1,15},{3,1}... | collective-permute-start | bytes 1572872 | tf_op jit(solution)/shard_map/ppermute | solution.py:15
  61.2 10.0 %collective-permute-start.18 = (bf16[3,128,512]{2,1,0:T(8,128)(2,1)S(1)}, bf16[3,128,512]{2,1,0:T(8,128)(2,1)S(1)}, u32[]{:S(2)}, u32[]{:S(2)}) collective-permute-start(bf16[3,128,512]{2,1,0:T(8,128)(2,1)S(1)} %pad_maximum_fusion.3), channel_id=1, source_target_pairs={{0,256},{256,0},{1,257},{257,1},{2,258},{258,2},{3,259},{259,3},{4... | collective-permute-start | bytes 1179656 | tf_op jit(solution)/shard_map/ppermute | solution.py:15
  65.8 13.3 %collective-permute-start.19 = (bf16[4,128,512]{2,1,0:T(8,128)(2,1)S(1)}, bf16[4,128,512]{2,1,0:T(8,128)(2,1)S(1)}, u32[]{:S(2)}, u32[]{:S(2)}) collective-permute-start(bf16[4,128,512]{2,1,0:T(8,128)(2,1)S(1)} %pad_maximum_fusion.2), channel_id=1, source_target_pairs={{0,256},{256,0},{1,257},{257,1},{2,258},{258,2},{3,259},{259,3},{4... | collective-permute-start | bytes 1572872 | tf_op jit(solution)/shard_map/ppermute | solution.py:15
  68.2 12.0 %collective-permute-start.2 = (bf16[2,1024,128]{2,1,0:T(8,128)(2,1)S(1)}, bf16[2,1024,128]{2,1,0:T(8,128)(2,1)S(1)}, u32[]{:S(2)}, u32[]{:S(2)}) collective-permute-start(bf16[2,1024,128]{2,1,0:T(8,128)(2,1)S(1)} %collective-permute-done.1.refs_2_), channel_id=1, source_target_pairs={{0,2},{2,4},{4,6},{6,8},{8,10},{10,12},{12,14},{14,0},{1,3},{3,5},... | collective-permute-start | bytes 1572872 | tf_op jit(solution)/shard_map/ppermute | solution.py:15
  71.2 13.4 %collective-permute-start.6 = (bf16[2,1024,128]{2,1,0:T(8,128)(2,1)S(1)}, bf16[2,1024,128]{2,1,0:T(8,128)(2,1)S(1)}, u32[]{:S(2)}, u32[]{:S(2)}) collective-permute-start(bf16[2,1024,128]{2,1,0:T(8,128)(2,1)S(1)} %collective-permute-done.5.refs_3_), channel_id=1, source_target_pairs={{0,14},{2,0},{4,2},{6,4},{8,6},{10,8},{12,10},{14,12},{1,15},{3,1}... | collective-permute-start | bytes 1572872 | tf_op jit(solution)/shard_map/ppermute | solution.py:15
  80.2 15.5 %collective-permute-start.3 = (bf16[2,1024,128]{2,1,0:T(8,128)(2,1)S(1)}, bf16[2,1024,128]{2,1,0:T(8,128)(2,1)S(1)}, u32[]{:S(2)}, u32[]{:S(2)}) collective-permute-start(bf16[2,1024,128]{2,1,0:T(8,128)(2,1)S(1)} %collective-permute-done.2.refs_4_), channel_id=1, source_target_pairs={{0,2},{2,4},{4,6},{6,8},{8,10},{10,12},{12,14},{14,0},{1,3},{3,5},... | collective-permute-start | bytes 1572872 | tf_op jit(solution)/shard_map/ppermute | solution.py:15
  84.6 14.4 %collective-permute-start.7 = (bf16[2,1024,128]{2,1,0:T(8,128)(2,1)S(1)}, bf16[2,1024,128]{2,1,0:T(8,128)(2,1)S(1)}, u32[]{:S(2)}, u32[]{:S(2)}) collective-permute-start(bf16[2,1024,128]{2,1,0:T(8,128)(2,1)S(1)} %collective-permute-done.6.refs_5_), channel_id=1, source_target_pairs={{0,14},{2,0},{4,2},{6,4},{8,6},{10,8},{12,10},{14,12},{1,15},{3,1}... | collective-permute-start | bytes 1572872 | tf_op jit(solution)/shard_map/ppermute | solution.py:15
  95.8 12.7 %collective-permute-start.4 = (bf16[1024,128]{1,0:T(8,128)(2,1)S(1)}, bf16[1024,128]{1,0:T(8,128)(2,1)S(1)}, u32[]{:S(2)}, u32[]{:S(2)}) collective-permute-start(bf16[1024,128]{1,0:T(8,128)(2,1)S(1)} %slice_bitcast_fusion.1), channel_id=1, source_target_pairs={{0,2},{2,4},{4,6},{6,8},{8,10},{10,12},{12,14},{14,0},{1,3},{3,5},... | collective-permute-start | bytes 786440 | tf_op jit(solution)/shard_map/ppermute | solution.py:15
  99.0 10.2 %collective-permute-start.8 = (bf16[1024,128]{1,0:T(8,128)(2,1)S(1)}, bf16[1024,128]{1,0:T(8,128)(2,1)S(1)}, u32[]{:S(2)}, u32[]{:S(2)}) collective-permute-start(bf16[1024,128]{1,0:T(8,128)(2,1)S(1)} %slice_bitcast_fusion), channel_id=1, source_target_pairs={{0,14},{2,0},{4,2},{6,4},{8,6},{10,8},{12,10},{14,12},{1,15},{3,1}... | collective-permute-start | bytes 786440 | tf_op jit(solution)/shard_map/ppermute | solution.py:15
  111.2 18.0 %collective-permute-start.20 = (f32[1024,256]{1,0:T(8,128)S(1)}, f32[1024,256]{1,0:T(8,128)S(1)}, u32[]{:S(2)}, u32[]{:S(2)}) collective-permute-start(f32[1024,256]{1,0:T(8,128)S(1)} %shard_map.84), channel_id=1, source_target_pairs={{0,1},{1,0},{2,3},{3,2},{4,5},{5,4},{6,7},{7,6},{8,9},{9,8},{10,11... | collective-permute-start | bytes 3145736 | tf_op jit(solution)/shard_map/ppermute | solution.py:15

commit v3 on v1

v3 whole, which is shorter than its diff:
```python
import jax
import jax.numpy as jnp
from jax import lax
from jax.experimental import pallas as pl
from jax.experimental.pallas import tpu as pltpu
from jax.sharding import Mesh
from jax.sharding import PartitionSpec as P

BLOCK = 512
TOKENS = 4096
XH, Z, XL, Y, C = 2, 8, 2, 8, 2


def transpose_chips(x):
    perm = []
    for xh in range(XH):
        for z in range(Z):
            for xl in range(XL):
                for y in range(Y):
                    src = ((xh * Z + z) * XL + xl) * Y + y
                    dst = ((xl * Z + y) * XL + xh) * Y + z
                    perm.append((src, dst))
    return lax.ppermute(x, ("xh", "z", "xl", "y"), perm)


def swap(x, axis):
    return lax.ppermute(x, axis, [(0, 1), (1, 0)])


def product_kernel(where_ref, act_ref, grad_ref, out_ref):
    xl, half = where_ref[0], where_ref[1]
    cols = out_ref.shape[1]
    at = pl.ds(pl.multiple_of(half * cols, cols), cols)
    total = None
    for pair in range(2):
        act = jnp.concatenate([act_ref[y, pair] for y in range(Y)], axis=1)
        grad = grad_ref[pair ^ xl, :, at]
        part = jnp.dot(act, grad, preferred_element_type=jnp.float32)
        total = part if total is None else total + part
    out_ref[...] = total


def product(where, act_all, grad_all):
    _, _, width, rows = act_all.shape
    cols = grad_all.shape[2] // 2
    tile = 128
    grid_spec = pltpu.PrefetchScalarGridSpec(
        num_scalar_prefetch=1,
        grid=(width // tile,),
        in_specs=[
            pl.BlockSpec((Y, 2, tile, rows), lambda i, where: (0, 0, i, 0)),
            pl.BlockSpec(grad_all.shape, lambda i, where: (0, 0, 0)),
        ],
        out_specs=pl.BlockSpec((tile, cols), lambda i, where: (i, 0)),
    )
    return pl.pallas_call(
        product_kernel,
        grid_spec=grid_spec,
        out_shape=jax.ShapeDtypeStruct((width, cols), jnp.float32),
        compiler_params=pltpu.CompilerParams(
            dimension_semantics=("arbitrary",), vmem_limit_bytes=56 * 1024 * 1024
        ),
        cost_estimate=pl.CostEstimate(
            flops=2 * width * cols * rows * 2 * Y,
            bytes_accessed=act_all.size * 2 + grad_all.size * 2 + width * cols * 4,
            transcendentals=0,
        ),
    )(where, act_all, grad_all)


def per_device(activations, act_basis, gradients, grad_basis):
    rows, act_width = activations.shape
    xl, c = lax.axis_index("xl"), lax.axis_index("c")

    grad_rot = jnp.dot(gradients, grad_basis, preferred_element_type=jnp.float32)
    grad_sq = (grad_rot * grad_rot).astype(jnp.bfloat16)
    own = transpose_chips(grad_sq)

    act_blocks = activations.reshape(rows, act_width // BLOCK, BLOCK)
    act_rot = jnp.einsum("tbk,bkj->bjt", act_blocks, act_basis, preferred_element_type=jnp.float32)
    act_sq = (act_rot * act_rot).astype(jnp.bfloat16).reshape(act_width, rows)
    act_pair = jnp.stack([act_sq, swap(act_sq, "xl")])
    act_all = lax.all_gather(act_pair, "y", axis=0)

    copies = jnp.broadcast_to(own, (XH * Z,) + own.shape)
    grad_all = lax.all_to_all(copies, ("xh", "z"), 0, 0, tiled=True)
    grad_all = grad_all.reshape(XH, Z * rows, gradients.shape[1])

    other = product(jnp.stack([xl, 1 - c]), act_all, grad_all)
    got = swap(other, "c")
    mine = product(jnp.stack([xl, c]), act_all, grad_all)
    return (mine + got) / TOKENS


def solution(mesh):
    chips = Mesh(mesh.devices.reshape(XH, Z, XL, Y, C), ("xh", "z", "xl", "y", "c"))
    feat, tok = ("xh", "z"), ("xl", "y", "c")
    return jax.shard_map(
        per_device,
        mesh=chips,
        in_specs=(P(tok, feat), P(feat, None, None), P(tok, feat), P(feat, None)),
        out_specs=P(feat, tok),
        check_vma=False,
    )
```

time: 134 us -> 136 us (1.015)
  starting transfers between devices: 71.6 us -> 46 us
  waiting for transfers between devices: 32.7 us -> 49.2 us
  Pallas kernels: 8.33 us -> 16.8 us
  other arithmetic: 2.23 us -> 4.5 us
    ppermute x12 -> x2, starting transfers between devices: 70.9 us -> 11.6 us  [swap(): return lax.ppermute(x, axis, [(0, 1), (1, 0)])]
    all_to_all x0 -> x1, waiting for transfers between devices: none -> 45.4 us  [per_device(): grad_all = lax.all_to_all(copies, ('xh', 'z'), 0, 0, tiled=True)]
    all_to_all x0 -> x1, starting transfers between devices: none -> 33.7 us  [per_device(): grad_all = lax.all_to_all(copies, ('xh', 'z'), 0, 0, tiled=True)]
    ppermute x12 -> x2, waiting for transfers between devices: 32.6 us -> 3.75 us  [swap(): return lax.ppermute(x, axis, [(0, 1), (1, 0)])]
    pallas_call x2, Pallas kernels: 8.33 us -> 16.8 us  [product(): pl.pallas_call(product_kernel, grid_spec=grid_spec, out_shape=jax.ShapeDt...]
    broadcast_in_dim x0 -> x1, local copies, waits for them, and re-layouts: none -> 1.53 us  [per_device(): copies = jnp.broadcast_to(own, (XH * Z,) + own.shape)]
    unnamed x25 -> x8, local copies, waits for them, and re-layouts: 3.57 us -> 2.55 us
  transfers between devices with their start and end apart: 14 -> 5, of which waited for: 4 -> 2; matrix products, arithmetic and copies ran while one was open for 1% -> 2% of each run, Pallas kernels for 3% -> 6%
where the time goes in v3:
time: 136 us
  waiting for transfers between devices  49.2 us (36%)
  starting transfers between devices  46 us (34%)
  Pallas kernels  16.8 us (12%)
  between operations  13.5 us (10%)
  other arithmetic  4.5 us (3%)
  local copies, waits for them, and re-layouts  4.08 us (3%)
  matrix products  1.71 us (1%)
    all_to_all x1, waiting for transfers between devices, per_device(): grad_all = lax.all_to_all(copies, ('xh', 'z'), 0, 0, tiled=True)  45.4 us
    all_to_all x1, starting transfers between devices, per_device(): grad_all = lax.all_to_all(copies, ('xh', 'z'), 0, 0, tiled=True)  33.7 us
    pallas_call x2, Pallas kernels, product(): pl.pallas_call(product_kernel, grid_spec=grid_spec, out_shape=jax.ShapeDt...  16.8 us
    ppermute x2, starting transfers between devices, swap(): return lax.ppermute(x, axis, [(0, 1), (1, 0)])  11.6 us
    ppermute x2, waiting for transfers between devices, swap(): return lax.ppermute(x, axis, [(0, 1), (1, 0)])  3.75 us
  transfers between devices with their start and end apart: 5, of which 2 were waited for; matrix products, arithmetic and copies ran while one was open for 2% of the time, Pallas kernels for 6%

profile of v3, /device:TPU:1, one launch (start us, length us, event | category | flops | bytes accessed | tf_op | source)
XLA Modules:
  0.0 135.8 jit_solution(9988619575113414488)
XLA Ops:
  6.5 0.0 copy-start
  6.5 0.0 copy-start.2
  6.5 0.0 copy-start.3
  6.5 0.0 all-gather.3.cloned.1.call-start
  6.5 1.2 copy-done
  7.8 1.5 %fusion = bf16[2,512,128]{2,1,0:T(8,128)(2,1)S(1)} fusion(bf16[2,512,512]{2,1,0:T(8,128)(2,1)S(1)} %copy-done, bf16[16,2,8,512]{3,2,1,0:T(8,128)(2,1)} %bitcast.21), kind=kOutput, calls=%fused_computation.1 | convolution fusion | flops 134479872 | bytes 1572864 | tf_op jit(solution)/shard_map/tbk,bkj->bjt/dot_general | solution.py:80
  9.2 3.9 %collective-permute-start = (bf16[1024,128]{1,0:T(8,128)(2,1)S(1)}, bf16[1024,128]{1,0:T(8,128)(2,1)S(1)}, u32[]{:S(2)}, u32[]{:S(2)}) collective-permute-start(bf16[1024,128]{1,0:T(8,128)(2,1)S(1)} %bitcast.19), channel_id=1, source_target_pairs={{0,16},{16,0},{1,17},{17,1},{2,18},{18,2},{3,19},{19,3},{4,20},{20... | collective-permute-start | bytes 786440 | tf_op jit(solution)/shard_map/ppermute | solution.py:27
  13.2 3.7 %collective-permute-done = bf16[1024,128]{1,0:T(8,128)(2,1)S(1)} collective-permute-done((bf16[1024,128]{1,0:T(8,128)(2,1)S(1)}, bf16[1024,128]{1,0:T(8,128)(2,1)S(1)}, u32[]{:S(2)}, u32[]{:S(2)}) %collective-permute-start) | collective-permute-done | bytes 262176 | tf_op jit(solution)/shard_map/ppermute | solution.py:27
  16.9 0.8 pad_maximum_fusion
  17.8 0.0 all-gather.3.cloned.1.call-update
  17.8 0.0 copy-done.2
  17.8 0.0 copy-done.3
  17.8 0.2 fusion.1
  18.1 0.7 collective-permute-start.1
  18.7 0.0 collective-permute-done.1
  18.8 1.5 %broadcast_in_dim.3 = bf16[16,128,512]{2,1,0:T(8,128)(2,1)} broadcast(bf16[128,512]{1,0:T(8,128)(2,1)S(1)} %collective-permute-done.1), dimensions={1,2} | broadcast | bytes 2228224 | tf_op jit(solution)/shard_map/broadcast_in_dim | solution.py:85
  20.3 33.7 %all-to-all-start = ((bf16[16,128,512]{2,1,0:T(8,128)(2,1)}), bf16[16,128,512]{2,1,0:T(8,128)(2,1)S(1)}, u32[]{:S(2)}, u32[]{:S(2)}) async-start(bf16[16,128,512]{2,1,0:T(8,128)(2,1)} %broadcast_in_dim.3), calls=%async_computation | async-start | bytes 4194304 | tf_op jit(solution)/shard_map/all_to_all | solution.py:86
  54.0 0.7 pad_add_fusion.1.where_ref
  54.7 45.4 %all-to-all-done = bf16[16,128,512]{2,1,0:T(8,128)(2,1)S(1)} async-done(((bf16[16,128,512]{2,1,0:T(8,128)(2,1)}), bf16[16,128,512]{2,1,0:T(8,128)(2,1)S(1)}, u32[]{:S(2)}, u32[]{:S(2)}) %all-to-all-start) | async-done | bytes 2097184 | tf_op jit(solution)/shard_map/all_to_all | solution.py:86
  100.1 0.0 copy-start.1
  100.1 0.0 all-gather.3.cloned.1.call-done
  100.1 1.3 copy-done.1
  101.5 8.4 %shard_map.47 = f32[1024,256]{1,0:T(8,128)} custom-call(s32[2]{0:T(128)} %pad_add_fusion.1.where_ref, bf16[8,2,1024,128]{3,2,1,0:T(8,128)(2,1)} %bitcast.17, bf16[2,1024,512]{2,1,0:T(8,128)(2,1)} %bitcast.15), custom_call_target="tpu_custom_call" | custom-call | flops 1073741824 | bytes 7340032 | tf_op jit(solution)/shard_map/pallas_call | solution.py:56
  109.8 7.7 %collective-permute-start.2 = (f32[1024,256]{1,0:T(8,128)}, f32[1024,256]{1,0:T(8,128)S(1)}, u32[]{:S(2)}, u32[]{:S(2)}) collective-permute-start(f32[1024,256]{1,0:T(8,128)} %shard_map.47), channel_id=1, source_target_pairs={{0,1},{1,0},{2,3},{3,2},{4,5},{5,4},{6,7},{7,6},{8,9},{9,8},{10,11... | collective-permute-start | bytes 3145736 | tf_op jit(solution)/shard_map/ppermute | solution.py:27
  117.5 0.7 pad_add_fusion.where_ref
  118.2 8.4 %shard_map.46 = f32[1024,256]{1,0:T(8,128)} custom-call(s32[2]{0:T(128)} %pad_add_fusion.where_ref, bf16[8,2,1024,128]{3,2,1,0:T(8,128)(2,1)} %bitcast.18, bf16[2,1024,512]{2,1,0:T(8,128)(2,1)} %bitcast.16), custom_call_target="tpu_custom_call" | custom-call | flops 1073741824 | bytes 7340032 | tf_op jit(solution)/shard_map/pallas_call | solution.py:56
  126.6 0.0 collective-permute-done.2
  126.6 2.3 %add_multiply_fusion = f32[1024,256]{1,0:T(8,128)} fusion(f32[1024,256]{1,0:T(8,128)} %shard_map.46, f32[1024,256]{1,0:T(8,128)S(1)} %collective-permute-done.2), kind=kLoop, calls=%fused_computation.4 | loop fusion | flops 524288 | bytes 3145728 | tf_op jit(solution)/shard_map/div | solution.py:92
Async XLA Ops:
  6.5 1.2 copy-start
  6.5 11.3 %copy-start.2 = (bf16[512,512]{1,0:T(8,128)(2,1)S(1)}, bf16[512,512]{1,0:T(8,128)(2,1)}, u32[]{:S(2)}) copy-start(bf16[512,512]{1,0:T(8,128)(2,1)} %param.7) | copy-start | bytes 1572868
  6.5 11.3 %copy-start.3 = (bf16[128,512]{1,0:T(8,128)(2,1)S(1)}, bf16[128,512]{1,0:T(8,128)(2,1)}, u32[]{:S(2)}) copy-start(bf16[128,512]{1,0:T(8,128)(2,1)} %param.6) | copy-start | bytes 393220
  6.5 93.6 %all-gather.3.cloned.1.call-start = ((), (), s32[]{:S(2)}) async-start(), calls=%async_computation.1 | async-start | bytes 4718592 | tf_op jit(solution)/shard_map/all_gather | solution.py:83
  9.2 7.7 %collective-permute-start = (bf16[1024,128]{1,0:T(8,128)(2,1)S(1)}, bf16[1024,128]{1,0:T(8,128)(2,1)S(1)}, u32[]{:S(2)}, u32[]{:S(2)}) collective-permute-start(bf16[1024,128]{1,0:T(8,128)(2,1)S(1)} %bitcast.19), channel_id=1, source_target_pairs={{0,16},{16,0},{1,17},{17,1},{2,18},{18,2},{3,19},{19,3},{4,20},{20... | collective-permute-start | bytes 786440 | tf_op jit(solution)/shard_map/ppermute | solution.py:27
  18.1 0.7 collective-permute-start.1
  20.3 79.9 %all-to-all-start = ((bf16[16,128,512]{2,1,0:T(8,128)(2,1)}), bf16[16,128,512]{2,1,0:T(8,128)(2,1)S(1)}, u32[]{:S(2)}, u32[]{:S(2)}) async-start(bf16[16,128,512]{2,1,0:T(8,128)(2,1)} %broadcast_in_dim.3), calls=%async_computation | async-start | bytes 4194304 | tf_op jit(solution)/shard_map/all_to_all | solution.py:86
  100.1 1.3 copy-start.1
  109.8 16.8 %collective-permute-start.2 = (f32[1024,256]{1,0:T(8,128)}, f32[1024,256]{1,0:T(8,128)S(1)}, u32[]{:S(2)}, u32[]{:S(2)}) collective-permute-start(f32[1024,256]{1,0:T(8,128)} %shard_map.47), channel_id=1, source_target_pairs={{0,1},{1,0},{2,3},{3,2},{4,5},{5,4},{6,7},{7,6},{8,9},{9,8},{10,11... | collective-permute-start | bytes 3145736 | tf_op jit(solution)/shard_map/ppermute | solution.py:27
Sparse Core Ops, SparseCore 0:
  17.9 67.7 all-gather.2

commit v4 on v2

v4 whole, which is shorter than its diff:
```python
import jax
import jax.numpy as jnp
from jax import lax
from jax.experimental import pallas as pl
from jax.experimental.pallas import tpu as pltpu
from jax.sharding import Mesh
from jax.sharding import PartitionSpec as P

BLOCK = 512
TOKENS = 4096
XH, Z, XL, Y, C = 2, 8, 2, 8, 2


def shift(x, axis, size, step):
    return lax.ppermute(x, axis, [(i, (i + step) % size) for i in range(size)])


def transpose_chips(x):
    perm = []
    for xh in range(XH):
        for z in range(Z):
            for xl in range(XL):
                for y in range(Y):
                    src = ((xh * Z + z) * XL + xl) * Y + y
                    dst = ((xl * Z + y) * XL + xh) * Y + z
                    perm.append((src, dst))
    return lax.ppermute(x, ("xh", "z", "xl", "y"), perm)


def vmem():
    return pl.BlockSpec(memory_space=pltpu.VMEM)


def products(places, pieces, grad_all, halved=False, acc=None, add=None, scale=None):
    _, width, rows = pieces[0].shape
    cols = grad_all.shape[2] // 2 if halved else grad_all.shape[2]
    n = len(pieces)
    extra = [] if acc is None else [acc]
    extra += [] if add is None else [add]
    tile = width // 2

    def kernel(*refs):
        places_ref, piece_refs, grad_ref, out_ref = refs[0], refs[1 : 1 + n], refs[1 + n], refs[-1]
        where = slice(None)
        if halved:
            where = pl.ds(pl.multiple_of(places_ref[2 * n] * cols, cols), cols)
        grad = jnp.concatenate([grad_ref[places_ref[i], :, where] for i in range(2 * n)], axis=0)
        for t in range(width // tile):
            at = slice(t * tile, (t + 1) * tile)
            lhs = jnp.concatenate([ref[k, at] for ref in piece_refs for k in range(2)], axis=1)
            total = jnp.dot(lhs, grad, preferred_element_type=jnp.float32)
            if acc is not None:
                total += refs[2 + n][at, where]
            if add is not None:
                total += refs[3 + n][at]
            out_ref[at] = total if scale is None else total * scale

    def size(a):
        return a.size * a.dtype.itemsize

    return pl.pallas_call(
        kernel,
        in_specs=[pl.BlockSpec(memory_space=pltpu.SMEM)] + [vmem()] * (n + 1 + len(extra)),
        out_specs=vmem(),
        out_shape=jax.ShapeDtypeStruct((width, cols), jnp.float32),
        compiler_params=pltpu.CompilerParams(vmem_limit_bytes=24 * 1024 * 1024),
        cost_estimate=pl.CostEstimate(
            flops=2 * width * cols * rows * 2 * n,
            bytes_accessed=sum(map(size, pieces)) + size(grad_all) + width * cols * 4,
            transcendentals=0,
        ),
    )(places, *pieces, grad_all, *extra)


def per_device(activations, act_basis, gradients, grad_basis):
    xl, y, c = (lax.axis_index(a) for a in ("xl", "y", "c"))
    rows, act_width = activations.shape

    grad_rot = jnp.dot(gradients, grad_basis, preferred_element_type=jnp.float32)
    grad_sq = (grad_rot * grad_rot).astype(jnp.bfloat16)
    activations, grad_sq = lax.optimization_barrier((activations, grad_sq))
    own = transpose_chips(grad_sq)

    act_blocks = activations.reshape(rows, act_width // BLOCK, BLOCK)
    act_rot = jnp.einsum("tbk,bkj->bjt", act_blocks, act_basis, preferred_element_type=jnp.float32)
    act_sq = (act_rot * act_rot).astype(jnp.bfloat16).reshape(act_width, rows)
    pair = jnp.stack([act_sq, shift(act_sq, "xl", XL, 1)])
    up = [pair]
    down = [pair]
    for _ in range(3):
        up.append(shift(up[-1], "y", Y, 1))
        down.append(shift(down[-1], "y", Y, -1))
    last = jnp.stack([shift(up[3][0], "y", Y, 1), shift(down[3][1], "y", Y, -1)])

    own, _ = lax.optimization_barrier((own, pair))
    copies = jnp.broadcast_to(own, (XH * Z,) + own.shape)
    grad_all = lax.all_to_all(copies, ("xh", "z"), 0, 0, tiled=True)
    grad_all = grad_all.reshape(XH * Z, rows, gradients.shape[1])

    def places(offsets, half=None):
        at = [(k ^ xl) * Y + (y + Y - d) % Y for d in offsets for k in range(2)]
        return jnp.stack(at + ([] if half is None else [half])).astype(jnp.int32)

    first = products(places([0, 1, -1, 2, -2]), [pair, up[1], down[1], up[2], down[2]], grad_all)
    second = products(places([3, -3]), [up[3], down[3]], grad_all, acc=first)
    other = products(places([4], 1 - c), [last], grad_all, True, acc=second)
    got = shift(other, "c", C, 1)
    return products(places([4], c), [last], grad_all, True, acc=second, add=got, scale=1.0 / TOKENS)


def solution(mesh):
    chips = Mesh(mesh.devices.reshape(XH, Z, XL, Y, C), ("xh", "z", "xl", "y", "c"))
    feat, tok = ("xh", "z"), ("xl", "y", "c")
    return jax.shard_map(
        per_device,
        mesh=chips,
        in_specs=(P(tok, feat), P(feat, None, None), P(tok, feat), P(feat, None)),
        out_specs=P(feat, tok),
        check_vma=False,
    )
```

time: 133 us -> 119 us (0.89)
  the two profiles are of different devices: /device:TPU:65 before, /device:TPU:1 now
where the time goes in v4:
time: 119 us; the launch traced here: 118 us
  starting transfers between devices  64.2 us (54%)
  waiting for transfers between devices  30.4 us (26%)
  local copies, waits for them, and re-layouts  11.7 us (10%)
  Pallas kernels  6.01 us (5%)
  other arithmetic  2.95 us (2%)
  matrix products  2.68 us (2%)
    ppermute x10, starting transfers between devices, shift(): return lax.ppermute(x, axis, [(i, (i + step) % size) for i in range(size)])  36.8 us
    ppermute x10, waiting for transfers between devices, shift(): return lax.ppermute(x, axis, [(i, (i + step) % size) for i in range(size)])  30.4 us
    all_to_all x1, starting transfers between devices, per_device(): grad_all = lax.all_to_all(copies, ('xh', 'z'), 0, 0, tiled=True)  26.7 us
    unnamed x30, local copies, waits for them, and re-layouts  9.2 us
    pallas_call x4, Pallas kernels, products(): pl.pallas_call(kernel, in_specs=[pl.BlockSpec(memory_space=pltpu.SMEM)] +...  6.01 us
  transfers between devices with their start and end apart: 12, of which 6 were waited for; matrix products, arithmetic and copies ran while one was open for 3% of the time, Pallas kernels for 0%

profile of v4, /device:TPU:1, one launch (start us, length us, event | category | flops | bytes accessed | tf_op | source)
XLA Modules:
  0.0 118.3 jit_solution(2487659332882972053)
XLA Ops:
  0.0 1.4 %fusion.2 = bf16[128,512]{1,0:T(8,128)(2,1)S(1)} fusion(bf16[128,512]{1,0:T(8,128)(2,1)} %param.6, bf16[512,512]{1,0:T(8,128)(2,1)} %param.7), kind=kOutput, calls=%fused_computation.4 | convolution fusion | flops 67239936 | bytes 786432 | tf_op jit(solution)/shard_map/dot_general | solution.py:79
  1.4 1.3 %fusion.1 = bf16[2,512,128]{1,2,0:T(8,128)(2,1)S(1)} fusion(bf16[2,512,512]{2,1,0:T(8,128)(2,1)S(1)} %copy-done, bf16[16,2,8,512]{3,2,1,0:T(8,128)(2,1)} %bitcast.38), kind=kOutput, calls=%fused_computation.3 | convolution fusion | flops 134479872 | bytes 1572864 | tf_op jit(solution)/shard_map/tbk,bkj->bjt/dot_general | solution.py:85
  2.9 3.9 %collective-permute-start = (bf16[1024,128]{1,0:T(8,128)(2,1)S(1)}, bf16[1024,128]{1,0:T(8,128)(2,1)S(1)}, u32[]{:S(2)}, u32[]{:S(2)}) collective-permute-start(bf16[1024,128]{1,0:T(8,128)(2,1)S(1)} %bitcast.36), channel_id=1, source_target_pairs={{0,16},{16,0},{1,17},{17,1},{2,18},{18,2},{3,19},{19,3},{4,20},{20... | collective-permute-start | bytes 786440 | tf_op jit(solution)/shard_map/ppermute | solution.py:15
  7.5 3.1 %collective-permute-done = bf16[1024,128]{1,0:T(8,128)(2,1)S(1)} collective-permute-done((bf16[1024,128]{1,0:T(8,128)(2,1)S(1)}, bf16[1024,128]{1,0:T(8,128)(2,1)S(1)}, u32[]{:S(2)}, u32[]{:S(2)}) %collective-permute-start) | collective-permute-done | bytes 262176 | tf_op jit(solution)/shard_map/ppermute | solution.py:15
  10.6 0.8 pad_maximum_fusion.refs_1_
  11.4 1.5 %broadcast_in_dim.3 = bf16[16,128,512]{2,1,0:T(8,128)(2,1)} broadcast(bf16[128,512]{1,0:T(8,128)(2,1)S(1)} %collective-permute-done.9), dimensions={1,2} | broadcast | bytes 2228224 | tf_op jit(solution)/shard_map/broadcast_in_dim | solution.py:96
  13.0 26.7 %all-to-all-start = ((bf16[16,128,512]{2,1,0:T(8,128)(2,1)}), bf16[16,128,512]{2,1,0:T(8,128)(2,1)S(1)}, u32[]{:S(2)}, u32[]{:S(2)}) async-start(bf16[16,128,512]{2,1,0:T(8,128)(2,1)} %broadcast_in_dim.3), calls=%async_computation | async-start | bytes 4194304 | tf_op jit(solution)/shard_map/all_to_all | solution.py:97
  39.7 2.6 %collective-permute-start.5 = (bf16[2,1024,128]{2,1,0:T(8,128)(2,1)}, bf16[2,1024,128]{2,1,0:T(8,128)(2,1)S(1)}, u32[]{:S(2)}, u32[]{:S(2)}) collective-permute-start(bf16[2,1024,128]{2,1,0:T(8,128)(2,1)} %pad_maximum_fusion.refs_1_), channel_id=1, source_target_pairs={{0,14},{2,0},{4,2},{6,4},{8,6},{10,8},{12,10},{14,12},{1,15},{3,1}... | collective-permute-start | bytes 1572872 | tf_op jit(solution)/shard_map/ppermute | solution.py:15
  42.3 2.7 %collective-permute-start.1 = (bf16[2,1024,128]{2,1,0:T(8,128)(2,1)}, bf16[2,1024,128]{2,1,0:T(8,128)(2,1)S(1)}, u32[]{:S(2)}, u32[]{:S(2)}) collective-permute-start(bf16[2,1024,128]{2,1,0:T(8,128)(2,1)} %pad_maximum_fusion.refs_1_), channel_id=1, source_target_pairs={{0,2},{2,4},{4,6},{6,8},{8,10},{10,12},{12,14},{14,0},{1,3},{3,5},... | collective-permute-start | bytes 1572872 | tf_op jit(solution)/shard_map/ppermute | solution.py:15
  45.0 8.5 %collective-permute-done.5.refs_3_ = bf16[2,1024,128]{2,1,0:T(8,128)(2,1)S(1)} collective-permute-done((bf16[2,1024,128]{2,1,0:T(8,128)(2,1)}, bf16[2,1024,128]{2,1,0:T(8,128)(2,1)S(1)}, u32[]{:S(2)}, u32[]{:S(2)}) %collective-permute-start.5) | collective-permute-done | bytes 524320 | tf_op jit(solution)/shard_map/ppermute | solution.py:15
  53.5 3.7 %collective-permute-start.6 = (bf16[2,1024,128]{2,1,0:T(8,128)(2,1)S(1)}, bf16[2,1024,128]{2,1,0:T(8,128)(2,1)S(1)}, u32[]{:S(2)}, u32[]{:S(2)}) collective-permute-start(bf16[2,1024,128]{2,1,0:T(8,128)(2,1)S(1)} %collective-permute-done.5.refs_3_), channel_id=1, source_target_pairs={{0,14},{2,0},{4,2},{6,4},{8,6},{10,8},{12,10},{14,12},{1,15},{3,1}... | collective-permute-start | bytes 1572872 | tf_op jit(solution)/shard_map/ppermute | solution.py:15
  58.1 1.9 %collective-permute-start.2 = (bf16[2,1024,128]{2,1,0:T(8,128)(2,1)S(1)}, bf16[2,1024,128]{2,1,0:T(8,128)(2,1)S(1)}, u32[]{:S(2)}, u32[]{:S(2)}) collective-permute-start(bf16[2,1024,128]{2,1,0:T(8,128)(2,1)S(1)} %collective-permute-done.1.refs_2_), channel_id=1, source_target_pairs={{0,2},{2,4},{4,6},{6,8},{8,10},{10,12},{12,14},{14,0},{1,3},{3,5},... | collective-permute-start | bytes 1572872 | tf_op jit(solution)/shard_map/ppermute | solution.py:15
  60.8 5.4 %collective-permute-done.6.refs_5_ = bf16[2,1024,128]{2,1,0:T(8,128)(2,1)S(1)} collective-permute-done((bf16[2,1024,128]{2,1,0:T(8,128)(2,1)S(1)}, bf16[2,1024,128]{2,1,0:T(8,128)(2,1)S(1)}, u32[]{:S(2)}, u32[]{:S(2)}) %collective-permute-start.6) | collective-permute-done | bytes 524320 | tf_op jit(solution)/shard_map/ppermute | solution.py:15
  66.2 4.9 %collective-permute-start.7 = (bf16[2,1024,128]{2,1,0:T(8,128)(2,1)S(1)}, bf16[2,1024,128]{2,1,0:T(8,128)(2,1)S(1)}, u32[]{:S(2)}, u32[]{:S(2)}) collective-permute-start(bf16[2,1024,128]{2,1,0:T(8,128)(2,1)S(1)} %collective-permute-done.6.refs_5_), channel_id=1, source_target_pairs={{0,14},{2,0},{4,2},{6,4},{8,6},{10,8},{12,10},{14,12},{1,15},{3,1}... | collective-permute-start | bytes 1572872 | tf_op jit(solution)/shard_map/ppermute | solution.py:15
  71.9 1.9 %collective-permute-start.3 = (bf16[2,1024,128]{2,1,0:T(8,128)(2,1)S(1)}, bf16[2,1024,128]{2,1,0:T(8,128)(2,1)S(1)}, u32[]{:S(2)}, u32[]{:S(2)}) collective-permute-start(bf16[2,1024,128]{2,1,0:T(8,128)(2,1)S(1)} %collective-permute-done.2.refs_4_), channel_id=1, source_target_pairs={{0,2},{2,4},{4,6},{6,8},{8,10},{10,12},{12,14},{14,0},{1,3},{3,5},... | collective-permute-start | bytes 1572872 | tf_op jit(solution)/shard_map/ppermute | solution.py:15
  73.8 4.8 %collective-permute-done.7.refs_2_ = bf16[2,1024,128]{2,1,0:T(8,128)(2,1)S(1)} collective-permute-done((bf16[2,1024,128]{2,1,0:T(8,128)(2,1)S(1)}, bf16[2,1024,128]{2,1,0:T(8,128)(2,1)S(1)}, u32[]{:S(2)}, u32[]{:S(2)}) %collective-permute-start.7) | collective-permute-done | bytes 524320 | tf_op jit(solution)/shard_map/ppermute | solution.py:15
  79.5 5.3 %collective-permute-start.8 = (bf16[1024,128]{1,0:T(8,128)(2,1)S(1)}, bf16[1024,128]{1,0:T(8,128)(2,1)}, u32[]{:S(2)}, u32[]{:S(2)}) collective-permute-start(bf16[1024,128]{1,0:T(8,128)(2,1)S(1)} %slice_bitcast_fusion), channel_id=1, source_target_pairs={{0,14},{2,0},{4,2},{6,4},{8,6},{10,8},{12,10},{14,12},{1,15},{3,1}... | collective-permute-start | bytes 786440 | tf_op jit(solution)/shard_map/ppermute | solution.py:15
  85.5 0.8 copy-done.5
  86.3 1.9 %collective-permute-start.4 = (bf16[1024,128]{1,0:T(8,128)(2,1)}, bf16[1024,128]{1,0:T(8,128)(2,1)}, u32[]{:S(2)}, u32[]{:S(2)}) collective-permute-start(bf16[1024,128]{1,0:T(8,128)(2,1)} %slice_bitcast_fusion.1), channel_id=1, source_target_pairs={{0,2},{2,4},{4,6},{6,8},{8,10},{10,12},{12,14},{14,0},{1,3},{3,5},... | collective-permute-start | bytes 786440 | tf_op jit(solution)/shard_map/ppermute | solution.py:15
  88.6 6.4 %collective-permute-done.4 = bf16[1024,128]{1,0:T(8,128)(2,1)} collective-permute-done((bf16[1024,128]{1,0:T(8,128)(2,1)}, bf16[1024,128]{1,0:T(8,128)(2,1)}, u32[]{:S(2)}, u32[]{:S(2)}) %collective-permute-start.4) | collective-permute-done | bytes 262176 | tf_op jit(solution)/shard_map/ppermute | solution.py:15
  94.9 1.9 %pad_maximum_fusion.1.refs_1_ = bf16[2,1024,128]{2,1,0:T(8,128)(2,1)} fusion(bf16[1,1024,128]{2,1,0:T(8,128)(2,1)} %bitcast.10, bf16[1,1024,128]{2,1,0:T(8,128)(2,1)} %bitcast.8), kind=kLoop, calls=%fused_computation.6 | loop fusion | flops 262144 | bytes 1048576 | tf_op jit(solution)/shard_map/stack | solution.py:93
  96.8 1.0 copy-done.2
  97.9 1.0 copy-done.8
  98.9 1.0 copy-done.10
  100.0 1.0 copy-done.12
  101.0 1.0 copy-done.14
  102.0 2.1 %shard_map.46.refs_4_ = f32[1024,512]{1,0:T(8,128)S(1)} custom-call(s32[10]{0:T(128)S(1)} %stack.107.refs_0_, bf16[2,1024,128]{2,1,0:T(8,128)(2,1)S(1)} %copy-done.2, bf16[2,1024,128]{2,1,0:T(8,128)(2,1)S(1)} %copy-done.10, bf16[2,1024,128]{2,1,0:T(8,128)(2,1)S(1)} %copy-done.8, bf16[2,1024,128]{2,1,0:T(8,128)(2,1)S(1)} %copy-done.14, ...), custom_call_target="tpu_custom_call" | custom-call | flops 1342177280 | bytes 6815744 | tf_op jit(solution)/shard_map/pallas_call | solution.py:61
  104.1 1.3 %shard_map.47.refs_3_ = f32[1024,512]{1,0:T(8,128)S(1)} custom-call(s32[4]{0:T(128)S(1)} %pad_add_fusion.2.refs_0_, bf16[2,1024,128]{2,1,0:T(8,128)(2,1)S(1)} %copy-done.6, bf16[2,1024,128]{2,1,0:T(8,128)(2,1)S(1)} %copy-done.4, bf16[16,128,512]{2,1,0:T(8,128)(2,1)S(1)} %all-to-all-done.refs_6_.refs_3_.refs_2_, f32[1024,512]{1,0:T(8,128)S(1)} %shard_map.46.refs_4_), custom_call_target="tpu_custom_call" | custom-call | flops 536870912 | bytes 5242880 | tf_op jit(solution)/shard_map/pallas_call | solution.py:61
  105.4 0.8 shard_map.48
  106.3 7.9 %collective-permute-start.10 = (f32[1024,256]{1,0:T(8,128)S(1)}, f32[1024,256]{1,0:T(8,128)S(1)}, u32[]{:S(2)}, u32[]{:S(2)}) collective-permute-start(f32[1024,256]{1,0:T(8,128)S(1)} %shard_map.48), channel_id=1, source_target_pairs={{0,1},{1,0},{2,3},{3,2},{4,5},{5,4},{6,7},{7,6},{8,9},{9,8},{10,11... | collective-permute-start | bytes 3145736 | tf_op jit(solution)/shard_map/ppermute | solution.py:15
  114.2 2.2 %collective-permute-done.10.refs_4_ = f32[1024,256]{1,0:T(8,128)S(1)} collective-permute-done((f32[1024,256]{1,0:T(8,128)S(1)}, f32[1024,256]{1,0:T(8,128)S(1)}, u32[]{:S(2)}, u32[]{:S(2)}) %collective-permute-start.10) | collective-permute-done | bytes 1048608 | tf_op jit(solution)/shard_map/ppermute | solution.py:15
  116.4 1.9 %shard_map.49 = f32[1024,256]{1,0:T(8,128)} custom-call(s32[3]{0:T(128)S(1)} %pad_add_fusion.refs_0_, bf16[2,1024,128]{2,1,0:T(8,128)(2,1)S(1)} %copy-done.1, bf16[16,128,512]{2,1,0:T(8,128)(2,1)S(1)} %all-to-all-done.refs_6_.refs_3_.refs_2_, f32[1024,512]{1,0:T(8,128)S(1)} %shard_map.47.refs_3_, f32[1024,256]{1,0:T(8,128)S(1)} %collective-permute-done.10.refs_4_), custom_call_target="tpu_custom_call" | custom-call | flops 134217728 | bytes 3670016 | tf_op jit(solution)/shard_map/pallas_call | solution.py:61
  (38 shorter events, 5.1 us)
Async XLA Ops:
  0.0 1.4 %copy-start = (bf16[2,512,512]{2,1,0:T(8,128)(2,1)S(1)}, bf16[2,512,512]{2,1,0:T(8,128)(2,1)}, u32[]{:S(2)}) copy-start(bf16[2,512,512]{2,1,0:T(8,128)(2,1)} %param.5) | copy-start | bytes 3145732
  2.9 7.7 %collective-permute-start = (bf16[1024,128]{1,0:T(8,128)(2,1)S(1)}, bf16[1024,128]{1,0:T(8,128)(2,1)S(1)}, u32[]{:S(2)}, u32[]{:S(2)}) collective-permute-start(bf16[1024,128]{1,0:T(8,128)(2,1)S(1)} %bitcast.36), channel_id=1, source_target_pairs={{0,16},{16,0},{1,17},{17,1},{2,18},{18,2},{3,19},{19,3},{4,20},{20... | collective-permute-start | bytes 786440 | tf_op jit(solution)/shard_map/ppermute | solution.py:15
  6.8 4.6 %collective-permute-start.9 = (bf16[128,512]{1,0:T(8,128)(2,1)S(1)}, bf16[128,512]{1,0:T(8,128)(2,1)S(1)}, u32[]{:S(2)}, u32[]{:S(2)}) collective-permute-start(bf16[128,512]{1,0:T(8,128)(2,1)S(1)} %fusion.2), channel_id=1, source_target_pairs={{0,0},{2,32},{4,64},{6,96},{8,128},{10,160},{12,192},{14,224},{16,... | collective-permute-start | bytes 393224 | tf_op jit(solution)/shard_map/ppermute | solution.py:27
  13.0 83.9 %all-to-all-start = ((bf16[16,128,512]{2,1,0:T(8,128)(2,1)}), bf16[16,128,512]{2,1,0:T(8,128)(2,1)S(1)}, u32[]{:S(2)}, u32[]{:S(2)}) async-start(bf16[16,128,512]{2,1,0:T(8,128)(2,1)} %broadcast_in_dim.3), calls=%async_computation | async-start | bytes 4194304 | tf_op jit(solution)/shard_map/all_to_all | solution.py:97
  39.7 13.8 %collective-permute-start.5 = (bf16[2,1024,128]{2,1,0:T(8,128)(2,1)}, bf16[2,1024,128]{2,1,0:T(8,128)(2,1)S(1)}, u32[]{:S(2)}, u32[]{:S(2)}) collective-permute-start(bf16[2,1024,128]{2,1,0:T(8,128)(2,1)} %pad_maximum_fusion.refs_1_), channel_id=1, source_target_pairs={{0,14},{2,0},{4,2},{6,4},{8,6},{10,8},{12,10},{14,12},{1,15},{3,1}... | collective-permute-start | bytes 1572872 | tf_op jit(solution)/shard_map/ppermute | solution.py:15
  42.3 15.7 %collective-permute-start.1 = (bf16[2,1024,128]{2,1,0:T(8,128)(2,1)}, bf16[2,1024,128]{2,1,0:T(8,128)(2,1)S(1)}, u32[]{:S(2)}, u32[]{:S(2)}) collective-permute-start(bf16[2,1024,128]{2,1,0:T(8,128)(2,1)} %pad_maximum_fusion.refs_1_), channel_id=1, source_target_pairs={{0,2},{2,4},{4,6},{6,8},{8,10},{10,12},{12,14},{14,0},{1,3},{3,5},... | collective-permute-start | bytes 1572872 | tf_op jit(solution)/shard_map/ppermute | solution.py:15
  53.5 12.7 %collective-permute-start.6 = (bf16[2,1024,128]{2,1,0:T(8,128)(2,1)S(1)}, bf16[2,1024,128]{2,1,0:T(8,128)(2,1)S(1)}, u32[]{:S(2)}, u32[]{:S(2)}) collective-permute-start(bf16[2,1024,128]{2,1,0:T(8,128)(2,1)S(1)} %collective-permute-done.5.refs_3_), channel_id=1, source_target_pairs={{0,14},{2,0},{4,2},{6,4},{8,6},{10,8},{12,10},{14,12},{1,15},{3,1}... | collective-permute-start | bytes 1572872 | tf_op jit(solution)/shard_map/ppermute | solution.py:15
  57.3 0.8 copy-start.7
  58.1 13.8 %collective-permute-start.2 = (bf16[2,1024,128]{2,1,0:T(8,128)(2,1)S(1)}, bf16[2,1024,128]{2,1,0:T(8,128)(2,1)S(1)}, u32[]{:S(2)}, u32[]{:S(2)}) collective-permute-start(bf16[2,1024,128]{2,1,0:T(8,128)(2,1)S(1)} %collective-permute-done.1.refs_2_), channel_id=1, source_target_pairs={{0,2},{2,4},{4,6},{6,8},{8,10},{10,12},{12,14},{14,0},{1,3},{3,5},... | collective-permute-start | bytes 1572872 | tf_op jit(solution)/shard_map/ppermute | solution.py:15
  60.0 0.8 copy-start.9
  66.2 12.5 %collective-permute-start.7 = (bf16[2,1024,128]{2,1,0:T(8,128)(2,1)S(1)}, bf16[2,1024,128]{2,1,0:T(8,128)(2,1)S(1)}, u32[]{:S(2)}, u32[]{:S(2)}) collective-permute-start(bf16[2,1024,128]{2,1,0:T(8,128)(2,1)S(1)} %collective-permute-done.6.refs_5_), channel_id=1, source_target_pairs={{0,14},{2,0},{4,2},{6,4},{8,6},{10,8},{12,10},{14,12},{1,15},{3,1}... | collective-permute-start | bytes 1572872 | tf_op jit(solution)/shard_map/ppermute | solution.py:15
  71.1 0.8 copy-start.11
  71.9 13.6 %copy-start.13 = (bf16[2,1024,128]{2,1,0:T(8,128)(2,1)}, bf16[2,1024,128]{2,1,0:T(8,128)(2,1)S(1)}, u32[]{:S(2)}) copy-start(bf16[2,1024,128]{2,1,0:T(8,128)(2,1)S(1)} %collective-permute-done.2.refs_4_) | copy-start | bytes 1572868
  71.9 12.9 %collective-permute-start.3 = (bf16[2,1024,128]{2,1,0:T(8,128)(2,1)S(1)}, bf16[2,1024,128]{2,1,0:T(8,128)(2,1)S(1)}, u32[]{:S(2)}, u32[]{:S(2)}) collective-permute-start(bf16[2,1024,128]{2,1,0:T(8,128)(2,1)S(1)} %collective-permute-done.2.refs_4_), channel_id=1, source_target_pairs={{0,2},{2,4},{4,6},{6,8},{8,10},{10,12},{12,14},{14,0},{1,3},{3,5},... | collective-permute-start | bytes 1572872 | tf_op jit(solution)/shard_map/ppermute | solution.py:15
  78.7 0.8 copy-start.3
  79.5 9.1 %collective-permute-start.8 = (bf16[1024,128]{1,0:T(8,128)(2,1)S(1)}, bf16[1024,128]{1,0:T(8,128)(2,1)}, u32[]{:S(2)}, u32[]{:S(2)}) collective-permute-start(bf16[1024,128]{1,0:T(8,128)(2,1)S(1)} %slice_bitcast_fusion), channel_id=1, source_target_pairs={{0,14},{2,0},{4,2},{6,4},{8,6},{10,8},{12,10},{14,12},{1,15},{3,1}... | collective-permute-start | bytes 786440 | tf_op jit(solution)/shard_map/ppermute | solution.py:15
  85.5 0.8 copy-start.5
  86.3 8.6 %collective-permute-start.4 = (bf16[1024,128]{1,0:T(8,128)(2,1)}, bf16[1024,128]{1,0:T(8,128)(2,1)}, u32[]{:S(2)}, u32[]{:S(2)}) collective-permute-start(bf16[1024,128]{1,0:T(8,128)(2,1)} %slice_bitcast_fusion.1), channel_id=1, source_target_pairs={{0,2},{2,4},{4,6},{6,8},{8,10},{10,12},{12,14},{14,0},{1,3},{3,5},... | collective-permute-start | bytes 786440 | tf_op jit(solution)/shard_map/ppermute | solution.py:15
  96.8 1.0 copy-start.2
  97.9 1.0 copy-start.8
  98.9 1.0 copy-start.10
  100.0 1.0 copy-start.12
  101.0 1.0 copy-start.14
  102.0 2.1 %copy-start.4 = (bf16[2,1024,128]{2,1,0:T(8,128)(2,1)S(1)}, bf16[2,1024,128]{2,1,0:T(8,128)(2,1)}, u32[]{:S(2)}) copy-start(bf16[2,1024,128]{2,1,0:T(8,128)(2,1)} %copy-done.3) | copy-start | bytes 1572868
  102.0 2.1 %copy-start.6 = (bf16[2,1024,128]{2,1,0:T(8,128)(2,1)S(1)}, bf16[2,1024,128]{2,1,0:T(8,128)(2,1)}, u32[]{:S(2)}) copy-start(bf16[2,1024,128]{2,1,0:T(8,128)(2,1)} %copy-done.5) | copy-start | bytes 1572868
  104.1 1.3 %copy-start.1 = (bf16[2,1024,128]{2,1,0:T(8,128)(2,1)S(1)}, bf16[2,1024,128]{2,1,0:T(8,128)(2,1)}, u32[]{:S(2)}) copy-start(bf16[2,1024,128]{2,1,0:T(8,128)(2,1)} %pad_maximum_fusion.1.refs_1_) | copy-start | bytes 1572868
  106.3 10.2 %collective-permute-start.10 = (f32[1024,256]{1,0:T(8,128)S(1)}, f32[1024,256]{1,0:T(8,128)S(1)}, u32[]{:S(2)}, u32[]{:S(2)}) collective-permute-start(f32[1024,256]{1,0:T(8,128)S(1)} %shard_map.48), channel_id=1, source_target_pairs={{0,1},{1,0},{2,3},{3,2},{4,5},{5,4},{6,7},{7,6},{8,9},{9,8},{10,11... | collective-permute-start | bytes 3145736 | tf_op jit(solution)/shard_map/ppermute | solution.py:15

commit v5 on v4

v5 whole, which is shorter than its diff:
```python
import jax
import jax.numpy as jnp
from jax import lax
from jax.experimental import pallas as pl
from jax.experimental.pallas import tpu as pltpu
from jax.sharding import Mesh
from jax.sharding import PartitionSpec as P

BLOCK = 512
TOKENS = 4096
XH, Z, XL, Y, C = 2, 8, 2, 8, 2


def shift(x, axis, size, step):
    return lax.ppermute(x, axis, [(i, (i + step) % size) for i in range(size)])


def transpose_chips(x):
    perm = []
    for xh in range(XH):
        for z in range(Z):
            for xl in range(XL):
                for y in range(Y):
                    src = ((xh * Z + z) * XL + xl) * Y + y
                    dst = ((xl * Z + y) * XL + xh) * Y + z
                    perm.append((src, dst))
    return lax.ppermute(x, ("xh", "z", "xl", "y"), perm)


def products(places, pieces, grad_all):
    width, rows = pieces[0].shape
    cols = grad_all.shape[2] // 2
    n = len(pieces)
    tile = width // 2
    per_group = 4

    def kernel(*refs):
        places_ref, piece_refs = refs[0], refs[1 : 1 + n]
        grad_ref, out_ref, held, grad_held, sems, grad_sem = refs[1 + n :]
        grad_copy = pltpu.make_async_copy(grad_ref, grad_held, grad_sem)
        grad_copy.start()
        copies = [pltpu.make_async_copy(piece_refs[i], held.at[i], sems.at[i]) for i in range(n)]
        for copy in copies:
            copy.start()
        grad_copy.wait()
        where = pl.ds(pl.multiple_of(places_ref[n] * cols, cols), cols)
        for first in range(0, n, per_group):
            group = range(first, min(first + per_group, n))
            grad = jnp.concatenate([grad_held[places_ref[i], :, where] for i in group], axis=0)
            for i in group:
                copies[i].wait()
            for t in range(width // tile):
                at = slice(t * tile, (t + 1) * tile)
                lhs = jnp.concatenate([held[i, at] for i in group], axis=1)
                total = jnp.dot(lhs, grad, preferred_element_type=jnp.float32)
                if first == 0:
                    out_ref[at] = total
                else:
                    out_ref[at] += total

    def size(a):
        return a.size * a.dtype.itemsize

    return pl.pallas_call(
        kernel,
        in_specs=[pl.BlockSpec(memory_space=pltpu.SMEM)]
        + [pl.BlockSpec(memory_space=pltpu.HBM)] * (n + 1),
        out_specs=pl.BlockSpec(memory_space=pltpu.VMEM),
        out_shape=jax.ShapeDtypeStruct((width, cols), jnp.float32),
        scratch_shapes=[
            pltpu.VMEM((n, width, rows), pieces[0].dtype),
            pltpu.VMEM(grad_all.shape, grad_all.dtype),
            pltpu.SemaphoreType.DMA((n,)),
            pltpu.SemaphoreType.DMA,
        ],
        compiler_params=pltpu.CompilerParams(vmem_limit_bytes=24 * 1024 * 1024),
        cost_estimate=pl.CostEstimate(
            flops=2 * width * cols * rows * n,
            bytes_accessed=sum(map(size, pieces)) + size(grad_all) + width * cols * 4,
            transcendentals=0,
        ),
    )(places, *pieces, grad_all)


def per_device(activations, act_basis, gradients, grad_basis):
    xl, y, c = (lax.axis_index(a) for a in ("xl", "y", "c"))
    rows, act_width = activations.shape

    grad_rot = jnp.dot(gradients, grad_basis, preferred_element_type=jnp.float32)
    grad_sq = (grad_rot * grad_rot).astype(jnp.bfloat16)
    own = transpose_chips(grad_sq)

    act_blocks = activations.reshape(rows, act_width // BLOCK, BLOCK)
    act_rot = jnp.einsum("tbk,bkj->bjt", act_blocks, act_basis, preferred_element_type=jnp.float32)
    act_sq = (act_rot * act_rot).astype(jnp.bfloat16).reshape(act_width, rows)
    near_up, near_down = [act_sq], [act_sq]
    for _ in range(3):
        near_up.append(shift(near_up[-1], "y", Y, 1))
        near_down.append(shift(near_down[-1], "y", Y, -1))
    near_up.append(shift(near_up[-1], "y", Y, 1))
    far_up = [shift(act_sq, "xl", XL, 1)]
    far_down = far_up[:]
    for _ in range(3):
        far_up.append(shift(far_up[-1], "y", Y, 1))
        far_down.append(shift(far_down[-1], "y", Y, -1))
    far_down.append(shift(far_down[-1], "y", Y, -1))

    own, _, _, _ = lax.optimization_barrier((own, near_up[1], near_down[1], far_up[0]))
    copies = jnp.broadcast_to(own, (XH * Z,) + own.shape)
    grad_all = lax.all_to_all(copies, ("xh", "z"), 0, 0, tiled=True)
    grad_all = grad_all.reshape(XH * Z, rows, gradients.shape[1])

    pieces, at = [], []
    for k in range(5):
        for way, ring, pair in ((-1, near_up, 0), (1, near_down, 0), (-1, far_up, 1), (1, far_down, 1)):
            if k < len(ring) and (k > 0 or way < 0):
                pieces.append(ring[k])
                at.append((pair ^ xl) * Y + (y + Y + way * k) % Y)

    def places(half):
        return jnp.stack(at + [half]).astype(jnp.int32)

    other = products(places(1 - c), pieces, grad_all)
    got = shift(other, "c", C, 1)
    mine = products(places(c), pieces, grad_all)
    return (mine + got) / TOKENS


def solution(mesh):
    chips = Mesh(mesh.devices.reshape(XH, Z, XL, Y, C), ("xh", "z", "xl", "y", "c"))
    feat, tok = ("xh", "z"), ("xl", "y", "c")
    return jax.shard_map(
        per_device,
        mesh=chips,
        in_specs=(P(tok, feat), P(feat, None, None), P(tok, feat), P(feat, None)),
        out_specs=P(feat, tok),
        check_vma=False,
    )
```

time: 119 us -> 127 us (1.067)
  waiting for transfers between devices: 30.4 us -> 13.2 us
  starting transfers between devices: 64.2 us -> 80.5 us
  local copies, waits for them, and re-layouts: 11.7 us -> 19.1 us
    ppermute x10 -> x16, waiting for transfers between devices: 30.4 us -> 6.56 us  [shift(): return lax.ppermute(x, axis, [(i, (i + step) % size) for i in range(size)])]
    ppermute x10 -> x16, starting transfers between devices: 36.8 us -> 51.4 us  [shift(): return lax.ppermute(x, axis, [(i, (i + step) % size) for i in range(size)])]
    unnamed x30 -> x44, local copies, waits for them, and re-layouts: 9.2 us -> 17.3 us
    all_to_all x1, waiting for transfers between devices: 0.01 us -> 6.65 us  [per_device(): grad_all = lax.all_to_all(copies, ('xh', 'z'), 0, 0, tiled=True)]
    another operation x5 -> x0, other arithmetic: 2.95 us -> none  [the longest x1 1.88 us: per_device(): jnp.stack([shift(up[3][0], 'y', Y, 1), shift(down[3][1], 'y', Y, -1)])]
    div x0 -> x1, other arithmetic: none -> 2.33 us  [per_device(): return (mine + got) / TOKENS]
    all_to_all x1, starting transfers between devices: 26.7 us -> 28.4 us  [per_device(): grad_all = lax.all_to_all(copies, ('xh', 'z'), 0, 0, tiled=True)]
    pallas_call x4 -> x2, Pallas kernels: 6.01 us -> 6.96 us  [products(): pl.pallas_call(kernel, in_specs=[pl.BlockSpec(memory_space=pltpu.SMEM)] +...]
  transfers between devices with their start and end apart: 12 -> 18, of which waited for: 6 -> 5; matrix products, arithmetic and copies ran while one was open for 3% -> 1% of each run, Pallas kernels for 0% -> 2%
where the time goes in v5:
time: 127 us; the launch traced here: 125 us
  starting transfers between devices  80.5 us (63%)
  local copies, waits for them, and re-layouts  19.1 us (15%)
  waiting for transfers between devices  13.2 us (10%)
  Pallas kernels  6.96 us (5%)
  matrix products  2.82 us (2%)
  other arithmetic  2.33 us (2%)
    ppermute x16, starting transfers between devices, shift(): return lax.ppermute(x, axis, [(i, (i + step) % size) for i in range(size)])  51.4 us
    all_to_all x1, starting transfers between devices, per_device(): grad_all = lax.all_to_all(copies, ('xh', 'z'), 0, 0, tiled=True)  28.4 us
    unnamed x44, local copies, waits for them, and re-layouts  17.3 us
    pallas_call x2, Pallas kernels, products(): pl.pallas_call(kernel, in_specs=[pl.BlockSpec(memory_space=pltpu.SMEM)] +...  6.96 us
    all_to_all x1, waiting for transfers between devices, per_device(): grad_all = lax.all_to_all(copies, ('xh', 'z'), 0, 0, tiled=True)  6.65 us
    ppermute x16, waiting for transfers between devices, shift(): return lax.ppermute(x, axis, [(i, (i + step) % size) for i in range(size)])  6.56 us
  transfers between devices with their start and end apart: 18, of which 5 were waited for; matrix products, arithmetic and copies ran while one was open for 1% of the time, Pallas kernels for 2%

profile of v5, /device:TPU:1, one launch (start us, length us, event | category | flops | bytes accessed | tf_op | source)
XLA Modules:
  0.0 125.3 jit_solution(4583306053792905876)
XLA Ops:
  0.0 1.2 copy-done
  1.2 1.5 %fusion = bf16[2,512,128]{2,1,0:T(8,128)(2,1)S(1)} fusion(bf16[2,512,512]{2,1,0:T(8,128)(2,1)S(1)} %copy-done, bf16[16,2,8,512]{3,2,1,0:T(8,128)(2,1)} %bitcast.31), kind=kOutput, calls=%fused_computation.1 | convolution fusion | flops 134479872 | bytes 1572864 | tf_op jit(solution)/shard_map/tbk,bkj->bjt/dot_general | solution.py:94
  2.7 5.9 %collective-permute-start.2 = (bf16[1024,128]{1,0:T(8,128)(2,1)S(1)}, bf16[1024,128]{1,0:T(8,128)(2,1)S(1)}, u32[]{:S(2)}, u32[]{:S(2)}) collective-permute-start(bf16[1024,128]{1,0:T(8,128)(2,1)S(1)} %bitcast.26), channel_id=1, source_target_pairs={{0,14},{2,0},{4,2},{6,4},{8,6},{10,8},{12,10},{14,12},{1,15},{3,1}... | collective-permute-start | bytes 786440 | tf_op jit(solution)/shard_map/ppermute | solution.py:15
  8.6 1.9 %collective-permute-start.1 = (bf16[1024,128]{1,0:T(8,128)(2,1)S(1)}, bf16[1024,128]{1,0:T(8,128)(2,1)S(1)}, u32[]{:S(2)}, u32[]{:S(2)}) collective-permute-start(bf16[1024,128]{1,0:T(8,128)(2,1)S(1)} %bitcast.27), channel_id=1, source_target_pairs={{0,2},{2,4},{4,6},{6,8},{8,10},{10,12},{12,14},{14,0},{1,3},{3,5},... | collective-permute-start | bytes 786440 | tf_op jit(solution)/shard_map/ppermute | solution.py:15
  10.6 3.1 %collective-permute-start = (bf16[1024,128]{1,0:T(8,128)(2,1)S(1)}, bf16[1024,128]{1,0:T(8,128)(2,1)S(1)}, u32[]{:S(2)}, u32[]{:S(2)}) collective-permute-start(bf16[1024,128]{1,0:T(8,128)(2,1)S(1)} %bitcast.28), channel_id=1, source_target_pairs={{0,16},{16,0},{1,17},{17,1},{2,18},{18,2},{3,19},{19,3},{4,20},{20... | collective-permute-start | bytes 786440 | tf_op jit(solution)/shard_map/ppermute | solution.py:15
  13.7 1.3 %fusion.1 = bf16[128,512]{1,0:T(8,128)(2,1)S(1)} fusion(bf16[128,512]{1,0:T(8,128)(2,1)} %param.6, bf16[512,512]{1,0:T(8,128)(2,1)} %param.7), kind=kOutput, calls=%fused_computation.3 | convolution fusion | flops 67239936 | bytes 786432 | tf_op jit(solution)/shard_map/dot_general | solution.py:89
  15.8 1.2 collective-permute-done.1.refs_3_
  17.0 1.0 collective-permute-done.refs_2_
  18.0 1.6 %broadcast_in_dim.3 = bf16[16,128,512]{2,1,0:T(8,128)(2,1)} broadcast(bf16[128,512]{1,0:T(8,128)(2,1)S(1)} %collective-permute-done.15), dimensions={1,2} | broadcast | bytes 2228224 | tf_op jit(solution)/shard_map/broadcast_in_dim | solution.py:109
  19.6 28.4 %all-to-all-start = ((bf16[16,128,512]{2,1,0:T(8,128)(2,1)}), bf16[16,128,512]{2,1,0:T(8,128)(2,1)S(1)}, u32[]{:S(2)}, u32[]{:S(2)}) async-start(bf16[16,128,512]{2,1,0:T(8,128)(2,1)} %broadcast_in_dim.3), calls=%async_computation | async-start | bytes 4194304 | tf_op jit(solution)/shard_map/all_to_all | solution.py:110
  48.0 2.1 %collective-permute-start.4 = (bf16[1024,128]{1,0:T(8,128)(2,1)}, bf16[1024,128]{1,0:T(8,128)(2,1)S(1)}, u32[]{:S(2)}, u32[]{:S(2)}) collective-permute-start(bf16[1024,128]{1,0:T(8,128)(2,1)} %copy-done.7), channel_id=1, source_target_pairs={{0,14},{2,0},{4,2},{6,4},{8,6},{10,8},{12,10},{14,12},{1,15},{3,1}... | collective-permute-start | bytes 786440 | tf_op jit(solution)/shard_map/ppermute | solution.py:15
  50.1 3.2 %collective-permute-start.5 = (bf16[1024,128]{1,0:T(8,128)(2,1)}, bf16[1024,128]{1,0:T(8,128)(2,1)S(1)}, u32[]{:S(2)}, u32[]{:S(2)}) collective-permute-start(bf16[1024,128]{1,0:T(8,128)(2,1)} %copy-done.4), channel_id=1, source_target_pairs={{0,2},{2,4},{4,6},{6,8},{8,10},{10,12},{12,14},{14,0},{1,3},{3,5},... | collective-permute-start | bytes 786440 | tf_op jit(solution)/shard_map/ppermute | solution.py:15
  53.3 1.9 %collective-permute-start.3 = (bf16[1024,128]{1,0:T(8,128)(2,1)}, bf16[1024,128]{1,0:T(8,128)(2,1)S(1)}, u32[]{:S(2)}, u32[]{:S(2)}) collective-permute-start(bf16[1024,128]{1,0:T(8,128)(2,1)} %copy-done.7), channel_id=1, source_target_pairs={{0,2},{2,4},{4,6},{6,8},{8,10},{10,12},{12,14},{14,0},{1,3},{3,5},... | collective-permute-start | bytes 786440 | tf_op jit(solution)/shard_map/ppermute | solution.py:15
  56.2 3.6 %collective-permute-start.8 = (bf16[1024,128]{1,0:T(8,128)(2,1)S(1)}, bf16[1024,128]{1,0:T(8,128)(2,1)S(1)}, u32[]{:S(2)}, u32[]{:S(2)}) collective-permute-start(bf16[1024,128]{1,0:T(8,128)(2,1)S(1)} %collective-permute-done.4.refs_6_), channel_id=1, source_target_pairs={{0,14},{2,0},{4,2},{6,4},{8,6},{10,8},{12,10},{14,12},{1,15},{3,1}... | collective-permute-start | bytes 786440 | tf_op jit(solution)/shard_map/ppermute | solution.py:15
  60.5 2.1 %collective-permute-start.6 = (bf16[1024,128]{1,0:T(8,128)(2,1)}, bf16[1024,128]{1,0:T(8,128)(2,1)}, u32[]{:S(2)}, u32[]{:S(2)}) collective-permute-start(bf16[1024,128]{1,0:T(8,128)(2,1)} %copy-done.1), channel_id=1, source_target_pairs={{0,14},{2,0},{4,2},{6,4},{8,6},{10,8},{12,10},{14,12},{1,15},{3,1}... | collective-permute-start | bytes 786440 | tf_op jit(solution)/shard_map/ppermute | solution.py:15
  62.6 3.2 %collective-permute-start.9 = (bf16[1024,128]{1,0:T(8,128)(2,1)S(1)}, bf16[1024,128]{1,0:T(8,128)(2,1)}, u32[]{:S(2)}, u32[]{:S(2)}) collective-permute-start(bf16[1024,128]{1,0:T(8,128)(2,1)S(1)} %collective-permute-done.5.refs_7_), channel_id=1, source_target_pairs={{0,2},{2,4},{4,6},{6,8},{8,10},{10,12},{12,14},{14,0},{1,3},{3,5},... | collective-permute-start | bytes 786440 | tf_op jit(solution)/shard_map/ppermute | solution.py:15
  66.5 1.9 %collective-permute-start.7 = (bf16[1024,128]{1,0:T(8,128)(2,1)S(1)}, bf16[1024,128]{1,0:T(8,128)(2,1)}, u32[]{:S(2)}, u32[]{:S(2)}) collective-permute-start(bf16[1024,128]{1,0:T(8,128)(2,1)S(1)} %collective-permute-done.3.refs_5_), channel_id=1, source_target_pairs={{0,2},{2,4},{4,6},{6,8},{8,10},{10,12},{12,14},{14,0},{1,3},{3,5},... | collective-permute-start | bytes 786440 | tf_op jit(solution)/shard_map/ppermute | solution.py:15
  69.1 4.6 %collective-permute-start.12 = (bf16[1024,128]{1,0:T(8,128)(2,1)S(1)}, bf16[1024,128]{1,0:T(8,128)(2,1)}, u32[]{:S(2)}, u32[]{:S(2)}) collective-permute-start(bf16[1024,128]{1,0:T(8,128)(2,1)S(1)} %collective-permute-done.8.refs_10_), channel_id=1, source_target_pairs={{0,14},{2,0},{4,2},{6,4},{8,6},{10,8},{12,10},{14,12},{1,15},{3,1}... | collective-permute-start | bytes 786440 | tf_op jit(solution)/shard_map/ppermute | solution.py:15
  74.4 2.1 %collective-permute-start.10 = (bf16[1024,128]{1,0:T(8,128)(2,1)}, bf16[1024,128]{1,0:T(8,128)(2,1)}, u32[]{:S(2)}, u32[]{:S(2)}) collective-permute-start(bf16[1024,128]{1,0:T(8,128)(2,1)} %collective-permute-done.6.refs_8_), channel_id=1, source_target_pairs={{0,14},{2,0},{4,2},{6,4},{8,6},{10,8},{12,10},{14,12},{1,15},{3,1}... | collective-permute-start | bytes 786440 | tf_op jit(solution)/shard_map/ppermute | solution.py:15
  76.5 3.2 %collective-permute-start.13 = (bf16[1024,128]{1,0:T(8,128)(2,1)}, bf16[1024,128]{1,0:T(8,128)(2,1)}, u32[]{:S(2)}, u32[]{:S(2)}) collective-permute-start(bf16[1024,128]{1,0:T(8,128)(2,1)} %collective-permute-done.9.refs_11_), channel_id=1, source_target_pairs={{0,2},{2,4},{4,6},{6,8},{8,10},{10,12},{12,14},{14,0},{1,3},{3,5},... | collective-permute-start | bytes 786440 | tf_op jit(solution)/shard_map/ppermute | solution.py:15
  79.7 1.9 %collective-permute-start.11 = (bf16[1024,128]{1,0:T(8,128)(2,1)}, bf16[1024,128]{1,0:T(8,128)(2,1)}, u32[]{:S(2)}, u32[]{:S(2)}) collective-permute-start(bf16[1024,128]{1,0:T(8,128)(2,1)} %collective-permute-done.7.refs_9_), channel_id=1, source_target_pairs={{0,2},{2,4},{4,6},{6,8},{8,10},{10,12},{12,14},{14,0},{1,3},{3,5},... | collective-permute-start | bytes 786440 | tf_op jit(solution)/shard_map/ppermute | solution.py:15
  81.7 4.6 %collective-permute-start.14 = (bf16[1024,128]{1,0:T(8,128)(2,1)}, bf16[1024,128]{1,0:T(8,128)(2,1)}, u32[]{:S(2)}, u32[]{:S(2)}) collective-permute-start(bf16[1024,128]{1,0:T(8,128)(2,1)} %collective-permute-done.12.refs_14_), channel_id=1, source_target_pairs={{0,14},{2,0},{4,2},{6,4},{8,6},{10,8},{12,10},{14,12},{1,15},{3,1}... | collective-permute-start | bytes 786440 | tf_op jit(solution)/shard_map/ppermute | solution.py:15
  86.5 3.4 %collective-permute-done.11.refs_13_ = bf16[1024,128]{1,0:T(8,128)(2,1)} collective-permute-done((bf16[1024,128]{1,0:T(8,128)(2,1)}, bf16[1024,128]{1,0:T(8,128)(2,1)}, u32[]{:S(2)}, u32[]{:S(2)}) %collective-permute-start.11) | collective-permute-done | bytes 262176 | tf_op jit(solution)/shard_map/ppermute | solution.py:15
  89.9 6.7 %all-to-all-done.refs_17_ = bf16[16,128,512]{2,1,0:T(8,128)(2,1)S(1)} async-done(((bf16[16,128,512]{2,1,0:T(8,128)(2,1)}), bf16[16,128,512]{2,1,0:T(8,128)(2,1)S(1)}, u32[]{:S(2)}, u32[]{:S(2)}) %all-to-all-start) | async-done | bytes 2097184 | tf_op jit(solution)/shard_map/all_to_all | solution.py:110
  96.5 0.9 copy-done.2
  97.5 0.9 copy-done.5
  99.4 0.9 copy-done.11
  100.3 0.9 copy-done.14
  103.2 4.0 %shard_map.47 = f32[1024,256]{1,0:T(8,128)} custom-call(s32[17]{0:T(128)S(1)} %stack.95.refs_0_, bf16[1024,128]{1,0:T(8,128)(2,1)S(1)} %bitcast.29, bf16[1024,128]{1,0:T(8,128)(2,1)S(1)} %copy-done.8, bf16[1024,128]{1,0:T(8,128)(2,1)S(1)} %copy-done.5, bf16[1024,128]{1,0:T(8,128)(2,1)S(1)} %copy-done.2, bf16[1024,128]{1,0:T(8,128)(2,1)S(1)} %copy-done.17, ...), custom_call_target="tpu_custom_call" | custom-call | flops 1073741824 | bytes 7340032 | tf_op jit(solution)/shard_map/pallas_call | solution.py:64
  107.1 6.0 %collective-permute-start.16 = (f32[1024,256]{1,0:T(8,128)}, f32[1024,256]{1,0:T(8,128)}, u32[]{:S(2)}, u32[]{:S(2)}) collective-permute-start(f32[1024,256]{1,0:T(8,128)} %shard_map.47), channel_id=1, source_target_pairs={{0,1},{1,0},{2,3},{3,2},{4,5},{5,4},{6,7},{7,6},{8,9},{9,8},{10,11... | collective-permute-start | bytes 3145736 | tf_op jit(solution)/shard_map/ppermute | solution.py:15
  120.0 3.0 %shard_map.46 = f32[1024,256]{1,0:T(8,128)S(1)} custom-call(s32[17]{0:T(128)S(1)} %stack.93.refs_0_, bf16[1024,128]{1,0:T(8,128)(2,1)S(1)} %bitcast.30, bf16[1024,128]{1,0:T(8,128)(2,1)S(1)} %copy-done.9, bf16[1024,128]{1,0:T(8,128)(2,1)S(1)} %copy-done.6, bf16[1024,128]{1,0:T(8,128)(2,1)S(1)} %copy-done.3, bf16[1024,128]{1,0:T(8,128)(2,1)S(1)} %copy-done.18, ...), custom_call_target="tpu_custom_call" | custom-call | flops 1073741824 | bytes 7340032 | tf_op jit(solution)/shard_map/pallas_call | solution.py:64
  123.0 2.3 %add_multiply_fusion = f32[1024,256]{1,0:T(8,128)} fusion(f32[1024,256]{1,0:T(8,128)S(1)} %shard_map.46, f32[1024,256]{1,0:T(8,128)} %collective-permute-done.16), kind=kLoop, calls=%fused_computation.4 | loop fusion | flops 524288 | bytes 3145728 | tf_op jit(solution)/shard_map/div | solution.py:126
  (56 shorter events, 14.1 us)
Async XLA Ops:
  0.0 1.2 copy-start
  2.7 13.0 %collective-permute-start.2 = (bf16[1024,128]{1,0:T(8,128)(2,1)S(1)}, bf16[1024,128]{1,0:T(8,128)(2,1)S(1)}, u32[]{:S(2)}, u32[]{:S(2)}) collective-permute-start(bf16[1024,128]{1,0:T(8,128)(2,1)S(1)} %bitcast.26), channel_id=1, source_target_pairs={{0,14},{2,0},{4,2},{6,4},{8,6},{10,8},{12,10},{14,12},{1,15},{3,1}... | collective-permute-start | bytes 786440 | tf_op jit(solution)/shard_map/ppermute | solution.py:15
  8.6 8.3 %collective-permute-start.1 = (bf16[1024,128]{1,0:T(8,128)(2,1)S(1)}, bf16[1024,128]{1,0:T(8,128)(2,1)S(1)}, u32[]{:S(2)}, u32[]{:S(2)}) collective-permute-start(bf16[1024,128]{1,0:T(8,128)(2,1)S(1)} %bitcast.27), channel_id=1, source_target_pairs={{0,2},{2,4},{4,6},{6,8},{8,10},{10,12},{12,14},{14,0},{1,3},{3,5},... | collective-permute-start | bytes 786440 | tf_op jit(solution)/shard_map/ppermute | solution.py:15
  10.6 7.4 %collective-permute-start = (bf16[1024,128]{1,0:T(8,128)(2,1)S(1)}, bf16[1024,128]{1,0:T(8,128)(2,1)S(1)}, u32[]{:S(2)}, u32[]{:S(2)}) collective-permute-start(bf16[1024,128]{1,0:T(8,128)(2,1)S(1)} %bitcast.28), channel_id=1, source_target_pairs={{0,16},{16,0},{1,17},{17,1},{2,18},{18,2},{3,19},{19,3},{4,20},{20... | collective-permute-start | bytes 786440 | tf_op jit(solution)/shard_map/ppermute | solution.py:15
  15.1 0.7 collective-permute-start.15
  15.7 3.8 %copy-start.1 = (bf16[1024,128]{1,0:T(8,128)(2,1)}, bf16[1024,128]{1,0:T(8,128)(2,1)S(1)}, u32[]{:S(2)}) copy-start(bf16[1024,128]{1,0:T(8,128)(2,1)S(1)} %collective-permute-done.2.refs_4_) | copy-start | bytes 786436
  17.0 2.6 %copy-start.4 = (bf16[1024,128]{1,0:T(8,128)(2,1)}, bf16[1024,128]{1,0:T(8,128)(2,1)S(1)}, u32[]{:S(2)}) copy-start(bf16[1024,128]{1,0:T(8,128)(2,1)S(1)} %collective-permute-done.1.refs_3_) | copy-start | bytes 786436
  18.0 1.6 %copy-start.7 = (bf16[1024,128]{1,0:T(8,128)(2,1)}, bf16[1024,128]{1,0:T(8,128)(2,1)S(1)}, u32[]{:S(2)}) copy-start(bf16[1024,128]{1,0:T(8,128)(2,1)S(1)} %collective-permute-done.refs_2_) | copy-start | bytes 786436
  19.6 77.0 %all-to-all-start = ((bf16[16,128,512]{2,1,0:T(8,128)(2,1)}), bf16[16,128,512]{2,1,0:T(8,128)(2,1)S(1)}, u32[]{:S(2)}, u32[]{:S(2)}) async-start(bf16[16,128,512]{2,1,0:T(8,128)(2,1)} %broadcast_in_dim.3), calls=%async_computation | async-start | bytes 4194304 | tf_op jit(solution)/shard_map/all_to_all | solution.py:110
  48.0 8.2 %collective-permute-start.4 = (bf16[1024,128]{1,0:T(8,128)(2,1)}, bf16[1024,128]{1,0:T(8,128)(2,1)S(1)}, u32[]{:S(2)}, u32[]{:S(2)}) collective-permute-start(bf16[1024,128]{1,0:T(8,128)(2,1)} %copy-done.7), channel_id=1, source_target_pairs={{0,14},{2,0},{4,2},{6,4},{8,6},{10,8},{12,10},{14,12},{1,15},{3,1}... | collective-permute-start | bytes 786440 | tf_op jit(solution)/shard_map/ppermute | solution.py:15
  50.1 12.5 %collective-permute-start.5 = (bf16[1024,128]{1,0:T(8,128)(2,1)}, bf16[1024,128]{1,0:T(8,128)(2,1)S(1)}, u32[]{:S(2)}, u32[]{:S(2)}) collective-permute-start(bf16[1024,128]{1,0:T(8,128)(2,1)} %copy-done.4), channel_id=1, source_target_pairs={{0,2},{2,4},{4,6},{6,8},{8,10},{10,12},{12,14},{14,0},{1,3},{3,5},... | collective-permute-start | bytes 786440 | tf_op jit(solution)/shard_map/ppermute | solution.py:15
  53.3 13.2 %collective-permute-start.3 = (bf16[1024,128]{1,0:T(8,128)(2,1)}, bf16[1024,128]{1,0:T(8,128)(2,1)S(1)}, u32[]{:S(2)}, u32[]{:S(2)}) collective-permute-start(bf16[1024,128]{1,0:T(8,128)(2,1)} %copy-done.7), channel_id=1, source_target_pairs={{0,2},{2,4},{4,6},{6,8},{8,10},{10,12},{12,14},{14,0},{1,3},{3,5},... | collective-permute-start | bytes 786440 | tf_op jit(solution)/shard_map/ppermute | solution.py:15
  56.2 13.0 %collective-permute-start.8 = (bf16[1024,128]{1,0:T(8,128)(2,1)S(1)}, bf16[1024,128]{1,0:T(8,128)(2,1)S(1)}, u32[]{:S(2)}, u32[]{:S(2)}) collective-permute-start(bf16[1024,128]{1,0:T(8,128)(2,1)S(1)} %collective-permute-done.4.refs_6_), channel_id=1, source_target_pairs={{0,14},{2,0},{4,2},{6,4},{8,6},{10,8},{12,10},{14,12},{1,15},{3,1}... | collective-permute-start | bytes 786440 | tf_op jit(solution)/shard_map/ppermute | solution.py:15
  60.5 13.9 %collective-permute-start.6 = (bf16[1024,128]{1,0:T(8,128)(2,1)}, bf16[1024,128]{1,0:T(8,128)(2,1)}, u32[]{:S(2)}, u32[]{:S(2)}) collective-permute-start(bf16[1024,128]{1,0:T(8,128)(2,1)} %copy-done.1), channel_id=1, source_target_pairs={{0,14},{2,0},{4,2},{6,4},{8,6},{10,8},{12,10},{14,12},{1,15},{3,1}... | collective-permute-start | bytes 786440 | tf_op jit(solution)/shard_map/ppermute | solution.py:15
  62.6 13.9 %collective-permute-start.9 = (bf16[1024,128]{1,0:T(8,128)(2,1)S(1)}, bf16[1024,128]{1,0:T(8,128)(2,1)}, u32[]{:S(2)}, u32[]{:S(2)}) collective-permute-start(bf16[1024,128]{1,0:T(8,128)(2,1)S(1)} %collective-permute-done.5.refs_7_), channel_id=1, source_target_pairs={{0,2},{2,4},{4,6},{6,8},{8,10},{10,12},{12,14},{14,0},{1,3},{3,5},... | collective-permute-start | bytes 786440 | tf_op jit(solution)/shard_map/ppermute | solution.py:15
  66.5 13.2 %collective-permute-start.7 = (bf16[1024,128]{1,0:T(8,128)(2,1)S(1)}, bf16[1024,128]{1,0:T(8,128)(2,1)}, u32[]{:S(2)}, u32[]{:S(2)}) collective-permute-start(bf16[1024,128]{1,0:T(8,128)(2,1)S(1)} %collective-permute-done.3.refs_5_), channel_id=1, source_target_pairs={{0,2},{2,4},{4,6},{6,8},{8,10},{10,12},{12,14},{14,0},{1,3},{3,5},... | collective-permute-start | bytes 786440 | tf_op jit(solution)/shard_map/ppermute | solution.py:15
  69.1 12.5 %collective-permute-start.12 = (bf16[1024,128]{1,0:T(8,128)(2,1)S(1)}, bf16[1024,128]{1,0:T(8,128)(2,1)}, u32[]{:S(2)}, u32[]{:S(2)}) collective-permute-start(bf16[1024,128]{1,0:T(8,128)(2,1)S(1)} %collective-permute-done.8.refs_10_), channel_id=1, source_target_pairs={{0,14},{2,0},{4,2},{6,4},{8,6},{10,8},{12,10},{14,12},{1,15},{3,1}... | collective-permute-start | bytes 786440 | tf_op jit(solution)/shard_map/ppermute | solution.py:15
  74.4 12.1 %collective-permute-start.10 = (bf16[1024,128]{1,0:T(8,128)(2,1)}, bf16[1024,128]{1,0:T(8,128)(2,1)}, u32[]{:S(2)}, u32[]{:S(2)}) collective-permute-start(bf16[1024,128]{1,0:T(8,128)(2,1)} %collective-permute-done.6.refs_8_), channel_id=1, source_target_pairs={{0,14},{2,0},{4,2},{6,4},{8,6},{10,8},{12,10},{14,12},{1,15},{3,1}... | collective-permute-start | bytes 786440 | tf_op jit(solution)/shard_map/ppermute | solution.py:15
  76.5 10.0 %collective-permute-start.13 = (bf16[1024,128]{1,0:T(8,128)(2,1)}, bf16[1024,128]{1,0:T(8,128)(2,1)}, u32[]{:S(2)}, u32[]{:S(2)}) collective-permute-start(bf16[1024,128]{1,0:T(8,128)(2,1)} %collective-permute-done.9.refs_11_), channel_id=1, source_target_pairs={{0,2},{2,4},{4,6},{6,8},{8,10},{10,12},{12,14},{14,0},{1,3},{3,5},... | collective-permute-start | bytes 786440 | tf_op jit(solution)/shard_map/ppermute | solution.py:15
  79.7 10.1 %collective-permute-start.11 = (bf16[1024,128]{1,0:T(8,128)(2,1)}, bf16[1024,128]{1,0:T(8,128)(2,1)}, u32[]{:S(2)}, u32[]{:S(2)}) collective-permute-start(bf16[1024,128]{1,0:T(8,128)(2,1)} %collective-permute-done.7.refs_9_), channel_id=1, source_target_pairs={{0,2},{2,4},{4,6},{6,8},{8,10},{10,12},{12,14},{14,0},{1,3},{3,5},... | collective-permute-start | bytes 786440 | tf_op jit(solution)/shard_map/ppermute | solution.py:15
  81.7 8.2 %collective-permute-start.14 = (bf16[1024,128]{1,0:T(8,128)(2,1)}, bf16[1024,128]{1,0:T(8,128)(2,1)}, u32[]{:S(2)}, u32[]{:S(2)}) collective-permute-start(bf16[1024,128]{1,0:T(8,128)(2,1)} %collective-permute-done.12.refs_14_), channel_id=1, source_target_pairs={{0,14},{2,0},{4,2},{6,4},{8,6},{10,8},{12,10},{14,12},{1,15},{3,1}... | collective-permute-start | bytes 786440 | tf_op jit(solution)/shard_map/ppermute | solution.py:15
  96.5 1.0 copy-start.2
  97.5 0.9 copy-start.5
  98.4 0.9 copy-start.8
  99.4 0.9 copy-start.11
  100.3 0.9 copy-start.14
  101.3 0.9 copy-start.17
  102.2 0.9 copy-start.20
  107.1 15.8 %collective-permute-start.16 = (f32[1024,256]{1,0:T(8,128)}, f32[1024,256]{1,0:T(8,128)}, u32[]{:S(2)}, u32[]{:S(2)}) collective-permute-start(f32[1024,256]{1,0:T(8,128)} %shard_map.47), channel_id=1, source_target_pairs={{0,1},{1,0},{2,3},{3,2},{4,5},{5,4},{6,7},{7,6},{8,9},{9,8},{10,11... | collective-permute-start | bytes 3145736 | tf_op jit(solution)/shard_map/ppermute | solution.py:15
  113.3 1.0 copy-start.3
  114.3 0.9 copy-start.6
  115.2 0.9 copy-start.9
  (8 other events, 6.6 us)

commit v6 on v5

--- a/solution.py
+++ b/solution.py
@@ -16,15 +16,15 @@
 
 
 def transpose_chips(x):
-    perm = []
-    for xh in range(XH):
-        for z in range(Z):
-            for xl in range(XL):
-                for y in range(Y):
-                    src = ((xh * Z + z) * XL + xl) * Y + y
-                    dst = ((xl * Z + y) * XL + xh) * Y + z
-                    perm.append((src, dst))
-    return lax.ppermute(x, ("xh", "z", "xl", "y"), perm)
+    chips = XH * Z
+    swaps = [[f * chips + m, m * chips + f] for f in range(chips) for m in range(f + 1, chips)]
+    fixed = [f * chips + f for f in range(chips)]
+    groups = swaps + [[fixed[i], fixed[i + 1]] for i in range(0, chips, 2)]
+    f = lax.axis_index("xh") * Z + lax.axis_index("z")
+    m = lax.axis_index("xl") * Y + lax.axis_index("y")
+    sent = jnp.broadcast_to(x, (2,) + x.shape)
+    got = lax.all_to_all(sent, ("xh", "z", "xl", "y"), 0, 0, axis_index_groups=groups)
+    return jnp.where(f > m, got[0], jnp.where(f < m, got[1], x))
 
 
 def products(places, pieces, grad_all):
@@ -73,7 +73,7 @@
             pltpu.SemaphoreType.DMA((n,)),
             pltpu.SemaphoreType.DMA,
         ],
-        compiler_params=pltpu.CompilerParams(vmem_limit_bytes=24 * 1024 * 1024),
+        compiler_params=pltpu.CompilerParams(vmem_limit_bytes=56 * 1024 * 1024),
         cost_estimate=pl.CostEstimate(
             flops=2 * width * cols * rows * n,
             bytes_accessed=sum(map(size, pieces)) + size(grad_all) + width * cols * 4,

time: 127 us -> 115 us (0.906)
  local copies, waits for them, and re-layouts: 19.1 us -> 4.94 us
  starting transfers between devices: 80.5 us -> 71 us
  waiting for transfers between devices: 13.2 us -> 20.7 us
  Pallas kernels: 6.96 us -> 12.1 us
    all_to_all x1, starting transfers between devices: 28.4 us -> 10 us  [per_device(): grad_all = lax.all_to_all(copies, ('xh', 'z'), 0, 0, tiled=True)]
    unnamed x44 -> x20, local copies, waits for them, and re-layouts: 17.3 us -> 1.38 us
    ppermute x16, waiting for transfers between devices: 6.56 us -> 12 us  [shift(): return lax.ppermute(x, axis, [(i, (i + step) % size) for i in range(size)])]
    all_to_all x0 -> x1, starting transfers between devices: none -> 5.2 us  [transpose_chips(): lax.all_to_all(sent, ('xh', 'z', 'xl', 'y'), 0, 0, axis_index_groups=groups)]
    pallas_call x2, Pallas kernels: 6.96 us -> 12.1 us  [products(): pl.pallas_call(kernel, in_specs=[pl.BlockSpec(memory_space=pltpu.SMEM)] +...]
    ppermute x16, starting transfers between devices: 51.4 us -> 55.8 us  [shift(): return lax.ppermute(x, axis, [(i, (i + step) % size) for i in range(size)])]
    all_to_all x1, waiting for transfers between devices: 6.65 us -> 8.64 us  [per_device(): grad_all = lax.all_to_all(copies, ('xh', 'z'), 0, 0, tiled=True)]
  transfers between devices with their start and end apart: 18 -> 18, of which waited for: 5 -> 4; matrix products, arithmetic and copies ran while one was open for 1% -> 2% of each run, Pallas kernels for 2% -> 5%
where the time goes in v6:
time: 115 us; the launch traced here: 114 us
  starting transfers between devices  71 us (62%)
  waiting for transfers between devices  20.7 us (18%)
  Pallas kernels  12.1 us (11%)
  local copies, waits for them, and re-layouts  4.94 us (4%)
  matrix products  2.9 us (3%)
  other arithmetic  2.36 us (2%)
    ppermute x16, starting transfers between devices, shift(): return lax.ppermute(x, axis, [(i, (i + step) % size) for i in range(size)])  55.8 us
    pallas_call x2, Pallas kernels, products(): pl.pallas_call(kernel, in_specs=[pl.BlockSpec(memory_space=pltpu.SMEM)] +...  12.1 us
    ppermute x16, waiting for transfers between devices, shift(): return lax.ppermute(x, axis, [(i, (i + step) % size) for i in range(size)])  12 us
    all_to_all x1, starting transfers between devices, per_device(): grad_all = lax.all_to_all(copies, ('xh', 'z'), 0, 0, tiled=True)  10 us
    all_to_all x1, waiting for transfers between devices, per_device(): grad_all = lax.all_to_all(copies, ('xh', 'z'), 0, 0, tiled=True)  8.64 us
    all_to_all x1, starting transfers between devices, transpose_chips(): lax.all_to_all(sent, ('xh', 'z', 'xl', 'y'), 0, 0, axis_index_groups=groups)  5.2 us
    div x1, other arithmetic, per_device(): return (mine + got) / TOKENS  2.33 us
  transfers between devices with their start and end apart: 18, of which 4 were waited for; matrix products, arithmetic and copies ran while one was open for 2% of the time, Pallas kernels for 5%

profile of v6, /device:TPU:1, one launch (start us, length us, event | category | flops | bytes accessed | tf_op | source)
XLA Modules:
  0.0 114.4 jit_solution(9466003885559514053)
XLA Ops:
  0.0 1.4 %fusion.1 = bf16[128,512]{1,0:T(8,128)(2,1)S(1)} fusion(bf16[128,512]{1,0:T(8,128)(2,1)} %param.6, bf16[512,512]{1,0:T(8,128)(2,1)} %param.7), kind=kOutput, calls=%fused_computation.3 | convolution fusion | flops 67239936 | bytes 786432 | tf_op jit(solution)/shard_map/dot_general | solution.py:89
  1.4 0.7 broadcast_in_dim.6
  2.2 5.2 %all-to-all-start = ((bf16[2,128,512]{2,1,0:T(8,128)(2,1)}), bf16[2,128,512]{2,1,0:T(8,128)(2,1)S(1)}, u32[]{:S(2)}, u32[]{:S(2)}) async-start(bf16[2,128,512]{2,1,0:T(8,128)(2,1)} %broadcast_in_dim.6), calls=%async_computation | async-start | bytes 524288 | tf_op jit(solution)/shard_map/all_to_all | solution.py:26
  7.4 1.5 %fusion = bf16[2,512,128]{2,1,0:T(8,128)(2,1)S(1)} fusion(bf16[2,512,512]{2,1,0:T(8,128)(2,1)S(1)} %copy-done, bf16[16,2,8,512]{3,2,1,0:T(8,128)(2,1)} %bitcast.41), kind=kOutput, calls=%fused_computation.1 | convolution fusion | flops 134479872 | bytes 1572864 | tf_op jit(solution)/shard_map/tbk,bkj->bjt/dot_general | solution.py:94
  8.8 10.0 %collective-permute-start.2 = (bf16[1024,128]{1,0:T(8,128)(2,1)S(1)}, bf16[1024,128]{1,0:T(8,128)(2,1)S(1)}, u32[]{:S(2)}, u32[]{:S(2)}) collective-permute-start(bf16[1024,128]{1,0:T(8,128)(2,1)S(1)} %bitcast.36), channel_id=1, source_target_pairs={{0,14},{2,0},{4,2},{6,4},{8,6},{10,8},{12,10},{14,12},{1,15},{3,1}... | collective-permute-start | bytes 786440 | tf_op jit(solution)/shard_map/ppermute | solution.py:15
  18.8 1.9 %collective-permute-start.1 = (bf16[1024,128]{1,0:T(8,128)(2,1)S(1)}, bf16[1024,128]{1,0:T(8,128)(2,1)S(1)}, u32[]{:S(2)}, u32[]{:S(2)}) collective-permute-start(bf16[1024,128]{1,0:T(8,128)(2,1)S(1)} %bitcast.37), channel_id=1, source_target_pairs={{0,2},{2,4},{4,6},{6,8},{8,10},{10,12},{12,14},{14,0},{1,3},{3,5},... | collective-permute-start | bytes 786440 | tf_op jit(solution)/shard_map/ppermute | solution.py:15
  20.7 4.0 %collective-permute-start = (bf16[1024,128]{1,0:T(8,128)(2,1)S(1)}, bf16[1024,128]{1,0:T(8,128)(2,1)S(1)}, u32[]{:S(2)}, u32[]{:S(2)}) collective-permute-start(bf16[1024,128]{1,0:T(8,128)(2,1)S(1)} %bitcast.38), channel_id=1, source_target_pairs={{0,16},{16,0},{1,17},{17,1},{2,18},{18,2},{3,19},{19,3},{4,20},{20... | collective-permute-start | bytes 786440 | tf_op jit(solution)/shard_map/ppermute | solution.py:15
  24.9 7.8 %collective-permute-done.1.refs_3_ = bf16[1024,128]{1,0:T(8,128)(2,1)S(1)} collective-permute-done((bf16[1024,128]{1,0:T(8,128)(2,1)S(1)}, bf16[1024,128]{1,0:T(8,128)(2,1)S(1)}, u32[]{:S(2)}, u32[]{:S(2)}) %collective-permute-start.1) | collective-permute-done | bytes 262176 | tf_op jit(solution)/shard_map/ppermute | solution.py:15
  32.7 1.5 %broadcast_in_dim.7 = bf16[16,128,512]{2,1,0:T(8,128)(2,1)} broadcast(bf16[128,512]{1,0:T(8,128)(2,1)S(1)} %fusion.5), dimensions={1,2} | broadcast | bytes 2228224 | tf_op jit(solution)/shard_map/broadcast_in_dim | solution.py:109
  34.3 10.0 %all-to-all-start.1 = ((bf16[16,128,512]{2,1,0:T(8,128)(2,1)}), bf16[16,128,512]{2,1,0:T(8,128)(2,1)S(1)}, u32[]{:S(2)}, u32[]{:S(2)}) async-start(bf16[16,128,512]{2,1,0:T(8,128)(2,1)} %broadcast_in_dim.7), calls=%async_computation.1 | async-start | bytes 4194304 | tf_op jit(solution)/shard_map/all_to_all | solution.py:110
  44.3 3.3 %collective-permute-start.4 = (bf16[1024,128]{1,0:T(8,128)(2,1)}, bf16[1024,128]{1,0:T(8,128)(2,1)S(1)}, u32[]{:S(2)}, u32[]{:S(2)}) collective-permute-start(bf16[1024,128]{1,0:T(8,128)(2,1)} %copy-done.5), channel_id=1, source_target_pairs={{0,14},{2,0},{4,2},{6,4},{8,6},{10,8},{12,10},{14,12},{1,15},{3,1}... | collective-permute-start | bytes 786440 | tf_op jit(solution)/shard_map/ppermute | solution.py:15
  47.6 2.0 %collective-permute-start.5 = (bf16[1024,128]{1,0:T(8,128)(2,1)}, bf16[1024,128]{1,0:T(8,128)(2,1)S(1)}, u32[]{:S(2)}, u32[]{:S(2)}) collective-permute-start(bf16[1024,128]{1,0:T(8,128)(2,1)} %copy-done.4), channel_id=1, source_target_pairs={{0,2},{2,4},{4,6},{6,8},{8,10},{10,12},{12,14},{14,0},{1,3},{3,5},... | collective-permute-start | bytes 786440 | tf_op jit(solution)/shard_map/ppermute | solution.py:15
  49.6 3.2 %collective-permute-start.3 = (bf16[1024,128]{1,0:T(8,128)(2,1)}, bf16[1024,128]{1,0:T(8,128)(2,1)S(1)}, u32[]{:S(2)}, u32[]{:S(2)}) collective-permute-start(bf16[1024,128]{1,0:T(8,128)(2,1)} %copy-done.5), channel_id=1, source_target_pairs={{0,2},{2,4},{4,6},{6,8},{8,10},{10,12},{12,14},{14,0},{1,3},{3,5},... | collective-permute-start | bytes 786440 | tf_op jit(solution)/shard_map/ppermute | solution.py:15
  52.8 3.6 %collective-permute-start.8 = (bf16[1024,128]{1,0:T(8,128)(2,1)S(1)}, bf16[1024,128]{1,0:T(8,128)(2,1)S(1)}, u32[]{:S(2)}, u32[]{:S(2)}) collective-permute-start(bf16[1024,128]{1,0:T(8,128)(2,1)S(1)} %collective-permute-done.4.refs_6_), channel_id=1, source_target_pairs={{0,14},{2,0},{4,2},{6,4},{8,6},{10,8},{12,10},{14,12},{1,15},{3,1}... | collective-permute-start | bytes 786440 | tf_op jit(solution)/shard_map/ppermute | solution.py:15
  56.4 3.0 %collective-permute-start.6 = (bf16[1024,128]{1,0:T(8,128)(2,1)}, bf16[1024,128]{1,0:T(8,128)(2,1)}, u32[]{:S(2)}, u32[]{:S(2)}) collective-permute-start(bf16[1024,128]{1,0:T(8,128)(2,1)} %copy-done.3), channel_id=1, source_target_pairs={{0,14},{2,0},{4,2},{6,4},{8,6},{10,8},{12,10},{14,12},{1,15},{3,1}... | collective-permute-start | bytes 786440 | tf_op jit(solution)/shard_map/ppermute | solution.py:15
  59.4 2.3 %collective-permute-start.9 = (bf16[1024,128]{1,0:T(8,128)(2,1)S(1)}, bf16[1024,128]{1,0:T(8,128)(2,1)}, u32[]{:S(2)}, u32[]{:S(2)}) collective-permute-start(bf16[1024,128]{1,0:T(8,128)(2,1)S(1)} %collective-permute-done.5.refs_7_), channel_id=1, source_target_pairs={{0,2},{2,4},{4,6},{6,8},{8,10},{10,12},{12,14},{14,0},{1,3},{3,5},... | collective-permute-start | bytes 786440 | tf_op jit(solution)/shard_map/ppermute | solution.py:15
  61.7 3.7 %collective-permute-start.7 = (bf16[1024,128]{1,0:T(8,128)(2,1)S(1)}, bf16[1024,128]{1,0:T(8,128)(2,1)}, u32[]{:S(2)}, u32[]{:S(2)}) collective-permute-start(bf16[1024,128]{1,0:T(8,128)(2,1)S(1)} %collective-permute-done.3.refs_5_), channel_id=1, source_target_pairs={{0,2},{2,4},{4,6},{6,8},{8,10},{10,12},{12,14},{14,0},{1,3},{3,5},... | collective-permute-start | bytes 786440 | tf_op jit(solution)/shard_map/ppermute | solution.py:15
  65.5 2.8 %collective-permute-start.12 = (bf16[1024,128]{1,0:T(8,128)(2,1)S(1)}, bf16[1024,128]{1,0:T(8,128)(2,1)}, u32[]{:S(2)}, u32[]{:S(2)}) collective-permute-start(bf16[1024,128]{1,0:T(8,128)(2,1)S(1)} %collective-permute-done.8.refs_10_), channel_id=1, source_target_pairs={{0,14},{2,0},{4,2},{6,4},{8,6},{10,8},{12,10},{14,12},{1,15},{3,1}... | collective-permute-start | bytes 786440 | tf_op jit(solution)/shard_map/ppermute | solution.py:15
  68.3 3.0 %collective-permute-start.10 = (bf16[1024,128]{1,0:T(8,128)(2,1)}, bf16[1024,128]{1,0:T(8,128)(2,1)}, u32[]{:S(2)}, u32[]{:S(2)}) collective-permute-start(bf16[1024,128]{1,0:T(8,128)(2,1)} %collective-permute-done.6.refs_8_), channel_id=1, source_target_pairs={{0,14},{2,0},{4,2},{6,4},{8,6},{10,8},{12,10},{14,12},{1,15},{3,1}... | collective-permute-start | bytes 786440 | tf_op jit(solution)/shard_map/ppermute | solution.py:15
  71.3 2.3 %collective-permute-start.13 = (bf16[1024,128]{1,0:T(8,128)(2,1)}, bf16[1024,128]{1,0:T(8,128)(2,1)}, u32[]{:S(2)}, u32[]{:S(2)}) collective-permute-start(bf16[1024,128]{1,0:T(8,128)(2,1)} %collective-permute-done.9.refs_11_), channel_id=1, source_target_pairs={{0,2},{2,4},{4,6},{6,8},{8,10},{10,12},{12,14},{14,0},{1,3},{3,5},... | collective-permute-start | bytes 786440 | tf_op jit(solution)/shard_map/ppermute | solution.py:15
  73.6 3.7 %collective-permute-start.11 = (bf16[1024,128]{1,0:T(8,128)(2,1)}, bf16[1024,128]{1,0:T(8,128)(2,1)}, u32[]{:S(2)}, u32[]{:S(2)}) collective-permute-start(bf16[1024,128]{1,0:T(8,128)(2,1)} %collective-permute-done.7.refs_9_), channel_id=1, source_target_pairs={{0,2},{2,4},{4,6},{6,8},{8,10},{10,12},{12,14},{14,0},{1,3},{3,5},... | collective-permute-start | bytes 786440 | tf_op jit(solution)/shard_map/ppermute | solution.py:15
  77.4 2.8 %collective-permute-start.14 = (bf16[1024,128]{1,0:T(8,128)(2,1)}, bf16[1024,128]{1,0:T(8,128)(2,1)}, u32[]{:S(2)}, u32[]{:S(2)}) collective-permute-start(bf16[1024,128]{1,0:T(8,128)(2,1)} %collective-permute-done.12.refs_14_), channel_id=1, source_target_pairs={{0,14},{2,0},{4,2},{6,4},{8,6},{10,8},{12,10},{14,12},{1,15},{3,1}... | collective-permute-start | bytes 786440 | tf_op jit(solution)/shard_map/ppermute | solution.py:15
  80.3 0.6 stack.95.refs_0_
  80.9 2.0 %collective-permute-done.11.refs_13_ = bf16[1024,128]{1,0:T(8,128)(2,1)} collective-permute-done((bf16[1024,128]{1,0:T(8,128)(2,1)}, bf16[1024,128]{1,0:T(8,128)(2,1)}, u32[]{:S(2)}, u32[]{:S(2)}) %collective-permute-start.11) | collective-permute-done | bytes 262176 | tf_op jit(solution)/shard_map/ppermute | solution.py:15
  83.0 2.1 %collective-permute-done.14.refs_16_ = bf16[1024,128]{1,0:T(8,128)(2,1)} collective-permute-done((bf16[1024,128]{1,0:T(8,128)(2,1)}, bf16[1024,128]{1,0:T(8,128)(2,1)}, u32[]{:S(2)}, u32[]{:S(2)}) %collective-permute-start.14) | collective-permute-done | bytes 262176 | tf_op jit(solution)/shard_map/ppermute | solution.py:15
  85.1 8.6 %all-to-all-done.1.refs_17_ = bf16[16,128,512]{2,1,0:T(8,128)(2,1)S(1)} async-done(((bf16[16,128,512]{2,1,0:T(8,128)(2,1)}), bf16[16,128,512]{2,1,0:T(8,128)(2,1)S(1)}, u32[]{:S(2)}, u32[]{:S(2)}) %all-to-all-start.1) | async-done | bytes 2097184 | tf_op jit(solution)/shard_map/all_to_all | solution.py:110
  93.7 1.3 %copy-done.1 = bf16[16,128,512]{2,1,0:T(8,128)(2,1)} copy-done((bf16[16,128,512]{2,1,0:T(8,128)(2,1)}, bf16[16,128,512]{2,1,0:T(8,128)(2,1)S(1)}, u32[]{:S(2)}) %copy-start.1) | copy-done | bytes 2097176
  95.1 6.0 %shard_map.47 = f32[1024,256]{1,0:T(8,128)} custom-call(s32[17]{0:T(128)} %stack.95.refs_0_, bf16[1024,128]{1,0:T(8,128)(2,1)} %bitcast.39, bf16[1024,128]{1,0:T(8,128)(2,1)} %copy-done.5, bf16[1024,128]{1,0:T(8,128)(2,1)} %copy-done.4, bf16[1024,128]{1,0:T(8,128)(2,1)} %copy-done.3, bf16[1024,128]{1,0:T(8,128)(2,1)} %copy-done.8, ...), custom_call_target="tpu_custom_call" | custom-call | flops 1073741824 | bytes 7340032 | tf_op jit(solution)/shard_map/pallas_call | solution.py:64
  101.1 4.3 %collective-permute-start.15 = (f32[1024,256]{1,0:T(8,128)}, f32[1024,256]{1,0:T(8,128)S(1)}, u32[]{:S(2)}, u32[]{:S(2)}) collective-permute-start(f32[1024,256]{1,0:T(8,128)} %shard_map.47), channel_id=1, source_target_pairs={{0,1},{1,0},{2,3},{3,2},{4,5},{5,4},{6,7},{7,6},{8,9},{9,8},{10,11... | collective-permute-start | bytes 3145736 | tf_op jit(solution)/shard_map/ppermute | solution.py:15
  105.4 0.6 stack.93.refs_0_
  106.0 6.0 %shard_map.46 = f32[1024,256]{1,0:T(8,128)} custom-call(s32[17]{0:T(128)} %stack.93.refs_0_, bf16[1024,128]{1,0:T(8,128)(2,1)} %bitcast.40, bf16[1024,128]{1,0:T(8,128)(2,1)} %copy-done.5, bf16[1024,128]{1,0:T(8,128)(2,1)} %copy-done.4, bf16[1024,128]{1,0:T(8,128)(2,1)} %copy-done.3, bf16[1024,128]{1,0:T(8,128)(2,1)} %copy-done.8, ...), custom_call_target="tpu_custom_call" | custom-call | flops 1073741824 | bytes 7340032 | tf_op jit(solution)/shard_map/pallas_call | solution.py:64
  112.1 2.3 %add_multiply_fusion = f32[1024,256]{1,0:T(8,128)} fusion(f32[1024,256]{1,0:T(8,128)} %shard_map.46, f32[1024,256]{1,0:T(8,128)S(1)} %collective-permute-done.15), kind=kLoop, calls=%fused_computation.4 | loop fusion | flops 524288 | bytes 3145728 | tf_op jit(solution)/shard_map/div | solution.py:126
  (34 shorter events, 0.1 us)
Async XLA Ops:
  0.0 7.4 %copy-start = (bf16[2,512,512]{2,1,0:T(8,128)(2,1)S(1)}, bf16[2,512,512]{2,1,0:T(8,128)(2,1)}, u32[]{:S(2)}) copy-start(bf16[2,512,512]{2,1,0:T(8,128)(2,1)} %param.5) | copy-start | bytes 3145732
  2.2 22.7 %all-to-all-start = ((bf16[2,128,512]{2,1,0:T(8,128)(2,1)}), bf16[2,128,512]{2,1,0:T(8,128)(2,1)S(1)}, u32[]{:S(2)}, u32[]{:S(2)}) async-start(bf16[2,128,512]{2,1,0:T(8,128)(2,1)} %broadcast_in_dim.6), calls=%async_computation | async-start | bytes 524288 | tf_op jit(solution)/shard_map/all_to_all | solution.py:26
  8.8 25.4 %copy-start.2 = (bf16[2,512,128]{2,1,0:T(8,128)(2,1)}, bf16[2,512,128]{2,1,0:T(8,128)(2,1)S(1)}, u32[]{:S(2)}) copy-start(bf16[2,512,128]{2,1,0:T(8,128)(2,1)S(1)} %fusion) | copy-start | bytes 786436
  8.8 16.0 %collective-permute-start.2 = (bf16[1024,128]{1,0:T(8,128)(2,1)S(1)}, bf16[1024,128]{1,0:T(8,128)(2,1)S(1)}, u32[]{:S(2)}, u32[]{:S(2)}) collective-permute-start(bf16[1024,128]{1,0:T(8,128)(2,1)S(1)} %bitcast.36), channel_id=1, source_target_pairs={{0,14},{2,0},{4,2},{6,4},{8,6},{10,8},{12,10},{14,12},{1,15},{3,1}... | collective-permute-start | bytes 786440 | tf_op jit(solution)/shard_map/ppermute | solution.py:15
  18.8 13.9 %collective-permute-start.1 = (bf16[1024,128]{1,0:T(8,128)(2,1)S(1)}, bf16[1024,128]{1,0:T(8,128)(2,1)S(1)}, u32[]{:S(2)}, u32[]{:S(2)}) collective-permute-start(bf16[1024,128]{1,0:T(8,128)(2,1)S(1)} %bitcast.37), channel_id=1, source_target_pairs={{0,2},{2,4},{4,6},{6,8},{8,10},{10,12},{12,14},{14,0},{1,3},{3,5},... | collective-permute-start | bytes 786440 | tf_op jit(solution)/shard_map/ppermute | solution.py:15
  20.7 12.0 %collective-permute-start = (bf16[1024,128]{1,0:T(8,128)(2,1)S(1)}, bf16[1024,128]{1,0:T(8,128)(2,1)S(1)}, u32[]{:S(2)}, u32[]{:S(2)}) collective-permute-start(bf16[1024,128]{1,0:T(8,128)(2,1)S(1)} %bitcast.38), channel_id=1, source_target_pairs={{0,16},{16,0},{1,17},{17,1},{2,18},{18,2},{3,19},{19,3},{4,20},{20... | collective-permute-start | bytes 786440 | tf_op jit(solution)/shard_map/ppermute | solution.py:15
  24.9 9.4 %copy-start.3 = (bf16[1024,128]{1,0:T(8,128)(2,1)}, bf16[1024,128]{1,0:T(8,128)(2,1)S(1)}, u32[]{:S(2)}) copy-start(bf16[1024,128]{1,0:T(8,128)(2,1)S(1)} %collective-permute-done.2.refs_4_) | copy-start | bytes 786436
  32.7 1.6 %copy-start.4 = (bf16[1024,128]{1,0:T(8,128)(2,1)}, bf16[1024,128]{1,0:T(8,128)(2,1)S(1)}, u32[]{:S(2)}) copy-start(bf16[1024,128]{1,0:T(8,128)(2,1)S(1)} %collective-permute-done.1.refs_3_) | copy-start | bytes 786436
  32.7 1.6 %copy-start.5 = (bf16[1024,128]{1,0:T(8,128)(2,1)}, bf16[1024,128]{1,0:T(8,128)(2,1)S(1)}, u32[]{:S(2)}) copy-start(bf16[1024,128]{1,0:T(8,128)(2,1)S(1)} %collective-permute-done.refs_2_) | copy-start | bytes 786436
  34.3 59.5 %all-to-all-start.1 = ((bf16[16,128,512]{2,1,0:T(8,128)(2,1)}), bf16[16,128,512]{2,1,0:T(8,128)(2,1)S(1)}, u32[]{:S(2)}, u32[]{:S(2)}) async-start(bf16[16,128,512]{2,1,0:T(8,128)(2,1)} %broadcast_in_dim.7), calls=%async_computation.1 | async-start | bytes 4194304 | tf_op jit(solution)/shard_map/all_to_all | solution.py:110
  44.3 8.5 %collective-permute-start.4 = (bf16[1024,128]{1,0:T(8,128)(2,1)}, bf16[1024,128]{1,0:T(8,128)(2,1)S(1)}, u32[]{:S(2)}, u32[]{:S(2)}) collective-permute-start(bf16[1024,128]{1,0:T(8,128)(2,1)} %copy-done.5), channel_id=1, source_target_pairs={{0,14},{2,0},{4,2},{6,4},{8,6},{10,8},{12,10},{14,12},{1,15},{3,1}... | collective-permute-start | bytes 786440 | tf_op jit(solution)/shard_map/ppermute | solution.py:15
  47.6 11.8 %collective-permute-start.5 = (bf16[1024,128]{1,0:T(8,128)(2,1)}, bf16[1024,128]{1,0:T(8,128)(2,1)S(1)}, u32[]{:S(2)}, u32[]{:S(2)}) collective-permute-start(bf16[1024,128]{1,0:T(8,128)(2,1)} %copy-done.4), channel_id=1, source_target_pairs={{0,2},{2,4},{4,6},{6,8},{8,10},{10,12},{12,14},{14,0},{1,3},{3,5},... | collective-permute-start | bytes 786440 | tf_op jit(solution)/shard_map/ppermute | solution.py:15
  49.6 12.1 %collective-permute-start.3 = (bf16[1024,128]{1,0:T(8,128)(2,1)}, bf16[1024,128]{1,0:T(8,128)(2,1)S(1)}, u32[]{:S(2)}, u32[]{:S(2)}) collective-permute-start(bf16[1024,128]{1,0:T(8,128)(2,1)} %copy-done.5), channel_id=1, source_target_pairs={{0,2},{2,4},{4,6},{6,8},{8,10},{10,12},{12,14},{14,0},{1,3},{3,5},... | collective-permute-start | bytes 786440 | tf_op jit(solution)/shard_map/ppermute | solution.py:15
  52.8 40.9 %copy-start.6 = (bf16[1024,128]{1,0:T(8,128)(2,1)}, bf16[1024,128]{1,0:T(8,128)(2,1)S(1)}, u32[]{:S(2)}) copy-start(bf16[1024,128]{1,0:T(8,128)(2,1)S(1)} %collective-permute-done.4.refs_6_) | copy-start | bytes 786436
  52.8 12.6 %collective-permute-start.8 = (bf16[1024,128]{1,0:T(8,128)(2,1)S(1)}, bf16[1024,128]{1,0:T(8,128)(2,1)S(1)}, u32[]{:S(2)}, u32[]{:S(2)}) collective-permute-start(bf16[1024,128]{1,0:T(8,128)(2,1)S(1)} %collective-permute-done.4.refs_6_), channel_id=1, source_target_pairs={{0,14},{2,0},{4,2},{6,4},{8,6},{10,8},{12,10},{14,12},{1,15},{3,1}... | collective-permute-start | bytes 786440 | tf_op jit(solution)/shard_map/ppermute | solution.py:15
  56.4 11.9 %collective-permute-start.6 = (bf16[1024,128]{1,0:T(8,128)(2,1)}, bf16[1024,128]{1,0:T(8,128)(2,1)}, u32[]{:S(2)}, u32[]{:S(2)}) collective-permute-start(bf16[1024,128]{1,0:T(8,128)(2,1)} %copy-done.3), channel_id=1, source_target_pairs={{0,14},{2,0},{4,2},{6,4},{8,6},{10,8},{12,10},{14,12},{1,15},{3,1}... | collective-permute-start | bytes 786440 | tf_op jit(solution)/shard_map/ppermute | solution.py:15
  59.4 6.1 %copy-start.7 = (bf16[1024,128]{1,0:T(8,128)(2,1)}, bf16[1024,128]{1,0:T(8,128)(2,1)S(1)}, u32[]{:S(2)}) copy-start(bf16[1024,128]{1,0:T(8,128)(2,1)S(1)} %collective-permute-done.5.refs_7_) | copy-start | bytes 786436
  59.4 11.9 %collective-permute-start.9 = (bf16[1024,128]{1,0:T(8,128)(2,1)S(1)}, bf16[1024,128]{1,0:T(8,128)(2,1)}, u32[]{:S(2)}, u32[]{:S(2)}) collective-permute-start(bf16[1024,128]{1,0:T(8,128)(2,1)S(1)} %collective-permute-done.5.refs_7_), channel_id=1, source_target_pairs={{0,2},{2,4},{4,6},{6,8},{8,10},{10,12},{12,14},{14,0},{1,3},{3,5},... | collective-permute-start | bytes 786440 | tf_op jit(solution)/shard_map/ppermute | solution.py:15
  61.7 9.6 %copy-start.8 = (bf16[1024,128]{1,0:T(8,128)(2,1)}, bf16[1024,128]{1,0:T(8,128)(2,1)S(1)}, u32[]{:S(2)}) copy-start(bf16[1024,128]{1,0:T(8,128)(2,1)S(1)} %collective-permute-done.3.refs_5_) | copy-start | bytes 786436
  61.7 11.9 %collective-permute-start.7 = (bf16[1024,128]{1,0:T(8,128)(2,1)S(1)}, bf16[1024,128]{1,0:T(8,128)(2,1)}, u32[]{:S(2)}, u32[]{:S(2)}) collective-permute-start(bf16[1024,128]{1,0:T(8,128)(2,1)S(1)} %collective-permute-done.3.refs_5_), channel_id=1, source_target_pairs={{0,2},{2,4},{4,6},{6,8},{8,10},{10,12},{12,14},{14,0},{1,3},{3,5},... | collective-permute-start | bytes 786440 | tf_op jit(solution)/shard_map/ppermute | solution.py:15
  65.5 8.1 %copy-start.9 = (bf16[1024,128]{1,0:T(8,128)(2,1)}, bf16[1024,128]{1,0:T(8,128)(2,1)S(1)}, u32[]{:S(2)}) copy-start(bf16[1024,128]{1,0:T(8,128)(2,1)S(1)} %collective-permute-done.8.refs_10_) | copy-start | bytes 786436
  65.5 11.9 %collective-permute-start.12 = (bf16[1024,128]{1,0:T(8,128)(2,1)S(1)}, bf16[1024,128]{1,0:T(8,128)(2,1)}, u32[]{:S(2)}, u32[]{:S(2)}) collective-permute-start(bf16[1024,128]{1,0:T(8,128)(2,1)S(1)} %collective-permute-done.8.refs_10_), channel_id=1, source_target_pairs={{0,14},{2,0},{4,2},{6,4},{8,6},{10,8},{12,10},{14,12},{1,15},{3,1}... | collective-permute-start | bytes 786440 | tf_op jit(solution)/shard_map/ppermute | solution.py:15
  68.3 12.6 %collective-permute-start.10 = (bf16[1024,128]{1,0:T(8,128)(2,1)}, bf16[1024,128]{1,0:T(8,128)(2,1)}, u32[]{:S(2)}, u32[]{:S(2)}) collective-permute-start(bf16[1024,128]{1,0:T(8,128)(2,1)} %collective-permute-done.6.refs_8_), channel_id=1, source_target_pairs={{0,14},{2,0},{4,2},{6,4},{8,6},{10,8},{12,10},{14,12},{1,15},{3,1}... | collective-permute-start | bytes 786440 | tf_op jit(solution)/shard_map/ppermute | solution.py:15
  71.3 9.6 %collective-permute-start.13 = (bf16[1024,128]{1,0:T(8,128)(2,1)}, bf16[1024,128]{1,0:T(8,128)(2,1)}, u32[]{:S(2)}, u32[]{:S(2)}) collective-permute-start(bf16[1024,128]{1,0:T(8,128)(2,1)} %collective-permute-done.9.refs_11_), channel_id=1, source_target_pairs={{0,2},{2,4},{4,6},{6,8},{8,10},{10,12},{12,14},{14,0},{1,3},{3,5},... | collective-permute-start | bytes 786440 | tf_op jit(solution)/shard_map/ppermute | solution.py:15
  73.6 9.3 %collective-permute-start.11 = (bf16[1024,128]{1,0:T(8,128)(2,1)}, bf16[1024,128]{1,0:T(8,128)(2,1)}, u32[]{:S(2)}, u32[]{:S(2)}) collective-permute-start(bf16[1024,128]{1,0:T(8,128)(2,1)} %collective-permute-done.7.refs_9_), channel_id=1, source_target_pairs={{0,2},{2,4},{4,6},{6,8},{8,10},{10,12},{12,14},{14,0},{1,3},{3,5},... | collective-permute-start | bytes 786440 | tf_op jit(solution)/shard_map/ppermute | solution.py:15
  77.4 7.7 %collective-permute-start.14 = (bf16[1024,128]{1,0:T(8,128)(2,1)}, bf16[1024,128]{1,0:T(8,128)(2,1)}, u32[]{:S(2)}, u32[]{:S(2)}) collective-permute-start(bf16[1024,128]{1,0:T(8,128)(2,1)} %collective-permute-done.12.refs_14_), channel_id=1, source_target_pairs={{0,14},{2,0},{4,2},{6,4},{8,6},{10,8},{12,10},{14,12},{1,15},{3,1}... | collective-permute-start | bytes 786440 | tf_op jit(solution)/shard_map/ppermute | solution.py:15
  93.7 1.3 %copy-start.1 = (bf16[16,128,512]{2,1,0:T(8,128)(2,1)}, bf16[16,128,512]{2,1,0:T(8,128)(2,1)S(1)}, u32[]{:S(2)}) copy-start(bf16[16,128,512]{2,1,0:T(8,128)(2,1)S(1)} %all-to-all-done.1.refs_17_) | copy-start | bytes 6291460
  101.1 10.9 %collective-permute-start.15 = (f32[1024,256]{1,0:T(8,128)}, f32[1024,256]{1,0:T(8,128)S(1)}, u32[]{:S(2)}, u32[]{:S(2)}) collective-permute-start(f32[1024,256]{1,0:T(8,128)} %shard_map.47), channel_id=1, source_target_pairs={{0,1},{1,0},{2,3},{3,2},{4,5},{5,4},{6,7},{7,6},{8,9},{9,8},{10,11... | collective-permute-start | bytes 3145736 | tf_op jit(solution)/shard_map/ppermute | solution.py:15

commit v7 on v6

--- a/solution.py
+++ b/solution.py
@@ -27,7 +27,7 @@
     return jnp.where(f > m, got[0], jnp.where(f < m, got[1], x))
 
 
-def products(places, pieces, grad_all):
+def products(places, pieces, grad_all, acc=None, vmem_mib=56):
     width, rows = pieces[0].shape
     cols = grad_all.shape[2] // 2
     n = len(pieces)
@@ -36,50 +36,67 @@
 
     def kernel(*refs):
         places_ref, piece_refs = refs[0], refs[1 : 1 + n]
-        grad_ref, out_ref, held, grad_held, sems, grad_sem = refs[1 + n :]
-        grad_copy = pltpu.make_async_copy(grad_ref, grad_held, grad_sem)
-        grad_copy.start()
+        grad_ref = refs[1 + n]
+        out_ref, held, grad_held, sems, grad_sems = refs[-5:]
+        grad_copies = [
+            pltpu.make_async_copy(grad_ref.at[places_ref[i]], grad_held.at[i], grad_sems.at[i]) for i in range(n)
+        ]
         copies = [pltpu.make_async_copy(piece_refs[i], held.at[i], sems.at[i]) for i in range(n)]
-        for copy in copies:
-            copy.start()
-        grad_copy.wait()
-        where = pl.ds(pl.multiple_of(places_ref[n] * cols, cols), cols)
+        if acc is not None:
+            half = places_ref[n]
+            acc_copy = pltpu.make_async_copy(refs[2 + n].at[half], out_ref, sems.at[n])
+            acc_copy.start()
+        for i in range(n):
+            grad_copies[i].start()
+            copies[i].start()
         for first in range(0, n, per_group):
             group = range(first, min(first + per_group, n))
-            grad = jnp.concatenate([grad_held[places_ref[i], :, where] for i in group], axis=0)
             for i in group:
+                grad_copies[i].wait()
                 copies[i].wait()
+            if acc is None:
+                grad = jnp.concatenate([grad_held[i] for i in group], axis=0)
+            else:
+                where = pl.ds(pl.multiple_of(half * cols, cols), cols)
+                grad = jnp.concatenate([grad_held[i, :, where] for i in group], axis=0)
+                acc_copy.wait()
             for t in range(width // tile):
                 at = slice(t * tile, (t + 1) * tile)
                 lhs = jnp.concatenate([held[i, at] for i in group], axis=1)
                 total = jnp.dot(lhs, grad, preferred_element_type=jnp.float32)
-                if first == 0:
-                    out_ref[at] = total
+                if acc is not None:
+                    out_ref[at] += total
+                elif first == 0:
+                    out_ref[0, at] = total[:, :cols]
+                    out_ref[1, at] = total[:, cols:]
                 else:
-                    out_ref[at] += total
+                    out_ref[0, at] += total[:, :cols]
+                    out_ref[1, at] += total[:, cols:]
 
     def size(a):
         return a.size * a.dtype.itemsize
 
+    shape = (2, width, cols) if acc is None else (width, cols)
+    extra = [] if acc is None else [acc]
     return pl.pallas_call(
         kernel,
         in_specs=[pl.BlockSpec(memory_space=pltpu.SMEM)]
-        + [pl.BlockSpec(memory_space=pltpu.HBM)] * (n + 1),
+        + [pl.BlockSpec(memory_space=pltpu.HBM)] * (n + 1 + len(extra)),
         out_specs=pl.BlockSpec(memory_space=pltpu.VMEM),
-        out_shape=jax.ShapeDtypeStruct((width, cols), jnp.float32),
+        out_shape=jax.ShapeDtypeStruct(shape, jnp.float32),
         scratch_shapes=[
             pltpu.VMEM((n, width, rows), pieces[0].dtype),
-            pltpu.VMEM(grad_all.shape, grad_all.dtype),
+            pltpu.VMEM((n,) + grad_all.shape[1:], grad_all.dtype),
+            pltpu.SemaphoreType.DMA((n + 1,)),
             pltpu.SemaphoreType.DMA((n,)),
-            pltpu.SemaphoreType.DMA,
         ],
-        compiler_params=pltpu.CompilerParams(vmem_limit_bytes=56 * 1024 * 1024),
+        compiler_params=pltpu.CompilerParams(vmem_limit_bytes=vmem_mib * 1024 * 1024),
         cost_estimate=pl.CostEstimate(
-            flops=2 * width * cols * rows * n,
-            bytes_accessed=sum(map(size, pieces)) + size(grad_all) + width * cols * 4,
+            flops=2 * width * cols * rows * n * (2 if acc is None else 1),
+            bytes_accessed=sum(map(size, pieces)) + size(grad_all) + width * cols * 8,
             transcendentals=0,
         ),
-    )(places, *pieces, grad_all)
+    )(places, *pieces, grad_all, *extra)
 
 
 def per_device(activations, act_basis, gradients, grad_basis):
@@ -105,7 +122,7 @@
         far_down.append(shift(far_down[-1], "y", Y, -1))
     far_down.append(shift(far_down[-1], "y", Y, -1))
 
-    own, _, _, _ = lax.optimization_barrier((own, near_up[1], near_down[1], far_up[0]))
+    own, _ = lax.optimization_barrier((own, near_up[1]))
     copies = jnp.broadcast_to(own, (XH * Z,) + own.shape)
     grad_all = lax.all_to_all(copies, ("xh", "z"), 0, 0, tiled=True)
     grad_all = grad_all.reshape(XH * Z, rows, gradients.shape[1])
@@ -117,13 +134,15 @@
                 pieces.append(ring[k])
                 at.append((pair ^ xl) * Y + (y + Y + way * k) % Y)
 
-    def places(half):
-        return jnp.stack(at + [half]).astype(jnp.int32)
+    early = len(pieces) - 2
+    first = products(jnp.stack(at[:early]).astype(jnp.int32), pieces[:early], grad_all)
 
-    other = products(places(1 - c), pieces, grad_all)
+    def rest(half):
+        return products(jnp.stack(at[early:] + [half]).astype(jnp.int32), pieces[early:], grad_all, first)
+
+    other = rest(1 - c)
     got = shift(other, "c", C, 1)
-    mine = products(places(c), pieces, grad_all)
-    return (mine + got) / TOKENS
+    return (rest(c) + got) / TOKENS
 
 
 def solution(mesh):

time: 115 us -> 124 us (1.078)
  the two profiles are of different devices: /device:TPU:1 before, /device:TPU:133 now
where the time goes in v7:
time: 124 us; the launch traced here: 123 us
  starting transfers between devices  64.7 us (52%)
  waiting for transfers between devices  34.1 us (28%)
  Pallas kernels  12.7 us (10%)
  local copies, waits for them, and re-layouts  4.93 us (4%)
  other arithmetic  3.56 us (3%)
  matrix products  2.9 us (2%)
    ppermute x16, starting transfers between devices, shift(): return lax.ppermute(x, axis, [(i, (i + step) % size) for i in range(size)])  50.4 us
    ppermute x16, waiting for transfers between devices, shift(): return lax.ppermute(x, axis, [(i, (i + step) % size) for i in range(size)])  34.1 us
    pallas_call x3, Pallas kernels, products(): pl.pallas_call(kernel, in_specs=[pl.BlockSpec(memory_space=pltpu.SMEM)] +...  12.7 us
    all_to_all x1, starting transfers between devices, per_device(): grad_all = lax.all_to_all(copies, ('xh', 'z'), 0, 0, tiled=True)  8.05 us
    all_to_all x1, starting transfers between devices, transpose_chips(): lax.all_to_all(sent, ('xh', 'z', 'xl', 'y'), 0, 0, axis_index_groups=groups)  6.33 us
  transfers between devices with their start and end apart: 18, of which 3 were waited for; matrix products, arithmetic and copies ran while one was open for 3% of the time, Pallas kernels for 8%

profile of v7, /device:TPU:133, one launch (start us, length us, event | category | flops | bytes accessed | tf_op | source)
XLA Modules:
  0.0 123.5 jit_solution(3451878925442492453)
XLA Ops:
  0.0 1.4 %fusion.1 = bf16[128,512]{1,0:T(8,128)(2,1)S(1)} fusion(bf16[128,512]{1,0:T(8,128)(2,1)} %param.6, bf16[512,512]{1,0:T(8,128)(2,1)} %param.7), kind=kOutput, calls=%fused_computation.3 | convolution fusion | flops 67239936 | bytes 786432 | tf_op jit(solution)/shard_map/dot_general | solution.py:106
  1.4 0.7 broadcast_in_dim.6
  2.2 6.3 %all-to-all-start = ((bf16[2,128,512]{2,1,0:T(8,128)(2,1)}), bf16[2,128,512]{2,1,0:T(8,128)(2,1)S(1)}, u32[]{:S(2)}, u32[]{:S(2)}) async-start(bf16[2,128,512]{2,1,0:T(8,128)(2,1)} %broadcast_in_dim.6), calls=%async_computation | async-start | bytes 524288 | tf_op jit(solution)/shard_map/all_to_all | solution.py:26
  8.5 1.5 %fusion = bf16[2,512,128]{2,1,0:T(8,128)(2,1)S(1)} fusion(bf16[2,512,512]{2,1,0:T(8,128)(2,1)S(1)} %copy-done, bf16[16,2,8,512]{3,2,1,0:T(8,128)(2,1)} %bitcast.40), kind=kOutput, calls=%fused_computation.1 | convolution fusion | flops 134479872 | bytes 1572864 | tf_op jit(solution)/shard_map/tbk,bkj->bjt/dot_general | solution.py:111
  10.0 1.9 %collective-permute-start = (bf16[1024,128]{1,0:T(8,128)(2,1)S(1)}, bf16[1024,128]{1,0:T(8,128)(2,1)S(1)}, u32[]{:S(2)}, u32[]{:S(2)}) collective-permute-start(bf16[1024,128]{1,0:T(8,128)(2,1)S(1)} %bitcast.36), channel_id=1, source_target_pairs={{0,2},{2,4},{4,6},{6,8},{8,10},{10,12},{12,14},{14,0},{1,3},{3,5},... | collective-permute-start | bytes 786440 | tf_op jit(solution)/shard_map/ppermute | solution.py:15
  12.0 16.5 %collective-permute-done.refs_3_ = bf16[1024,128]{1,0:T(8,128)(2,1)S(1)} collective-permute-done((bf16[1024,128]{1,0:T(8,128)(2,1)S(1)}, bf16[1024,128]{1,0:T(8,128)(2,1)S(1)}, u32[]{:S(2)}, u32[]{:S(2)}) %collective-permute-start) | collective-permute-done | bytes 262176 | tf_op jit(solution)/shard_map/ppermute | solution.py:15
  28.5 1.5 %broadcast_in_dim.7 = bf16[16,128,512]{2,1,0:T(8,128)(2,1)} broadcast(bf16[128,512]{1,0:T(8,128)(2,1)S(1)} %fusion.5), dimensions={1,2} | broadcast | bytes 2228224 | tf_op jit(solution)/shard_map/broadcast_in_dim | solution.py:126
  30.0 8.0 %all-to-all-start.1 = ((bf16[16,128,512]{2,1,0:T(8,128)(2,1)}), bf16[16,128,512]{2,1,0:T(8,128)(2,1)S(1)}, u32[]{:S(2)}, u32[]{:S(2)}) async-start(bf16[16,128,512]{2,1,0:T(8,128)(2,1)} %broadcast_in_dim.7), calls=%async_computation.1 | async-start | bytes 4194304 | tf_op jit(solution)/shard_map/all_to_all | solution.py:127
  38.1 1.9 %collective-permute-start.4 = (bf16[1024,128]{1,0:T(8,128)(2,1)S(1)}, bf16[1024,128]{1,0:T(8,128)(2,1)S(1)}, u32[]{:S(2)}, u32[]{:S(2)}) collective-permute-start(bf16[1024,128]{1,0:T(8,128)(2,1)S(1)} %bitcast.37), channel_id=1, source_target_pairs={{0,16},{16,0},{1,17},{17,1},{2,18},{18,2},{3,19},{19,3},{4,20},{20... | collective-permute-start | bytes 786440 | tf_op jit(solution)/shard_map/ppermute | solution.py:15
  40.0 15.8 %collective-permute-done.4.refs_2_ = bf16[1024,128]{1,0:T(8,128)(2,1)S(1)} collective-permute-done((bf16[1024,128]{1,0:T(8,128)(2,1)S(1)}, bf16[1024,128]{1,0:T(8,128)(2,1)S(1)}, u32[]{:S(2)}, u32[]{:S(2)}) %collective-permute-start.4) | collective-permute-done | bytes 262176 | tf_op jit(solution)/shard_map/ppermute | solution.py:15
  55.8 2.9 %collective-permute-start.5 = (bf16[1024,128]{1,0:T(8,128)(2,1)S(1)}, bf16[1024,128]{1,0:T(8,128)(2,1)S(1)}, u32[]{:S(2)}, u32[]{:S(2)}) collective-permute-start(bf16[1024,128]{1,0:T(8,128)(2,1)S(1)} %collective-permute-done.4.refs_2_), channel_id=1, source_target_pairs={{0,14},{2,0},{4,2},{6,4},{8,6},{10,8},{12,10},{14,12},{1,15},{3,1}... | collective-permute-start | bytes 786440 | tf_op jit(solution)/shard_map/ppermute | solution.py:15
  58.7 6.1 %collective-permute-start.9 = (bf16[1024,128]{1,0:T(8,128)(2,1)S(1)}, bf16[1024,128]{1,0:T(8,128)(2,1)S(1)}, u32[]{:S(2)}, u32[]{:S(2)}) collective-permute-start(bf16[1024,128]{1,0:T(8,128)(2,1)S(1)} %bitcast.38), channel_id=1, source_target_pairs={{0,14},{2,0},{4,2},{6,4},{8,6},{10,8},{12,10},{14,12},{1,15},{3,1}... | collective-permute-start | bytes 786440 | tf_op jit(solution)/shard_map/ppermute | solution.py:15
  64.8 1.9 %collective-permute-start.10 = (bf16[1024,128]{1,0:T(8,128)(2,1)S(1)}, bf16[1024,128]{1,0:T(8,128)(2,1)S(1)}, u32[]{:S(2)}, u32[]{:S(2)}) collective-permute-start(bf16[1024,128]{1,0:T(8,128)(2,1)S(1)} %collective-permute-done.4.refs_2_), channel_id=1, source_target_pairs={{0,2},{2,4},{4,6},{6,8},{8,10},{10,12},{12,14},{14,0},{1,3},{3,5},... | collective-permute-start | bytes 786440 | tf_op jit(solution)/shard_map/ppermute | solution.py:15
  66.8 1.9 %collective-permute-start.1 = (bf16[1024,128]{1,0:T(8,128)(2,1)}, bf16[1024,128]{1,0:T(8,128)(2,1)}, u32[]{:S(2)}, u32[]{:S(2)}) collective-permute-start(bf16[1024,128]{1,0:T(8,128)(2,1)} %copy-done.4), channel_id=1, source_target_pairs={{0,2},{2,4},{4,6},{6,8},{8,10},{10,12},{12,14},{14,0},{1,3},{3,5},... | collective-permute-start | bytes 786440 | tf_op jit(solution)/shard_map/ppermute | solution.py:15
  68.7 4.6 %collective-permute-start.6 = (bf16[1024,128]{1,0:T(8,128)(2,1)S(1)}, bf16[1024,128]{1,0:T(8,128)(2,1)}, u32[]{:S(2)}, u32[]{:S(2)}) collective-permute-start(bf16[1024,128]{1,0:T(8,128)(2,1)S(1)} %collective-permute-done.5.refs_6_), channel_id=1, source_target_pairs={{0,14},{2,0},{4,2},{6,4},{8,6},{10,8},{12,10},{14,12},{1,15},{3,1}... | collective-permute-start | bytes 786440 | tf_op jit(solution)/shard_map/ppermute | solution.py:15
  73.3 3.4 %collective-permute-start.11 = (bf16[1024,128]{1,0:T(8,128)(2,1)S(1)}, bf16[1024,128]{1,0:T(8,128)(2,1)}, u32[]{:S(2)}, u32[]{:S(2)}) collective-permute-start(bf16[1024,128]{1,0:T(8,128)(2,1)S(1)} %collective-permute-done.9.refs_4_), channel_id=1, source_target_pairs={{0,14},{2,0},{4,2},{6,4},{8,6},{10,8},{12,10},{14,12},{1,15},{3,1}... | collective-permute-start | bytes 786440 | tf_op jit(solution)/shard_map/ppermute | solution.py:15
  76.7 1.9 %collective-permute-start.12 = (bf16[1024,128]{1,0:T(8,128)(2,1)S(1)}, bf16[1024,128]{1,0:T(8,128)(2,1)}, u32[]{:S(2)}, u32[]{:S(2)}) collective-permute-start(bf16[1024,128]{1,0:T(8,128)(2,1)S(1)} %collective-permute-done.10.refs_5_), channel_id=1, source_target_pairs={{0,2},{2,4},{4,6},{6,8},{8,10},{10,12},{12,14},{14,0},{1,3},{3,5},... | collective-permute-start | bytes 786440 | tf_op jit(solution)/shard_map/ppermute | solution.py:15
  78.6 1.8 %collective-permute-done.1.refs_7_ = bf16[1024,128]{1,0:T(8,128)(2,1)} collective-permute-done((bf16[1024,128]{1,0:T(8,128)(2,1)}, bf16[1024,128]{1,0:T(8,128)(2,1)}, u32[]{:S(2)}, u32[]{:S(2)}) %collective-permute-start.1) | collective-permute-done | bytes 262176 | tf_op jit(solution)/shard_map/ppermute | solution.py:15
  80.5 1.9 %collective-permute-start.2 = (bf16[1024,128]{1,0:T(8,128)(2,1)}, bf16[1024,128]{1,0:T(8,128)(2,1)}, u32[]{:S(2)}, u32[]{:S(2)}) collective-permute-start(bf16[1024,128]{1,0:T(8,128)(2,1)} %collective-permute-done.1.refs_7_), channel_id=1, source_target_pairs={{0,2},{2,4},{4,6},{6,8},{8,10},{10,12},{12,14},{14,0},{1,3},{3,5},... | collective-permute-start | bytes 786440 | tf_op jit(solution)/shard_map/ppermute | solution.py:15
  82.4 4.6 %collective-permute-start.7 = (bf16[1024,128]{1,0:T(8,128)(2,1)}, bf16[1024,128]{1,0:T(8,128)(2,1)}, u32[]{:S(2)}, u32[]{:S(2)}) collective-permute-start(bf16[1024,128]{1,0:T(8,128)(2,1)} %collective-permute-done.6.refs_10_), channel_id=1, source_target_pairs={{0,14},{2,0},{4,2},{6,4},{8,6},{10,8},{12,10},{14,12},{1,15},{3,1}... | collective-permute-start | bytes 786440 | tf_op jit(solution)/shard_map/ppermute | solution.py:15
  87.0 1.9 %collective-permute-start.13 = (bf16[1024,128]{1,0:T(8,128)(2,1)}, bf16[1024,128]{1,0:T(8,128)(2,1)}, u32[]{:S(2)}, u32[]{:S(2)}) collective-permute-start(bf16[1024,128]{1,0:T(8,128)(2,1)} %collective-permute-done.11.refs_8_), channel_id=1, source_target_pairs={{0,14},{2,0},{4,2},{6,4},{8,6},{10,8},{12,10},{14,12},{1,15},{3,1}... | collective-permute-start | bytes 786440 | tf_op jit(solution)/shard_map/ppermute | solution.py:15
  88.9 3.4 %collective-permute-start.14 = (bf16[1024,128]{1,0:T(8,128)(2,1)}, bf16[1024,128]{1,0:T(8,128)(2,1)}, u32[]{:S(2)}, u32[]{:S(2)}) collective-permute-start(bf16[1024,128]{1,0:T(8,128)(2,1)} %collective-permute-done.12.refs_9_), channel_id=1, source_target_pairs={{0,2},{2,4},{4,6},{6,8},{8,10},{10,12},{12,14},{14,0},{1,3},{3,5},... | collective-permute-start | bytes 786440 | tf_op jit(solution)/shard_map/ppermute | solution.py:15
  93.0 1.9 %collective-permute-start.3 = (bf16[1024,128]{1,0:T(8,128)(2,1)}, bf16[1024,128]{1,0:T(8,128)(2,1)S(1)}, u32[]{:S(2)}, u32[]{:S(2)}) collective-permute-start(bf16[1024,128]{1,0:T(8,128)(2,1)} %collective-permute-done.2.refs_11_), channel_id=1, source_target_pairs={{0,2},{2,4},{4,6},{6,8},{8,10},{10,12},{12,14},{14,0},{1,3},{3,5},... | collective-permute-start | bytes 786440 | tf_op jit(solution)/shard_map/ppermute | solution.py:15
  94.9 4.6 %collective-permute-start.8 = (bf16[1024,128]{1,0:T(8,128)(2,1)}, bf16[1024,128]{1,0:T(8,128)(2,1)}, u32[]{:S(2)}, u32[]{:S(2)}) collective-permute-start(bf16[1024,128]{1,0:T(8,128)(2,1)} %collective-permute-done.7.refs_14_), channel_id=1, source_target_pairs={{0,14},{2,0},{4,2},{6,4},{8,6},{10,8},{12,10},{14,12},{1,15},{3,1}... | collective-permute-start | bytes 786440 | tf_op jit(solution)/shard_map/ppermute | solution.py:15
  99.5 0.6 pad_add_fusion.2.refs_0_
  100.1 1.3 %copy-done.1 = bf16[16,128,512]{2,1,0:T(8,128)(2,1)} copy-done((bf16[16,128,512]{2,1,0:T(8,128)(2,1)}, bf16[16,128,512]{2,1,0:T(8,128)(2,1)S(1)}, u32[]{:S(2)}) %copy-start.1) | copy-done | bytes 2097176
  101.5 5.9 %shard_map.46.refs_4_ = f32[2,1024,256]{2,1,0:T(8,128)} custom-call(s32[14]{0:T(128)} %stack.83.refs_0_, bf16[1024,128]{1,0:T(8,128)(2,1)} %bitcast.39, bf16[1024,128]{1,0:T(8,128)(2,1)} %copy-done.5, bf16[1024,128]{1,0:T(8,128)(2,1)} %copy-done.4, bf16[1024,128]{1,0:T(8,128)(2,1)} %copy-done.7, bf16[1024,128]{1,0:T(8,128)(2,1)} %copy-done.8, ...), custom_call_target="tpu_custom_call" | custom-call | flops 1879048192 | bytes 7864320 | tf_op jit(solution)/shard_map/pallas_call | solution.py:81
  107.4 0.7 copy-done.2
  108.1 3.5 %shard_map.48 = f32[1024,256]{1,0:T(8,128)} custom-call(s32[3]{0:T(128)} %pad_add_fusion.2.refs_0_, bf16[1024,128]{1,0:T(8,128)(2,1)} %copy-done.2, bf16[1024,128]{1,0:T(8,128)(2,1)} %collective-permute-done.8.refs_2_, bf16[16,128,512]{2,1,0:T(8,128)(2,1)} %copy-done.1, f32[2,1024,256]{2,1,0:T(8,128)} %shard_map.46.refs_4_), custom_call_target="tpu_custom_call" | custom-call | flops 134217728 | bytes 4718592 | tf_op jit(solution)/shard_map/pallas_call | solution.py:81
  111.5 5.5 %collective-permute-start.15 = (f32[1024,256]{1,0:T(8,128)}, f32[1024,256]{1,0:T(8,128)S(1)}, u32[]{:S(2)}, u32[]{:S(2)}) collective-permute-start(f32[1024,256]{1,0:T(8,128)} %shard_map.48), channel_id=1, source_target_pairs={{0,1},{1,0},{2,3},{3,2},{4,5},{5,4},{6,7},{7,6},{8,9},{9,8},{10,11... | collective-permute-start | bytes 3145736 | tf_op jit(solution)/shard_map/ppermute | solution.py:15
  117.7 3.4 %shard_map.47 = f32[1024,256]{1,0:T(8,128)} custom-call(s32[3]{0:T(128)} %pad_add_fusion.refs_0_, bf16[1024,128]{1,0:T(8,128)(2,1)} %copy-done.2, bf16[1024,128]{1,0:T(8,128)(2,1)} %collective-permute-done.8.refs_2_, bf16[16,128,512]{2,1,0:T(8,128)(2,1)} %copy-done.1, f32[2,1024,256]{2,1,0:T(8,128)} %shard_map.46.refs_4_), custom_call_target="tpu_custom_call" | custom-call | flops 134217728 | bytes 4718592 | tf_op jit(solution)/shard_map/pallas_call | solution.py:81
  121.1 2.3 %add_multiply_fusion = f32[1024,256]{1,0:T(8,128)} fusion(f32[1024,256]{1,0:T(8,128)} %shard_map.47, f32[1024,256]{1,0:T(8,128)S(1)} %collective-permute-done.15), kind=kLoop, calls=%fused_computation.4 | loop fusion | flops 524288 | bytes 3145728 | tf_op jit(solution)/shard_map/div | solution.py:145
  (34 shorter events, 1.3 us)
Async XLA Ops:
  0.0 8.5 %copy-start = (bf16[2,512,512]{2,1,0:T(8,128)(2,1)S(1)}, bf16[2,512,512]{2,1,0:T(8,128)(2,1)}, u32[]{:S(2)}) copy-start(bf16[2,512,512]{2,1,0:T(8,128)(2,1)} %param.5) | copy-start | bytes 3145732
  2.2 9.8 %all-to-all-start = ((bf16[2,128,512]{2,1,0:T(8,128)(2,1)}), bf16[2,128,512]{2,1,0:T(8,128)(2,1)S(1)}, u32[]{:S(2)}, u32[]{:S(2)}) async-start(bf16[2,128,512]{2,1,0:T(8,128)(2,1)} %broadcast_in_dim.6), calls=%async_computation | async-start | bytes 524288 | tf_op jit(solution)/shard_map/all_to_all | solution.py:26
  10.0 48.7 %copy-start.3 = (bf16[2,512,128]{2,1,0:T(8,128)(2,1)}, bf16[2,512,128]{2,1,0:T(8,128)(2,1)S(1)}, u32[]{:S(2)}) copy-start(bf16[2,512,128]{2,1,0:T(8,128)(2,1)S(1)} %fusion) | copy-start | bytes 786436
  10.0 18.5 %collective-permute-start = (bf16[1024,128]{1,0:T(8,128)(2,1)S(1)}, bf16[1024,128]{1,0:T(8,128)(2,1)S(1)}, u32[]{:S(2)}, u32[]{:S(2)}) collective-permute-start(bf16[1024,128]{1,0:T(8,128)(2,1)S(1)} %bitcast.36), channel_id=1, source_target_pairs={{0,2},{2,4},{4,6},{6,8},{8,10},{10,12},{12,14},{14,0},{1,3},{3,5},... | collective-permute-start | bytes 786440 | tf_op jit(solution)/shard_map/ppermute | solution.py:15
  28.5 1.6 %copy-start.4 = (bf16[1024,128]{1,0:T(8,128)(2,1)}, bf16[1024,128]{1,0:T(8,128)(2,1)S(1)}, u32[]{:S(2)}) copy-start(bf16[1024,128]{1,0:T(8,128)(2,1)S(1)} %collective-permute-done.refs_3_) | copy-start | bytes 786436
  30.0 70.1 %all-to-all-start.1 = ((bf16[16,128,512]{2,1,0:T(8,128)(2,1)}), bf16[16,128,512]{2,1,0:T(8,128)(2,1)S(1)}, u32[]{:S(2)}, u32[]{:S(2)}) async-start(bf16[16,128,512]{2,1,0:T(8,128)(2,1)} %broadcast_in_dim.7), calls=%async_computation.1 | async-start | bytes 4194304 | tf_op jit(solution)/shard_map/all_to_all | solution.py:127
  38.1 17.7 %collective-permute-start.4 = (bf16[1024,128]{1,0:T(8,128)(2,1)S(1)}, bf16[1024,128]{1,0:T(8,128)(2,1)S(1)}, u32[]{:S(2)}, u32[]{:S(2)}) collective-permute-start(bf16[1024,128]{1,0:T(8,128)(2,1)S(1)} %bitcast.37), channel_id=1, source_target_pairs={{0,16},{16,0},{1,17},{17,1},{2,18},{18,2},{3,19},{19,3},{4,20},{20... | collective-permute-start | bytes 786440 | tf_op jit(solution)/shard_map/ppermute | solution.py:15
  55.8 17.5 %copy-start.5 = (bf16[1024,128]{1,0:T(8,128)(2,1)}, bf16[1024,128]{1,0:T(8,128)(2,1)S(1)}, u32[]{:S(2)}) copy-start(bf16[1024,128]{1,0:T(8,128)(2,1)S(1)} %collective-permute-done.4.refs_2_) | copy-start | bytes 786436
  55.8 12.9 %collective-permute-start.5 = (bf16[1024,128]{1,0:T(8,128)(2,1)S(1)}, bf16[1024,128]{1,0:T(8,128)(2,1)S(1)}, u32[]{:S(2)}, u32[]{:S(2)}) collective-permute-start(bf16[1024,128]{1,0:T(8,128)(2,1)S(1)} %collective-permute-done.4.refs_2_), channel_id=1, source_target_pairs={{0,14},{2,0},{4,2},{6,4},{8,6},{10,8},{12,10},{14,12},{1,15},{3,1}... | collective-permute-start | bytes 786440 | tf_op jit(solution)/shard_map/ppermute | solution.py:15
  58.7 14.6 %collective-permute-start.9 = (bf16[1024,128]{1,0:T(8,128)(2,1)S(1)}, bf16[1024,128]{1,0:T(8,128)(2,1)S(1)}, u32[]{:S(2)}, u32[]{:S(2)}) collective-permute-start(bf16[1024,128]{1,0:T(8,128)(2,1)S(1)} %bitcast.38), channel_id=1, source_target_pairs={{0,14},{2,0},{4,2},{6,4},{8,6},{10,8},{12,10},{14,12},{1,15},{3,1}... | collective-permute-start | bytes 786440 | tf_op jit(solution)/shard_map/ppermute | solution.py:15
  64.8 11.9 %collective-permute-start.10 = (bf16[1024,128]{1,0:T(8,128)(2,1)S(1)}, bf16[1024,128]{1,0:T(8,128)(2,1)S(1)}, u32[]{:S(2)}, u32[]{:S(2)}) collective-permute-start(bf16[1024,128]{1,0:T(8,128)(2,1)S(1)} %collective-permute-done.4.refs_2_), channel_id=1, source_target_pairs={{0,2},{2,4},{4,6},{6,8},{8,10},{10,12},{12,14},{14,0},{1,3},{3,5},... | collective-permute-start | bytes 786440 | tf_op jit(solution)/shard_map/ppermute | solution.py:15
  66.8 13.7 %collective-permute-start.1 = (bf16[1024,128]{1,0:T(8,128)(2,1)}, bf16[1024,128]{1,0:T(8,128)(2,1)}, u32[]{:S(2)}, u32[]{:S(2)}) collective-permute-start(bf16[1024,128]{1,0:T(8,128)(2,1)} %copy-done.4), channel_id=1, source_target_pairs={{0,2},{2,4},{4,6},{6,8},{8,10},{10,12},{12,14},{14,0},{1,3},{3,5},... | collective-permute-start | bytes 786440 | tf_op jit(solution)/shard_map/ppermute | solution.py:15
  68.7 8.0 %copy-start.6 = (bf16[1024,128]{1,0:T(8,128)(2,1)}, bf16[1024,128]{1,0:T(8,128)(2,1)S(1)}, u32[]{:S(2)}) copy-start(bf16[1024,128]{1,0:T(8,128)(2,1)S(1)} %collective-permute-done.5.refs_6_) | copy-start | bytes 786436
  68.7 13.7 %collective-permute-start.6 = (bf16[1024,128]{1,0:T(8,128)(2,1)S(1)}, bf16[1024,128]{1,0:T(8,128)(2,1)}, u32[]{:S(2)}, u32[]{:S(2)}) collective-permute-start(bf16[1024,128]{1,0:T(8,128)(2,1)S(1)} %collective-permute-done.5.refs_6_), channel_id=1, source_target_pairs={{0,14},{2,0},{4,2},{6,4},{8,6},{10,8},{12,10},{14,12},{1,15},{3,1}... | collective-permute-start | bytes 786440 | tf_op jit(solution)/shard_map/ppermute | solution.py:15
  73.3 9.1 %copy-start.7 = (bf16[1024,128]{1,0:T(8,128)(2,1)}, bf16[1024,128]{1,0:T(8,128)(2,1)S(1)}, u32[]{:S(2)}) copy-start(bf16[1024,128]{1,0:T(8,128)(2,1)S(1)} %collective-permute-done.9.refs_4_) | copy-start | bytes 786436
  73.3 13.7 %collective-permute-start.11 = (bf16[1024,128]{1,0:T(8,128)(2,1)S(1)}, bf16[1024,128]{1,0:T(8,128)(2,1)}, u32[]{:S(2)}, u32[]{:S(2)}) collective-permute-start(bf16[1024,128]{1,0:T(8,128)(2,1)S(1)} %collective-permute-done.9.refs_4_), channel_id=1, source_target_pairs={{0,14},{2,0},{4,2},{6,4},{8,6},{10,8},{12,10},{14,12},{1,15},{3,1}... | collective-permute-start | bytes 786440 | tf_op jit(solution)/shard_map/ppermute | solution.py:15
  76.7 10.3 %copy-start.8 = (bf16[1024,128]{1,0:T(8,128)(2,1)}, bf16[1024,128]{1,0:T(8,128)(2,1)S(1)}, u32[]{:S(2)}) copy-start(bf16[1024,128]{1,0:T(8,128)(2,1)S(1)} %collective-permute-done.10.refs_5_) | copy-start | bytes 786436
  76.7 12.2 %collective-permute-start.12 = (bf16[1024,128]{1,0:T(8,128)(2,1)S(1)}, bf16[1024,128]{1,0:T(8,128)(2,1)}, u32[]{:S(2)}, u32[]{:S(2)}) collective-permute-start(bf16[1024,128]{1,0:T(8,128)(2,1)S(1)} %collective-permute-done.10.refs_5_), channel_id=1, source_target_pairs={{0,2},{2,4},{4,6},{6,8},{8,10},{10,12},{12,14},{14,0},{1,3},{3,5},... | collective-permute-start | bytes 786440 | tf_op jit(solution)/shard_map/ppermute | solution.py:15
  80.5 12.5 %collective-permute-start.2 = (bf16[1024,128]{1,0:T(8,128)(2,1)}, bf16[1024,128]{1,0:T(8,128)(2,1)}, u32[]{:S(2)}, u32[]{:S(2)}) collective-permute-start(bf16[1024,128]{1,0:T(8,128)(2,1)} %collective-permute-done.1.refs_7_), channel_id=1, source_target_pairs={{0,2},{2,4},{4,6},{6,8},{8,10},{10,12},{12,14},{14,0},{1,3},{3,5},... | collective-permute-start | bytes 786440 | tf_op jit(solution)/shard_map/ppermute | solution.py:15
  82.4 12.5 %collective-permute-start.7 = (bf16[1024,128]{1,0:T(8,128)(2,1)}, bf16[1024,128]{1,0:T(8,128)(2,1)}, u32[]{:S(2)}, u32[]{:S(2)}) collective-permute-start(bf16[1024,128]{1,0:T(8,128)(2,1)} %collective-permute-done.6.refs_10_), channel_id=1, source_target_pairs={{0,14},{2,0},{4,2},{6,4},{8,6},{10,8},{12,10},{14,12},{1,15},{3,1}... | collective-permute-start | bytes 786440 | tf_op jit(solution)/shard_map/ppermute | solution.py:15
  87.0 13.1 %collective-permute-start.13 = (bf16[1024,128]{1,0:T(8,128)(2,1)}, bf16[1024,128]{1,0:T(8,128)(2,1)}, u32[]{:S(2)}, u32[]{:S(2)}) collective-permute-start(bf16[1024,128]{1,0:T(8,128)(2,1)} %collective-permute-done.11.refs_8_), channel_id=1, source_target_pairs={{0,14},{2,0},{4,2},{6,4},{8,6},{10,8},{12,10},{14,12},{1,15},{3,1}... | collective-permute-start | bytes 786440 | tf_op jit(solution)/shard_map/ppermute | solution.py:15
  88.9 11.2 %collective-permute-start.14 = (bf16[1024,128]{1,0:T(8,128)(2,1)}, bf16[1024,128]{1,0:T(8,128)(2,1)}, u32[]{:S(2)}, u32[]{:S(2)}) collective-permute-start(bf16[1024,128]{1,0:T(8,128)(2,1)} %collective-permute-done.12.refs_9_), channel_id=1, source_target_pairs={{0,2},{2,4},{4,6},{6,8},{8,10},{10,12},{12,14},{14,0},{1,3},{3,5},... | collective-permute-start | bytes 786440 | tf_op jit(solution)/shard_map/ppermute | solution.py:15
  93.0 14.3 %collective-permute-start.3 = (bf16[1024,128]{1,0:T(8,128)(2,1)}, bf16[1024,128]{1,0:T(8,128)(2,1)S(1)}, u32[]{:S(2)}, u32[]{:S(2)}) collective-permute-start(bf16[1024,128]{1,0:T(8,128)(2,1)} %collective-permute-done.2.refs_11_), channel_id=1, source_target_pairs={{0,2},{2,4},{4,6},{6,8},{8,10},{10,12},{12,14},{14,0},{1,3},{3,5},... | collective-permute-start | bytes 786440 | tf_op jit(solution)/shard_map/ppermute | solution.py:15
  94.9 12.4 %collective-permute-start.8 = (bf16[1024,128]{1,0:T(8,128)(2,1)}, bf16[1024,128]{1,0:T(8,128)(2,1)}, u32[]{:S(2)}, u32[]{:S(2)}) collective-permute-start(bf16[1024,128]{1,0:T(8,128)(2,1)} %collective-permute-done.7.refs_14_), channel_id=1, source_target_pairs={{0,14},{2,0},{4,2},{6,4},{8,6},{10,8},{12,10},{14,12},{1,15},{3,1}... | collective-permute-start | bytes 786440 | tf_op jit(solution)/shard_map/ppermute | solution.py:15
  100.1 1.3 %copy-start.1 = (bf16[16,128,512]{2,1,0:T(8,128)(2,1)}, bf16[16,128,512]{2,1,0:T(8,128)(2,1)S(1)}, u32[]{:S(2)}) copy-start(bf16[16,128,512]{2,1,0:T(8,128)(2,1)S(1)} %all-to-all-done.1.refs_15_.refs_3_) | copy-start | bytes 6291460
  107.3 0.7 copy-start.2
  111.5 9.6 %collective-permute-start.15 = (f32[1024,256]{1,0:T(8,128)}, f32[1024,256]{1,0:T(8,128)S(1)}, u32[]{:S(2)}, u32[]{:S(2)}) collective-permute-start(f32[1024,256]{1,0:T(8,128)} %shard_map.48), channel_id=1, source_target_pairs={{0,1},{1,0},{2,3},{3,2},{4,5},{5,4},{6,7},{7,6},{8,9},{9,8},{10,11... | collective-permute-start | bytes 3145736 | tf_op jit(solution)/shard_map/ppermute | solution.py:15

commit v8 on v3

v8 whole, which is shorter than its diff:
```python
import jax
import jax.numpy as jnp
from jax import lax
from jax.experimental import pallas as pl
from jax.experimental.pallas import tpu as pltpu
from jax.sharding import Mesh
from jax.sharding import PartitionSpec as P

BLOCK = 512
TOKENS = 4096
XH, Z, XL, Y, C = 2, 8, 2, 8, 2


def transpose_chips(x, sent):
    chips = XH * Z
    swaps = [[f * chips + m, m * chips + f] for f in range(chips) for m in range(f + 1, chips)]
    fixed = [f * chips + f for f in range(chips)]
    groups = swaps + [[fixed[i], fixed[i + 1]] for i in range(0, chips, 2)]
    f = lax.axis_index("xh") * Z + lax.axis_index("z")
    m = lax.axis_index("xl") * Y + lax.axis_index("y")
    got = lax.all_to_all(sent, ("xh", "z", "xl", "y"), 0, 0, axis_index_groups=groups)
    return jnp.where(f > m, got[0], jnp.where(f < m, got[1], x))


def swap(x, axis):
    return lax.ppermute(x, axis, [(0, 1), (1, 0)])


def product(swapped, act_all, near, far):
    _, _, width, rows = act_all.shape
    cols = near.shape[2]
    tile = width // 2

    def kernel(swapped_ref, act_ref, near_ref, far_ref, out_ref):
        def go(blocks):
            for t in range(width // tile):
                at = slice(t * tile, (t + 1) * tile)
                total = None
                for pair in range(2):
                    act = jnp.concatenate([act_ref[y, pair, at] for y in range(Y)], axis=1)
                    grad = jnp.concatenate([blocks[pair][y] for y in range(Y)], axis=0)
                    part = jnp.dot(act, grad, preferred_element_type=jnp.float32)
                    total = part if total is None else total + part
                out_ref[at] = total

        @pl.when(swapped_ref[0] == 0)
        def _():
            go((near_ref, far_ref))

        @pl.when(swapped_ref[0] != 0)
        def _():
            go((far_ref, near_ref))

    vmem = pl.BlockSpec(memory_space=pltpu.VMEM)
    return pl.pallas_call(
        kernel,
        in_specs=[pl.BlockSpec(memory_space=pltpu.SMEM), vmem, vmem, vmem],
        out_specs=vmem,
        out_shape=jax.ShapeDtypeStruct((width, cols), jnp.float32),
        compiler_params=pltpu.CompilerParams(vmem_limit_bytes=16 * 1024 * 1024),
        cost_estimate=pl.CostEstimate(
            flops=2 * width * cols * rows * 2 * Y,
            bytes_accessed=act_all.size * 2 + near.size * 4 + width * cols * 4,
            transcendentals=0,
        ),
    )(swapped, act_all, near, far)


def per_device(activations, act_basis, gradients, grad_basis):
    rows, act_width = activations.shape
    xh, c = lax.axis_index("xh"), lax.axis_index("c")

    grad_rot = jnp.dot(gradients, grad_basis, preferred_element_type=jnp.float32)
    grad_sq = (grad_rot * grad_rot).astype(jnp.bfloat16)
    grad_pair = jnp.broadcast_to(grad_sq, (2,) + grad_sq.shape)
    own = transpose_chips(grad_sq, grad_pair)

    act_blocks = activations.reshape(rows, act_width // BLOCK, BLOCK)
    act_rot = jnp.einsum("tbk,bkj->bjt", act_blocks, act_basis, preferred_element_type=jnp.float32)
    act_sq = (act_rot * act_rot).astype(jnp.bfloat16).reshape(act_width, rows)
    act_pair = lax.all_gather(act_sq, "xl", axis=0)
    act_pair, _ = lax.optimization_barrier((act_pair, own))
    act_all = lax.all_gather(act_pair, "y", axis=0)

    def gathered(half):
        cols = own.shape[1] // 2
        mine = lax.dynamic_slice_in_dim(own, half * cols, cols, 1)
        near = lax.all_to_all(jnp.broadcast_to(mine, (Z,) + mine.shape), "z", 0, 0)
        return near, swap(near, "xh")

    swapped = xh[None]
    theirs, ours = gathered(1 - c), gathered(c)
    act_all, _ = lax.optimization_barrier((act_all, ours))
    other = product(swapped, act_all, *theirs)
    got = swap(other, "c")
    mine = product(swapped, act_all, *ours)
    return (mine + got) / TOKENS


def solution(mesh):
    chips = Mesh(mesh.devices.reshape(XH, Z, XL, Y, C), ("xh", "z", "xl", "y", "c"))
    feat, tok = ("xh", "z"), ("xl", "y", "c")
    return jax.shard_map(
        per_device,
        mesh=chips,
        in_specs=(P(tok, feat), P(feat, None, None), P(tok, feat), P(feat, None)),
        out_specs=P(feat, tok),
        check_vma=False,
    )
```

time: 136 us -> 109 us (0.80)
  blocking collectives: 0 us -> 38.7 us
  waiting for transfers between devices: 49.2 us -> 23.4 us
  starting transfers between devices: 46 us -> 22.4 us
  Pallas kernels: 16.8 us -> 2.5 us
  other arithmetic: 4.5 us -> 1.13 us
    all_to_all x1 -> x2, waiting for transfers between devices: 45.4 us -> 7.58 us  [the longest x1 7.58 us: gathered(): near = lax.all_to_all(jnp.broadcast_to(mine, (Z,) + mine.shape), 'z', 0, 0)]
    all_to_all x0 -> x1, blocking collectives: none -> 32.7 us  [gathered(): near = lax.all_to_all(jnp.broadcast_to(mine, (Z,) + mine.shape), 'z', 0, 0)]
    all_to_all x1 -> x2, starting transfers between devices: 33.7 us -> 8.7 us  [the longest x1 5.2 us: transpose_chips(): lax.all_to_all(sent, ('xh', 'z', 'xl', 'y'), 0, 0, axis_index_groups=groups)]
    all_gather x1, waiting for transfers between devices: 0.01 us -> 14.8 us  [per_device(): act_all = lax.all_gather(act_pair, 'y', axis=0)]
    pallas_call x2, Pallas kernels: 16.8 us -> 2.5 us  [product(): pl.pallas_call(kernel, in_specs=[pl.BlockSpec(memory_space=pltpu.SMEM), v...]
    all_gather x0 -> x1, blocking collectives: none -> 6.01 us  [per_device(): act_pair = lax.all_gather(act_sq, 'xl', axis=0)]
    ppermute x2 -> x3, waiting for transfers between devices: 3.75 us -> 1.01 us  [swap(): return lax.ppermute(x, axis, [(0, 1), (1, 0)])]
    another operation x3 -> x0, other arithmetic: 2.17 us -> none  [the longest x1 0.84 us: per_device(): act_pair = jnp.stack([act_sq, swap(act_sq, 'xl')])]
  transfers between devices with their start and end apart: 5 -> 6, of which waited for: 2 -> 3; matrix products, arithmetic and copies ran while one was open for 2% -> 2% of each run, Pallas kernels for 6% -> 1%
where the time goes in v8:
time: 109 us; the launch traced here: 108 us
  blocking collectives  38.7 us (36%)
  waiting for transfers between devices  23.4 us (21%)
  starting transfers between devices  22.4 us (21%)
  between operations  13.5 us (12%)
  local copies, waits for them, and re-layouts  3.79 us (3%)
  matrix products  2.9 us (3%)
  Pallas kernels  2.5 us (2%)
  other arithmetic  1.13 us (1%)
    all_to_all x1, blocking collectives, gathered(): near = lax.all_to_all(jnp.broadcast_to(mine, (Z,) + mine.shape), 'z', 0, 0)  32.7 us
    all_gather x1, waiting for transfers between devices, per_device(): act_all = lax.all_gather(act_pair, 'y', axis=0)  14.8 us
    ppermute x3, starting transfers between devices, swap(): return lax.ppermute(x, axis, [(0, 1), (1, 0)])  13.6 us
    all_to_all x1, waiting for transfers between devices, gathered(): near = lax.all_to_all(jnp.broadcast_to(mine, (Z,) + mine.shape), 'z', 0, 0)  7.58 us
    all_gather x1, blocking collectives, per_device(): act_pair = lax.all_gather(act_sq, 'xl', axis=0)  6.01 us
    all_to_all x1, starting transfers between devices, transpose_chips(): lax.all_to_all(sent, ('xh', 'z', 'xl', 'y'), 0, 0, axis_index_groups=groups)  5.2 us
    all_to_all x1, starting transfers between devices, gathered(): near = lax.all_to_all(jnp.broadcast_to(mine, (Z,) + mine.shape), 'z', 0, 0)  3.5 us
    pallas_call x2, Pallas kernels, product(): pl.pallas_call(kernel, in_specs=[pl.BlockSpec(memory_space=pltpu.SMEM), v...  2.5 us
  transfers between devices with their start and end apart: 6, of which 3 were waited for; matrix products, arithmetic and copies ran while one was open for 2% of the time, Pallas kernels for 1%

profile of v8, /device:TPU:1, one launch (start us, length us, event | category | flops | bytes accessed | tf_op | source)
XLA Modules:
  0.0 108.2 jit_solution(5233911009600948172)
XLA Ops:
  6.5 0.0 copy-start
  6.5 1.4 %fusion.1 = bf16[128,512]{1,0:T(8,128)(2,1)S(1)} fusion(bf16[128,512]{1,0:T(8,128)(2,1)} %param.6, bf16[512,512]{1,0:T(8,128)(2,1)} %param.7), kind=kOutput, calls=%fused_computation.3 | convolution fusion | flops 67239936 | bytes 786432 | tf_op jit(solution)/shard_map/dot_general | solution.py:73
  8.0 0.7 broadcast_in_dim.13
  8.7 5.2 %all-to-all-start = ((bf16[2,128,512]{2,1,0:T(8,128)(2,1)}), bf16[2,128,512]{2,1,0:T(8,128)(2,1)S(1)}, u32[]{:S(2)}, u32[]{:S(2)}) async-start(bf16[2,128,512]{2,1,0:T(8,128)(2,1)} %broadcast_in_dim.13), calls=%async_computation | async-start | bytes 524288 | tf_op jit(solution)/shard_map/all_to_all | solution.py:21
  13.9 0.0 all-gather.3.cloned.1.call-start
  13.9 0.0 copy-done
  13.9 1.5 %fusion = bf16[2,512,128]{2,1,0:T(8,128)(2,1)S(1)} fusion(bf16[2,512,512]{2,1,0:T(8,128)(2,1)S(1)} %copy-done, bf16[16,2,8,512]{3,2,1,0:T(8,128)(2,1)} %bitcast.23), kind=kOutput, calls=%fused_computation.1 | convolution fusion | flops 134479872 | bytes 1572864 | tf_op jit(solution)/shard_map/tbk,bkj->bjt/dot_general | solution.py:79
  15.4 6.0 %all_gather.9 = bf16[2,1024,128]{2,1,0:T(8,128)(2,1)} all-gather(bf16[1,1024,128]{2,1,0:T(8,128)(2,1)S(1)} %bitcast.22), channel_id=1, replica_groups=mesh['xh'=2,'z'=8,'xl'=2,'y'=8,'c'=2] {'xl'}, dimensions={0}, use_global_device_ids=true | all-gather | bytes 786432 | tf_op jit(solution)/shard_map/all_gather | solution.py:81
  21.4 0.0 all-to-all-done
  21.4 0.0 all-gather.3.cloned.1.call-update
  21.5 32.7 %all_to_all.15.near_ref = bf16[8,128,256]{2,1,0:T(8,128)(2,1)S(1)} all-to-all(bf16[8,128,256]{2,1,0:T(8,128)(2,1)S(1)} %broadcast_in_dim.14), channel_id=1, replica_groups=mesh['xh'=2,'z'=8,'xl'=2,'y'=8,'c'=2] {'z'}, dimensions={0} | all-to-all | bytes 1048576 | tf_op jit(solution)/shard_map/all_to_all | solution.py:88
  54.2 0.8 broadcast_in_dim.15
  55.0 3.5 %all-to-all-start.2 = ((bf16[8,128,256]{2,1,0:T(8,128)(2,1)}), bf16[8,128,256]{2,1,0:T(8,128)(2,1)S(1)}, u32[]{:S(2)}, u32[]{:S(2)}) async-start(bf16[8,128,256]{2,1,0:T(8,128)(2,1)} %broadcast_in_dim.15), calls=%async_computation.2 | async-start | bytes 1048576 | tf_op jit(solution)/shard_map/all_to_all | solution.py:88
  58.5 5.5 %collective-permute-start = (bf16[8,128,256]{2,1,0:T(8,128)(2,1)S(1)}, bf16[8,128,256]{2,1,0:T(8,128)(2,1)S(1)}, u32[]{:S(2)}, u32[]{:S(2)}) collective-permute-start(bf16[8,128,256]{2,1,0:T(8,128)(2,1)S(1)} %all_to_all.15.near_ref), channel_id=1, source_target_pairs={{0,256},{256,0},{1,257},{257,1},{2,258},{258,2},{3,259},{259,3},{4... | collective-permute-start | bytes 1572872 | tf_op jit(solution)/shard_map/ppermute | solution.py:26
  64.1 7.6 %all-to-all-done.2.near_ref = bf16[8,128,256]{2,1,0:T(8,128)(2,1)S(1)} async-done(((bf16[8,128,256]{2,1,0:T(8,128)(2,1)}), bf16[8,128,256]{2,1,0:T(8,128)(2,1)S(1)}, u32[]{:S(2)}, u32[]{:S(2)}) %all-to-all-start.2) | async-done | bytes 524320 | tf_op jit(solution)/shard_map/all_to_all | solution.py:88
  71.7 5.5 %collective-permute-start.1 = (bf16[8,128,256]{2,1,0:T(8,128)(2,1)S(1)}, bf16[8,128,256]{2,1,0:T(8,128)(2,1)S(1)}, u32[]{:S(2)}, u32[]{:S(2)}) collective-permute-start(bf16[8,128,256]{2,1,0:T(8,128)(2,1)S(1)} %all-to-all-done.2.near_ref), channel_id=1, source_target_pairs={{0,256},{256,0},{1,257},{257,1},{2,258},{258,2},{3,259},{259,3},{4... | collective-permute-start | bytes 1572872 | tf_op jit(solution)/shard_map/ppermute | solution.py:26
  77.2 0.0 collective-permute-done.far_ref
  77.2 14.8 %all-gather.3.cloned.1.call-done = bf16[16,1024,128]{2,1,0:T(8,128)(2,1)} async-done(((bf16[2,1024,128]{2,1,0:T(8,128)(2,1)}), bf16[16,1024,128]{2,1,0:T(8,128)(2,1)}) %all-gather.3.cloned.1.call-update) | async-done | bytes 4194320 | tf_op jit(solution)/shard_map/all_gather | solution.py:83
  92.0 0.0 collective-permute-done.1.far_ref
  92.0 0.0 copy-start.1
  92.0 2.2 %copy-done.1 = bf16[16,1024,128]{2,1,0:T(8,128)(2,1)S(1)} copy-done((bf16[16,1024,128]{2,1,0:T(8,128)(2,1)S(1)}, bf16[16,1024,128]{2,1,0:T(8,128)(2,1)}, u32[]{:S(2)}) %copy-start.1) | copy-done | bytes 4194328
  94.2 1.2 %shard_map.47 = f32[1024,256]{1,0:T(8,128)S(1)} custom-call(s32[1]{0:T(128)} %bitcast.swapped_ref, bf16[8,2,1024,128]{3,2,1,0:T(8,128)(2,1)S(1)} %bitcast.20, bf16[8,128,256]{2,1,0:T(8,128)(2,1)S(1)} %all-to-all-done.2.near_ref, bf16[8,128,256]{2,1,0:T(8,128)(2,1)S(1)} %collective-permute-done.1.far_ref), custom_call_target="tpu_custom_call" | custom-call | flops 1073741824 | bytes 6291456 | tf_op jit(solution)/shard_map/pallas_call | solution.py:55
  95.4 2.6 %collective-permute-start.2 = (f32[1024,256]{1,0:T(8,128)S(1)}, f32[1024,256]{1,0:T(8,128)S(1)}, u32[]{:S(2)}, u32[]{:S(2)}) collective-permute-start(f32[1024,256]{1,0:T(8,128)S(1)} %shard_map.47), channel_id=1, source_target_pairs={{0,1},{1,0},{2,3},{3,2},{4,5},{5,4},{6,7},{7,6},{8,9},{9,8},{10,11... | collective-permute-start | bytes 3145736 | tf_op jit(solution)/shard_map/ppermute | solution.py:26
  98.0 1.3 %shard_map.46 = f32[1024,256]{1,0:T(8,128)S(1)} custom-call(s32[1]{0:T(128)} %bitcast.swapped_ref, bf16[8,2,1024,128]{3,2,1,0:T(8,128)(2,1)S(1)} %bitcast.21, bf16[8,128,256]{2,1,0:T(8,128)(2,1)S(1)} %all_to_all.15.near_ref, bf16[8,128,256]{2,1,0:T(8,128)(2,1)S(1)} %collective-permute-done.far_ref), custom_call_target="tpu_custom_call" | custom-call | flops 1073741824 | bytes 6291456 | tf_op jit(solution)/shard_map/pallas_call | solution.py:55
  99.3 1.0 collective-permute-done.2
  100.3 1.1 %add_multiply_fusion = f32[1024,256]{1,0:T(8,128)} fusion(f32[1024,256]{1,0:T(8,128)S(1)} %shard_map.46, f32[1024,256]{1,0:T(8,128)S(1)} %collective-permute-done.2), kind=kLoop, calls=%fused_computation.4 | loop fusion | flops 524288 | bytes 3145728 | tf_op jit(solution)/shard_map/div | solution.py:97
  (3 shorter events, 0.1 us)
Async XLA Ops:
  6.5 7.4 %copy-start = (bf16[2,512,512]{2,1,0:T(8,128)(2,1)S(1)}, bf16[2,512,512]{2,1,0:T(8,128)(2,1)}, u32[]{:S(2)}) copy-start(bf16[2,512,512]{2,1,0:T(8,128)(2,1)} %param.5) | copy-start | bytes 3145732
  8.7 12.7 %all-to-all-start = ((bf16[2,128,512]{2,1,0:T(8,128)(2,1)}), bf16[2,128,512]{2,1,0:T(8,128)(2,1)S(1)}, u32[]{:S(2)}, u32[]{:S(2)}) async-start(bf16[2,128,512]{2,1,0:T(8,128)(2,1)} %broadcast_in_dim.13), calls=%async_computation | async-start | bytes 524288 | tf_op jit(solution)/shard_map/all_to_all | solution.py:21
  13.9 78.1 %all-gather.3.cloned.1.call-start = ((), (), s32[]{:S(2)}) async-start(), calls=%async_computation.3 | async-start | bytes 4718592 | tf_op jit(solution)/shard_map/all_gather | solution.py:83
  55.0 16.6 %all-to-all-start.2 = ((bf16[8,128,256]{2,1,0:T(8,128)(2,1)}), bf16[8,128,256]{2,1,0:T(8,128)(2,1)S(1)}, u32[]{:S(2)}, u32[]{:S(2)}) async-start(bf16[8,128,256]{2,1,0:T(8,128)(2,1)} %broadcast_in_dim.15), calls=%async_computation.2 | async-start | bytes 1048576 | tf_op jit(solution)/shard_map/all_to_all | solution.py:88
  58.5 18.7 %collective-permute-start = (bf16[8,128,256]{2,1,0:T(8,128)(2,1)S(1)}, bf16[8,128,256]{2,1,0:T(8,128)(2,1)S(1)}, u32[]{:S(2)}, u32[]{:S(2)}) collective-permute-start(bf16[8,128,256]{2,1,0:T(8,128)(2,1)S(1)} %all_to_all.15.near_ref), channel_id=1, source_target_pairs={{0,256},{256,0},{1,257},{257,1},{2,258},{258,2},{3,259},{259,3},{4... | collective-permute-start | bytes 1572872 | tf_op jit(solution)/shard_map/ppermute | solution.py:26
  71.7 20.3 %collective-permute-start.1 = (bf16[8,128,256]{2,1,0:T(8,128)(2,1)S(1)}, bf16[8,128,256]{2,1,0:T(8,128)(2,1)S(1)}, u32[]{:S(2)}, u32[]{:S(2)}) collective-permute-start(bf16[8,128,256]{2,1,0:T(8,128)(2,1)S(1)} %all-to-all-done.2.near_ref), channel_id=1, source_target_pairs={{0,256},{256,0},{1,257},{257,1},{2,258},{258,2},{3,259},{259,3},{4... | collective-permute-start | bytes 1572872 | tf_op jit(solution)/shard_map/ppermute | solution.py:26
  92.0 2.2 %copy-start.1 = (bf16[16,1024,128]{2,1,0:T(8,128)(2,1)S(1)}, bf16[16,1024,128]{2,1,0:T(8,128)(2,1)}, u32[]{:S(2)}) copy-start(bf16[16,1024,128]{2,1,0:T(8,128)(2,1)} %all-gather.3.cloned.1.call-done) | copy-start | bytes 12582916
  95.4 4.9 %collective-permute-start.2 = (f32[1024,256]{1,0:T(8,128)S(1)}, f32[1024,256]{1,0:T(8,128)S(1)}, u32[]{:S(2)}, u32[]{:S(2)}) collective-permute-start(f32[1024,256]{1,0:T(8,128)S(1)} %shard_map.47), channel_id=1, source_target_pairs={{0,1},{1,0},{2,3},{3,2},{4,5},{5,4},{6,7},{7,6},{8,9},{9,8},{10,11... | collective-permute-start | bytes 3145736 | tf_op jit(solution)/shard_map/ppermute | solution.py:26
Sparse Core Ops, SparseCore 0:
  21.6 70.3 all-gather.2

commit v9 on v8

v9 whole, which is shorter than its diff:
```python
import jax
import jax.numpy as jnp
from jax import lax
from jax.experimental import pallas as pl
from jax.experimental.pallas import tpu as pltpu
from jax.sharding import Mesh
from jax.sharding import PartitionSpec as P

BLOCK = 512
TOKENS = 4096
XH, Z, XL, Y, C = 2, 8, 2, 8, 2


def transpose_chips(x, sent):
    chips = XH * Z
    swaps = [[f * chips + m, m * chips + f] for f in range(chips) for m in range(f + 1, chips)]
    fixed = [f * chips + f for f in range(chips)]
    groups = swaps + [[fixed[i], fixed[i + 1]] for i in range(0, chips, 2)]
    f = lax.axis_index("xh") * Z + lax.axis_index("z")
    m = lax.axis_index("xl") * Y + lax.axis_index("y")
    got = lax.all_to_all(sent, ("xh", "z", "xl", "y"), 0, 0, axis_index_groups=groups)
    return jnp.where(f > m, got[0], jnp.where(f < m, got[1], x))


def swap(x, axis):
    return lax.ppermute(x, axis, [(0, 1), (1, 0)])


def shift(x, axis, size, step):
    return lax.ppermute(x, axis, [(i, (i + step) % size) for i in range(size)])


def product(places, act_all, sides, near, far):
    rest, rows = sides[0].shape
    width = act_all.shape[1] - rest
    cols = near.shape[2] // 2
    tile = width // 2

    def kernel(places_ref, act_ref, *refs):
        side_refs, (near_ref, far_ref, out_ref) = refs[:Y], refs[Y:]
        where = pl.ds(pl.multiple_of(places_ref[1] * cols, cols), cols)

        def go(own_ref, other_ref):
            own = jnp.concatenate([own_ref[y, :, where] for y in range(Y)], axis=0)
            other = jnp.concatenate([other_ref[y, :, where] for y in range(Y)], axis=0)
            for t in range(2):
                at = slice(t * tile, (t + 1) * tile)
                lhs = jnp.concatenate([act_ref[y, at] for y in range(Y)], axis=1)
                total = jnp.dot(lhs, own, preferred_element_type=jnp.float32)
                if t == 0:
                    lhs = jnp.concatenate([act_ref[y, width:] for y in range(Y)], axis=1)
                else:
                    lhs = jnp.concatenate([ref[...] for ref in side_refs], axis=1)
                    other = jnp.concatenate([other_ref[places_ref[2 + d], :, where] for d in range(Y)], axis=0)
                out_ref[at] = total + jnp.dot(lhs, other, preferred_element_type=jnp.float32)

        @pl.when(places_ref[0] == 0)
        def _():
            go(near_ref, far_ref)

        @pl.when(places_ref[0] != 0)
        def _():
            go(far_ref, near_ref)

    vmem = pl.BlockSpec(memory_space=pltpu.VMEM)
    return pl.pallas_call(
        kernel,
        in_specs=[pl.BlockSpec(memory_space=pltpu.SMEM)] + [vmem] * (Y + 3),
        out_specs=vmem,
        out_shape=jax.ShapeDtypeStruct((width, cols), jnp.float32),
        compiler_params=pltpu.CompilerParams(vmem_limit_bytes=16 * 1024 * 1024),
        cost_estimate=pl.CostEstimate(
            flops=2 * width * cols * rows * 2 * Y,
            bytes_accessed=(act_all.size + rest * rows * Y + near.size * 2) * 2 + width * cols * 4,
            transcendentals=0,
        ),
    )(places, act_all, *sides, near, far)


def per_device(activations, act_basis, gradients, grad_basis):
    rows, act_width = activations.shape
    xh, y, c = (lax.axis_index(a) for a in ("xh", "y", "c"))

    grad_rot = jnp.dot(gradients, grad_basis, preferred_element_type=jnp.float32)
    grad_sq = (grad_rot * grad_rot).astype(jnp.bfloat16)
    grad_pair = jnp.broadcast_to(grad_sq, (2,) + grad_sq.shape)
    own = transpose_chips(grad_sq, grad_pair)

    act_blocks = activations.reshape(rows, act_width // BLOCK, BLOCK)
    act_rot = jnp.einsum("tbk,bkj->bjt", act_blocks, act_basis, preferred_element_type=jnp.float32)
    act_sq = (act_rot * act_rot).astype(jnp.bfloat16).reshape(act_width, rows)
    act_pair = lax.all_gather(act_sq, "xl", axis=0, tiled=True)
    split = act_pair.shape[0] * 3 // 4
    sent, _ = lax.optimization_barrier((act_pair[:split], own))
    act_all = lax.all_gather(sent, "y", axis=0)

    near = lax.all_to_all(jnp.broadcast_to(own, (Z,) + own.shape), "z", 0, 0)
    sides = [act_pair[split:]]
    sides += [shift(sides[0], "y", Y, d) for d in (1, 7, 2, 6, 3, 5, 4)]
    near, _ = lax.optimization_barrier((near, sides[1:5]))
    far = swap(near, "xh")
    side_y = [(y + Y - d) % Y for d in (0, 1, 7, 2, 6, 3, 5, 4)]

    def places(half):
        return jnp.stack([xh, half] + side_y).astype(jnp.int32)

    other = product(places(1 - c), act_all, sides, near, far)
    got = swap(other, "c")
    mine = product(places(c), act_all, sides, near, far)
    return (mine + got) / TOKENS


def solution(mesh):
    chips = Mesh(mesh.devices.reshape(XH, Z, XL, Y, C), ("xh", "z", "xl", "y", "c"))
    feat, tok = ("xh", "z"), ("xl", "y", "c")
    return jax.shard_map(
        per_device,
        mesh=chips,
        in_specs=(P(tok, feat), P(feat, None, None), P(tok, feat), P(feat, None)),
        out_specs=P(feat, tok),
        check_vma=False,
    )
```

time: 109 us -> 130 us (1.19)
  starting transfers between devices: 22.4 us -> 57.7 us
  blocking collectives: 38.7 us -> 5.9 us
  local copies, waits for them, and re-layouts: 3.79 us -> 11.5 us
  waiting for transfers between devices: 23.4 us -> 29.6 us
  Pallas kernels: 2.5 us -> 5.56 us
    all_to_all x1 -> x0, blocking collectives: 32.7 us -> none  [gathered(): near = lax.all_to_all(jnp.broadcast_to(mine, (Z,) + mine.shape), 'z', 0, 0)]
    ppermute x0 -> x7, waiting for transfers between devices: none -> 25.4 us  [shift(): return lax.ppermute(x, axis, [(i, (i + step) % size) for i in range(size)])]
    ppermute x0 -> x7, starting transfers between devices: none -> 24 us  [shift(): return lax.ppermute(x, axis, [(i, (i + step) % size) for i in range(size)])]
    all_to_all x1, starting transfers between devices: 3.5 us -> 18.4 us  [per_device(): near = lax.all_to_all(jnp.broadcast_to(own, (Z,) + own.shape), 'z', 0, 0)]
    all_gather x1, waiting for transfers between devices: 14.8 us -> 0.01 us  [per_device(): act_all = lax.all_gather(sent, 'y', axis=0)]
    unnamed x4 -> x18, local copies, waits for them, and re-layouts: 2.19 us -> 8.73 us
    ppermute x3 -> x2, starting transfers between devices: 13.6 us -> 10.1 us  [swap(): return lax.ppermute(x, axis, [(0, 1), (1, 0)])]
    all_to_all x1, waiting for transfers between devices: 7.58 us -> 4.12 us  [per_device(): near = lax.all_to_all(jnp.broadcast_to(own, (Z,) + own.shape), 'z', 0, 0)]
  transfers between devices with their start and end apart: 6 -> 12, of which waited for: 3 -> 6; matrix products, arithmetic and copies ran while one was open for 2% -> 3% of each run, Pallas kernels for 1% -> 2%
where the time goes in v9:
time: 130 us; the launch traced here: 129 us
  starting transfers between devices  57.7 us (44%)
  waiting for transfers between devices  29.6 us (23%)
  between operations  13.6 us (10%)
  local copies, waits for them, and re-layouts  11.5 us (9%)
  blocking collectives  5.9 us (5%)
  Pallas kernels  5.56 us (4%)
  matrix products  2.9 us (2%)
  other arithmetic  2.35 us (2%)
    ppermute x7, waiting for transfers between devices, shift(): return lax.ppermute(x, axis, [(i, (i + step) % size) for i in range(size)])  25.4 us
    ppermute x7, starting transfers between devices, shift(): return lax.ppermute(x, axis, [(i, (i + step) % size) for i in range(size)])  24 us
    all_to_all x1, starting transfers between devices, per_device(): near = lax.all_to_all(jnp.broadcast_to(own, (Z,) + own.shape), 'z', 0, 0)  18.4 us
    ppermute x2, starting transfers between devices, swap(): return lax.ppermute(x, axis, [(0, 1), (1, 0)])  10.1 us
    unnamed x18, local copies, waits for them, and re-layouts  8.73 us
    all_gather x1, blocking collectives, per_device(): act_pair = lax.all_gather(act_sq, 'xl', axis=0, tiled=True)  5.9 us
    pallas_call x2, Pallas kernels, product(): pl.pallas_call(kernel, in_specs=[pl.BlockSpec(memory_space=pltpu.SMEM)] +...  5.56 us
    all_to_all x1, starting transfers between devices, transpose_chips(): lax.all_to_all(sent, ('xh', 'z', 'xl', 'y'), 0, 0, axis_index_groups=groups)  5.2 us
  transfers between devices with their start and end apart: 12, of which 6 were waited for; matrix products, arithmetic and copies ran while one was open for 3% of the time, Pallas kernels for 2%

profile of v9, /device:TPU:1, one launch (start us, length us, event | category | flops | bytes accessed | tf_op | source)
XLA Modules:
  0.0 129.0 jit_solution(15714404661921325423)
XLA Ops:
  6.5 1.4 %fusion.1 = bf16[128,512]{1,0:T(8,128)(2,1)S(1)} fusion(bf16[128,512]{1,0:T(8,128)(2,1)} %param.6, bf16[512,512]{1,0:T(8,128)(2,1)} %param.7), kind=kOutput, calls=%fused_computation.3 | convolution fusion | flops 67239936 | bytes 786432 | tf_op jit(solution)/shard_map/dot_general | solution.py:84
  8.0 0.7 broadcast_in_dim.6
  8.7 5.2 %all-to-all-start = ((bf16[2,128,512]{2,1,0:T(8,128)(2,1)}), bf16[2,128,512]{2,1,0:T(8,128)(2,1)S(1)}, u32[]{:S(2)}, u32[]{:S(2)}) async-start(bf16[2,128,512]{2,1,0:T(8,128)(2,1)} %broadcast_in_dim.6), calls=%async_computation | async-start | bytes 524288 | tf_op jit(solution)/shard_map/all_to_all | solution.py:21
  13.9 1.5 %fusion = bf16[2,512,128]{2,1,0:T(8,128)(2,1)S(1)} fusion(bf16[2,512,512]{2,1,0:T(8,128)(2,1)S(1)} %copy-done, bf16[16,2,8,512]{3,2,1,0:T(8,128)(2,1)} %bitcast.33), kind=kOutput, calls=%fused_computation.1 | convolution fusion | flops 134479872 | bytes 1572864 | tf_op jit(solution)/shard_map/tbk,bkj->bjt/dot_general | solution.py:90
  15.4 5.9 %all_gather.9 = bf16[2048,128]{1,0:T(8,128)(2,1)S(1)} all-gather(bf16[1024,128]{1,0:T(8,128)(2,1)S(1)} %bitcast.32), channel_id=1, replica_groups=mesh['xh'=2,'z'=8,'xl'=2,'y'=8,'c'=2] {'xl'}, dimensions={0}, use_global_device_ids=true | all-gather | bytes 786432 | tf_op jit(solution)/shard_map/all_gather | solution.py:92
  21.3 0.8 slice.16
  22.1 1.1 broadcast_in_dim.7
  23.2 18.4 %all-to-all-start.1 = ((bf16[8,128,512]{2,1,0:T(8,128)(2,1)}), bf16[8,128,512]{2,1,0:T(8,128)(2,1)S(1)}, u32[]{:S(2)}, u32[]{:S(2)}) async-start(bf16[8,128,512]{2,1,0:T(8,128)(2,1)} %broadcast_in_dim.7), calls=%async_computation.1 | async-start | bytes 2097152 | tf_op jit(solution)/shard_map/all_to_all | solution.py:97
  41.6 2.5 %collective-permute-start.3 = (bf16[512,128]{1,0:T(8,128)(2,1)S(1)}, bf16[512,128]{1,0:T(8,128)(2,1)S(1)}, u32[]{:S(2)}, u32[]{:S(2)}) collective-permute-start(bf16[512,128]{1,0:T(8,128)(2,1)S(1)} %slice.19.refs_0_), channel_id=1, source_target_pairs={{0,12},{2,14},{4,0},{6,2},{8,4},{10,6},{12,8},{14,10},{1,13},{3,15... | collective-permute-start | bytes 393224 | tf_op jit(solution)/shard_map/ppermute | solution.py:30
  44.1 3.7 %collective-permute-start.2 = (bf16[512,128]{1,0:T(8,128)(2,1)S(1)}, bf16[512,128]{1,0:T(8,128)(2,1)S(1)}, u32[]{:S(2)}, u32[]{:S(2)}) collective-permute-start(bf16[512,128]{1,0:T(8,128)(2,1)S(1)} %slice.19.refs_0_), channel_id=1, source_target_pairs={{0,4},{2,6},{4,8},{6,10},{8,12},{10,14},{12,0},{14,2},{1,5},{3,7},... | collective-permute-start | bytes 393224 | tf_op jit(solution)/shard_map/ppermute | solution.py:30
  47.8 4.6 %collective-permute-start.1 = (bf16[512,128]{1,0:T(8,128)(2,1)S(1)}, bf16[512,128]{1,0:T(8,128)(2,1)S(1)}, u32[]{:S(2)}, u32[]{:S(2)}) collective-permute-start(bf16[512,128]{1,0:T(8,128)(2,1)S(1)} %slice.19.refs_0_), channel_id=1, source_target_pairs={{0,14},{2,0},{4,2},{6,4},{8,6},{10,8},{12,10},{14,12},{1,15},{3,1}... | collective-permute-start | bytes 393224 | tf_op jit(solution)/shard_map/ppermute | solution.py:30
  52.4 1.9 %collective-permute-start = (bf16[512,128]{1,0:T(8,128)(2,1)S(1)}, bf16[512,128]{1,0:T(8,128)(2,1)S(1)}, u32[]{:S(2)}, u32[]{:S(2)}) collective-permute-start(bf16[512,128]{1,0:T(8,128)(2,1)S(1)} %slice.19.refs_0_), channel_id=1, source_target_pairs={{0,2},{2,4},{4,6},{6,8},{8,10},{10,12},{12,14},{14,0},{1,3},{3,5},... | collective-permute-start | bytes 393224 | tf_op jit(solution)/shard_map/ppermute | solution.py:30
  54.4 3.8 %collective-permute-done.1.refs_2_ = bf16[512,128]{1,0:T(8,128)(2,1)S(1)} collective-permute-done((bf16[512,128]{1,0:T(8,128)(2,1)S(1)}, bf16[512,128]{1,0:T(8,128)(2,1)S(1)}, u32[]{:S(2)}, u32[]{:S(2)}) %collective-permute-start.1) | collective-permute-done | bytes 131104 | tf_op jit(solution)/shard_map/ppermute | solution.py:30
  58.8 5.5 %collective-permute-done.refs_1_ = bf16[512,128]{1,0:T(8,128)(2,1)S(1)} collective-permute-done((bf16[512,128]{1,0:T(8,128)(2,1)S(1)}, bf16[512,128]{1,0:T(8,128)(2,1)S(1)}, u32[]{:S(2)}, u32[]{:S(2)}) %collective-permute-start) | collective-permute-done | bytes 131104 | tf_op jit(solution)/shard_map/ppermute | solution.py:30
  64.9 4.1 %all-to-all-done.1.refs_8_ = bf16[8,128,512]{2,1,0:T(8,128)(2,1)S(1)} async-done(((bf16[8,128,512]{2,1,0:T(8,128)(2,1)}), bf16[8,128,512]{2,1,0:T(8,128)(2,1)S(1)}, u32[]{:S(2)}, u32[]{:S(2)}) %all-to-all-start.1) | async-done | bytes 1048608 | tf_op jit(solution)/shard_map/all_to_all | solution.py:97
  69.1 5.5 %collective-permute-start.7 = (bf16[8,128,512]{2,1,0:T(8,128)(2,1)S(1)}, bf16[8,128,512]{2,1,0:T(8,128)(2,1)S(1)}, u32[]{:S(2)}, u32[]{:S(2)}) collective-permute-start(bf16[8,128,512]{2,1,0:T(8,128)(2,1)S(1)} %all-to-all-done.1.refs_8_), channel_id=1, source_target_pairs={{0,256},{256,0},{1,257},{257,1},{2,258},{258,2},{3,259},{259,3},{4... | collective-permute-start | bytes 3145736 | tf_op jit(solution)/shard_map/ppermute | solution.py:26
  74.6 3.3 %collective-permute-start.6 = (bf16[512,128]{1,0:T(8,128)(2,1)S(1)}, bf16[512,128]{1,0:T(8,128)(2,1)}, u32[]{:S(2)}, u32[]{:S(2)}) collective-permute-start(bf16[512,128]{1,0:T(8,128)(2,1)S(1)} %slice.19.refs_0_), channel_id=1, source_target_pairs={{0,8},{2,10},{4,12},{6,14},{8,0},{10,2},{12,4},{14,6},{1,9},{3,11}... | collective-permute-start | bytes 393224 | tf_op jit(solution)/shard_map/ppermute | solution.py:30
  77.9 6.0 %collective-permute-start.5 = (bf16[512,128]{1,0:T(8,128)(2,1)S(1)}, bf16[512,128]{1,0:T(8,128)(2,1)}, u32[]{:S(2)}, u32[]{:S(2)}) collective-permute-start(bf16[512,128]{1,0:T(8,128)(2,1)S(1)} %slice.19.refs_0_), channel_id=1, source_target_pairs={{0,10},{2,12},{4,14},{6,0},{8,2},{10,4},{12,6},{14,8},{1,11},{3,13... | collective-permute-start | bytes 393224 | tf_op jit(solution)/shard_map/ppermute | solution.py:30
  83.9 1.9 %collective-permute-start.4 = (bf16[512,128]{1,0:T(8,128)(2,1)S(1)}, bf16[512,128]{1,0:T(8,128)(2,1)}, u32[]{:S(2)}, u32[]{:S(2)}) collective-permute-start(bf16[512,128]{1,0:T(8,128)(2,1)S(1)} %slice.19.refs_0_), channel_id=1, source_target_pairs={{0,6},{2,8},{4,10},{6,12},{8,14},{10,0},{12,2},{14,4},{1,7},{3,9},... | collective-permute-start | bytes 393224 | tf_op jit(solution)/shard_map/ppermute | solution.py:30
  86.0 3.2 %collective-permute-done.6.refs_7_ = bf16[512,128]{1,0:T(8,128)(2,1)} collective-permute-done((bf16[512,128]{1,0:T(8,128)(2,1)S(1)}, bf16[512,128]{1,0:T(8,128)(2,1)}, u32[]{:S(2)}, u32[]{:S(2)}) %collective-permute-start.6) | collective-permute-done | bytes 131104 | tf_op jit(solution)/shard_map/ppermute | solution.py:30
  89.2 6.9 %collective-permute-done.5.refs_6_ = bf16[512,128]{1,0:T(8,128)(2,1)} collective-permute-done((bf16[512,128]{1,0:T(8,128)(2,1)S(1)}, bf16[512,128]{1,0:T(8,128)(2,1)}, u32[]{:S(2)}, u32[]{:S(2)}) %collective-permute-start.5) | collective-permute-done | bytes 131104 | tf_op jit(solution)/shard_map/ppermute | solution.py:30
  96.1 6.1 %collective-permute-done.4.refs_5_ = bf16[512,128]{1,0:T(8,128)(2,1)} collective-permute-done((bf16[512,128]{1,0:T(8,128)(2,1)S(1)}, bf16[512,128]{1,0:T(8,128)(2,1)}, u32[]{:S(2)}, u32[]{:S(2)}) %collective-permute-start.4) | collective-permute-done | bytes 131104 | tf_op jit(solution)/shard_map/ppermute | solution.py:30
  102.2 1.9 %copy-done.1 = bf16[12288,128]{1,0:T(8,128)(2,1)S(1)} copy-done((bf16[12288,128]{1,0:T(8,128)(2,1)S(1)}, bf16[12288,128]{1,0:T(8,128)(2,1)}, u32[]{:S(2)}) %copy-start.1) | copy-done | bytes 3145752
  104.1 0.9 copy-done.4
  105.0 0.9 copy-done.7
  105.9 3.3 %shard_map.47 = f32[1024,256]{1,0:T(8,128)} custom-call(s32[10]{0:T(128)S(1)} %stack.60.places_ref, bf16[8,1536,128]{2,1,0:T(8,128)(2,1)S(1)} %bitcast.30, bf16[512,128]{1,0:T(8,128)(2,1)S(1)} %slice.19.refs_0_, bf16[512,128]{1,0:T(8,128)(2,1)S(1)} %copy-done.7, bf16[512,128]{1,0:T(8,128)(2,1)S(1)} %copy-done.4, ...), custom_call_target="tpu_custom_call" | custom-call | flops 1073741824 | bytes 7340032 | tf_op jit(solution)/shard_map/pallas_call | solution.py:66
  109.2 4.5 %collective-permute-start.8 = (f32[1024,256]{1,0:T(8,128)}, f32[1024,256]{1,0:T(8,128)}, u32[]{:S(2)}, u32[]{:S(2)}) collective-permute-start(f32[1024,256]{1,0:T(8,128)} %shard_map.47), channel_id=1, source_target_pairs={{0,1},{1,0},{2,3},{3,2},{4,5},{5,4},{6,7},{7,6},{8,9},{9,8},{10,11... | collective-permute-start | bytes 3145736 | tf_op jit(solution)/shard_map/ppermute | solution.py:26
  113.8 1.9 %copy-done.2 = bf16[12288,128]{1,0:T(8,128)(2,1)S(1)} copy-done((bf16[12288,128]{1,0:T(8,128)(2,1)S(1)}, bf16[12288,128]{1,0:T(8,128)(2,1)}, u32[]{:S(2)}) %copy-start.2) | copy-done | bytes 3145752
  115.7 0.9 copy-done.5
  116.6 0.9 copy-done.8
  117.5 2.3 %shard_map.46 = f32[1024,256]{1,0:T(8,128)S(1)} custom-call(s32[10]{0:T(128)S(1)} %stack.58.places_ref, bf16[8,1536,128]{2,1,0:T(8,128)(2,1)S(1)} %bitcast.31, bf16[512,128]{1,0:T(8,128)(2,1)S(1)} %slice.19.refs_0_, bf16[512,128]{1,0:T(8,128)(2,1)S(1)} %copy-done.8, bf16[512,128]{1,0:T(8,128)(2,1)S(1)} %copy-done.5, ...), custom_call_target="tpu_custom_call" | custom-call | flops 1073741824 | bytes 7340032 | tf_op jit(solution)/shard_map/pallas_call | solution.py:66
  119.9 2.3 %add_multiply_fusion = f32[1024,256]{1,0:T(8,128)} fusion(f32[1024,256]{1,0:T(8,128)S(1)} %shard_map.46, f32[1024,256]{1,0:T(8,128)} %collective-permute-done.8), kind=kLoop, calls=%fused_computation.4 | loop fusion | flops 524288 | bytes 3145728 | tf_op jit(solution)/shard_map/div | solution.py:110
  (24 shorter events, 1.6 us)
Async XLA Ops:
  6.5 7.4 %copy-start = (bf16[2,512,512]{2,1,0:T(8,128)(2,1)S(1)}, bf16[2,512,512]{2,1,0:T(8,128)(2,1)}, u32[]{:S(2)}) copy-start(bf16[2,512,512]{2,1,0:T(8,128)(2,1)} %param.5) | copy-start | bytes 3145732
  8.7 13.4 %all-to-all-start = ((bf16[2,128,512]{2,1,0:T(8,128)(2,1)}), bf16[2,128,512]{2,1,0:T(8,128)(2,1)S(1)}, u32[]{:S(2)}, u32[]{:S(2)}) async-start(bf16[2,128,512]{2,1,0:T(8,128)(2,1)} %broadcast_in_dim.6), calls=%async_computation | async-start | bytes 524288 | tf_op jit(solution)/shard_map/all_to_all | solution.py:21
  13.9 88.3 %all-gather.3.cloned.1.call-start = ((), (), s32[]{:S(2)}) async-start(), calls=%async_computation.2 | async-start | bytes 3538944 | tf_op jit(solution)/shard_map/all_gather | solution.py:95
  23.2 45.9 %all-to-all-start.1 = ((bf16[8,128,512]{2,1,0:T(8,128)(2,1)}), bf16[8,128,512]{2,1,0:T(8,128)(2,1)S(1)}, u32[]{:S(2)}, u32[]{:S(2)}) async-start(bf16[8,128,512]{2,1,0:T(8,128)(2,1)} %broadcast_in_dim.7), calls=%async_computation.1 | async-start | bytes 2097152 | tf_op jit(solution)/shard_map/all_to_all | solution.py:97
  41.6 12.8 %collective-permute-start.3 = (bf16[512,128]{1,0:T(8,128)(2,1)S(1)}, bf16[512,128]{1,0:T(8,128)(2,1)S(1)}, u32[]{:S(2)}, u32[]{:S(2)}) collective-permute-start(bf16[512,128]{1,0:T(8,128)(2,1)S(1)} %slice.19.refs_0_), channel_id=1, source_target_pairs={{0,12},{2,14},{4,0},{6,2},{8,4},{10,6},{12,8},{14,10},{1,13},{3,15... | collective-permute-start | bytes 393224 | tf_op jit(solution)/shard_map/ppermute | solution.py:30
  44.1 10.3 %collective-permute-start.2 = (bf16[512,128]{1,0:T(8,128)(2,1)S(1)}, bf16[512,128]{1,0:T(8,128)(2,1)S(1)}, u32[]{:S(2)}, u32[]{:S(2)}) collective-permute-start(bf16[512,128]{1,0:T(8,128)(2,1)S(1)} %slice.19.refs_0_), channel_id=1, source_target_pairs={{0,4},{2,6},{4,8},{6,10},{8,12},{10,14},{12,0},{14,2},{1,5},{3,7},... | collective-permute-start | bytes 393224 | tf_op jit(solution)/shard_map/ppermute | solution.py:30
  47.8 10.3 %collective-permute-start.1 = (bf16[512,128]{1,0:T(8,128)(2,1)S(1)}, bf16[512,128]{1,0:T(8,128)(2,1)S(1)}, u32[]{:S(2)}, u32[]{:S(2)}) collective-permute-start(bf16[512,128]{1,0:T(8,128)(2,1)S(1)} %slice.19.refs_0_), channel_id=1, source_target_pairs={{0,14},{2,0},{4,2},{6,4},{8,6},{10,8},{12,10},{14,12},{1,15},{3,1}... | collective-permute-start | bytes 393224 | tf_op jit(solution)/shard_map/ppermute | solution.py:30
  52.4 11.8 %collective-permute-start = (bf16[512,128]{1,0:T(8,128)(2,1)S(1)}, bf16[512,128]{1,0:T(8,128)(2,1)S(1)}, u32[]{:S(2)}, u32[]{:S(2)}) collective-permute-start(bf16[512,128]{1,0:T(8,128)(2,1)S(1)} %slice.19.refs_0_), channel_id=1, source_target_pairs={{0,2},{2,4},{4,6},{6,8},{8,10},{10,12},{12,14},{14,0},{1,3},{3,5},... | collective-permute-start | bytes 393224 | tf_op jit(solution)/shard_map/ppermute | solution.py:30
  58.1 0.7 copy-start.3
  64.3 0.7 copy-start.6
  69.1 33.2 %collective-permute-start.7 = (bf16[8,128,512]{2,1,0:T(8,128)(2,1)S(1)}, bf16[8,128,512]{2,1,0:T(8,128)(2,1)S(1)}, u32[]{:S(2)}, u32[]{:S(2)}) collective-permute-start(bf16[8,128,512]{2,1,0:T(8,128)(2,1)S(1)} %all-to-all-done.1.refs_8_), channel_id=1, source_target_pairs={{0,256},{256,0},{1,257},{257,1},{2,258},{258,2},{3,259},{259,3},{4... | collective-permute-start | bytes 3145736 | tf_op jit(solution)/shard_map/ppermute | solution.py:26
  74.6 14.6 %collective-permute-start.6 = (bf16[512,128]{1,0:T(8,128)(2,1)S(1)}, bf16[512,128]{1,0:T(8,128)(2,1)}, u32[]{:S(2)}, u32[]{:S(2)}) collective-permute-start(bf16[512,128]{1,0:T(8,128)(2,1)S(1)} %slice.19.refs_0_), channel_id=1, source_target_pairs={{0,8},{2,10},{4,12},{6,14},{8,0},{10,2},{12,4},{14,6},{1,9},{3,11}... | collective-permute-start | bytes 393224 | tf_op jit(solution)/shard_map/ppermute | solution.py:30
  77.9 18.2 %collective-permute-start.5 = (bf16[512,128]{1,0:T(8,128)(2,1)S(1)}, bf16[512,128]{1,0:T(8,128)(2,1)}, u32[]{:S(2)}, u32[]{:S(2)}) collective-permute-start(bf16[512,128]{1,0:T(8,128)(2,1)S(1)} %slice.19.refs_0_), channel_id=1, source_target_pairs={{0,10},{2,12},{4,14},{6,0},{8,2},{10,4},{12,6},{14,8},{1,11},{3,13... | collective-permute-start | bytes 393224 | tf_op jit(solution)/shard_map/ppermute | solution.py:30
  83.9 18.3 %collective-permute-start.4 = (bf16[512,128]{1,0:T(8,128)(2,1)S(1)}, bf16[512,128]{1,0:T(8,128)(2,1)}, u32[]{:S(2)}, u32[]{:S(2)}) collective-permute-start(bf16[512,128]{1,0:T(8,128)(2,1)S(1)} %slice.19.refs_0_), channel_id=1, source_target_pairs={{0,6},{2,8},{4,10},{6,12},{8,14},{10,0},{12,2},{14,4},{1,7},{3,9},... | collective-permute-start | bytes 393224 | tf_op jit(solution)/shard_map/ppermute | solution.py:30
  102.2 1.9 %copy-start.1 = (bf16[12288,128]{1,0:T(8,128)(2,1)S(1)}, bf16[12288,128]{1,0:T(8,128)(2,1)}, u32[]{:S(2)}) copy-start(bf16[12288,128]{1,0:T(8,128)(2,1)} %all-gather.3.cloned.1.call-done) | copy-start | bytes 9437188
  104.1 0.9 copy-start.4
  105.0 0.9 copy-start.7
  109.2 10.6 %collective-permute-start.8 = (f32[1024,256]{1,0:T(8,128)}, f32[1024,256]{1,0:T(8,128)}, u32[]{:S(2)}, u32[]{:S(2)}) collective-permute-start(f32[1024,256]{1,0:T(8,128)} %shard_map.47), channel_id=1, source_target_pairs={{0,1},{1,0},{2,3},{3,2},{4,5},{5,4},{6,7},{7,6},{8,9},{9,8},{10,11... | collective-permute-start | bytes 3145736 | tf_op jit(solution)/shard_map/ppermute | solution.py:26
  113.8 1.9 %copy-start.2 = (bf16[12288,128]{1,0:T(8,128)(2,1)S(1)}, bf16[12288,128]{1,0:T(8,128)(2,1)}, u32[]{:S(2)}) copy-start(bf16[12288,128]{1,0:T(8,128)(2,1)} %all-gather.3.cloned.1.call-done) | copy-start | bytes 9437188
  115.7 0.9 copy-start.5
  116.6 0.9 copy-start.8
Sparse Core Ops, SparseCore 0:
  22.2 79.2 all-gather.2

commit v10 on v6

v10 whole, which is shorter than its diff:
```python
import jax
import jax.numpy as jnp
from jax import lax
from jax.experimental import pallas as pl
from jax.experimental.pallas import tpu as pltpu
from jax.sharding import Mesh
from jax.sharding import PartitionSpec as P

BLOCK = 512
TOKENS = 4096
XH, Z, XL, Y, C = 2, 8, 2, 8, 2


def shift(x, axis, size, step):
    return lax.ppermute(x, axis, [(i, (i + step) % size) for i in range(size)])


def transpose_chips(x):
    chips = XH * Z
    swaps = [[f * chips + m, m * chips + f] for f in range(chips) for m in range(f + 1, chips)]
    fixed = [f * chips + f for f in range(chips)]
    groups = swaps + [[fixed[i], fixed[i + 1]] for i in range(0, chips, 2)]
    f = lax.axis_index("xh") * Z + lax.axis_index("z")
    m = lax.axis_index("xl") * Y + lax.axis_index("y")
    sent = jnp.broadcast_to(x, (2,) + x.shape)
    got = lax.all_to_all(sent, ("xh", "z", "xl", "y"), 0, 0, axis_index_groups=groups)
    return jnp.where(f > m, got[0], jnp.where(f < m, got[1], x))


def products(places, pieces, near, far):
    width, rows = pieces[0].shape
    cols = near.shape[2] // 2
    n = len(pieces)
    tile = width // 2
    per_group = 4

    def kernel(places_ref, *refs):
        piece_refs, (near_ref, far_ref, out_ref, held, grads, sems, grad_sems) = refs[:n], refs[n:]
        where = pl.ds(pl.multiple_of(places_ref[1] * cols, cols), cols)
        grad_copies = [
            pltpu.make_async_copy(ref.at[:, :, where], grads.at[i], grad_sems.at[i])
            for i, ref in enumerate((near_ref, far_ref))
        ]
        for copy in grad_copies:
            copy.start()
        copies = [pltpu.make_async_copy(piece_refs[i], held.at[i], sems.at[i]) for i in range(n)]
        for copy in copies:
            copy.start()
        for copy in grad_copies:
            copy.wait()
        for first in range(0, n, per_group):
            group = range(first, first + per_group)
            grad = jnp.concatenate([grads[(i % 2) ^ places_ref[0], places_ref[2 + i]] for i in group], axis=0)
            for i in group:
                copies[i].wait()
            for t in range(width // tile):
                at = slice(t * tile, (t + 1) * tile)
                lhs = jnp.concatenate([held[i, at] for i in group], axis=1)
                total = jnp.dot(lhs, grad, preferred_element_type=jnp.float32)
                if first == 0:
                    out_ref[at] = total
                else:
                    out_ref[at] += total

    def size(a):
        return a.size * a.dtype.itemsize

    hbm = pl.BlockSpec(memory_space=pltpu.HBM)
    return pl.pallas_call(
        kernel,
        in_specs=[pl.BlockSpec(memory_space=pltpu.SMEM)] + [hbm] * (n + 2),
        out_specs=pl.BlockSpec(memory_space=pltpu.VMEM),
        out_shape=jax.ShapeDtypeStruct((width, cols), jnp.float32),
        scratch_shapes=[
            pltpu.VMEM((n, width, rows), pieces[0].dtype),
            pltpu.VMEM((2,) + near.shape[:2] + (cols,), near.dtype),
            pltpu.SemaphoreType.DMA((n,)),
            pltpu.SemaphoreType.DMA((2,)),
        ],
        compiler_params=pltpu.CompilerParams(vmem_limit_bytes=56 * 1024 * 1024),
        cost_estimate=pl.CostEstimate(
            flops=2 * width * cols * rows * n,
            bytes_accessed=sum(map(size, pieces)) + size(near) + width * cols * 4,
            transcendentals=0,
        ),
    )(places, *pieces, near, far)


def per_device(activations, act_basis, gradients, grad_basis):
    xh, xl, y, c = (lax.axis_index(a) for a in ("xh", "xl", "y", "c"))
    rows, act_width = activations.shape

    grad_rot = jnp.dot(gradients, grad_basis, preferred_element_type=jnp.float32)
    grad_sq = (grad_rot * grad_rot).astype(jnp.bfloat16)
    own = transpose_chips(grad_sq)

    act_blocks = activations.reshape(rows, act_width // BLOCK, BLOCK)
    act_rot = jnp.einsum("tbk,bkj->bjt", act_blocks, act_basis, preferred_element_type=jnp.float32)
    act_sq = (act_rot * act_rot).astype(jnp.bfloat16).reshape(act_width, rows)
    near_up, near_down = [act_sq], [act_sq]
    far_up = [shift(act_sq, "xl", XL, 1)]
    far_down = far_up[:]
    near_up.append(shift(act_sq, "y", Y, 1))
    near_down.append(shift(act_sq, "y", Y, -1))
    own, _ = lax.optimization_barrier((own, (near_up[1], near_down[1], far_up[0])))
    near = lax.all_to_all(jnp.broadcast_to(own, (Z,) + own.shape), "z", 0, 0)
    for k in range(1, 4):
        far_up.append(shift(far_up[-1], "y", Y, 1))
        far_down.append(shift(far_down[-1], "y", Y, -1))
        near_up.append(shift(near_up[-1], "y", Y, 1))
        if k < 3:
            near_down.append(shift(near_down[-1], "y", Y, -1))
    far_down.append(shift(far_down[-1], "y", Y, -1))

    near, _ = lax.optimization_barrier((near, (near_up[2], near_down[2], far_up[1], far_down[1])))
    far = shift(near, "xh", XH, 1)

    pieces, at = [near_up[0], far_up[0]], [y, y]
    for k in range(1, 4):
        pieces += [near_up[k], far_up[k], near_down[k], far_down[k]]
        at += [(y + Y - k) % Y] * 2 + [(y + k) % Y] * 2
    pieces += [near_up[4], far_down[4]]
    at += [(y + 4) % Y] * 2

    def places(half):
        return jnp.stack([xh ^ xl, half] + at).astype(jnp.int32)

    other = products(places(1 - c), pieces, near, far)
    got = shift(other, "c", C, 1)
    mine = products(places(c), pieces, near, far)
    return (mine + got) / TOKENS


def solution(mesh):
    chips = Mesh(mesh.devices.reshape(XH, Z, XL, Y, C), ("xh", "z", "xl", "y", "c"))
    feat, tok = ("xh", "z"), ("xl", "y", "c")
    return jax.shard_map(
        per_device,
        mesh=chips,
        in_specs=(P(tok, feat), P(feat, None, None), P(tok, feat), P(feat, None)),
        out_specs=P(feat, tok),
        check_vma=False,
    )
```

time: 115 us -> 127 us (1.10)
  waiting for transfers between devices: 20.7 us -> 28.5 us
  starting transfers between devices: 71 us -> 76 us
    ppermute x16 -> x17, starting transfers between devices: 55.8 us -> 65.1 us  [shift(): return lax.ppermute(x, axis, [(i, (i + step) % size) for i in range(size)])]
    ppermute x16 -> x17, waiting for transfers between devices: 12 us -> 20.3 us  [shift(): return lax.ppermute(x, axis, [(i, (i + step) % size) for i in range(size)])]
    all_to_all x1, starting transfers between devices: 10 us -> 5.53 us  [per_device(): near = lax.all_to_all(jnp.broadcast_to(own, (Z,) + own.shape), 'z', 0, 0)]
  transfers between devices with their start and end apart: 18 -> 19, of which waited for: 4 -> 6; matrix products, arithmetic and copies ran while one was open for 2% -> 1% of each run, Pallas kernels for 5% -> 4%
where the time goes in v10:
time: 127 us; the launch traced here: 126 us
  starting transfers between devices  76 us (60%)
  waiting for transfers between devices  28.5 us (22%)
  Pallas kernels  11.2 us (9%)
  local copies, waits for them, and re-layouts  5.58 us (4%)
  other arithmetic  2.35 us (2%)
  matrix products  1.95 us (2%)
    ppermute x17, starting transfers between devices, shift(): return lax.ppermute(x, axis, [(i, (i + step) % size) for i in range(size)])  65.1 us
    ppermute x17, waiting for transfers between devices, shift(): return lax.ppermute(x, axis, [(i, (i + step) % size) for i in range(size)])  20.3 us
    pallas_call x2, Pallas kernels, products(): pl.pallas_call(kernel, in_specs=[pl.BlockSpec(memory_space=pltpu.SMEM)] +...  11.2 us
    all_to_all x1, waiting for transfers between devices, per_device(): near = lax.all_to_all(jnp.broadcast_to(own, (Z,) + own.shape), 'z', 0, 0)  8.22 us
    all_to_all x1, starting transfers between devices, per_device(): near = lax.all_to_all(jnp.broadcast_to(own, (Z,) + own.shape), 'z', 0, 0)  5.53 us
    all_to_all x1, starting transfers between devices, transpose_chips(): lax.all_to_all(sent, ('xh', 'z', 'xl', 'y'), 0, 0, axis_index_groups=groups)  5.33 us
  transfers between devices with their start and end apart: 19, of which 6 were waited for; matrix products, arithmetic and copies ran while one was open for 1% of the time, Pallas kernels for 4%

profile of v10, /device:TPU:1, one launch (start us, length us, event | category | flops | bytes accessed | tf_op | source)
XLA Modules:
  0.0 126.0 jit_solution(14438166882748489894)
XLA Ops:
  0.0 1.4 %fusion.1 = bf16[128,512]{1,0:T(8,128)(2,1)S(1)} fusion(bf16[128,512]{1,0:T(8,128)(2,1)} %param.6, bf16[512,512]{1,0:T(8,128)(2,1)} %param.7), kind=kOutput, calls=%fused_computation.3 | convolution fusion | flops 67239936 | bytes 786432 | tf_op jit(solution)/shard_map/dot_general | solution.py:93
  1.4 0.7 broadcast_in_dim.6
  2.2 5.3 %all-to-all-start = ((bf16[2,128,512]{2,1,0:T(8,128)(2,1)}), bf16[2,128,512]{2,1,0:T(8,128)(2,1)S(1)}, u32[]{:S(2)}, u32[]{:S(2)}) async-start(bf16[2,128,512]{2,1,0:T(8,128)(2,1)} %broadcast_in_dim.6), calls=%async_computation | async-start | bytes 524288 | tf_op jit(solution)/shard_map/all_to_all | solution.py:26
  8.0 10.0 %collective-permute-start.3 = (bf16[1024,128]{1,0:T(8,128)(2,1)S(1)}, bf16[1024,128]{1,0:T(8,128)(2,1)S(1)}, u32[]{:S(2)}, u32[]{:S(2)}) collective-permute-start(bf16[1024,128]{1,0:T(8,128)(2,1)S(1)} %bitcast.29), channel_id=1, source_target_pairs={{0,14},{2,0},{4,2},{6,4},{8,6},{10,8},{12,10},{14,12},{1,15},{3,1}... | collective-permute-start | bytes 786440 | tf_op jit(solution)/shard_map/ppermute | solution.py:15
  18.0 1.9 %collective-permute-start.1 = (bf16[1024,128]{1,0:T(8,128)(2,1)S(1)}, bf16[1024,128]{1,0:T(8,128)(2,1)S(1)}, u32[]{:S(2)}, u32[]{:S(2)}) collective-permute-start(bf16[1024,128]{1,0:T(8,128)(2,1)S(1)} %bitcast.30), channel_id=1, source_target_pairs={{0,2},{2,4},{4,6},{6,8},{8,10},{10,12},{12,14},{14,0},{1,3},{3,5},... | collective-permute-start | bytes 786440 | tf_op jit(solution)/shard_map/ppermute | solution.py:15
  19.9 4.0 %collective-permute-start = (bf16[1024,128]{1,0:T(8,128)(2,1)S(1)}, bf16[1024,128]{1,0:T(8,128)(2,1)S(1)}, u32[]{:S(2)}, u32[]{:S(2)}) collective-permute-start(bf16[1024,128]{1,0:T(8,128)(2,1)S(1)} %bitcast.31), channel_id=1, source_target_pairs={{0,16},{16,0},{1,17},{17,1},{2,18},{18,2},{3,19},{19,3},{4,20},{20... | collective-permute-start | bytes 786440 | tf_op jit(solution)/shard_map/ppermute | solution.py:15
  24.1 8.8 %collective-permute-done.1.refs_2_ = bf16[1024,128]{1,0:T(8,128)(2,1)S(1)} collective-permute-done((bf16[1024,128]{1,0:T(8,128)(2,1)S(1)}, bf16[1024,128]{1,0:T(8,128)(2,1)S(1)}, u32[]{:S(2)}, u32[]{:S(2)}) %collective-permute-start.1) | collective-permute-done | bytes 262176 | tf_op jit(solution)/shard_map/ppermute | solution.py:15
  32.8 1.1 broadcast_in_dim.7
  34.0 5.5 %all-to-all-start.1 = ((bf16[8,128,512]{2,1,0:T(8,128)(2,1)}), bf16[8,128,512]{2,1,0:T(8,128)(2,1)S(1)}, u32[]{:S(2)}, u32[]{:S(2)}) async-start(bf16[8,128,512]{2,1,0:T(8,128)(2,1)} %broadcast_in_dim.7), calls=%async_computation.1 | async-start | bytes 2097152 | tf_op jit(solution)/shard_map/all_to_all | solution.py:106
  39.5 3.7 %collective-permute-start.7 = (bf16[1024,128]{1,0:T(8,128)(2,1)S(1)}, bf16[1024,128]{1,0:T(8,128)(2,1)S(1)}, u32[]{:S(2)}, u32[]{:S(2)}) collective-permute-start(bf16[1024,128]{1,0:T(8,128)(2,1)S(1)} %collective-permute-done.3.refs_4_), channel_id=1, source_target_pairs={{0,14},{2,0},{4,2},{6,4},{8,6},{10,8},{12,10},{14,12},{1,15},{3,1}... | collective-permute-start | bytes 786440 | tf_op jit(solution)/shard_map/ppermute | solution.py:15
  43.2 1.9 %collective-permute-start.5 = (bf16[1024,128]{1,0:T(8,128)(2,1)S(1)}, bf16[1024,128]{1,0:T(8,128)(2,1)S(1)}, u32[]{:S(2)}, u32[]{:S(2)}) collective-permute-start(bf16[1024,128]{1,0:T(8,128)(2,1)S(1)} %collective-permute-done.1.refs_2_), channel_id=1, source_target_pairs={{0,2},{2,4},{4,6},{6,8},{8,10},{10,12},{12,14},{14,0},{1,3},{3,5},... | collective-permute-start | bytes 786440 | tf_op jit(solution)/shard_map/ppermute | solution.py:15
  45.1 4.6 %collective-permute-start.4 = (bf16[1024,128]{1,0:T(8,128)(2,1)S(1)}, bf16[1024,128]{1,0:T(8,128)(2,1)S(1)}, u32[]{:S(2)}, u32[]{:S(2)}) collective-permute-start(bf16[1024,128]{1,0:T(8,128)(2,1)S(1)} %collective-permute-done.refs_1_), channel_id=1, source_target_pairs={{0,14},{2,0},{4,2},{6,4},{8,6},{10,8},{12,10},{14,12},{1,15},{3,1}... | collective-permute-start | bytes 786440 | tf_op jit(solution)/shard_map/ppermute | solution.py:15
  49.7 1.9 %collective-permute-start.2 = (bf16[1024,128]{1,0:T(8,128)(2,1)S(1)}, bf16[1024,128]{1,0:T(8,128)(2,1)}, u32[]{:S(2)}, u32[]{:S(2)}) collective-permute-start(bf16[1024,128]{1,0:T(8,128)(2,1)S(1)} %collective-permute-done.refs_1_), channel_id=1, source_target_pairs={{0,2},{2,4},{4,6},{6,8},{8,10},{10,12},{12,14},{14,0},{1,3},{3,5},... | collective-permute-start | bytes 786440 | tf_op jit(solution)/shard_map/ppermute | solution.py:15
  51.8 1.2 collective-permute-done.4.refs_5_
  53.8 4.6 %collective-permute-done.2.refs_3_ = bf16[1024,128]{1,0:T(8,128)(2,1)} collective-permute-done((bf16[1024,128]{1,0:T(8,128)(2,1)S(1)}, bf16[1024,128]{1,0:T(8,128)(2,1)}, u32[]{:S(2)}, u32[]{:S(2)}) %collective-permute-start.2) | collective-permute-done | bytes 262176 | tf_op jit(solution)/shard_map/ppermute | solution.py:15
  58.4 8.2 %all-to-all-done.1.refs_16_ = bf16[8,128,512]{2,1,0:T(8,128)(2,1)S(1)} async-done(((bf16[8,128,512]{2,1,0:T(8,128)(2,1)}), bf16[8,128,512]{2,1,0:T(8,128)(2,1)S(1)}, u32[]{:S(2)}, u32[]{:S(2)}) %all-to-all-start.1) | async-done | bytes 1048608 | tf_op jit(solution)/shard_map/all_to_all | solution.py:106
  66.6 5.5 %collective-permute-start.15 = (bf16[8,128,512]{2,1,0:T(8,128)(2,1)S(1)}, bf16[8,128,512]{2,1,0:T(8,128)(2,1)S(1)}, u32[]{:S(2)}, u32[]{:S(2)}) collective-permute-start(bf16[8,128,512]{2,1,0:T(8,128)(2,1)S(1)} %all-to-all-done.1.refs_16_), channel_id=1, source_target_pairs={{0,256},{256,0},{1,257},{257,1},{2,258},{258,2},{3,259},{259,3},{4... | collective-permute-start | bytes 3145736 | tf_op jit(solution)/shard_map/ppermute | solution.py:15
  72.1 3.3 %collective-permute-start.8 = (bf16[1024,128]{1,0:T(8,128)(2,1)}, bf16[1024,128]{1,0:T(8,128)(2,1)S(1)}, u32[]{:S(2)}, u32[]{:S(2)}) collective-permute-start(bf16[1024,128]{1,0:T(8,128)(2,1)} %copy-done.9), channel_id=1, source_target_pairs={{0,14},{2,0},{4,2},{6,4},{8,6},{10,8},{12,10},{14,12},{1,15},{3,1}... | collective-permute-start | bytes 786440 | tf_op jit(solution)/shard_map/ppermute | solution.py:15
  75.4 2.0 %collective-permute-start.9 = (bf16[1024,128]{1,0:T(8,128)(2,1)}, bf16[1024,128]{1,0:T(8,128)(2,1)}, u32[]{:S(2)}, u32[]{:S(2)}) collective-permute-start(bf16[1024,128]{1,0:T(8,128)(2,1)} %copy-done.8), channel_id=1, source_target_pairs={{0,2},{2,4},{4,6},{6,8},{8,10},{10,12},{12,14},{14,0},{1,3},{3,5},... | collective-permute-start | bytes 786440 | tf_op jit(solution)/shard_map/ppermute | solution.py:15
  77.4 3.2 %collective-permute-start.6 = (bf16[1024,128]{1,0:T(8,128)(2,1)}, bf16[1024,128]{1,0:T(8,128)(2,1)}, u32[]{:S(2)}, u32[]{:S(2)}) collective-permute-start(bf16[1024,128]{1,0:T(8,128)(2,1)} %collective-permute-done.2.refs_3_), channel_id=1, source_target_pairs={{0,2},{2,4},{4,6},{6,8},{8,10},{10,12},{12,14},{14,0},{1,3},{3,5},... | collective-permute-start | bytes 786440 | tf_op jit(solution)/shard_map/ppermute | solution.py:15
  80.7 0.7 copy-done.10
  81.4 5.6 %collective-permute-start.12 = (bf16[1024,128]{1,0:T(8,128)(2,1)S(1)}, bf16[1024,128]{1,0:T(8,128)(2,1)}, u32[]{:S(2)}, u32[]{:S(2)}) collective-permute-start(bf16[1024,128]{1,0:T(8,128)(2,1)S(1)} %collective-permute-done.8.refs_9_), channel_id=1, source_target_pairs={{0,14},{2,0},{4,2},{6,4},{8,6},{10,8},{12,10},{14,12},{1,15},{3,1}... | collective-permute-start | bytes 786440 | tf_op jit(solution)/shard_map/ppermute | solution.py:15
  87.0 4.1 %collective-permute-start.11 = (bf16[1024,128]{1,0:T(8,128)(2,1)S(1)}, bf16[1024,128]{1,0:T(8,128)(2,1)}, u32[]{:S(2)}, u32[]{:S(2)}) collective-permute-start(bf16[1024,128]{1,0:T(8,128)(2,1)S(1)} %collective-permute-done.7.refs_8_), channel_id=1, source_target_pairs={{0,14},{2,0},{4,2},{6,4},{8,6},{10,8},{12,10},{14,12},{1,15},{3,1}... | collective-permute-start | bytes 786440 | tf_op jit(solution)/shard_map/ppermute | solution.py:15
  91.1 1.9 %collective-permute-start.13 = (bf16[1024,128]{1,0:T(8,128)(2,1)}, bf16[1024,128]{1,0:T(8,128)(2,1)}, u32[]{:S(2)}, u32[]{:S(2)}) collective-permute-start(bf16[1024,128]{1,0:T(8,128)(2,1)} %collective-permute-done.9.refs_10_), channel_id=1, source_target_pairs={{0,2},{2,4},{4,6},{6,8},{8,10},{10,12},{12,14},{14,0},{1,3},{3,5},... | collective-permute-start | bytes 786440 | tf_op jit(solution)/shard_map/ppermute | solution.py:15
  93.1 1.9 %collective-permute-start.10 = (bf16[1024,128]{1,0:T(8,128)(2,1)}, bf16[1024,128]{1,0:T(8,128)(2,1)}, u32[]{:S(2)}, u32[]{:S(2)}) collective-permute-start(bf16[1024,128]{1,0:T(8,128)(2,1)} %collective-permute-done.6.refs_7_), channel_id=1, source_target_pairs={{0,2},{2,4},{4,6},{6,8},{8,10},{10,12},{12,14},{14,0},{1,3},{3,5},... | collective-permute-start | bytes 786440 | tf_op jit(solution)/shard_map/ppermute | solution.py:15
  95.0 4.6 %collective-permute-start.14 = (bf16[1024,128]{1,0:T(8,128)(2,1)}, bf16[1024,128]{1,0:T(8,128)(2,1)}, u32[]{:S(2)}, u32[]{:S(2)}) collective-permute-start(bf16[1024,128]{1,0:T(8,128)(2,1)} %collective-permute-done.12.refs_13_), channel_id=1, source_target_pairs={{0,14},{2,0},{4,2},{6,4},{8,6},{10,8},{12,10},{14,12},{1,15},{3,1}... | collective-permute-start | bytes 786440 | tf_op jit(solution)/shard_map/ppermute | solution.py:15
  100.3 5.5 %collective-permute-done.10.refs_11_ = bf16[1024,128]{1,0:T(8,128)(2,1)} collective-permute-done((bf16[1024,128]{1,0:T(8,128)(2,1)}, bf16[1024,128]{1,0:T(8,128)(2,1)}, u32[]{:S(2)}, u32[]{:S(2)}) %collective-permute-start.10) | collective-permute-done | bytes 262176 | tf_op jit(solution)/shard_map/ppermute | solution.py:15
  105.9 1.0 copy-done.2
  106.9 5.6 %shard_map.47 = f32[1024,256]{1,0:T(8,128)} custom-call(s32[18]{0:T(128)} %stack.76.places_ref, bf16[1024,128]{1,0:T(8,128)(2,1)} %bitcast.32, bf16[1024,128]{1,0:T(8,128)(2,1)} %copy-done.6, bf16[1024,128]{1,0:T(8,128)(2,1)} %copy-done.5, bf16[1024,128]{1,0:T(8,128)(2,1)} %collective-permute-done.2.refs_3_, bf16[1024,128]{1,0:T(8,128)(2,1)} %copy-done.4, ...), custom_call_target="tpu_custom_call" | custom-call | flops 1073741824 | bytes 6291456 | tf_op jit(solution)/shard_map/pallas_call | solution.py:69
  112.5 4.9 %collective-permute-start.16 = (f32[1024,256]{1,0:T(8,128)}, f32[1024,256]{1,0:T(8,128)S(1)}, u32[]{:S(2)}, u32[]{:S(2)}) collective-permute-start(f32[1024,256]{1,0:T(8,128)} %shard_map.47), channel_id=1, source_target_pairs={{0,1},{1,0},{2,3},{3,2},{4,5},{5,4},{6,7},{7,6},{8,9},{9,8},{10,11... | collective-permute-start | bytes 3145736 | tf_op jit(solution)/shard_map/ppermute | solution.py:15
  118.1 5.6 %shard_map.46 = f32[1024,256]{1,0:T(8,128)} custom-call(s32[18]{0:T(128)} %stack.36.places_ref, bf16[1024,128]{1,0:T(8,128)(2,1)} %bitcast.33, bf16[1024,128]{1,0:T(8,128)(2,1)} %copy-done.6, bf16[1024,128]{1,0:T(8,128)(2,1)} %copy-done.5, bf16[1024,128]{1,0:T(8,128)(2,1)} %collective-permute-done.2.refs_3_, bf16[1024,128]{1,0:T(8,128)(2,1)} %copy-done.4, ...), custom_call_target="tpu_custom_call" | custom-call | flops 1073741824 | bytes 6291456 | tf_op jit(solution)/shard_map/pallas_call | solution.py:69
  123.7 2.3 %add_multiply_fusion = f32[1024,256]{1,0:T(8,128)} fusion(f32[1024,256]{1,0:T(8,128)} %shard_map.46, f32[1024,256]{1,0:T(8,128)S(1)} %collective-permute-done.16), kind=kLoop, calls=%fused_computation.4 | loop fusion | flops 524288 | bytes 3145728 | tf_op jit(solution)/shard_map/div | solution.py:131
  (40 shorter events, 2.8 us)
Async XLA Ops:
  0.0 7.5 %copy-start = (bf16[2,512,512]{2,1,0:T(8,128)(2,1)S(1)}, bf16[2,512,512]{2,1,0:T(8,128)(2,1)}, u32[]{:S(2)}) copy-start(bf16[2,512,512]{2,1,0:T(8,128)(2,1)} %param.5) | copy-start | bytes 3145732
  2.2 5.3 %copy-start.11 = (bf16[128,1024]{1,0:T(8,128)(2,1)S(1)}, bf16[128,1024]{1,0:T(8,128)(2,1)}, u32[]{:S(2)}) copy-start(bf16[128,1024]{1,0:T(8,128)(2,1)} %param.4) | copy-start | bytes 786436
  2.2 21.8 %all-to-all-start = ((bf16[2,128,512]{2,1,0:T(8,128)(2,1)}), bf16[2,128,512]{2,1,0:T(8,128)(2,1)S(1)}, u32[]{:S(2)}, u32[]{:S(2)}) async-start(bf16[2,128,512]{2,1,0:T(8,128)(2,1)} %broadcast_in_dim.6), calls=%async_computation | async-start | bytes 524288 | tf_op jit(solution)/shard_map/all_to_all | solution.py:26
  8.0 16.0 %copy-start.3 = (bf16[2,512,128]{2,1,0:T(8,128)(2,1)}, bf16[2,512,128]{2,1,0:T(8,128)(2,1)S(1)}, u32[]{:S(2)}) copy-start(bf16[2,512,128]{2,1,0:T(8,128)(2,1)S(1)} %fusion) | copy-start | bytes 786436
  8.0 16.0 %collective-permute-start.3 = (bf16[1024,128]{1,0:T(8,128)(2,1)S(1)}, bf16[1024,128]{1,0:T(8,128)(2,1)S(1)}, u32[]{:S(2)}, u32[]{:S(2)}) collective-permute-start(bf16[1024,128]{1,0:T(8,128)(2,1)S(1)} %bitcast.29), channel_id=1, source_target_pairs={{0,14},{2,0},{4,2},{6,4},{8,6},{10,8},{12,10},{14,12},{1,15},{3,1}... | collective-permute-start | bytes 786440 | tf_op jit(solution)/shard_map/ppermute | solution.py:15
  18.0 14.8 %collective-permute-start.1 = (bf16[1024,128]{1,0:T(8,128)(2,1)S(1)}, bf16[1024,128]{1,0:T(8,128)(2,1)S(1)}, u32[]{:S(2)}, u32[]{:S(2)}) collective-permute-start(bf16[1024,128]{1,0:T(8,128)(2,1)S(1)} %bitcast.30), channel_id=1, source_target_pairs={{0,2},{2,4},{4,6},{6,8},{8,10},{10,12},{12,14},{14,0},{1,3},{3,5},... | collective-permute-start | bytes 786440 | tf_op jit(solution)/shard_map/ppermute | solution.py:15
  19.9 12.9 %collective-permute-start = (bf16[1024,128]{1,0:T(8,128)(2,1)S(1)}, bf16[1024,128]{1,0:T(8,128)(2,1)S(1)}, u32[]{:S(2)}, u32[]{:S(2)}) collective-permute-start(bf16[1024,128]{1,0:T(8,128)(2,1)S(1)} %bitcast.31), channel_id=1, source_target_pairs={{0,16},{16,0},{1,17},{17,1},{2,18},{18,2},{3,19},{19,3},{4,20},{20... | collective-permute-start | bytes 786440 | tf_op jit(solution)/shard_map/ppermute | solution.py:15
  24.1 15.5 %copy-start.4 = (bf16[1024,128]{1,0:T(8,128)(2,1)}, bf16[1024,128]{1,0:T(8,128)(2,1)S(1)}, u32[]{:S(2)}) copy-start(bf16[1024,128]{1,0:T(8,128)(2,1)S(1)} %collective-permute-done.3.refs_4_) | copy-start | bytes 786436
  32.8 10.4 %copy-start.5 = (bf16[1024,128]{1,0:T(8,128)(2,1)}, bf16[1024,128]{1,0:T(8,128)(2,1)S(1)}, u32[]{:S(2)}) copy-start(bf16[1024,128]{1,0:T(8,128)(2,1)S(1)} %collective-permute-done.1.refs_2_) | copy-start | bytes 786436
  32.8 16.9 %copy-start.6 = (bf16[1024,128]{1,0:T(8,128)(2,1)}, bf16[1024,128]{1,0:T(8,128)(2,1)S(1)}, u32[]{:S(2)}) copy-start(bf16[1024,128]{1,0:T(8,128)(2,1)S(1)} %collective-permute-done.refs_1_) | copy-start | bytes 786436
  34.0 32.6 %all-to-all-start.1 = ((bf16[8,128,512]{2,1,0:T(8,128)(2,1)}), bf16[8,128,512]{2,1,0:T(8,128)(2,1)S(1)}, u32[]{:S(2)}, u32[]{:S(2)}) async-start(bf16[8,128,512]{2,1,0:T(8,128)(2,1)} %broadcast_in_dim.7), calls=%async_computation.1 | async-start | bytes 2097152 | tf_op jit(solution)/shard_map/all_to_all | solution.py:106
  39.5 12.2 %collective-permute-start.7 = (bf16[1024,128]{1,0:T(8,128)(2,1)S(1)}, bf16[1024,128]{1,0:T(8,128)(2,1)S(1)}, u32[]{:S(2)}, u32[]{:S(2)}) collective-permute-start(bf16[1024,128]{1,0:T(8,128)(2,1)S(1)} %collective-permute-done.3.refs_4_), channel_id=1, source_target_pairs={{0,14},{2,0},{4,2},{6,4},{8,6},{10,8},{12,10},{14,12},{1,15},{3,1}... | collective-permute-start | bytes 786440 | tf_op jit(solution)/shard_map/ppermute | solution.py:15
  43.2 8.6 %collective-permute-start.5 = (bf16[1024,128]{1,0:T(8,128)(2,1)S(1)}, bf16[1024,128]{1,0:T(8,128)(2,1)S(1)}, u32[]{:S(2)}, u32[]{:S(2)}) collective-permute-start(bf16[1024,128]{1,0:T(8,128)(2,1)S(1)} %collective-permute-done.1.refs_2_), channel_id=1, source_target_pairs={{0,2},{2,4},{4,6},{6,8},{8,10},{10,12},{12,14},{14,0},{1,3},{3,5},... | collective-permute-start | bytes 786440 | tf_op jit(solution)/shard_map/ppermute | solution.py:15
  45.1 7.9 %collective-permute-start.4 = (bf16[1024,128]{1,0:T(8,128)(2,1)S(1)}, bf16[1024,128]{1,0:T(8,128)(2,1)S(1)}, u32[]{:S(2)}, u32[]{:S(2)}) collective-permute-start(bf16[1024,128]{1,0:T(8,128)(2,1)S(1)} %collective-permute-done.refs_1_), channel_id=1, source_target_pairs={{0,14},{2,0},{4,2},{6,4},{8,6},{10,8},{12,10},{14,12},{1,15},{3,1}... | collective-permute-start | bytes 786440 | tf_op jit(solution)/shard_map/ppermute | solution.py:15
  49.7 8.6 %collective-permute-start.2 = (bf16[1024,128]{1,0:T(8,128)(2,1)S(1)}, bf16[1024,128]{1,0:T(8,128)(2,1)}, u32[]{:S(2)}, u32[]{:S(2)}) collective-permute-start(bf16[1024,128]{1,0:T(8,128)(2,1)S(1)} %collective-permute-done.refs_1_), channel_id=1, source_target_pairs={{0,2},{2,4},{4,6},{6,8},{8,10},{10,12},{12,14},{14,0},{1,3},{3,5},... | collective-permute-start | bytes 786440 | tf_op jit(solution)/shard_map/ppermute | solution.py:15
  51.7 54.2 %copy-start.7 = (bf16[1024,128]{1,0:T(8,128)(2,1)}, bf16[1024,128]{1,0:T(8,128)(2,1)S(1)}, u32[]{:S(2)}) copy-start(bf16[1024,128]{1,0:T(8,128)(2,1)S(1)} %collective-permute-done.7.refs_8_) | copy-start | bytes 786436
  51.8 6.5 %copy-start.8 = (bf16[1024,128]{1,0:T(8,128)(2,1)}, bf16[1024,128]{1,0:T(8,128)(2,1)S(1)}, u32[]{:S(2)}) copy-start(bf16[1024,128]{1,0:T(8,128)(2,1)S(1)} %collective-permute-done.5.refs_6_) | copy-start | bytes 786436
  53.1 0.7 copy-start.9
  66.6 39.3 %copy-start.1 = (bf16[8,128,512]{2,1,0:T(8,128)(2,1)}, bf16[8,128,512]{2,1,0:T(8,128)(2,1)S(1)}, u32[]{:S(2)}) copy-start(bf16[8,128,512]{2,1,0:T(8,128)(2,1)S(1)} %all-to-all-done.1.refs_16_) | copy-start | bytes 3145732
  66.6 39.3 %collective-permute-start.15 = (bf16[8,128,512]{2,1,0:T(8,128)(2,1)S(1)}, bf16[8,128,512]{2,1,0:T(8,128)(2,1)S(1)}, u32[]{:S(2)}, u32[]{:S(2)}) collective-permute-start(bf16[8,128,512]{2,1,0:T(8,128)(2,1)S(1)} %all-to-all-done.1.refs_16_), channel_id=1, source_target_pairs={{0,256},{256,0},{1,257},{257,1},{2,258},{258,2},{3,259},{259,3},{4... | collective-permute-start | bytes 3145736 | tf_op jit(solution)/shard_map/ppermute | solution.py:15
  72.1 8.5 %collective-permute-start.8 = (bf16[1024,128]{1,0:T(8,128)(2,1)}, bf16[1024,128]{1,0:T(8,128)(2,1)S(1)}, u32[]{:S(2)}, u32[]{:S(2)}) collective-permute-start(bf16[1024,128]{1,0:T(8,128)(2,1)} %copy-done.9), channel_id=1, source_target_pairs={{0,14},{2,0},{4,2},{6,4},{8,6},{10,8},{12,10},{14,12},{1,15},{3,1}... | collective-permute-start | bytes 786440 | tf_op jit(solution)/shard_map/ppermute | solution.py:15
  75.4 15.7 %collective-permute-start.9 = (bf16[1024,128]{1,0:T(8,128)(2,1)}, bf16[1024,128]{1,0:T(8,128)(2,1)}, u32[]{:S(2)}, u32[]{:S(2)}) collective-permute-start(bf16[1024,128]{1,0:T(8,128)(2,1)} %copy-done.8), channel_id=1, source_target_pairs={{0,2},{2,4},{4,6},{6,8},{8,10},{10,12},{12,14},{14,0},{1,3},{3,5},... | collective-permute-start | bytes 786440 | tf_op jit(solution)/shard_map/ppermute | solution.py:15
  77.4 15.6 %collective-permute-start.6 = (bf16[1024,128]{1,0:T(8,128)(2,1)}, bf16[1024,128]{1,0:T(8,128)(2,1)}, u32[]{:S(2)}, u32[]{:S(2)}) collective-permute-start(bf16[1024,128]{1,0:T(8,128)(2,1)} %collective-permute-done.2.refs_3_), channel_id=1, source_target_pairs={{0,2},{2,4},{4,6},{6,8},{8,10},{10,12},{12,14},{14,0},{1,3},{3,5},... | collective-permute-start | bytes 786440 | tf_op jit(solution)/shard_map/ppermute | solution.py:15
  80.7 0.7 copy-start.10
  81.4 13.6 %collective-permute-start.12 = (bf16[1024,128]{1,0:T(8,128)(2,1)S(1)}, bf16[1024,128]{1,0:T(8,128)(2,1)}, u32[]{:S(2)}, u32[]{:S(2)}) collective-permute-start(bf16[1024,128]{1,0:T(8,128)(2,1)S(1)} %collective-permute-done.8.refs_9_), channel_id=1, source_target_pairs={{0,14},{2,0},{4,2},{6,4},{8,6},{10,8},{12,10},{14,12},{1,15},{3,1}... | collective-permute-start | bytes 786440 | tf_op jit(solution)/shard_map/ppermute | solution.py:15
  87.0 13.3 %collective-permute-start.11 = (bf16[1024,128]{1,0:T(8,128)(2,1)S(1)}, bf16[1024,128]{1,0:T(8,128)(2,1)}, u32[]{:S(2)}, u32[]{:S(2)}) collective-permute-start(bf16[1024,128]{1,0:T(8,128)(2,1)S(1)} %collective-permute-done.7.refs_8_), channel_id=1, source_target_pairs={{0,14},{2,0},{4,2},{6,4},{8,6},{10,8},{12,10},{14,12},{1,15},{3,1}... | collective-permute-start | bytes 786440 | tf_op jit(solution)/shard_map/ppermute | solution.py:15
  91.1 9.2 %collective-permute-start.13 = (bf16[1024,128]{1,0:T(8,128)(2,1)}, bf16[1024,128]{1,0:T(8,128)(2,1)}, u32[]{:S(2)}, u32[]{:S(2)}) collective-permute-start(bf16[1024,128]{1,0:T(8,128)(2,1)} %collective-permute-done.9.refs_10_), channel_id=1, source_target_pairs={{0,2},{2,4},{4,6},{6,8},{8,10},{10,12},{12,14},{14,0},{1,3},{3,5},... | collective-permute-start | bytes 786440 | tf_op jit(solution)/shard_map/ppermute | solution.py:15
  93.1 12.8 %collective-permute-start.10 = (bf16[1024,128]{1,0:T(8,128)(2,1)}, bf16[1024,128]{1,0:T(8,128)(2,1)}, u32[]{:S(2)}, u32[]{:S(2)}) collective-permute-start(bf16[1024,128]{1,0:T(8,128)(2,1)} %collective-permute-done.6.refs_7_), channel_id=1, source_target_pairs={{0,2},{2,4},{4,6},{6,8},{8,10},{10,12},{12,14},{14,0},{1,3},{3,5},... | collective-permute-start | bytes 786440 | tf_op jit(solution)/shard_map/ppermute | solution.py:15
  95.0 10.8 %collective-permute-start.14 = (bf16[1024,128]{1,0:T(8,128)(2,1)}, bf16[1024,128]{1,0:T(8,128)(2,1)}, u32[]{:S(2)}, u32[]{:S(2)}) collective-permute-start(bf16[1024,128]{1,0:T(8,128)(2,1)} %collective-permute-done.12.refs_13_), channel_id=1, source_target_pairs={{0,14},{2,0},{4,2},{6,4},{8,6},{10,8},{12,10},{14,12},{1,15},{3,1}... | collective-permute-start | bytes 786440 | tf_op jit(solution)/shard_map/ppermute | solution.py:15
  105.9 1.0 copy-start.2
  112.5 11.2 %collective-permute-start.16 = (f32[1024,256]{1,0:T(8,128)}, f32[1024,256]{1,0:T(8,128)S(1)}, u32[]{:S(2)}, u32[]{:S(2)}) collective-permute-start(f32[1024,256]{1,0:T(8,128)} %shard_map.47), channel_id=1, source_target_pairs={{0,1},{1,0},{2,3},{3,2},{4,5},{5,4},{6,7},{7,6},{8,9},{9,8},{10,11... | collective-permute-start | bytes 3145736 | tf_op jit(solution)/shard_map/ppermute | solution.py:15

commit v11 on v8

--- a/solution.py
+++ b/solution.py
@@ -26,12 +26,12 @@
     return lax.ppermute(x, axis, [(0, 1), (1, 0)])
 
 
-def product(swapped, act_all, near, far):
+def product(swapped, act_all, near, far, parts):
     _, _, width, rows = act_all.shape
     cols = near.shape[2]
     tile = width // 2
 
-    def kernel(swapped_ref, act_ref, near_ref, far_ref, out_ref):
+    def kernel(swapped_ref, act_ref, near_ref, far_ref, *out_refs):
         def go(blocks):
             for t in range(width // tile):
                 at = slice(t * tile, (t + 1) * tile)
@@ -41,7 +41,10 @@
                     grad = jnp.concatenate([blocks[pair][y] for y in range(Y)], axis=0)
                     part = jnp.dot(act, grad, preferred_element_type=jnp.float32)
                     total = part if total is None else total + part
-                out_ref[at] = total
+                if parts == 1:
+                    out_refs[0][at] = total
+                else:
+                    out_refs[t][...] = total
 
         @pl.when(swapped_ref[0] == 0)
         def _():
@@ -55,8 +58,8 @@
     return pl.pallas_call(
         kernel,
         in_specs=[pl.BlockSpec(memory_space=pltpu.SMEM), vmem, vmem, vmem],
-        out_specs=vmem,
-        out_shape=jax.ShapeDtypeStruct((width, cols), jnp.float32),
+        out_specs=[vmem] * parts,
+        out_shape=[jax.ShapeDtypeStruct((width // parts, cols), jnp.float32)] * parts,
         compiler_params=pltpu.CompilerParams(vmem_limit_bytes=16 * 1024 * 1024),
         cost_estimate=pl.CostEstimate(
             flops=2 * width * cols * rows * 2 * Y,
@@ -75,26 +78,28 @@
     grad_pair = jnp.broadcast_to(grad_sq, (2,) + grad_sq.shape)
     own = transpose_chips(grad_sq, grad_pair)
 
+    activations, _ = lax.optimization_barrier((activations, grad_pair))
     act_blocks = activations.reshape(rows, act_width // BLOCK, BLOCK)
     act_rot = jnp.einsum("tbk,bkj->bjt", act_blocks, act_basis, preferred_element_type=jnp.float32)
     act_sq = (act_rot * act_rot).astype(jnp.bfloat16).reshape(act_width, rows)
     act_pair = lax.all_gather(act_sq, "xl", axis=0)
-    act_pair, _ = lax.optimization_barrier((act_pair, own))
     act_all = lax.all_gather(act_pair, "y", axis=0)
 
+    cols = own.shape[1] // 2
+
     def gathered(half):
-        cols = own.shape[1] // 2
         mine = lax.dynamic_slice_in_dim(own, half * cols, cols, 1)
-        near = lax.all_to_all(jnp.broadcast_to(mine, (Z,) + mine.shape), "z", 0, 0)
-        return near, swap(near, "xh")
+        return lax.all_to_all(jnp.broadcast_to(mine, (Z,) + mine.shape), "z", 0, 0)
 
+    near_other, near_mine = gathered(1 - c), gathered(c)
+    far_other = swap(near_other, "xh")
+    far_mine = swap(near_mine, "xh")
     swapped = xh[None]
-    theirs, ours = gathered(1 - c), gathered(c)
-    act_all, _ = lax.optimization_barrier((act_all, ours))
-    other = product(swapped, act_all, *theirs)
-    got = swap(other, "c")
-    mine = product(swapped, act_all, *ours)
-    return (mine + got) / TOKENS
+    act_all, _ = lax.optimization_barrier((act_all, near_mine))
+    other = product(swapped, act_all, near_other, far_other, 2)
+    got = [swap(part, "c") for part in other]
+    (mine,) = product(swapped, act_all, near_mine, far_mine, 1)
+    return (mine + jnp.concatenate(got)) / TOKENS
 
 
 def solution(mesh):

time: 109 us -> 107 us (0.982)
  waiting for transfers between devices: 23.4 us -> 13.5 us
  starting transfers between devices: 22.4 us -> 30.6 us
    all_gather x1, waiting for transfers between devices: 14.8 us -> 1.45 us  [per_device(): act_all = lax.all_gather(act_pair, 'y', axis=0)]
    ppermute x3 -> x4, starting transfers between devices: 13.6 us -> 20.2 us  [swap(): return lax.ppermute(x, axis, [(0, 1), (1, 0)])]
    all_to_all x1, waiting for transfers between devices: 0.01 us -> 4.93 us  [transpose_chips(): lax.all_to_all(sent, ('xh', 'z', 'xl', 'y'), 0, 0, axis_index_groups=groups)]
    all_to_all x1, starting transfers between devices: 5.2 us -> 6.61 us  [transpose_chips(): lax.all_to_all(sent, ('xh', 'z', 'xl', 'y'), 0, 0, axis_index_groups=groups)]
  transfers between devices with their start and end apart: 6 -> 7, of which waited for: 3 -> 4; matrix products, arithmetic and copies ran while one was open for 2% -> 1% of each run, Pallas kernels for 1% -> 2%
where the time goes in v11:
time: 107 us; the launch traced here: 106 us
  blocking collectives  38.5 us (36%)
  starting transfers between devices  30.6 us (29%)
  waiting for transfers between devices  13.5 us (13%)
  between operations  13.5 us (13%)
  local copies, waits for them, and re-layouts  3.96 us (4%)
  matrix products  2.68 us (3%)
  Pallas kernels  2.5 us (2%)
  other arithmetic  1.13 us (1%)
    all_to_all x1, blocking collectives, gathered(): return lax.all_to_all(jnp.broadcast_to(mine, (Z,) + mine.shape), 'z', 0, 0)  31.9 us
    ppermute x4, starting transfers between devices, swap(): return lax.ppermute(x, axis, [(0, 1), (1, 0)])  20.2 us
    all_to_all x1, starting transfers between devices, transpose_chips(): lax.all_to_all(sent, ('xh', 'z', 'xl', 'y'), 0, 0, axis_index_groups=groups)  6.61 us
    all_gather x1, blocking collectives, per_device(): act_pair = lax.all_gather(act_sq, 'xl', axis=0)  6.56 us
    all_to_all x1, waiting for transfers between devices, gathered(): return lax.all_to_all(jnp.broadcast_to(mine, (Z,) + mine.shape), 'z', 0, 0)  6.51 us
    all_to_all x1, waiting for transfers between devices, transpose_chips(): lax.all_to_all(sent, ('xh', 'z', 'xl', 'y'), 0, 0, axis_index_groups=groups)  4.93 us
    all_to_all x1, starting transfers between devices, gathered(): return lax.all_to_all(jnp.broadcast_to(mine, (Z,) + mine.shape), 'z', 0, 0)  3.79 us
    pallas_call x2, Pallas kernels, product(): pl.pallas_call(kernel, in_specs=[pl.BlockSpec(memory_space=pltpu.SMEM), v...  2.5 us
  transfers between devices with their start and end apart: 7, of which 4 were waited for; matrix products, arithmetic and copies ran while one was open for 1% of the time, Pallas kernels for 2%

profile of v11, /device:TPU:1, one launch (start us, length us, event | category | flops | bytes accessed | tf_op | source)
XLA Modules:
  0.0 106.4 jit_solution(18433785826820670556)
XLA Ops:
  6.5 0.0 copy-start
  6.5 0.0 all-gather.3.cloned.1.call-start
  6.5 1.4 %fusion.2 = bf16[128,512]{1,0:T(8,128)(2,1)S(1)} fusion(bf16[128,512]{1,0:T(8,128)(2,1)} %param.6, bf16[512,512]{1,0:T(8,128)(2,1)} %param.7), kind=kOutput, calls=%fused_computation.4 | convolution fusion | flops 67239936 | bytes 786432 | tf_op jit(solution)/shard_map/dot_general | solution.py:76
  8.0 0.7 broadcast_in_dim.13
  8.7 0.0 copy-done
  8.7 1.3 %fusion.1 = bf16[2,512,128]{1,2,0:T(8,128)(2,1)S(1)} fusion(bf16[2,512,512]{2,1,0:T(8,128)(2,1)S(1)} %copy-done, bf16[16,2,8,512]{3,2,1,0:T(8,128)(2,1)} %bitcast.25), kind=kOutput, calls=%fused_computation.3 | convolution fusion | flops 134479872 | bytes 1572864 | tf_op jit(solution)/shard_map/tbk,bkj->bjt/dot_general | solution.py:83
  10.0 0.2 copy.9
  10.1 6.6 %all_gather.9 = bf16[2,1024,128]{2,1,0:T(8,128)(2,1)} all-gather(bf16[1,1024,128]{2,1,0:T(8,128)(2,1)S(1)} %bitcast.24), channel_id=1, replica_groups=mesh['xh'=2,'z'=8,'xl'=2,'y'=8,'c'=2] {'xl'}, dimensions={0}, use_global_device_ids=true | all-gather | bytes 786432 | tf_op jit(solution)/shard_map/all_gather | solution.py:85
  16.7 0.0 all-gather.3.cloned.1.call-update
  16.7 6.6 %all-to-all-start = ((bf16[2,128,512]{2,1,0:T(8,128)(2,1)}), bf16[2,128,512]{2,1,0:T(8,128)(2,1)S(1)}, u32[]{:S(2)}, u32[]{:S(2)}) async-start(bf16[2,128,512]{2,1,0:T(8,128)(2,1)} %broadcast_in_dim.13), calls=%async_computation | async-start | bytes 524288 | tf_op jit(solution)/shard_map/all_to_all | solution.py:21
  23.3 4.9 %all-to-all-done = bf16[2,128,512]{2,1,0:T(8,128)(2,1)S(1)} async-done(((bf16[2,128,512]{2,1,0:T(8,128)(2,1)}), bf16[2,128,512]{2,1,0:T(8,128)(2,1)S(1)}, u32[]{:S(2)}, u32[]{:S(2)}) %all-to-all-start) | async-done | bytes 262176 | tf_op jit(solution)/shard_map/all_to_all | solution.py:21
  28.4 31.9 %all_to_all.15.near_ref = bf16[8,128,256]{2,1,0:T(8,128)(2,1)S(1)} all-to-all(bf16[8,128,256]{2,1,0:T(8,128)(2,1)S(1)} %broadcast_in_dim.15), channel_id=1, replica_groups=mesh['xh'=2,'z'=8,'xl'=2,'y'=8,'c'=2] {'z'}, dimensions={0} | all-to-all | bytes 1048576 | tf_op jit(solution)/shard_map/all_to_all | solution.py:92
  60.3 0.8 broadcast_in_dim.14
  61.1 3.8 %all-to-all-start.1 = ((bf16[8,128,256]{2,1,0:T(8,128)(2,1)}), bf16[8,128,256]{2,1,0:T(8,128)(2,1)S(1)}, u32[]{:S(2)}, u32[]{:S(2)}) async-start(bf16[8,128,256]{2,1,0:T(8,128)(2,1)} %broadcast_in_dim.14), calls=%async_computation.1 | async-start | bytes 1048576 | tf_op jit(solution)/shard_map/all_to_all | solution.py:92
  64.9 5.5 %collective-permute-start.1 = (bf16[8,128,256]{2,1,0:T(8,128)(2,1)S(1)}, bf16[8,128,256]{2,1,0:T(8,128)(2,1)S(1)}, u32[]{:S(2)}, u32[]{:S(2)}) collective-permute-start(bf16[8,128,256]{2,1,0:T(8,128)(2,1)S(1)} %all_to_all.15.near_ref), channel_id=1, source_target_pairs={{0,256},{256,0},{1,257},{257,1},{2,258},{258,2},{3,259},{259,3},{4... | collective-permute-start | bytes 1572872 | tf_op jit(solution)/shard_map/ppermute | solution.py:26
  70.4 6.5 %all-to-all-done.1.near_ref = bf16[8,128,256]{2,1,0:T(8,128)(2,1)S(1)} async-done(((bf16[8,128,256]{2,1,0:T(8,128)(2,1)}), bf16[8,128,256]{2,1,0:T(8,128)(2,1)S(1)}, u32[]{:S(2)}, u32[]{:S(2)}) %all-to-all-start.1) | async-done | bytes 524320 | tf_op jit(solution)/shard_map/all_to_all | solution.py:92
  76.9 5.6 %collective-permute-start = (bf16[8,128,256]{2,1,0:T(8,128)(2,1)S(1)}, bf16[8,128,256]{2,1,0:T(8,128)(2,1)S(1)}, u32[]{:S(2)}, u32[]{:S(2)}) collective-permute-start(bf16[8,128,256]{2,1,0:T(8,128)(2,1)S(1)} %all-to-all-done.1.near_ref), channel_id=1, source_target_pairs={{0,256},{256,0},{1,257},{257,1},{2,258},{258,2},{3,259},{259,3},{4... | collective-permute-start | bytes 1572872 | tf_op jit(solution)/shard_map/ppermute | solution.py:26
  82.5 1.5 %all-gather.3.cloned.1.call-done = bf16[16,1024,128]{2,1,0:T(8,128)(2,1)} async-done(((bf16[2,1024,128]{2,1,0:T(8,128)(2,1)}), bf16[16,1024,128]{2,1,0:T(8,128)(2,1)}) %all-gather.3.cloned.1.call-update) | async-done | bytes 4194320 | tf_op jit(solution)/shard_map/all_gather | solution.py:86
  84.0 0.0 collective-permute-done.1.far_ref
  84.0 0.0 copy-start.1
  84.0 2.2 %copy-done.1 = bf16[16,1024,128]{2,1,0:T(8,128)(2,1)S(1)} copy-done((bf16[16,1024,128]{2,1,0:T(8,128)(2,1)S(1)}, bf16[16,1024,128]{2,1,0:T(8,128)(2,1)}, u32[]{:S(2)}) %copy-start.1) | copy-done | bytes 4194328
  86.2 1.2 %shard_map.47 = (f32[512,256]{1,0:T(8,128)S(1)}, f32[512,256]{1,0:T(8,128)S(1)}) custom-call(s32[1]{0:T(128)} %bitcast.swapped_ref, bf16[8,2,1024,128]{3,2,1,0:T(8,128)(2,1)S(1)} %bitcast.22, bf16[8,128,256]{2,1,0:T(8,128)(2,1)S(1)} %all_to_all.15.near_ref, bf16[8,128,256]{2,1,0:T(8,128)(2,1)S(1)} %collective-permute-done.1.far_ref), custom_call_target="tpu_custom_call" | custom-call | flops 1073741824 | bytes 6291456 | tf_op jit(solution)/shard_map/pallas_call | solution.py:58
  87.4 7.2 %collective-permute-start.2 = (f32[512,256]{1,0:T(8,128)S(1)}, f32[512,256]{1,0:T(8,128)S(1)}, u32[]{:S(2)}, u32[]{:S(2)}) collective-permute-start(f32[512,256]{1,0:T(8,128)S(1)} %get-tuple-element.11), channel_id=1, source_target_pairs={{0,1},{1,0},{2,3},{3,2},{4,5},{5,4},{6,7},{7,6},{8,9},{9,8},{10,11... | collective-permute-start | bytes 1572872 | tf_op jit(solution)/shard_map/ppermute | solution.py:26
  94.6 1.9 %collective-permute-start.3 = (f32[512,256]{1,0:T(8,128)S(1)}, f32[512,256]{1,0:T(8,128)S(1)}, u32[]{:S(2)}, u32[]{:S(2)}) collective-permute-start(f32[512,256]{1,0:T(8,128)S(1)} %get-tuple-element.12), channel_id=1, source_target_pairs={{0,1},{1,0},{2,3},{3,2},{4,5},{5,4},{6,7},{7,6},{8,9},{9,8},{10,11... | collective-permute-start | bytes 1572872 | tf_op jit(solution)/shard_map/ppermute | solution.py:26
  96.5 0.0 collective-permute-done.far_ref
  96.6 1.3 %shard_map.46 = f32[1024,256]{1,0:T(8,128)S(1)} custom-call(s32[1]{0:T(128)} %bitcast.swapped_ref, bf16[8,2,1024,128]{3,2,1,0:T(8,128)(2,1)S(1)} %bitcast.23, bf16[8,128,256]{2,1,0:T(8,128)(2,1)S(1)} %all-to-all-done.1.near_ref, bf16[8,128,256]{2,1,0:T(8,128)(2,1)S(1)} %collective-permute-done.far_ref), custom_call_target="tpu_custom_call" | custom-call | flops 1073741824 | bytes 6291456 | tf_op jit(solution)/shard_map/pallas_call | solution.py:58
  97.8 0.0 collective-permute-done.2
  97.8 0.6 collective-permute-done.3
  98.4 1.1 %fusion.3 = f32[1024,256]{1,0:T(8,128)} fusion(f32[1024,256]{1,0:T(8,128)S(1)} %shard_map.46, f32[512,256]{1,0:T(8,128)S(1)} %collective-permute-done.3, f32[512,256]{1,0:T(8,128)S(1)} %collective-permute-done.2), kind=kLoop, calls=%fused_computation.6 | loop fusion | flops 786432 | bytes 3145728 | tf_op jit(solution)/shard_map/div | solution.py:102
  (3 shorter events, 0.1 us)
Async XLA Ops:
  6.5 2.2 %copy-start = (bf16[2,512,512]{2,1,0:T(8,128)(2,1)S(1)}, bf16[2,512,512]{2,1,0:T(8,128)(2,1)}, u32[]{:S(2)}) copy-start(bf16[2,512,512]{2,1,0:T(8,128)(2,1)} %param.5) | copy-start | bytes 3145732
  6.5 77.4 %all-gather.3.cloned.1.call-start = ((), (), s32[]{:S(2)}) async-start(), calls=%async_computation.3 | async-start | bytes 4718592 | tf_op jit(solution)/shard_map/all_gather | solution.py:86
  16.7 11.5 %all-to-all-start = ((bf16[2,128,512]{2,1,0:T(8,128)(2,1)}), bf16[2,128,512]{2,1,0:T(8,128)(2,1)S(1)}, u32[]{:S(2)}, u32[]{:S(2)}) async-start(bf16[2,128,512]{2,1,0:T(8,128)(2,1)} %broadcast_in_dim.13), calls=%async_computation | async-start | bytes 524288 | tf_op jit(solution)/shard_map/all_to_all | solution.py:21
  61.1 15.8 %all-to-all-start.1 = ((bf16[8,128,256]{2,1,0:T(8,128)(2,1)}), bf16[8,128,256]{2,1,0:T(8,128)(2,1)S(1)}, u32[]{:S(2)}, u32[]{:S(2)}) async-start(bf16[8,128,256]{2,1,0:T(8,128)(2,1)} %broadcast_in_dim.14), calls=%async_computation.1 | async-start | bytes 1048576 | tf_op jit(solution)/shard_map/all_to_all | solution.py:92
  64.9 19.1 %collective-permute-start.1 = (bf16[8,128,256]{2,1,0:T(8,128)(2,1)S(1)}, bf16[8,128,256]{2,1,0:T(8,128)(2,1)S(1)}, u32[]{:S(2)}, u32[]{:S(2)}) collective-permute-start(bf16[8,128,256]{2,1,0:T(8,128)(2,1)S(1)} %all_to_all.15.near_ref), channel_id=1, source_target_pairs={{0,256},{256,0},{1,257},{257,1},{2,258},{258,2},{3,259},{259,3},{4... | collective-permute-start | bytes 1572872 | tf_op jit(solution)/shard_map/ppermute | solution.py:26
  76.9 19.6 %collective-permute-start = (bf16[8,128,256]{2,1,0:T(8,128)(2,1)S(1)}, bf16[8,128,256]{2,1,0:T(8,128)(2,1)S(1)}, u32[]{:S(2)}, u32[]{:S(2)}) collective-permute-start(bf16[8,128,256]{2,1,0:T(8,128)(2,1)S(1)} %all-to-all-done.1.near_ref), channel_id=1, source_target_pairs={{0,256},{256,0},{1,257},{257,1},{2,258},{258,2},{3,259},{259,3},{4... | collective-permute-start | bytes 1572872 | tf_op jit(solution)/shard_map/ppermute | solution.py:26
  84.0 2.2 %copy-start.1 = (bf16[16,1024,128]{2,1,0:T(8,128)(2,1)S(1)}, bf16[16,1024,128]{2,1,0:T(8,128)(2,1)}, u32[]{:S(2)}) copy-start(bf16[16,1024,128]{2,1,0:T(8,128)(2,1)} %all-gather.3.cloned.1.call-done) | copy-start | bytes 12582916
  87.4 10.4 %collective-permute-start.2 = (f32[512,256]{1,0:T(8,128)S(1)}, f32[512,256]{1,0:T(8,128)S(1)}, u32[]{:S(2)}, u32[]{:S(2)}) collective-permute-start(f32[512,256]{1,0:T(8,128)S(1)} %get-tuple-element.11), channel_id=1, source_target_pairs={{0,1},{1,0},{2,3},{3,2},{4,5},{5,4},{6,7},{7,6},{8,9},{9,8},{10,11... | collective-permute-start | bytes 1572872 | tf_op jit(solution)/shard_map/ppermute | solution.py:26
  94.6 3.8 %collective-permute-start.3 = (f32[512,256]{1,0:T(8,128)S(1)}, f32[512,256]{1,0:T(8,128)S(1)}, u32[]{:S(2)}, u32[]{:S(2)}) collective-permute-start(f32[512,256]{1,0:T(8,128)S(1)} %get-tuple-element.12), channel_id=1, source_target_pairs={{0,1},{1,0},{2,3},{3,2},{4,5},{5,4},{6,7},{7,6},{8,9},{9,8},{10,11... | collective-permute-start | bytes 1572872 | tf_op jit(solution)/shard_map/ppermute | solution.py:26
Sparse Core Ops, SparseCore 0:
  16.8 67.0 all-gather.2

commit v12 on v11

--- a/solution.py
+++ b/solution.py
@@ -69,6 +69,21 @@
     )(swapped, act_all, near, far)
 
 
+def copies(x, count):
+    def kernel(x_ref, out_ref):
+        out_ref[...] = jnp.broadcast_to(x_ref[...][None], out_ref.shape)
+
+    vmem = pl.BlockSpec(memory_space=pltpu.VMEM)
+    return pl.pallas_call(
+        kernel,
+        in_specs=[vmem],
+        out_specs=vmem,
+        out_shape=jax.ShapeDtypeStruct((count,) + x.shape, x.dtype),
+        compiler_params=pltpu.CompilerParams(vmem_limit_bytes=16 * 1024 * 1024),
+        cost_estimate=pl.CostEstimate(flops=100_000_000_000, bytes_accessed=(count + 1) * x.size * 2, transcendentals=0),
+    )(x)
+
+
 def per_device(activations, act_basis, gradients, grad_basis):
     rows, act_width = activations.shape
     xh, c = lax.axis_index("xh"), lax.axis_index("c")
@@ -78,7 +93,6 @@
     grad_pair = jnp.broadcast_to(grad_sq, (2,) + grad_sq.shape)
     own = transpose_chips(grad_sq, grad_pair)
 
-    activations, _ = lax.optimization_barrier((activations, grad_pair))
     act_blocks = activations.reshape(rows, act_width // BLOCK, BLOCK)
     act_rot = jnp.einsum("tbk,bkj->bjt", act_blocks, act_basis, preferred_element_type=jnp.float32)
     act_sq = (act_rot * act_rot).astype(jnp.bfloat16).reshape(act_width, rows)
@@ -89,7 +103,7 @@
 
     def gathered(half):
         mine = lax.dynamic_slice_in_dim(own, half * cols, cols, 1)
-        return lax.all_to_all(jnp.broadcast_to(mine, (Z,) + mine.shape), "z", 0, 0)
+        return lax.all_to_all(copies(mine, Z), "z", 0, 0)
 
     near_other, near_mine = gathered(1 - c), gathered(c)
     far_other = swap(near_other, "xh")

time: 107 us -> 110 us (1.028)
  blocking collectives: 38.5 us -> 6.01 us
  waiting for transfers between devices: 13.5 us -> 36.4 us
  starting transfers between devices: 30.6 us -> 42.7 us
  Pallas kernels: 2.5 us -> 4.16 us
    all_to_all x1 -> x0, blocking collectives: 31.9 us -> none  [gathered(): return lax.all_to_all(jnp.broadcast_to(mine, (Z,) + mine.shape), 'z', 0, 0)]
    all_to_all x1 -> x2, starting transfers between devices: 3.79 us -> 21.9 us  [gathered(): return lax.all_to_all(copies(mine, Z), 'z', 0, 0)]
    all_to_all x1 -> x2, waiting for transfers between devices: 6.51 us -> 22.8 us  [gathered(): return lax.all_to_all(copies(mine, Z), 'z', 0, 0)]
    all_gather x1, waiting for transfers between devices: 1.45 us -> 13 us  [per_device(): act_all = lax.all_gather(act_pair, 'y', axis=0)]
    all_to_all x1, waiting for transfers between devices: 4.93 us -> 0.01 us  [transpose_chips(): lax.all_to_all(sent, ('xh', 'z', 'xl', 'y'), 0, 0, axis_index_groups=groups)]
    ppermute x4, starting transfers between devices: 20.2 us -> 15.6 us  [swap(): return lax.ppermute(x, axis, [(0, 1), (1, 0)])]
    pallas_call x0 -> x2, Pallas kernels: none -> 1.66 us  [copies(): pl.pallas_call(kernel, in_specs=[vmem], out_specs=vmem, out_shape=jax.Sha...]
    all_to_all x1, starting transfers between devices: 6.61 us -> 5.2 us  [transpose_chips(): lax.all_to_all(sent, ('xh', 'z', 'xl', 'y'), 0, 0, axis_index_groups=groups)]
  transfers between devices with their start and end apart: 7 -> 8, of which waited for: 4 -> 4; matrix products, arithmetic and copies ran while one was open for 1% -> 1% of each run, Pallas kernels for 2% -> 4%
where the time goes in v12:
time: 110 us
  starting transfers between devices  42.7 us (39%)
  waiting for transfers between devices  36.4 us (33%)
  between operations  13.5 us (12%)
  blocking collectives  6.01 us (5%)
  Pallas kernels  4.16 us (4%)
  local copies, waits for them, and re-layouts  2.93 us (3%)
  matrix products  2.9 us (3%)
  other arithmetic  1.13 us (1%)
    all_to_all x2, waiting for transfers between devices, gathered(): return lax.all_to_all(copies(mine, Z), 'z', 0, 0)  22.8 us
    all_to_all x2, starting transfers between devices, gathered(): return lax.all_to_all(copies(mine, Z), 'z', 0, 0)  21.9 us
    ppermute x4, starting transfers between devices, swap(): return lax.ppermute(x, axis, [(0, 1), (1, 0)])  15.6 us
    all_gather x1, waiting for transfers between devices, per_device(): act_all = lax.all_gather(act_pair, 'y', axis=0)  13 us
    all_gather x1, blocking collectives, per_device(): act_pair = lax.all_gather(act_sq, 'xl', axis=0)  6.01 us
    all_to_all x1, starting transfers between devices, transpose_chips(): lax.all_to_all(sent, ('xh', 'z', 'xl', 'y'), 0, 0, axis_index_groups=groups)  5.2 us
    pallas_call x2, Pallas kernels, product(): pl.pallas_call(kernel, in_specs=[pl.BlockSpec(memory_space=pltpu.SMEM), v...  2.5 us
  transfers between devices with their start and end apart: 8, of which 4 were waited for; matrix products, arithmetic and copies ran while one was open for 1% of the time, Pallas kernels for 4%

profile of v12, /device:TPU:1, one launch (start us, length us, event | category | flops | bytes accessed | tf_op | source)
XLA Modules:
  0.0 109.7 jit_solution(15250447130731327087)
XLA Ops:
  6.5 0.0 copy-start
  6.5 1.4 %fusion.1 = bf16[128,512]{1,0:T(8,128)(2,1)S(1)} fusion(bf16[128,512]{1,0:T(8,128)(2,1)} %param.6, bf16[512,512]{1,0:T(8,128)(2,1)} %param.7), kind=kOutput, calls=%fused_computation.3 | convolution fusion | flops 67239936 | bytes 786432 | tf_op jit(solution)/shard_map/dot_general | solution.py:91
  8.0 0.7 broadcast_in_dim.7
  8.7 5.2 %all-to-all-start = ((bf16[2,128,512]{2,1,0:T(8,128)(2,1)}), bf16[2,128,512]{2,1,0:T(8,128)(2,1)S(1)}, u32[]{:S(2)}, u32[]{:S(2)}) async-start(bf16[2,128,512]{2,1,0:T(8,128)(2,1)} %broadcast_in_dim.7), calls=%async_computation | async-start | bytes 524288 | tf_op jit(solution)/shard_map/all_to_all | solution.py:21
  13.9 0.0 all-gather.3.cloned.1.call-start
  13.9 0.0 copy-done
  13.9 1.5 %fusion = bf16[2,512,128]{2,1,0:T(8,128)(2,1)S(1)} fusion(bf16[2,512,512]{2,1,0:T(8,128)(2,1)S(1)} %copy-done, bf16[16,2,8,512]{3,2,1,0:T(8,128)(2,1)} %bitcast.23), kind=kOutput, calls=%fused_computation.1 | convolution fusion | flops 134479872 | bytes 1572864 | tf_op jit(solution)/shard_map/tbk,bkj->bjt/dot_general | solution.py:97
  15.4 6.0 %all_gather.9 = bf16[2,1024,128]{2,1,0:T(8,128)(2,1)} all-gather(bf16[1,1024,128]{2,1,0:T(8,128)(2,1)S(1)} %bitcast.22), channel_id=1, replica_groups=mesh['xh'=2,'z'=8,'xl'=2,'y'=8,'c'=2] {'xl'}, dimensions={0}, use_global_device_ids=true | all-gather | bytes 786432 | tf_op jit(solution)/shard_map/all_gather | solution.py:99
  21.4 0.0 all-gather.3.cloned.1.call-update
  21.4 0.0 all-to-all-done
  21.5 0.8 shard_map.48
  22.3 18.4 %all-to-all-start.2 = ((bf16[8,128,256]{2,1,0:T(8,128)(2,1)}), bf16[8,128,256]{2,1,0:T(8,128)(2,1)S(1)}, u32[]{:S(2)}, u32[]{:S(2)}) async-start(bf16[8,128,256]{2,1,0:T(8,128)(2,1)} %shard_map.48), calls=%async_computation.2 | async-start | bytes 1048576 | tf_op jit(solution)/shard_map/all_to_all | solution.py:106
  40.7 0.8 shard_map.46
  41.6 14.2 %all-to-all-done.2.near_ref = bf16[8,128,256]{2,1,0:T(8,128)(2,1)S(1)} async-done(((bf16[8,128,256]{2,1,0:T(8,128)(2,1)}), bf16[8,128,256]{2,1,0:T(8,128)(2,1)S(1)}, u32[]{:S(2)}, u32[]{:S(2)}) %all-to-all-start.2) | async-done | bytes 524320 | tf_op jit(solution)/shard_map/all_to_all | solution.py:106
  55.8 3.5 %all-to-all-start.1 = ((bf16[8,128,256]{2,1,0:T(8,128)(2,1)}), bf16[8,128,256]{2,1,0:T(8,128)(2,1)S(1)}, u32[]{:S(2)}, u32[]{:S(2)}) async-start(bf16[8,128,256]{2,1,0:T(8,128)(2,1)} %shard_map.46), calls=%async_computation.1 | async-start | bytes 1048576 | tf_op jit(solution)/shard_map/all_to_all | solution.py:106
  59.3 5.5 %collective-permute-start.1 = (bf16[8,128,256]{2,1,0:T(8,128)(2,1)S(1)}, bf16[8,128,256]{2,1,0:T(8,128)(2,1)S(1)}, u32[]{:S(2)}, u32[]{:S(2)}) collective-permute-start(bf16[8,128,256]{2,1,0:T(8,128)(2,1)S(1)} %all-to-all-done.2.near_ref), channel_id=1, source_target_pairs={{0,256},{256,0},{1,257},{257,1},{2,258},{258,2},{3,259},{259,3},{4... | collective-permute-start | bytes 1572872 | tf_op jit(solution)/shard_map/ppermute | solution.py:26
  64.9 8.5 %all-to-all-done.1.near_ref = bf16[8,128,256]{2,1,0:T(8,128)(2,1)S(1)} async-done(((bf16[8,128,256]{2,1,0:T(8,128)(2,1)}), bf16[8,128,256]{2,1,0:T(8,128)(2,1)S(1)}, u32[]{:S(2)}, u32[]{:S(2)}) %all-to-all-start.1) | async-done | bytes 524320 | tf_op jit(solution)/shard_map/all_to_all | solution.py:106
  73.4 5.5 %collective-permute-start = (bf16[8,128,256]{2,1,0:T(8,128)(2,1)S(1)}, bf16[8,128,256]{2,1,0:T(8,128)(2,1)S(1)}, u32[]{:S(2)}, u32[]{:S(2)}) collective-permute-start(bf16[8,128,256]{2,1,0:T(8,128)(2,1)S(1)} %all-to-all-done.1.near_ref), channel_id=1, source_target_pairs={{0,256},{256,0},{1,257},{257,1},{2,258},{258,2},{3,259},{259,3},{4... | collective-permute-start | bytes 1572872 | tf_op jit(solution)/shard_map/ppermute | solution.py:26
  78.9 13.0 %all-gather.3.cloned.1.call-done = bf16[16,1024,128]{2,1,0:T(8,128)(2,1)} async-done(((bf16[2,1024,128]{2,1,0:T(8,128)(2,1)}), bf16[16,1024,128]{2,1,0:T(8,128)(2,1)}) %all-gather.3.cloned.1.call-update) | async-done | bytes 4194320 | tf_op jit(solution)/shard_map/all_gather | solution.py:100
  91.9 0.0 collective-permute-done.1.far_ref
  91.9 0.0 copy-start.1
  91.9 2.2 %copy-done.1 = bf16[16,1024,128]{2,1,0:T(8,128)(2,1)S(1)} copy-done((bf16[16,1024,128]{2,1,0:T(8,128)(2,1)S(1)}, bf16[16,1024,128]{2,1,0:T(8,128)(2,1)}, u32[]{:S(2)}) %copy-start.1) | copy-done | bytes 4194328
  94.1 1.2 %shard_map.49 = (f32[512,256]{1,0:T(8,128)S(1)}, f32[512,256]{1,0:T(8,128)S(1)}) custom-call(s32[1]{0:T(128)} %bitcast.swapped_ref, bf16[8,2,1024,128]{3,2,1,0:T(8,128)(2,1)S(1)} %bitcast.20, bf16[8,128,256]{2,1,0:T(8,128)(2,1)S(1)} %all-to-all-done.2.near_ref, bf16[8,128,256]{2,1,0:T(8,128)(2,1)S(1)} %collective-permute-done.1.far_ref), custom_call_target="tpu_custom_call" | custom-call | flops 1073741824 | bytes 6291456 | tf_op jit(solution)/shard_map/pallas_call | solution.py:58
  95.4 2.6 %collective-permute-start.2 = (f32[512,256]{1,0:T(8,128)S(1)}, f32[512,256]{1,0:T(8,128)S(1)}, u32[]{:S(2)}, u32[]{:S(2)}) collective-permute-start(f32[512,256]{1,0:T(8,128)S(1)} %get-tuple-element.9), channel_id=1, source_target_pairs={{0,1},{1,0},{2,3},{3,2},{4,5},{5,4},{6,7},{7,6},{8,9},{9,8},{10,11... | collective-permute-start | bytes 1572872 | tf_op jit(solution)/shard_map/ppermute | solution.py:26
  98.0 1.9 %collective-permute-start.3 = (f32[512,256]{1,0:T(8,128)S(1)}, f32[512,256]{1,0:T(8,128)S(1)}, u32[]{:S(2)}, u32[]{:S(2)}) collective-permute-start(f32[512,256]{1,0:T(8,128)S(1)} %get-tuple-element.10), channel_id=1, source_target_pairs={{0,1},{1,0},{2,3},{3,2},{4,5},{5,4},{6,7},{7,6},{8,9},{9,8},{10,11... | collective-permute-start | bytes 1572872 | tf_op jit(solution)/shard_map/ppermute | solution.py:26
  99.9 0.0 collective-permute-done.far_ref
  99.9 1.3 %shard_map.47 = f32[1024,256]{1,0:T(8,128)S(1)} custom-call(s32[1]{0:T(128)} %bitcast.swapped_ref, bf16[8,2,1024,128]{3,2,1,0:T(8,128)(2,1)S(1)} %bitcast.21, bf16[8,128,256]{2,1,0:T(8,128)(2,1)S(1)} %all-to-all-done.1.near_ref, bf16[8,128,256]{2,1,0:T(8,128)(2,1)S(1)} %collective-permute-done.far_ref), custom_call_target="tpu_custom_call" | custom-call | flops 1073741824 | bytes 6291456 | tf_op jit(solution)/shard_map/pallas_call | solution.py:58
  101.2 0.0 collective-permute-done.2
  101.2 0.6 collective-permute-done.3
  101.8 1.1 %fusion.2 = f32[1024,256]{1,0:T(8,128)} fusion(f32[1024,256]{1,0:T(8,128)S(1)} %shard_map.47, f32[512,256]{1,0:T(8,128)S(1)} %collective-permute-done.3, f32[512,256]{1,0:T(8,128)S(1)} %collective-permute-done.2), kind=kLoop, calls=%fused_computation.5 | loop fusion | flops 786432 | bytes 3145728 | tf_op jit(solution)/shard_map/div | solution.py:116
  (2 shorter events, 0.0 us)
Async XLA Ops:
  6.5 7.4 %copy-start = (bf16[2,512,512]{2,1,0:T(8,128)(2,1)S(1)}, bf16[2,512,512]{2,1,0:T(8,128)(2,1)}, u32[]{:S(2)}) copy-start(bf16[2,512,512]{2,1,0:T(8,128)(2,1)} %param.5) | copy-start | bytes 3145732
  8.7 12.7 %all-to-all-start = ((bf16[2,128,512]{2,1,0:T(8,128)(2,1)}), bf16[2,128,512]{2,1,0:T(8,128)(2,1)S(1)}, u32[]{:S(2)}, u32[]{:S(2)}) async-start(bf16[2,128,512]{2,1,0:T(8,128)(2,1)} %broadcast_in_dim.7), calls=%async_computation | async-start | bytes 524288 | tf_op jit(solution)/shard_map/all_to_all | solution.py:21
  13.9 78.0 %all-gather.3.cloned.1.call-start = ((), (), s32[]{:S(2)}) async-start(), calls=%async_computation.3 | async-start | bytes 4718592 | tf_op jit(solution)/shard_map/all_gather | solution.py:100
  22.3 33.5 %all-to-all-start.2 = ((bf16[8,128,256]{2,1,0:T(8,128)(2,1)}), bf16[8,128,256]{2,1,0:T(8,128)(2,1)S(1)}, u32[]{:S(2)}, u32[]{:S(2)}) async-start(bf16[8,128,256]{2,1,0:T(8,128)(2,1)} %shard_map.48), calls=%async_computation.2 | async-start | bytes 1048576 | tf_op jit(solution)/shard_map/all_to_all | solution.py:106
  55.8 17.6 %all-to-all-start.1 = ((bf16[8,128,256]{2,1,0:T(8,128)(2,1)}), bf16[8,128,256]{2,1,0:T(8,128)(2,1)S(1)}, u32[]{:S(2)}, u32[]{:S(2)}) async-start(bf16[8,128,256]{2,1,0:T(8,128)(2,1)} %shard_map.46), calls=%async_computation.1 | async-start | bytes 1048576 | tf_op jit(solution)/shard_map/all_to_all | solution.py:106
  59.3 32.6 %collective-permute-start.1 = (bf16[8,128,256]{2,1,0:T(8,128)(2,1)S(1)}, bf16[8,128,256]{2,1,0:T(8,128)(2,1)S(1)}, u32[]{:S(2)}, u32[]{:S(2)}) collective-permute-start(bf16[8,128,256]{2,1,0:T(8,128)(2,1)S(1)} %all-to-all-done.2.near_ref), channel_id=1, source_target_pairs={{0,256},{256,0},{1,257},{257,1},{2,258},{258,2},{3,259},{259,3},{4... | collective-permute-start | bytes 1572872 | tf_op jit(solution)/shard_map/ppermute | solution.py:26
  73.4 26.5 %collective-permute-start = (bf16[8,128,256]{2,1,0:T(8,128)(2,1)S(1)}, bf16[8,128,256]{2,1,0:T(8,128)(2,1)S(1)}, u32[]{:S(2)}, u32[]{:S(2)}) collective-permute-start(bf16[8,128,256]{2,1,0:T(8,128)(2,1)S(1)} %all-to-all-done.1.near_ref), channel_id=1, source_target_pairs={{0,256},{256,0},{1,257},{257,1},{2,258},{258,2},{3,259},{259,3},{4... | collective-permute-start | bytes 1572872 | tf_op jit(solution)/shard_map/ppermute | solution.py:26
  91.9 2.2 %copy-start.1 = (bf16[16,1024,128]{2,1,0:T(8,128)(2,1)S(1)}, bf16[16,1024,128]{2,1,0:T(8,128)(2,1)}, u32[]{:S(2)}) copy-start(bf16[16,1024,128]{2,1,0:T(8,128)(2,1)} %all-gather.3.cloned.1.call-done) | copy-start | bytes 12582916
  95.4 5.8 %collective-permute-start.2 = (f32[512,256]{1,0:T(8,128)S(1)}, f32[512,256]{1,0:T(8,128)S(1)}, u32[]{:S(2)}, u32[]{:S(2)}) collective-permute-start(f32[512,256]{1,0:T(8,128)S(1)} %get-tuple-element.9), channel_id=1, source_target_pairs={{0,1},{1,0},{2,3},{3,2},{4,5},{5,4},{6,7},{7,6},{8,9},{9,8},{10,11... | collective-permute-start | bytes 1572872 | tf_op jit(solution)/shard_map/ppermute | solution.py:26
  98.0 3.8 %collective-permute-start.3 = (f32[512,256]{1,0:T(8,128)S(1)}, f32[512,256]{1,0:T(8,128)S(1)}, u32[]{:S(2)}, u32[]{:S(2)}) collective-permute-start(f32[512,256]{1,0:T(8,128)S(1)} %get-tuple-element.10), channel_id=1, source_target_pairs={{0,1},{1,0},{2,3},{3,2},{4,5},{5,4},{6,7},{7,6},{8,9},{9,8},{10,11... | collective-permute-start | bytes 1572872 | tf_op jit(solution)/shard_map/ppermute | solution.py:26
Sparse Core Ops, SparseCore 0:
  21.5 70.3 all-gather.2

commit v13 on v12

--- a/solution.py
+++ b/solution.py
@@ -80,23 +80,25 @@
         out_specs=vmem,
         out_shape=jax.ShapeDtypeStruct((count,) + x.shape, x.dtype),
         compiler_params=pltpu.CompilerParams(vmem_limit_bytes=16 * 1024 * 1024),
-        cost_estimate=pl.CostEstimate(flops=100_000_000_000, bytes_accessed=(count + 1) * x.size * 2, transcendentals=0),
+        cost_estimate=pl.CostEstimate(flops=50_000_000_000, bytes_accessed=(count + 1) * x.size * 2, transcendentals=0),
     )(x)
 
 
 def per_device(activations, act_basis, gradients, grad_basis):
     rows, act_width = activations.shape
-    xh, c = lax.axis_index("xh"), lax.axis_index("c")
+    xh, xl, c = (lax.axis_index(a) for a in ("xh", "xl", "c"))
 
+    act_blocks = activations.reshape(rows, act_width // BLOCK, BLOCK)
+    act_rot = jnp.einsum("tbk,bkj->bjt", act_blocks, act_basis, preferred_element_type=jnp.float32)
+    act_sq = (act_rot * act_rot).astype(jnp.bfloat16).reshape(act_width, rows)
+
+    gradients, _ = lax.optimization_barrier((gradients, act_sq))
     grad_rot = jnp.dot(gradients, grad_basis, preferred_element_type=jnp.float32)
     grad_sq = (grad_rot * grad_rot).astype(jnp.bfloat16)
     grad_pair = jnp.broadcast_to(grad_sq, (2,) + grad_sq.shape)
     own = transpose_chips(grad_sq, grad_pair)
 
-    act_blocks = activations.reshape(rows, act_width // BLOCK, BLOCK)
-    act_rot = jnp.einsum("tbk,bkj->bjt", act_blocks, act_basis, preferred_element_type=jnp.float32)
-    act_sq = (act_rot * act_rot).astype(jnp.bfloat16).reshape(act_width, rows)
-    act_pair = lax.all_gather(act_sq, "xl", axis=0)
+    act_pair = jnp.stack([act_sq, swap(act_sq, "xl")])
     act_all = lax.all_gather(act_pair, "y", axis=0)
 
     cols = own.shape[1] // 2
@@ -108,7 +110,7 @@
     near_other, near_mine = gathered(1 - c), gathered(c)
     far_other = swap(near_other, "xh")
     far_mine = swap(near_mine, "xh")
-    swapped = xh[None]
+    swapped = (xh ^ xl)[None]
     act_all, _ = lax.optimization_barrier((act_all, near_mine))
     other = product(swapped, act_all, near_other, far_other, 2)
     got = [swap(part, "c") for part in other]

time: 110 us -> 109 us (level)
  blocking collectives: 6.01 us -> 0 us
  starting transfers between devices: 42.7 us -> 45.3 us
  local copies, waits for them, and re-layouts: 2.93 us -> 4.16 us
    all_gather x1 -> x0, blocking collectives: 6.01 us -> none  [per_device(): act_pair = lax.all_gather(act_sq, 'xl', axis=0)]
    all_gather x1, waiting for transfers between devices: 13 us -> 7.15 us  [per_device(): act_all = lax.all_gather(act_pair, 'y', axis=0)]
    all_to_all x1, waiting for transfers between devices: 0.01 us -> 4.05 us  [transpose_chips(): lax.all_to_all(sent, ('xh', 'z', 'xl', 'y'), 0, 0, axis_index_groups=groups)]
    ppermute x4 -> x5, starting transfers between devices: 15.6 us -> 19 us  [swap(): return lax.ppermute(x, axis, [(0, 1), (1, 0)])]
    all_to_all x2, waiting for transfers between devices: 22.8 us -> 24.7 us  [gathered(): return lax.all_to_all(copies(mine, Z), 'z', 0, 0)]
    unnamed x4, local copies, waits for them, and re-layouts: 2.19 us -> 3.41 us
  transfers between devices with their start and end apart: 8 -> 9, of which waited for: 4 -> 5; matrix products, arithmetic and copies ran while one was open for 1% -> 3% of each run, Pallas kernels for 4% -> 4%
where the time goes in v13:
time: 109 us; the launch traced here: 108 us
  starting transfers between devices  45.3 us (42%)
  waiting for transfers between devices  36.6 us (34%)
  between operations  13.5 us (12%)
  Pallas kernels  4.17 us (4%)
  local copies, waits for them, and re-layouts  4.16 us (4%)
  matrix products  2.82 us (3%)
  other arithmetic  1.97 us (2%)
    all_to_all x2, waiting for transfers between devices, gathered(): return lax.all_to_all(copies(mine, Z), 'z', 0, 0)  24.7 us
    all_to_all x2, starting transfers between devices, gathered(): return lax.all_to_all(copies(mine, Z), 'z', 0, 0)  21.9 us
    ppermute x5, starting transfers between devices, swap(): return lax.ppermute(x, axis, [(0, 1), (1, 0)])  19 us
    all_gather x1, waiting for transfers between devices, per_device(): act_all = lax.all_gather(act_pair, 'y', axis=0)  7.15 us
    all_to_all x1, starting transfers between devices, transpose_chips(): lax.all_to_all(sent, ('xh', 'z', 'xl', 'y'), 0, 0, axis_index_groups=groups)  4.37 us
    all_to_all x1, waiting for transfers between devices, transpose_chips(): lax.all_to_all(sent, ('xh', 'z', 'xl', 'y'), 0, 0, axis_index_groups=groups)  4.05 us
    unnamed x4, local copies, waits for them, and re-layouts  3.41 us
    pallas_call x2, Pallas kernels, product(): pl.pallas_call(kernel, in_specs=[pl.BlockSpec(memory_space=pltpu.SMEM), v...  2.5 us
  transfers between devices with their start and end apart: 9, of which 5 were waited for; matrix products, arithmetic and copies ran while one was open for 3% of the time, Pallas kernels for 4%

profile of v13, /device:TPU:1, one launch (start us, length us, event | category | flops | bytes accessed | tf_op | source)
XLA Modules:
  0.0 108.5 jit_solution(13469729308320906109)
XLA Ops:
  6.5 0.0 copy-start
  6.5 1.2 %copy-done = bf16[2,512,512]{2,1,0:T(8,128)(2,1)S(1)} copy-done((bf16[2,512,512]{2,1,0:T(8,128)(2,1)S(1)}, bf16[2,512,512]{2,1,0:T(8,128)(2,1)}, u32[]{:S(2)}) %copy-start) | copy-done | bytes 1048600
  7.8 1.5 %fusion = bf16[2,512,128]{2,1,0:T(8,128)(2,1)S(1)} fusion(bf16[2,512,512]{2,1,0:T(8,128)(2,1)S(1)} %copy-done, bf16[16,2,8,512]{3,2,1,0:T(8,128)(2,1)} %bitcast.26), kind=kOutput, calls=%fused_computation.1 | convolution fusion | flops 134479872 | bytes 1572864 | tf_op jit(solution)/shard_map/tbk,bkj->bjt/dot_general | solution.py:92
  9.2 3.9 %collective-permute-start = (bf16[1024,128]{1,0:T(8,128)(2,1)S(1)}, bf16[1024,128]{1,0:T(8,128)(2,1)S(1)}, u32[]{:S(2)}, u32[]{:S(2)}) collective-permute-start(bf16[1024,128]{1,0:T(8,128)(2,1)S(1)} %bitcast.24), channel_id=1, source_target_pairs={{0,16},{16,0},{1,17},{17,1},{2,18},{18,2},{3,19},{19,3},{4,20},{20... | collective-permute-start | bytes 786440 | tf_op jit(solution)/shard_map/ppermute | solution.py:26
  13.2 1.3 %fusion.1 = bf16[128,512]{1,0:T(8,128)(2,1)S(1)} fusion(bf16[128,512]{1,0:T(8,128)(2,1)} %param.6, bf16[512,512]{1,0:T(8,128)(2,1)} %param.7), kind=kOutput, calls=%fused_computation.3 | convolution fusion | flops 67239936 | bytes 786432 | tf_op jit(solution)/shard_map/dot_general | solution.py:96
  14.5 0.7 broadcast_in_dim.7
  15.3 4.4 %all-to-all-start = ((bf16[2,128,512]{2,1,0:T(8,128)(2,1)}), bf16[2,128,512]{2,1,0:T(8,128)(2,1)S(1)}, u32[]{:S(2)}, u32[]{:S(2)}) async-start(bf16[2,128,512]{2,1,0:T(8,128)(2,1)} %broadcast_in_dim.7), calls=%async_computation | async-start | bytes 524288 | tf_op jit(solution)/shard_map/all_to_all | solution.py:21
  19.6 0.0 all-gather.3.cloned.1.call-start
  19.6 0.0 collective-permute-done
  19.7 0.8 pad_maximum_fusion
  20.5 0.0 all-gather.3.cloned.1.call-update
  20.5 4.1 %all-to-all-done = bf16[2,128,512]{2,1,0:T(8,128)(2,1)S(1)} async-done(((bf16[2,128,512]{2,1,0:T(8,128)(2,1)}), bf16[2,128,512]{2,1,0:T(8,128)(2,1)S(1)}, u32[]{:S(2)}, u32[]{:S(2)}) %all-to-all-start) | async-done | bytes 262176 | tf_op jit(solution)/shard_map/all_to_all | solution.py:21
  24.6 0.8 shard_map.48
  25.5 18.4 %all-to-all-start.2 = ((bf16[8,128,256]{2,1,0:T(8,128)(2,1)}), bf16[8,128,256]{2,1,0:T(8,128)(2,1)S(1)}, u32[]{:S(2)}, u32[]{:S(2)}) async-start(bf16[8,128,256]{2,1,0:T(8,128)(2,1)} %shard_map.48), calls=%async_computation.2 | async-start | bytes 1048576 | tf_op jit(solution)/shard_map/all_to_all | solution.py:108
  43.9 0.8 shard_map.46
  44.7 15.1 %all-to-all-done.2.near_ref = bf16[8,128,256]{2,1,0:T(8,128)(2,1)S(1)} async-done(((bf16[8,128,256]{2,1,0:T(8,128)(2,1)}), bf16[8,128,256]{2,1,0:T(8,128)(2,1)S(1)}, u32[]{:S(2)}, u32[]{:S(2)}) %all-to-all-start.2) | async-done | bytes 524320 | tf_op jit(solution)/shard_map/all_to_all | solution.py:108
  59.9 3.5 %all-to-all-start.1 = ((bf16[8,128,256]{2,1,0:T(8,128)(2,1)}), bf16[8,128,256]{2,1,0:T(8,128)(2,1)S(1)}, u32[]{:S(2)}, u32[]{:S(2)}) async-start(bf16[8,128,256]{2,1,0:T(8,128)(2,1)} %shard_map.46), calls=%async_computation.1 | async-start | bytes 1048576 | tf_op jit(solution)/shard_map/all_to_all | solution.py:108
  63.4 5.3 %collective-permute-start.2 = (bf16[8,128,256]{2,1,0:T(8,128)(2,1)S(1)}, bf16[8,128,256]{2,1,0:T(8,128)(2,1)S(1)}, u32[]{:S(2)}, u32[]{:S(2)}) collective-permute-start(bf16[8,128,256]{2,1,0:T(8,128)(2,1)S(1)} %all-to-all-done.2.near_ref), channel_id=1, source_target_pairs={{0,256},{256,0},{1,257},{257,1},{2,258},{258,2},{3,259},{259,3},{4... | collective-permute-start | bytes 1572872 | tf_op jit(solution)/shard_map/ppermute | solution.py:26
  68.6 9.6 %all-to-all-done.1.near_ref = bf16[8,128,256]{2,1,0:T(8,128)(2,1)S(1)} async-done(((bf16[8,128,256]{2,1,0:T(8,128)(2,1)}), bf16[8,128,256]{2,1,0:T(8,128)(2,1)S(1)}, u32[]{:S(2)}, u32[]{:S(2)}) %all-to-all-start.1) | async-done | bytes 524320 | tf_op jit(solution)/shard_map/all_to_all | solution.py:108
  78.3 5.2 %collective-permute-start.1 = (bf16[8,128,256]{2,1,0:T(8,128)(2,1)S(1)}, bf16[8,128,256]{2,1,0:T(8,128)(2,1)S(1)}, u32[]{:S(2)}, u32[]{:S(2)}) collective-permute-start(bf16[8,128,256]{2,1,0:T(8,128)(2,1)S(1)} %all-to-all-done.1.near_ref), channel_id=1, source_target_pairs={{0,256},{256,0},{1,257},{257,1},{2,258},{258,2},{3,259},{259,3},{4... | collective-permute-start | bytes 1572872 | tf_op jit(solution)/shard_map/ppermute | solution.py:26
  83.5 7.2 %all-gather.3.cloned.1.call-done = bf16[16,1024,128]{2,1,0:T(8,128)(2,1)} async-done(((bf16[2,1024,128]{2,1,0:T(8,128)(2,1)}), bf16[16,1024,128]{2,1,0:T(8,128)(2,1)}) %all-gather.3.cloned.1.call-update) | async-done | bytes 4194320 | tf_op jit(solution)/shard_map/all_gather | solution.py:102
  90.7 0.0 collective-permute-done.2.far_ref
  90.7 0.0 copy-start.1
  90.7 2.2 %copy-done.1 = bf16[16,1024,128]{2,1,0:T(8,128)(2,1)S(1)} copy-done((bf16[16,1024,128]{2,1,0:T(8,128)(2,1)S(1)}, bf16[16,1024,128]{2,1,0:T(8,128)(2,1)}, u32[]{:S(2)}) %copy-start.1) | copy-done | bytes 4194328
  92.9 1.2 %shard_map.49 = (f32[512,256]{1,0:T(8,128)S(1)}, f32[512,256]{1,0:T(8,128)S(1)}) custom-call(s32[1]{0:T(128)} %bitcast.swapped_ref, bf16[8,2,1024,128]{3,2,1,0:T(8,128)(2,1)S(1)} %bitcast.22, bf16[8,128,256]{2,1,0:T(8,128)(2,1)S(1)} %all-to-all-done.2.near_ref, bf16[8,128,256]{2,1,0:T(8,128)(2,1)S(1)} %collective-permute-done.2.far_ref), custom_call_target="tpu_custom_call" | custom-call | flops 1073741824 | bytes 6291456 | tf_op jit(solution)/shard_map/pallas_call | solution.py:58
  94.1 2.6 %collective-permute-start.3 = (f32[512,256]{1,0:T(8,128)S(1)}, f32[512,256]{1,0:T(8,128)S(1)}, u32[]{:S(2)}, u32[]{:S(2)}) collective-permute-start(f32[512,256]{1,0:T(8,128)S(1)} %get-tuple-element.11), channel_id=1, source_target_pairs={{0,1},{1,0},{2,3},{3,2},{4,5},{5,4},{6,7},{7,6},{8,9},{9,8},{10,11... | collective-permute-start | bytes 1572872 | tf_op jit(solution)/shard_map/ppermute | solution.py:26
  96.7 1.9 %collective-permute-start.4 = (f32[512,256]{1,0:T(8,128)S(1)}, f32[512,256]{1,0:T(8,128)S(1)}, u32[]{:S(2)}, u32[]{:S(2)}) collective-permute-start(f32[512,256]{1,0:T(8,128)S(1)} %get-tuple-element.12), channel_id=1, source_target_pairs={{0,1},{1,0},{2,3},{3,2},{4,5},{5,4},{6,7},{7,6},{8,9},{9,8},{10,11... | collective-permute-start | bytes 1572872 | tf_op jit(solution)/shard_map/ppermute | solution.py:26
  98.6 0.0 collective-permute-done.1.far_ref
  98.6 1.3 %shard_map.47 = f32[1024,256]{1,0:T(8,128)S(1)} custom-call(s32[1]{0:T(128)} %bitcast.swapped_ref, bf16[8,2,1024,128]{3,2,1,0:T(8,128)(2,1)S(1)} %bitcast.23, bf16[8,128,256]{2,1,0:T(8,128)(2,1)S(1)} %all-to-all-done.1.near_ref, bf16[8,128,256]{2,1,0:T(8,128)(2,1)S(1)} %collective-permute-done.1.far_ref), custom_call_target="tpu_custom_call" | custom-call | flops 1073741824 | bytes 6291456 | tf_op jit(solution)/shard_map/pallas_call | solution.py:58
  99.9 0.0 collective-permute-done.3
  99.9 0.6 collective-permute-done.4
  100.5 1.1 %fusion.2 = f32[1024,256]{1,0:T(8,128)} fusion(f32[1024,256]{1,0:T(8,128)S(1)} %shard_map.47, f32[512,256]{1,0:T(8,128)S(1)} %collective-permute-done.4, f32[512,256]{1,0:T(8,128)S(1)} %collective-permute-done.3), kind=kLoop, calls=%fused_computation.5 | loop fusion | flops 786432 | bytes 3145728 | tf_op jit(solution)/shard_map/div | solution.py:118
  (2 shorter events, 0.0 us)
Async XLA Ops:
  6.5 1.2 %copy-start = (bf16[2,512,512]{2,1,0:T(8,128)(2,1)S(1)}, bf16[2,512,512]{2,1,0:T(8,128)(2,1)}, u32[]{:S(2)}) copy-start(bf16[2,512,512]{2,1,0:T(8,128)(2,1)} %param.5) | copy-start | bytes 3145732
  9.2 10.4 %collective-permute-start = (bf16[1024,128]{1,0:T(8,128)(2,1)S(1)}, bf16[1024,128]{1,0:T(8,128)(2,1)S(1)}, u32[]{:S(2)}, u32[]{:S(2)}) collective-permute-start(bf16[1024,128]{1,0:T(8,128)(2,1)S(1)} %bitcast.24), channel_id=1, source_target_pairs={{0,16},{16,0},{1,17},{17,1},{2,18},{18,2},{3,19},{19,3},{4,20},{20... | collective-permute-start | bytes 786440 | tf_op jit(solution)/shard_map/ppermute | solution.py:26
  15.3 9.3 %all-to-all-start = ((bf16[2,128,512]{2,1,0:T(8,128)(2,1)}), bf16[2,128,512]{2,1,0:T(8,128)(2,1)S(1)}, u32[]{:S(2)}, u32[]{:S(2)}) async-start(bf16[2,128,512]{2,1,0:T(8,128)(2,1)} %broadcast_in_dim.7), calls=%async_computation | async-start | bytes 524288 | tf_op jit(solution)/shard_map/all_to_all | solution.py:21
  19.6 71.0 %all-gather.3.cloned.1.call-start = ((), (), s32[]{:S(2)}) async-start(), calls=%async_computation.3 | async-start | bytes 4718592 | tf_op jit(solution)/shard_map/all_gather | solution.py:102
  25.5 34.4 %all-to-all-start.2 = ((bf16[8,128,256]{2,1,0:T(8,128)(2,1)}), bf16[8,128,256]{2,1,0:T(8,128)(2,1)S(1)}, u32[]{:S(2)}, u32[]{:S(2)}) async-start(bf16[8,128,256]{2,1,0:T(8,128)(2,1)} %shard_map.48), calls=%async_computation.2 | async-start | bytes 1048576 | tf_op jit(solution)/shard_map/all_to_all | solution.py:108
  59.9 18.4 %all-to-all-start.1 = ((bf16[8,128,256]{2,1,0:T(8,128)(2,1)}), bf16[8,128,256]{2,1,0:T(8,128)(2,1)S(1)}, u32[]{:S(2)}, u32[]{:S(2)}) async-start(bf16[8,128,256]{2,1,0:T(8,128)(2,1)} %shard_map.46), calls=%async_computation.1 | async-start | bytes 1048576 | tf_op jit(solution)/shard_map/all_to_all | solution.py:108
  63.4 27.3 %collective-permute-start.2 = (bf16[8,128,256]{2,1,0:T(8,128)(2,1)S(1)}, bf16[8,128,256]{2,1,0:T(8,128)(2,1)S(1)}, u32[]{:S(2)}, u32[]{:S(2)}) collective-permute-start(bf16[8,128,256]{2,1,0:T(8,128)(2,1)S(1)} %all-to-all-done.2.near_ref), channel_id=1, source_target_pairs={{0,256},{256,0},{1,257},{257,1},{2,258},{258,2},{3,259},{259,3},{4... | collective-permute-start | bytes 1572872 | tf_op jit(solution)/shard_map/ppermute | solution.py:26
  78.3 20.4 %collective-permute-start.1 = (bf16[8,128,256]{2,1,0:T(8,128)(2,1)S(1)}, bf16[8,128,256]{2,1,0:T(8,128)(2,1)S(1)}, u32[]{:S(2)}, u32[]{:S(2)}) collective-permute-start(bf16[8,128,256]{2,1,0:T(8,128)(2,1)S(1)} %all-to-all-done.1.near_ref), channel_id=1, source_target_pairs={{0,256},{256,0},{1,257},{257,1},{2,258},{258,2},{3,259},{259,3},{4... | collective-permute-start | bytes 1572872 | tf_op jit(solution)/shard_map/ppermute | solution.py:26
  90.7 2.2 %copy-start.1 = (bf16[16,1024,128]{2,1,0:T(8,128)(2,1)S(1)}, bf16[16,1024,128]{2,1,0:T(8,128)(2,1)}, u32[]{:S(2)}) copy-start(bf16[16,1024,128]{2,1,0:T(8,128)(2,1)} %all-gather.3.cloned.1.call-done) | copy-start | bytes 12582916
  94.1 5.8 %collective-permute-start.3 = (f32[512,256]{1,0:T(8,128)S(1)}, f32[512,256]{1,0:T(8,128)S(1)}, u32[]{:S(2)}, u32[]{:S(2)}) collective-permute-start(f32[512,256]{1,0:T(8,128)S(1)} %get-tuple-element.11), channel_id=1, source_target_pairs={{0,1},{1,0},{2,3},{3,2},{4,5},{5,4},{6,7},{7,6},{8,9},{9,8},{10,11... | collective-permute-start | bytes 1572872 | tf_op jit(solution)/shard_map/ppermute | solution.py:26
  96.7 3.8 %collective-permute-start.4 = (f32[512,256]{1,0:T(8,128)S(1)}, f32[512,256]{1,0:T(8,128)S(1)}, u32[]{:S(2)}, u32[]{:S(2)}) collective-permute-start(f32[512,256]{1,0:T(8,128)S(1)} %get-tuple-element.12), channel_id=1, source_target_pairs={{0,1},{1,0},{2,3},{3,2},{4,5},{5,4},{6,7},{7,6},{8,9},{9,8},{10,11... | collective-permute-start | bytes 1572872 | tf_op jit(solution)/shard_map/ppermute | solution.py:26
Sparse Core Ops, SparseCore 0:
  22.5 68.0 all-gather.2

commit v14 on v11

--- a/solution.py
+++ b/solution.py
@@ -71,18 +71,20 @@
 
 def per_device(activations, act_basis, gradients, grad_basis):
     rows, act_width = activations.shape
-    xh, c = lax.axis_index("xh"), lax.axis_index("c")
+    xh, xl, c = (lax.axis_index(a) for a in ("xh", "xl", "c"))
 
     grad_rot = jnp.dot(gradients, grad_basis, preferred_element_type=jnp.float32)
     grad_sq = (grad_rot * grad_rot).astype(jnp.bfloat16)
     grad_pair = jnp.broadcast_to(grad_sq, (2,) + grad_sq.shape)
     own = transpose_chips(grad_sq, grad_pair)
 
-    activations, _ = lax.optimization_barrier((activations, grad_pair))
-    act_blocks = activations.reshape(rows, act_width // BLOCK, BLOCK)
-    act_rot = jnp.einsum("tbk,bkj->bjt", act_blocks, act_basis, preferred_element_type=jnp.float32)
-    act_sq = (act_rot * act_rot).astype(jnp.bfloat16).reshape(act_width, rows)
-    act_pair = lax.all_gather(act_sq, "xl", axis=0)
+    def rotated(act):
+        blocks = act.reshape(rows, act_width // BLOCK, BLOCK)
+        rot = jnp.einsum("tbk,bkj->bjt", blocks, act_basis, preferred_element_type=jnp.float32)
+        return (rot * rot).astype(jnp.bfloat16).reshape(act_width, rows)
+
+    others, _ = lax.optimization_barrier((swap(activations, "xl"), grad_pair))
+    act_pair = jnp.stack([rotated(activations), rotated(others)])
     act_all = lax.all_gather(act_pair, "y", axis=0)
 
     cols = own.shape[1] // 2
@@ -94,7 +96,7 @@
     near_other, near_mine = gathered(1 - c), gathered(c)
     far_other = swap(near_other, "xh")
     far_mine = swap(near_mine, "xh")
-    swapped = xh[None]
+    swapped = (xh ^ xl)[None]
     act_all, _ = lax.optimization_barrier((act_all, near_mine))
     other = product(swapped, act_all, near_other, far_other, 2)
     got = [swap(part, "c") for part in other]

time: 107 us -> 107 us (level)
  blocking collectives: 38.5 us -> 31.9 us
  starting transfers between devices: 30.6 us -> 34.7 us
  waiting for transfers between devices: 13.5 us -> 14.6 us
    all_gather x1 -> x0, blocking collectives: 6.56 us -> none  [per_device(): act_pair = lax.all_gather(act_sq, 'xl', axis=0)]
    ppermute x4 -> x5, starting transfers between devices: 20.2 us -> 24.3 us  [swap(): return lax.ppermute(x, axis, [(0, 1), (1, 0)])]
    ppermute x4 -> x5, waiting for transfers between devices: 0.6 us -> 1.72 us  [swap(): return lax.ppermute(x, axis, [(0, 1), (1, 0)])]
  transfers between devices with their start and end apart: 7 -> 8, of which waited for: 4 -> 5; matrix products, arithmetic and copies ran while one was open for 1% -> 4% of each run, Pallas kernels for 2% -> 2%
where the time goes in v14:
time: 107 us; the launch traced here: 106 us
  starting transfers between devices  34.7 us (32%)
  blocking collectives  31.9 us (30%)
  waiting for transfers between devices  14.6 us (14%)
  between operations  13.5 us (13%)
  local copies, waits for them, and re-layouts  3.96 us (4%)
  matrix products  3.13 us (3%)
  Pallas kernels  2.5 us (2%)
  other arithmetic  1.97 us (2%)
    all_to_all x1, blocking collectives, gathered(): return lax.all_to_all(jnp.broadcast_to(mine, (Z,) + mine.shape), 'z', 0, 0)  31.9 us
    ppermute x5, starting transfers between devices, swap(): return lax.ppermute(x, axis, [(0, 1), (1, 0)])  24.3 us
    all_to_all x1, starting transfers between devices, transpose_chips(): lax.all_to_all(sent, ('xh', 'z', 'xl', 'y'), 0, 0, axis_index_groups=groups)  6.58 us
    all_to_all x1, waiting for transfers between devices, gathered(): return lax.all_to_all(jnp.broadcast_to(mine, (Z,) + mine.shape), 'z', 0, 0)  6.51 us
    all_to_all x1, waiting for transfers between devices, transpose_chips(): lax.all_to_all(sent, ('xh', 'z', 'xl', 'y'), 0, 0, axis_index_groups=groups)  4.93 us
    all_to_all x1, starting transfers between devices, gathered(): return lax.all_to_all(jnp.broadcast_to(mine, (Z,) + mine.shape), 'z', 0, 0)  3.84 us
    pallas_call x2, Pallas kernels, product(): pl.pallas_call(kernel, in_specs=[pl.BlockSpec(memory_space=pltpu.SMEM), v...  2.5 us
    unnamed x4, local copies, waits for them, and re-layouts  2.19 us
  transfers between devices with their start and end apart: 8, of which 5 were waited for; matrix products, arithmetic and copies ran while one was open for 4% of the time, Pallas kernels for 2%

profile of v14, /device:TPU:1, one launch (start us, length us, event | category | flops | bytes accessed | tf_op | source)
XLA Modules:
  0.0 106.3 jit_solution(10663819380364356147)
XLA Ops:
  6.5 0.0 copy-start
  6.5 0.0 all-gather.3.cloned.1.call-start
  6.5 4.1 %collective-permute-start = (bf16[128,1024]{1,0:T(8,128)(2,1)}, bf16[128,1024]{1,0:T(8,128)(2,1)S(1)}, u32[]{:S(2)}, u32[]{:S(2)}) collective-permute-start(bf16[128,1024]{1,0:T(8,128)(2,1)} %param.4), channel_id=1, source_target_pairs={{0,16},{16,0},{1,17},{17,1},{2,18},{18,2},{3,19},{19,3},{4,20},{20... | collective-permute-start | bytes 786440 | tf_op jit(solution)/shard_map/ppermute | solution.py:26
  10.6 1.3 %fusion.3 = bf16[128,512]{1,0:T(8,128)(2,1)S(1)} fusion(bf16[128,512]{1,0:T(8,128)(2,1)} %param.6, bf16[512,512]{1,0:T(8,128)(2,1)} %param.7), kind=kOutput, calls=%fused_computation.6 | convolution fusion | flops 67239936 | bytes 786432 | tf_op jit(solution)/shard_map/dot_general | solution.py:76
  12.0 0.0 copy-done
  12.0 1.5 %fusion = bf16[2,512,128]{2,1,0:T(8,128)(2,1)S(1)} fusion(bf16[2,512,512]{2,1,0:T(8,128)(2,1)S(1)} %copy-done, bf16[16,2,8,512]{3,2,1,0:T(8,128)(2,1)} %bitcast.32), kind=kOutput, calls=%fused_computation.2 | convolution fusion | flops 134479872 | bytes 1572864 | tf_op jit(solution)/shard_map/tbk,bkj->bjt/dot_general | solution.py:83
  13.5 1.1 %collective-permute-done = bf16[128,1024]{1,0:T(8,128)(2,1)S(1)} collective-permute-done((bf16[128,1024]{1,0:T(8,128)(2,1)}, bf16[128,1024]{1,0:T(8,128)(2,1)S(1)}, u32[]{:S(2)}, u32[]{:S(2)}) %collective-permute-start) | collective-permute-done | bytes 262176 | tf_op jit(solution)/shard_map/ppermute | solution.py:26
  14.6 0.7 broadcast_in_dim.13
  15.3 0.3 fusion.2
  15.6 0.2 copy.15
  15.8 0.8 pad_maximum_fusion
  16.6 0.0 all-gather.3.cloned.1.call-update
  16.7 6.6 %all-to-all-start = ((bf16[2,128,512]{2,1,0:T(8,128)(2,1)}), bf16[2,128,512]{2,1,0:T(8,128)(2,1)S(1)}, u32[]{:S(2)}, u32[]{:S(2)}) async-start(bf16[2,128,512]{2,1,0:T(8,128)(2,1)} %broadcast_in_dim.13), calls=%async_computation | async-start | bytes 524288 | tf_op jit(solution)/shard_map/all_to_all | solution.py:21
  23.2 4.9 %all-to-all-done = bf16[2,128,512]{2,1,0:T(8,128)(2,1)S(1)} async-done(((bf16[2,128,512]{2,1,0:T(8,128)(2,1)}), bf16[2,128,512]{2,1,0:T(8,128)(2,1)S(1)}, u32[]{:S(2)}, u32[]{:S(2)}) %all-to-all-start) | async-done | bytes 262176 | tf_op jit(solution)/shard_map/all_to_all | solution.py:21
  28.3 31.9 %all_to_all.15.near_ref = bf16[8,128,256]{2,1,0:T(8,128)(2,1)S(1)} all-to-all(bf16[8,128,256]{2,1,0:T(8,128)(2,1)S(1)} %broadcast_in_dim.15), channel_id=1, replica_groups=mesh['xh'=2,'z'=8,'xl'=2,'y'=8,'c'=2] {'z'}, dimensions={0} | all-to-all | bytes 1048576 | tf_op jit(solution)/shard_map/all_to_all | solution.py:94
  60.1 0.8 broadcast_in_dim.14
  61.0 3.8 %all-to-all-start.1 = ((bf16[8,128,256]{2,1,0:T(8,128)(2,1)}), bf16[8,128,256]{2,1,0:T(8,128)(2,1)S(1)}, u32[]{:S(2)}, u32[]{:S(2)}) async-start(bf16[8,128,256]{2,1,0:T(8,128)(2,1)} %broadcast_in_dim.14), calls=%async_computation.1 | async-start | bytes 1048576 | tf_op jit(solution)/shard_map/all_to_all | solution.py:94
  64.8 5.5 %collective-permute-start.2 = (bf16[8,128,256]{2,1,0:T(8,128)(2,1)S(1)}, bf16[8,128,256]{2,1,0:T(8,128)(2,1)S(1)}, u32[]{:S(2)}, u32[]{:S(2)}) collective-permute-start(bf16[8,128,256]{2,1,0:T(8,128)(2,1)S(1)} %all_to_all.15.near_ref), channel_id=1, source_target_pairs={{0,256},{256,0},{1,257},{257,1},{2,258},{258,2},{3,259},{259,3},{4... | collective-permute-start | bytes 1572872 | tf_op jit(solution)/shard_map/ppermute | solution.py:26
  70.4 6.5 %all-to-all-done.1.near_ref = bf16[8,128,256]{2,1,0:T(8,128)(2,1)S(1)} async-done(((bf16[8,128,256]{2,1,0:T(8,128)(2,1)}), bf16[8,128,256]{2,1,0:T(8,128)(2,1)S(1)}, u32[]{:S(2)}, u32[]{:S(2)}) %all-to-all-start.1) | async-done | bytes 524320 | tf_op jit(solution)/shard_map/all_to_all | solution.py:94
  76.9 5.5 %collective-permute-start.1 = (bf16[8,128,256]{2,1,0:T(8,128)(2,1)S(1)}, bf16[8,128,256]{2,1,0:T(8,128)(2,1)S(1)}, u32[]{:S(2)}, u32[]{:S(2)}) collective-permute-start(bf16[8,128,256]{2,1,0:T(8,128)(2,1)S(1)} %all-to-all-done.1.near_ref), channel_id=1, source_target_pairs={{0,256},{256,0},{1,257},{257,1},{2,258},{258,2},{3,259},{259,3},{4... | collective-permute-start | bytes 1572872 | tf_op jit(solution)/shard_map/ppermute | solution.py:26
  82.4 1.5 %all-gather.3.cloned.1.call-done = bf16[16,1024,128]{2,1,0:T(8,128)(2,1)} async-done(((bf16[2,1024,128]{2,1,0:T(8,128)(2,1)}), bf16[16,1024,128]{2,1,0:T(8,128)(2,1)}) %all-gather.3.cloned.1.call-update) | async-done | bytes 4194320 | tf_op jit(solution)/shard_map/all_gather | solution.py:88
  83.9 0.0 collective-permute-done.2.far_ref
  83.9 0.0 copy-start.1
  83.9 2.2 %copy-done.1 = bf16[16,1024,128]{2,1,0:T(8,128)(2,1)S(1)} copy-done((bf16[16,1024,128]{2,1,0:T(8,128)(2,1)S(1)}, bf16[16,1024,128]{2,1,0:T(8,128)(2,1)}, u32[]{:S(2)}) %copy-start.1) | copy-done | bytes 4194328
  86.1 1.2 %shard_map.47 = (f32[512,256]{1,0:T(8,128)S(1)}, f32[512,256]{1,0:T(8,128)S(1)}) custom-call(s32[1]{0:T(128)} %bitcast.swapped_ref, bf16[8,2,1024,128]{3,2,1,0:T(8,128)(2,1)S(1)} %bitcast.28, bf16[8,128,256]{2,1,0:T(8,128)(2,1)S(1)} %all_to_all.15.near_ref, bf16[8,128,256]{2,1,0:T(8,128)(2,1)S(1)} %collective-permute-done.2.far_ref), custom_call_target="tpu_custom_call" | custom-call | flops 1073741824 | bytes 6291456 | tf_op jit(solution)/shard_map/pallas_call | solution.py:58
  87.3 7.2 %collective-permute-start.3 = (f32[512,256]{1,0:T(8,128)S(1)}, f32[512,256]{1,0:T(8,128)S(1)}, u32[]{:S(2)}, u32[]{:S(2)}) collective-permute-start(f32[512,256]{1,0:T(8,128)S(1)} %get-tuple-element.11), channel_id=1, source_target_pairs={{0,1},{1,0},{2,3},{3,2},{4,5},{5,4},{6,7},{7,6},{8,9},{9,8},{10,11... | collective-permute-start | bytes 1572872 | tf_op jit(solution)/shard_map/ppermute | solution.py:26
  94.5 1.9 %collective-permute-start.4 = (f32[512,256]{1,0:T(8,128)S(1)}, f32[512,256]{1,0:T(8,128)S(1)}, u32[]{:S(2)}, u32[]{:S(2)}) collective-permute-start(f32[512,256]{1,0:T(8,128)S(1)} %get-tuple-element.12), channel_id=1, source_target_pairs={{0,1},{1,0},{2,3},{3,2},{4,5},{5,4},{6,7},{7,6},{8,9},{9,8},{10,11... | collective-permute-start | bytes 1572872 | tf_op jit(solution)/shard_map/ppermute | solution.py:26
  96.4 0.0 collective-permute-done.1.far_ref
  96.4 1.3 %shard_map.46 = f32[1024,256]{1,0:T(8,128)S(1)} custom-call(s32[1]{0:T(128)} %bitcast.swapped_ref, bf16[8,2,1024,128]{3,2,1,0:T(8,128)(2,1)S(1)} %bitcast.29, bf16[8,128,256]{2,1,0:T(8,128)(2,1)S(1)} %all-to-all-done.1.near_ref, bf16[8,128,256]{2,1,0:T(8,128)(2,1)S(1)} %collective-permute-done.1.far_ref), custom_call_target="tpu_custom_call" | custom-call | flops 1073741824 | bytes 6291456 | tf_op jit(solution)/shard_map/pallas_call | solution.py:58
  97.7 0.0 collective-permute-done.3
  97.7 0.6 collective-permute-done.4
  98.3 1.1 %fusion.4 = f32[1024,256]{1,0:T(8,128)} fusion(f32[1024,256]{1,0:T(8,128)S(1)} %shard_map.46, f32[512,256]{1,0:T(8,128)S(1)} %collective-permute-done.4, f32[512,256]{1,0:T(8,128)S(1)} %collective-permute-done.3), kind=kLoop, calls=%fused_computation.8 | loop fusion | flops 786432 | bytes 3145728 | tf_op jit(solution)/shard_map/div | solution.py:104
  (3 shorter events, 0.1 us)
Async XLA Ops:
  6.5 5.4 %copy-start = (bf16[2,512,512]{2,1,0:T(8,128)(2,1)S(1)}, bf16[2,512,512]{2,1,0:T(8,128)(2,1)}, u32[]{:S(2)}) copy-start(bf16[2,512,512]{2,1,0:T(8,128)(2,1)} %param.5) | copy-start | bytes 3145732
  6.5 77.3 %all-gather.3.cloned.1.call-start = ((), (), s32[]{:S(2)}) async-start(), calls=%async_computation.3 | async-start | bytes 4718592 | tf_op jit(solution)/shard_map/all_gather | solution.py:88
  6.5 8.0 %collective-permute-start = (bf16[128,1024]{1,0:T(8,128)(2,1)}, bf16[128,1024]{1,0:T(8,128)(2,1)S(1)}, u32[]{:S(2)}, u32[]{:S(2)}) collective-permute-start(bf16[128,1024]{1,0:T(8,128)(2,1)} %param.4), channel_id=1, source_target_pairs={{0,16},{16,0},{1,17},{17,1},{2,18},{18,2},{3,19},{19,3},{4,20},{20... | collective-permute-start | bytes 786440 | tf_op jit(solution)/shard_map/ppermute | solution.py:26
  16.7 11.5 %all-to-all-start = ((bf16[2,128,512]{2,1,0:T(8,128)(2,1)}), bf16[2,128,512]{2,1,0:T(8,128)(2,1)S(1)}, u32[]{:S(2)}, u32[]{:S(2)}) async-start(bf16[2,128,512]{2,1,0:T(8,128)(2,1)} %broadcast_in_dim.13), calls=%async_computation | async-start | bytes 524288 | tf_op jit(solution)/shard_map/all_to_all | solution.py:21
  61.0 15.9 %all-to-all-start.1 = ((bf16[8,128,256]{2,1,0:T(8,128)(2,1)}), bf16[8,128,256]{2,1,0:T(8,128)(2,1)S(1)}, u32[]{:S(2)}, u32[]{:S(2)}) async-start(bf16[8,128,256]{2,1,0:T(8,128)(2,1)} %broadcast_in_dim.14), calls=%async_computation.1 | async-start | bytes 1048576 | tf_op jit(solution)/shard_map/all_to_all | solution.py:94
  64.8 19.1 %collective-permute-start.2 = (bf16[8,128,256]{2,1,0:T(8,128)(2,1)S(1)}, bf16[8,128,256]{2,1,0:T(8,128)(2,1)S(1)}, u32[]{:S(2)}, u32[]{:S(2)}) collective-permute-start(bf16[8,128,256]{2,1,0:T(8,128)(2,1)S(1)} %all_to_all.15.near_ref), channel_id=1, source_target_pairs={{0,256},{256,0},{1,257},{257,1},{2,258},{258,2},{3,259},{259,3},{4... | collective-permute-start | bytes 1572872 | tf_op jit(solution)/shard_map/ppermute | solution.py:26
  76.9 19.6 %collective-permute-start.1 = (bf16[8,128,256]{2,1,0:T(8,128)(2,1)S(1)}, bf16[8,128,256]{2,1,0:T(8,128)(2,1)S(1)}, u32[]{:S(2)}, u32[]{:S(2)}) collective-permute-start(bf16[8,128,256]{2,1,0:T(8,128)(2,1)S(1)} %all-to-all-done.1.near_ref), channel_id=1, source_target_pairs={{0,256},{256,0},{1,257},{257,1},{2,258},{258,2},{3,259},{259,3},{4... | collective-permute-start | bytes 1572872 | tf_op jit(solution)/shard_map/ppermute | solution.py:26
  83.9 2.2 %copy-start.1 = (bf16[16,1024,128]{2,1,0:T(8,128)(2,1)S(1)}, bf16[16,1024,128]{2,1,0:T(8,128)(2,1)}, u32[]{:S(2)}) copy-start(bf16[16,1024,128]{2,1,0:T(8,128)(2,1)} %all-gather.3.cloned.1.call-done) | copy-start | bytes 12582916
  87.3 10.4 %collective-permute-start.3 = (f32[512,256]{1,0:T(8,128)S(1)}, f32[512,256]{1,0:T(8,128)S(1)}, u32[]{:S(2)}, u32[]{:S(2)}) collective-permute-start(f32[512,256]{1,0:T(8,128)S(1)} %get-tuple-element.11), channel_id=1, source_target_pairs={{0,1},{1,0},{2,3},{3,2},{4,5},{5,4},{6,7},{7,6},{8,9},{9,8},{10,11... | collective-permute-start | bytes 1572872 | tf_op jit(solution)/shard_map/ppermute | solution.py:26
  94.5 3.8 %collective-permute-start.4 = (f32[512,256]{1,0:T(8,128)S(1)}, f32[512,256]{1,0:T(8,128)S(1)}, u32[]{:S(2)}, u32[]{:S(2)}) collective-permute-start(f32[512,256]{1,0:T(8,128)S(1)} %get-tuple-element.12), channel_id=1, source_target_pairs={{0,1},{1,0},{2,3},{3,2},{4,5},{5,4},{6,7},{7,6},{8,9},{9,8},{10,11... | collective-permute-start | bytes 1572872 | tf_op jit(solution)/shard_map/ppermute | solution.py:26
Sparse Core Ops, SparseCore 0:
  16.8 67.0 all-gather.2

commit v15 on v14

--- a/solution.py
+++ b/solution.py
@@ -20,6 +20,12 @@
     m = lax.axis_index("xl") * Y + lax.axis_index("y")
     got = lax.all_to_all(sent, ("xh", "z", "xl", "y"), 0, 0, axis_index_groups=groups)
     return jnp.where(f > m, got[0], jnp.where(f < m, got[1], x))
+
+
+def mirror_chips(x):
+    chips = XH * Z
+    perm = [(f * chips + m, m * chips + f) for f in range(chips) for m in range(chips)]
+    return lax.ppermute(x, ("xh", "z", "xl", "y"), perm)
 
 
 def swap(x, axis):
@@ -75,25 +81,28 @@
 
     grad_rot = jnp.dot(gradients, grad_basis, preferred_element_type=jnp.float32)
     grad_sq = (grad_rot * grad_rot).astype(jnp.bfloat16)
-    grad_pair = jnp.broadcast_to(grad_sq, (2,) + grad_sq.shape)
-    own = transpose_chips(grad_sq, grad_pair)
+    cols = grad_sq.shape[1] // 2
+
+    def half_of(half):
+        return lax.dynamic_slice_in_dim(grad_sq, half * cols, cols, 1)
+
+    grad_other, grad_mine = half_of(1 - c), half_of(c)
+    grad_pair = jnp.broadcast_to(grad_other, (2,) + grad_other.shape)
 
     def rotated(act):
         blocks = act.reshape(rows, act_width // BLOCK, BLOCK)
         rot = jnp.einsum("tbk,bkj->bjt", blocks, act_basis, preferred_element_type=jnp.float32)
         return (rot * rot).astype(jnp.bfloat16).reshape(act_width, rows)
 
-    others, _ = lax.optimization_barrier((swap(activations, "xl"), grad_pair))
+    others, _ = lax.optimization_barrier((swap(activations, "xl"), (grad_pair, grad_mine)))
     act_pair = jnp.stack([rotated(activations), rotated(others)])
     act_all = lax.all_gather(act_pair, "y", axis=0)
 
-    cols = own.shape[1] // 2
+    def gathered(own):
+        return lax.all_to_all(jnp.broadcast_to(own, (Z,) + own.shape), "z", 0, 0)
 
-    def gathered(half):
-        mine = lax.dynamic_slice_in_dim(own, half * cols, cols, 1)
-        return lax.all_to_all(jnp.broadcast_to(mine, (Z,) + mine.shape), "z", 0, 0)
-
-    near_other, near_mine = gathered(1 - c), gathered(c)
+    near_other = gathered(transpose_chips(grad_other, grad_pair))
+    near_mine = gathered(mirror_chips(grad_mine))
     far_other = swap(near_other, "xh")
     far_mine = swap(near_mine, "xh")
     swapped = (xh ^ xl)[None]

time: 107 us -> 118 us (1.10)
  the two profiles are of different devices: /device:TPU:1 before, /device:TPU:58 now
where the time goes in v15:
time: 118 us; the launch traced here: 117 us
  waiting for transfers between devices  46.9 us (40%)
  starting transfers between devices  44.6 us (38%)
  between operations  13.5 us (11%)
  local copies, waits for them, and re-layouts  4.72 us (4%)
  matrix products  3.13 us (3%)
  Pallas kernels  2.48 us (2%)
  other arithmetic  1.97 us (2%)
    all_to_all x2, starting transfers between devices, gathered(): return lax.all_to_all(jnp.broadcast_to(own, (Z,) + own.shape), 'z', 0, 0)  21.5 us
    all_to_all x2, waiting for transfers between devices, gathered(): return lax.all_to_all(jnp.broadcast_to(own, (Z,) + own.shape), 'z', 0, 0)  16 us
    ppermute x1, waiting for transfers between devices, mirror_chips(): return lax.ppermute(x, ('xh', 'z', 'xl', 'y'), perm)  11.2 us
    ppermute x5, starting transfers between devices, swap(): return lax.ppermute(x, axis, [(0, 1), (1, 0)])  10.7 us
    all_to_all x1, starting transfers between devices, transpose_chips(): lax.all_to_all(sent, ('xh', 'z', 'xl', 'y'), 0, 0, axis_index_groups=groups)  10.5 us
    ppermute x5, waiting for transfers between devices, swap(): return lax.ppermute(x, axis, [(0, 1), (1, 0)])  10.3 us
    all_to_all x1, waiting for transfers between devices, transpose_chips(): lax.all_to_all(sent, ('xh', 'z', 'xl', 'y'), 0, 0, axis_index_groups=groups)  9.4 us
    pallas_call x2, Pallas kernels, product(): pl.pallas_call(kernel, in_specs=[pl.BlockSpec(memory_space=pltpu.SMEM), v...  2.48 us
  transfers between devices with their start and end apart: 10, of which 6 were waited for; matrix products, arithmetic and copies ran while one was open for 4% of the time, Pallas kernels for 2%

profile of v15, /device:TPU:58, one launch (start us, length us, event | category | flops | bytes accessed | tf_op | source)
XLA Modules:
  0.0 117.3 jit_solution(9637302762726920558)
XLA Ops:
  6.5 2.6 %collective-permute-start = (bf16[128,1024]{1,0:T(8,128)(2,1)}, bf16[128,1024]{1,0:T(8,128)(2,1)S(1)}, u32[]{:S(2)}, u32[]{:S(2)}) collective-permute-start(bf16[128,1024]{1,0:T(8,128)(2,1)} %param.4), channel_id=1, source_target_pairs={{0,16},{16,0},{1,17},{17,1},{2,18},{18,2},{3,19},{19,3},{4,20},{20... | collective-permute-start | bytes 786440 | tf_op jit(solution)/shard_map/ppermute | solution.py:32
  9.1 1.3 %fusion.3 = bf16[128,512]{1,0:T(8,128)(2,1)S(1)} fusion(bf16[128,512]{1,0:T(8,128)(2,1)} %param.6, bf16[512,512]{1,0:T(8,128)(2,1)} %param.7), kind=kOutput, calls=%fused_computation.6 | convolution fusion | flops 67239936 | bytes 786432 | tf_op jit(solution)/shard_map/dot_general | solution.py:82
  10.5 1.5 %fusion = bf16[2,512,128]{2,1,0:T(8,128)(2,1)S(1)} fusion(bf16[2,512,512]{2,1,0:T(8,128)(2,1)S(1)} %copy-done, bf16[16,2,8,512]{3,2,1,0:T(8,128)(2,1)} %bitcast.32), kind=kOutput, calls=%fused_computation.2 | convolution fusion | flops 134479872 | bytes 1572864 | tf_op jit(solution)/shard_map/tbk,bkj->bjt/dot_general | solution.py:94
  12.0 4.8 %collective-permute-done = bf16[128,1024]{1,0:T(8,128)(2,1)S(1)} collective-permute-done((bf16[128,1024]{1,0:T(8,128)(2,1)}, bf16[128,1024]{1,0:T(8,128)(2,1)S(1)}, u32[]{:S(2)}, u32[]{:S(2)}) %collective-permute-start) | collective-permute-done | bytes 262176 | tf_op jit(solution)/shard_map/ppermute | solution.py:32
  16.8 0.7 broadcast_in_dim.13
  17.5 0.3 fusion.2
  17.8 0.2 copy.15
  18.0 0.8 pad_maximum_fusion
  18.8 0.0 all-gather.3.cloned.1.call-update
  18.8 10.5 %all-to-all-start.1 = ((bf16[2,128,256]{2,1,0:T(8,128)(2,1)}), bf16[2,128,256]{2,1,0:T(8,128)(2,1)S(1)}, u32[]{:S(2)}, u32[]{:S(2)}) async-start(bf16[2,128,256]{2,1,0:T(8,128)(2,1)} %broadcast_in_dim.13), calls=%async_computation.1 | async-start | bytes 262144 | tf_op jit(solution)/shard_map/all_to_all | solution.py:21
  29.3 9.4 %all-to-all-done.1 = bf16[2,128,256]{2,1,0:T(8,128)(2,1)S(1)} async-done(((bf16[2,128,256]{2,1,0:T(8,128)(2,1)}), bf16[2,128,256]{2,1,0:T(8,128)(2,1)S(1)}, u32[]{:S(2)}, u32[]{:S(2)}) %all-to-all-start.1) | async-done | bytes 131104 | tf_op jit(solution)/shard_map/all_to_all | solution.py:21
  38.7 0.8 broadcast_in_dim.15
  39.5 13.7 %all-to-all-start.2 = ((bf16[8,128,256]{2,1,0:T(8,128)(2,1)}), bf16[8,128,256]{2,1,0:T(8,128)(2,1)S(1)}, u32[]{:S(2)}, u32[]{:S(2)}) async-start(bf16[8,128,256]{2,1,0:T(8,128)(2,1)} %broadcast_in_dim.15), calls=%async_computation.2 | async-start | bytes 1048576 | tf_op jit(solution)/shard_map/all_to_all | solution.py:102
  53.2 1.9 %collective-permute-start.1 = (bf16[128,256]{1,0:T(8,128)(2,1)S(1)}, bf16[128,256]{1,0:T(8,128)(2,1)S(1)}, u32[]{:S(2)}, u32[]{:S(2)}) collective-permute-start(bf16[128,256]{1,0:T(8,128)(2,1)S(1)} %get-tuple-element.13), channel_id=1, source_target_pairs={{0,0},{2,32},{4,64},{6,96},{8,128},{10,160},{12,192},{14,224},{16,... | collective-permute-start | bytes 196616 | tf_op jit(solution)/shard_map/ppermute | solution.py:28
  55.2 11.2 %collective-permute-done.1 = bf16[128,256]{1,0:T(8,128)(2,1)S(1)} collective-permute-done((bf16[128,256]{1,0:T(8,128)(2,1)S(1)}, bf16[128,256]{1,0:T(8,128)(2,1)S(1)}, u32[]{:S(2)}, u32[]{:S(2)}) %collective-permute-start.1) | collective-permute-done | bytes 65568 | tf_op jit(solution)/shard_map/ppermute | solution.py:28
  66.4 1.3 %all-to-all-done.2.near_ref = bf16[8,128,256]{2,1,0:T(8,128)(2,1)S(1)} async-done(((bf16[8,128,256]{2,1,0:T(8,128)(2,1)}), bf16[8,128,256]{2,1,0:T(8,128)(2,1)S(1)}, u32[]{:S(2)}, u32[]{:S(2)}) %all-to-all-start.2) | async-done | bytes 524320 | tf_op jit(solution)/shard_map/all_to_all | solution.py:102
  67.7 0.8 broadcast_in_dim.14
  68.5 7.8 %all-to-all-start = ((bf16[8,128,256]{2,1,0:T(8,128)(2,1)}), bf16[8,128,256]{2,1,0:T(8,128)(2,1)S(1)}, u32[]{:S(2)}, u32[]{:S(2)}) async-start(bf16[8,128,256]{2,1,0:T(8,128)(2,1)} %broadcast_in_dim.14), calls=%async_computation | async-start | bytes 1048576 | tf_op jit(solution)/shard_map/all_to_all | solution.py:102
  76.3 1.9 %collective-permute-start.3 = (bf16[8,128,256]{2,1,0:T(8,128)(2,1)S(1)}, bf16[8,128,256]{2,1,0:T(8,128)(2,1)S(1)}, u32[]{:S(2)}, u32[]{:S(2)}) collective-permute-start(bf16[8,128,256]{2,1,0:T(8,128)(2,1)S(1)} %all-to-all-done.2.near_ref), channel_id=1, source_target_pairs={{0,256},{256,0},{1,257},{257,1},{2,258},{258,2},{3,259},{259,3},{4... | collective-permute-start | bytes 1572872 | tf_op jit(solution)/shard_map/ppermute | solution.py:32
  78.2 14.7 %all-to-all-done.near_ref = bf16[8,128,256]{2,1,0:T(8,128)(2,1)S(1)} async-done(((bf16[8,128,256]{2,1,0:T(8,128)(2,1)}), bf16[8,128,256]{2,1,0:T(8,128)(2,1)S(1)}, u32[]{:S(2)}, u32[]{:S(2)}) %all-to-all-start) | async-done | bytes 524320 | tf_op jit(solution)/shard_map/all_to_all | solution.py:102
  92.9 1.9 %collective-permute-start.2 = (bf16[8,128,256]{2,1,0:T(8,128)(2,1)S(1)}, bf16[8,128,256]{2,1,0:T(8,128)(2,1)S(1)}, u32[]{:S(2)}, u32[]{:S(2)}) collective-permute-start(bf16[8,128,256]{2,1,0:T(8,128)(2,1)S(1)} %all-to-all-done.near_ref), channel_id=1, source_target_pairs={{0,256},{256,0},{1,257},{257,1},{2,258},{258,2},{3,259},{259,3},{4... | collective-permute-start | bytes 1572872 | tf_op jit(solution)/shard_map/ppermute | solution.py:32
  94.8 0.0 all-gather.3.cloned.1.call-done
  94.9 0.0 collective-permute-done.3.far_ref
  94.9 2.2 %copy-done.1 = bf16[16,1024,128]{2,1,0:T(8,128)(2,1)S(1)} copy-done((bf16[16,1024,128]{2,1,0:T(8,128)(2,1)S(1)}, bf16[16,1024,128]{2,1,0:T(8,128)(2,1)}, u32[]{:S(2)}) %copy-start.1) | copy-done | bytes 4194328
  97.1 1.2 %shard_map.47 = (f32[512,256]{1,0:T(8,128)S(1)}, f32[512,256]{1,0:T(8,128)S(1)}) custom-call(s32[1]{0:T(128)} %bitcast.swapped_ref, bf16[8,2,1024,128]{3,2,1,0:T(8,128)(2,1)S(1)} %bitcast.28, bf16[8,128,256]{2,1,0:T(8,128)(2,1)S(1)} %all-to-all-done.2.near_ref, bf16[8,128,256]{2,1,0:T(8,128)(2,1)S(1)} %collective-permute-done.3.far_ref), custom_call_target="tpu_custom_call" | custom-call | flops 1073741824 | bytes 6291456 | tf_op jit(solution)/shard_map/pallas_call | solution.py:64
  98.3 1.9 %collective-permute-start.4 = (f32[512,256]{1,0:T(8,128)S(1)}, f32[512,256]{1,0:T(8,128)S(1)}, u32[]{:S(2)}, u32[]{:S(2)}) collective-permute-start(f32[512,256]{1,0:T(8,128)S(1)} %get-tuple-element.11), channel_id=1, source_target_pairs={{0,1},{1,0},{2,3},{3,2},{4,5},{5,4},{6,7},{7,6},{8,9},{9,8},{10,11... | collective-permute-start | bytes 1572872 | tf_op jit(solution)/shard_map/ppermute | solution.py:32
  100.3 2.4 %collective-permute-start.5 = (f32[512,256]{1,0:T(8,128)S(1)}, f32[512,256]{1,0:T(8,128)S(1)}, u32[]{:S(2)}, u32[]{:S(2)}) collective-permute-start(f32[512,256]{1,0:T(8,128)S(1)} %get-tuple-element.12), channel_id=1, source_target_pairs={{0,1},{1,0},{2,3},{3,2},{4,5},{5,4},{6,7},{7,6},{8,9},{9,8},{10,11... | collective-permute-start | bytes 1572872 | tf_op jit(solution)/shard_map/ppermute | solution.py:32
  102.7 5.5 %collective-permute-done.2.far_ref = bf16[8,128,256]{2,1,0:T(8,128)(2,1)S(1)} collective-permute-done((bf16[8,128,256]{2,1,0:T(8,128)(2,1)S(1)}, bf16[8,128,256]{2,1,0:T(8,128)(2,1)S(1)}, u32[]{:S(2)}, u32[]{:S(2)}) %collective-permute-start.2) | collective-permute-done | bytes 524320 | tf_op jit(solution)/shard_map/ppermute | solution.py:32
  108.1 1.2 %shard_map.46 = f32[1024,256]{1,0:T(8,128)S(1)} custom-call(s32[1]{0:T(128)} %bitcast.swapped_ref, bf16[8,2,1024,128]{3,2,1,0:T(8,128)(2,1)S(1)} %bitcast.29, bf16[8,128,256]{2,1,0:T(8,128)(2,1)S(1)} %all-to-all-done.near_ref, bf16[8,128,256]{2,1,0:T(8,128)(2,1)S(1)} %collective-permute-done.2.far_ref), custom_call_target="tpu_custom_call" | custom-call | flops 1073741824 | bytes 6291456 | tf_op jit(solution)/shard_map/pallas_call | solution.py:64
  109.4 0.0 collective-permute-done.4
  109.4 0.0 collective-permute-done.5
  109.4 1.1 fusion.4
  (6 shorter events, 0.0 us)
Async XLA Ops:
  6.5 4.0 %copy-start = (bf16[2,512,512]{2,1,0:T(8,128)(2,1)S(1)}, bf16[2,512,512]{2,1,0:T(8,128)(2,1)}, u32[]{:S(2)}) copy-start(bf16[2,512,512]{2,1,0:T(8,128)(2,1)} %param.5) | copy-start | bytes 3145732
  6.5 88.3 %all-gather.3.cloned.1.call-start = ((), (), s32[]{:S(2)}) async-start(), calls=%async_computation.3 | async-start | bytes 4718592 | tf_op jit(solution)/shard_map/all_gather | solution.py:99
  6.5 10.3 %collective-permute-start = (bf16[128,1024]{1,0:T(8,128)(2,1)}, bf16[128,1024]{1,0:T(8,128)(2,1)S(1)}, u32[]{:S(2)}, u32[]{:S(2)}) collective-permute-start(bf16[128,1024]{1,0:T(8,128)(2,1)} %param.4), channel_id=1, source_target_pairs={{0,16},{16,0},{1,17},{17,1},{2,18},{18,2},{3,19},{19,3},{4,20},{20... | collective-permute-start | bytes 786440 | tf_op jit(solution)/shard_map/ppermute | solution.py:32
  18.8 19.8 %all-to-all-start.1 = ((bf16[2,128,256]{2,1,0:T(8,128)(2,1)}), bf16[2,128,256]{2,1,0:T(8,128)(2,1)S(1)}, u32[]{:S(2)}, u32[]{:S(2)}) async-start(bf16[2,128,256]{2,1,0:T(8,128)(2,1)} %broadcast_in_dim.13), calls=%async_computation.1 | async-start | bytes 262144 | tf_op jit(solution)/shard_map/all_to_all | solution.py:21
  39.5 28.1 %all-to-all-start.2 = ((bf16[8,128,256]{2,1,0:T(8,128)(2,1)}), bf16[8,128,256]{2,1,0:T(8,128)(2,1)S(1)}, u32[]{:S(2)}, u32[]{:S(2)}) async-start(bf16[8,128,256]{2,1,0:T(8,128)(2,1)} %broadcast_in_dim.15), calls=%async_computation.2 | async-start | bytes 1048576 | tf_op jit(solution)/shard_map/all_to_all | solution.py:102
  53.2 13.1 %collective-permute-start.1 = (bf16[128,256]{1,0:T(8,128)(2,1)S(1)}, bf16[128,256]{1,0:T(8,128)(2,1)S(1)}, u32[]{:S(2)}, u32[]{:S(2)}) collective-permute-start(bf16[128,256]{1,0:T(8,128)(2,1)S(1)} %get-tuple-element.13), channel_id=1, source_target_pairs={{0,0},{2,32},{4,64},{6,96},{8,128},{10,160},{12,192},{14,224},{16,... | collective-permute-start | bytes 196616 | tf_op jit(solution)/shard_map/ppermute | solution.py:28
  68.5 24.4 %all-to-all-start = ((bf16[8,128,256]{2,1,0:T(8,128)(2,1)}), bf16[8,128,256]{2,1,0:T(8,128)(2,1)S(1)}, u32[]{:S(2)}, u32[]{:S(2)}) async-start(bf16[8,128,256]{2,1,0:T(8,128)(2,1)} %broadcast_in_dim.14), calls=%async_computation | async-start | bytes 1048576 | tf_op jit(solution)/shard_map/all_to_all | solution.py:102
  76.3 18.6 %collective-permute-start.3 = (bf16[8,128,256]{2,1,0:T(8,128)(2,1)S(1)}, bf16[8,128,256]{2,1,0:T(8,128)(2,1)S(1)}, u32[]{:S(2)}, u32[]{:S(2)}) collective-permute-start(bf16[8,128,256]{2,1,0:T(8,128)(2,1)S(1)} %all-to-all-done.2.near_ref), channel_id=1, source_target_pairs={{0,256},{256,0},{1,257},{257,1},{2,258},{258,2},{3,259},{259,3},{4... | collective-permute-start | bytes 1572872 | tf_op jit(solution)/shard_map/ppermute | solution.py:32
  92.9 15.2 %collective-permute-start.2 = (bf16[8,128,256]{2,1,0:T(8,128)(2,1)S(1)}, bf16[8,128,256]{2,1,0:T(8,128)(2,1)S(1)}, u32[]{:S(2)}, u32[]{:S(2)}) collective-permute-start(bf16[8,128,256]{2,1,0:T(8,128)(2,1)S(1)} %all-to-all-done.near_ref), channel_id=1, source_target_pairs={{0,256},{256,0},{1,257},{257,1},{2,258},{258,2},{3,259},{259,3},{4... | collective-permute-start | bytes 1572872 | tf_op jit(solution)/shard_map/ppermute | solution.py:32
  94.9 2.2 %copy-start.1 = (bf16[16,1024,128]{2,1,0:T(8,128)(2,1)S(1)}, bf16[16,1024,128]{2,1,0:T(8,128)(2,1)}, u32[]{:S(2)}) copy-start(bf16[16,1024,128]{2,1,0:T(8,128)(2,1)} %all-gather.3.cloned.1.call-done) | copy-start | bytes 12582916
  98.3 11.1 %collective-permute-start.4 = (f32[512,256]{1,0:T(8,128)S(1)}, f32[512,256]{1,0:T(8,128)S(1)}, u32[]{:S(2)}, u32[]{:S(2)}) collective-permute-start(f32[512,256]{1,0:T(8,128)S(1)} %get-tuple-element.11), channel_id=1, source_target_pairs={{0,1},{1,0},{2,3},{3,2},{4,5},{5,4},{6,7},{7,6},{8,9},{9,8},{10,11... | collective-permute-start | bytes 1572872 | tf_op jit(solution)/shard_map/ppermute | solution.py:32
  100.3 9.1 %collective-permute-start.5 = (f32[512,256]{1,0:T(8,128)S(1)}, f32[512,256]{1,0:T(8,128)S(1)}, u32[]{:S(2)}, u32[]{:S(2)}) collective-permute-start(f32[512,256]{1,0:T(8,128)S(1)} %get-tuple-element.12), channel_id=1, source_target_pairs={{0,1},{1,0},{2,3},{3,2},{4,5},{5,4},{6,7},{7,6},{8,9},{9,8},{10,11... | collective-permute-start | bytes 1572872 | tf_op jit(solution)/shard_map/ppermute | solution.py:32
Sparse Core Ops, SparseCore 0:
  19.0 64.3 all-gather.2

commit v16 on v13

--- a/solution.py
+++ b/solution.py
@@ -88,17 +88,15 @@
     rows, act_width = activations.shape
     xh, xl, c = (lax.axis_index(a) for a in ("xh", "xl", "c"))
 
-    act_blocks = activations.reshape(rows, act_width // BLOCK, BLOCK)
-    act_rot = jnp.einsum("tbk,bkj->bjt", act_blocks, act_basis, preferred_element_type=jnp.float32)
-    act_sq = (act_rot * act_rot).astype(jnp.bfloat16).reshape(act_width, rows)
-
-    gradients, _ = lax.optimization_barrier((gradients, act_sq))
     grad_rot = jnp.dot(gradients, grad_basis, preferred_element_type=jnp.float32)
     grad_sq = (grad_rot * grad_rot).astype(jnp.bfloat16)
     grad_pair = jnp.broadcast_to(grad_sq, (2,) + grad_sq.shape)
     own = transpose_chips(grad_sq, grad_pair)
 
-    act_pair = jnp.stack([act_sq, swap(act_sq, "xl")])
+    act_in = jnp.stack([activations, swap(activations, "xl")])
+    act_in = act_in.reshape(2, rows, act_width // BLOCK, BLOCK)
+    act_rot = jnp.einsum("ptbk,bkj->pbjt", act_in, act_basis, preferred_element_type=jnp.float32)
+    act_pair = (act_rot * act_rot).astype(jnp.bfloat16).reshape(2, act_width, rows)
     act_all = lax.all_gather(act_pair, "y", axis=0)
 
     cols = own.shape[1] // 2

time: 109 us -> 107 us (0.982)
  local copies, waits for them, and re-layouts: 4.16 us -> 5.43 us
    unnamed x4 -> x5, local copies, waits for them, and re-layouts: 3.41 us -> 3.4 us
  transfers between devices with their start and end apart: 9 -> 9, of which waited for: 5 -> 5; matrix products, arithmetic and copies ran while one was open for 3% -> 4% of each run, Pallas kernels for 4% -> 4%
where the time goes in v16:
time: 107 us
  starting transfers between devices  45.3 us (42%)
  waiting for transfers between devices  35.7 us (33%)
  between operations  13.5 us (13%)
  local copies, waits for them, and re-layouts  5.43 us (5%)
  Pallas kernels  4.17 us (4%)
  matrix products  1.78 us (2%)
  other arithmetic  1.13 us (1%)
    all_to_all x2, waiting for transfers between devices, gathered(): return lax.all_to_all(copies(mine, Z), 'z', 0, 0)  24.8 us
    all_to_all x2, starting transfers between devices, gathered(): return lax.all_to_all(copies(mine, Z), 'z', 0, 0)  21.9 us
    ppermute x5, starting transfers between devices, swap(): return lax.ppermute(x, axis, [(0, 1), (1, 0)])  19 us
    all_gather x1, waiting for transfers between devices, per_device(): act_all = lax.all_gather(act_pair, 'y', axis=0)  7.15 us
    all_to_all x1, starting transfers between devices, transpose_chips(): lax.all_to_all(sent, ('xh', 'z', 'xl', 'y'), 0, 0, axis_index_groups=groups)  4.37 us
    unnamed x5, local copies, waits for them, and re-layouts  3.4 us
    all_to_all x1, waiting for transfers between devices, transpose_chips(): lax.all_to_all(sent, ('xh', 'z', 'xl', 'y'), 0, 0, axis_index_groups=groups)  3.13 us
    pallas_call x2, Pallas kernels, product(): pl.pallas_call(kernel, in_specs=[pl.BlockSpec(memory_space=pltpu.SMEM), v...  2.5 us
  transfers between devices with their start and end apart: 9, of which 5 were waited for; matrix products, arithmetic and copies ran while one was open for 4% of the time, Pallas kernels for 4%

profile of v16, /device:TPU:1, one launch (start us, length us, event | category | flops | bytes accessed | tf_op | source)
XLA Modules:
  0.0 107.0 jit_solution(12580810266118887739)
XLA Ops:
  6.5 1.2 %copy.15 = bf16[128,1024]{0,1:T(8,128)(2,1)S(1)} copy(bf16[128,1024]{1,0:T(8,128)(2,1)} %param.4) | data formatting | bytes 524288 | tf_op args[0]
  7.7 3.9 %collective-permute-start = (bf16[128,1024]{0,1:T(8,128)(2,1)S(1)}, bf16[128,1024]{0,1:T(8,128)(2,1)S(1)}, u32[]{:S(2)}, u32[]{:S(2)}) collective-permute-start(bf16[128,1024]{0,1:T(8,128)(2,1)S(1)} %copy.15), channel_id=1, source_target_pairs={{0,16},{16,0},{1,17},{17,1},{2,18},{18,2},{3,19},{19,3},{4,20},{20... | collective-permute-start | bytes 786440 | tf_op jit(solution)/shard_map/ppermute | solution.py:26
  11.7 1.3 %fusion.2 = bf16[128,512]{1,0:T(8,128)(2,1)S(1)} fusion(bf16[128,512]{1,0:T(8,128)(2,1)} %param.6, bf16[512,512]{1,0:T(8,128)(2,1)} %param.7), kind=kOutput, calls=%fused_computation.4 | convolution fusion | flops 67239936 | bytes 786432 | tf_op jit(solution)/shard_map/dot_general | solution.py:91
  13.1 0.7 broadcast_in_dim.7
  13.8 4.4 %all-to-all-start = ((bf16[2,128,512]{2,1,0:T(8,128)(2,1)}), bf16[2,128,512]{2,1,0:T(8,128)(2,1)S(1)}, u32[]{:S(2)}, u32[]{:S(2)}) async-start(bf16[2,128,512]{2,1,0:T(8,128)(2,1)} %broadcast_in_dim.7), calls=%async_computation | async-start | bytes 524288 | tf_op jit(solution)/shard_map/all_to_all | solution.py:21
  18.2 0.0 all-gather.2.cloned.1.call-start
  18.2 0.1 copy.17
  18.3 0.0 collective-permute-done
  18.3 0.1 copy.18
  18.5 0.4 fusion.1
  18.9 1.0 copy.19
  19.9 0.0 all-gather.2.cloned.1.call-update
  19.9 3.1 %all-to-all-done = bf16[2,128,512]{2,1,0:T(8,128)(2,1)S(1)} async-done(((bf16[2,128,512]{2,1,0:T(8,128)(2,1)}), bf16[2,128,512]{2,1,0:T(8,128)(2,1)S(1)}, u32[]{:S(2)}, u32[]{:S(2)}) %all-to-all-start) | async-done | bytes 262176 | tf_op jit(solution)/shard_map/all_to_all | solution.py:21
  23.1 0.8 shard_map.48
  24.0 18.4 %all-to-all-start.2 = ((bf16[8,128,256]{2,1,0:T(8,128)(2,1)}), bf16[8,128,256]{2,1,0:T(8,128)(2,1)S(1)}, u32[]{:S(2)}, u32[]{:S(2)}) async-start(bf16[8,128,256]{2,1,0:T(8,128)(2,1)} %shard_map.48), calls=%async_computation.2 | async-start | bytes 1048576 | tf_op jit(solution)/shard_map/all_to_all | solution.py:106
  42.4 0.8 shard_map.46
  43.2 15.1 %all-to-all-done.2.near_ref = bf16[8,128,256]{2,1,0:T(8,128)(2,1)S(1)} async-done(((bf16[8,128,256]{2,1,0:T(8,128)(2,1)}), bf16[8,128,256]{2,1,0:T(8,128)(2,1)S(1)}, u32[]{:S(2)}, u32[]{:S(2)}) %all-to-all-start.2) | async-done | bytes 524320 | tf_op jit(solution)/shard_map/all_to_all | solution.py:106
  58.4 3.5 %all-to-all-start.1 = ((bf16[8,128,256]{2,1,0:T(8,128)(2,1)}), bf16[8,128,256]{2,1,0:T(8,128)(2,1)S(1)}, u32[]{:S(2)}, u32[]{:S(2)}) async-start(bf16[8,128,256]{2,1,0:T(8,128)(2,1)} %shard_map.46), calls=%async_computation.1 | async-start | bytes 1048576 | tf_op jit(solution)/shard_map/all_to_all | solution.py:106
  61.9 5.3 %collective-permute-start.2 = (bf16[8,128,256]{2,1,0:T(8,128)(2,1)S(1)}, bf16[8,128,256]{2,1,0:T(8,128)(2,1)S(1)}, u32[]{:S(2)}, u32[]{:S(2)}) collective-permute-start(bf16[8,128,256]{2,1,0:T(8,128)(2,1)S(1)} %all-to-all-done.2.near_ref), channel_id=1, source_target_pairs={{0,256},{256,0},{1,257},{257,1},{2,258},{258,2},{3,259},{259,3},{4... | collective-permute-start | bytes 1572872 | tf_op jit(solution)/shard_map/ppermute | solution.py:26
  67.1 9.6 %all-to-all-done.1.near_ref = bf16[8,128,256]{2,1,0:T(8,128)(2,1)S(1)} async-done(((bf16[8,128,256]{2,1,0:T(8,128)(2,1)}), bf16[8,128,256]{2,1,0:T(8,128)(2,1)S(1)}, u32[]{:S(2)}, u32[]{:S(2)}) %all-to-all-start.1) | async-done | bytes 524320 | tf_op jit(solution)/shard_map/all_to_all | solution.py:106
  76.8 5.2 %collective-permute-start.1 = (bf16[8,128,256]{2,1,0:T(8,128)(2,1)S(1)}, bf16[8,128,256]{2,1,0:T(8,128)(2,1)S(1)}, u32[]{:S(2)}, u32[]{:S(2)}) collective-permute-start(bf16[8,128,256]{2,1,0:T(8,128)(2,1)S(1)} %all-to-all-done.1.near_ref), channel_id=1, source_target_pairs={{0,256},{256,0},{1,257},{257,1},{2,258},{258,2},{3,259},{259,3},{4... | collective-permute-start | bytes 1572872 | tf_op jit(solution)/shard_map/ppermute | solution.py:26
  82.0 7.2 %all-gather.2.cloned.1.call-done.act_ref = bf16[8,2,1024,128]{3,2,1,0:T(8,128)(2,1)} async-done(((bf16[1,2,1024,128]{3,2,1,0:T(8,128)(2,1)}), bf16[8,2,1024,128]{3,2,1,0:T(8,128)(2,1)}) %all-gather.2.cloned.1.call-update) | async-done | bytes 4194320 | tf_op jit(solution)/shard_map/all_gather | solution.py:100
  89.2 0.0 collective-permute-done.2.far_ref
  89.2 2.2 %copy-done.1 = bf16[8,2,1024,128]{3,2,1,0:T(8,128)(2,1)S(1)} copy-done((bf16[8,2,1024,128]{3,2,1,0:T(8,128)(2,1)S(1)}, bf16[8,2,1024,128]{3,2,1,0:T(8,128)(2,1)}, u32[]{:S(2)}) %copy-start.1) | copy-done | bytes 4194328
  91.4 1.2 %shard_map.49 = (f32[512,256]{1,0:T(8,128)S(1)}, f32[512,256]{1,0:T(8,128)S(1)}) custom-call(s32[1]{0:T(128)} %bitcast.swapped_ref, bf16[8,2,1024,128]{3,2,1,0:T(8,128)(2,1)S(1)} %copy-done.1, bf16[8,128,256]{2,1,0:T(8,128)(2,1)S(1)} %all-to-all-done.2.near_ref, bf16[8,128,256]{2,1,0:T(8,128)(2,1)S(1)} %collective-permute-done.2.far_ref), custom_call_target="tpu_custom_call" | custom-call | flops 1073741824 | bytes 6291456 | tf_op jit(solution)/shard_map/pallas_call | solution.py:58
  92.6 2.6 %collective-permute-start.3 = (f32[512,256]{1,0:T(8,128)S(1)}, f32[512,256]{1,0:T(8,128)S(1)}, u32[]{:S(2)}, u32[]{:S(2)}) collective-permute-start(f32[512,256]{1,0:T(8,128)S(1)} %get-tuple-element.9), channel_id=1, source_target_pairs={{0,1},{1,0},{2,3},{3,2},{4,5},{5,4},{6,7},{7,6},{8,9},{9,8},{10,11... | collective-permute-start | bytes 1572872 | tf_op jit(solution)/shard_map/ppermute | solution.py:26
  95.2 1.9 %collective-permute-start.4 = (f32[512,256]{1,0:T(8,128)S(1)}, f32[512,256]{1,0:T(8,128)S(1)}, u32[]{:S(2)}, u32[]{:S(2)}) collective-permute-start(f32[512,256]{1,0:T(8,128)S(1)} %get-tuple-element.10), channel_id=1, source_target_pairs={{0,1},{1,0},{2,3},{3,2},{4,5},{5,4},{6,7},{7,6},{8,9},{9,8},{10,11... | collective-permute-start | bytes 1572872 | tf_op jit(solution)/shard_map/ppermute | solution.py:26
  97.1 0.0 collective-permute-done.1.far_ref
  97.2 1.3 %shard_map.47 = f32[1024,256]{1,0:T(8,128)S(1)} custom-call(s32[1]{0:T(128)} %bitcast.swapped_ref, bf16[8,2,1024,128]{3,2,1,0:T(8,128)(2,1)S(1)} %copy-done.1, bf16[8,128,256]{2,1,0:T(8,128)(2,1)S(1)} %all-to-all-done.1.near_ref, bf16[8,128,256]{2,1,0:T(8,128)(2,1)S(1)} %collective-permute-done.1.far_ref), custom_call_target="tpu_custom_call" | custom-call | flops 1073741824 | bytes 6291456 | tf_op jit(solution)/shard_map/pallas_call | solution.py:58
  98.4 0.0 collective-permute-done.3
  98.4 0.6 collective-permute-done.4
  99.0 1.1 %fusion.3 = f32[1024,256]{1,0:T(8,128)} fusion(f32[1024,256]{1,0:T(8,128)S(1)} %shard_map.47, f32[512,256]{1,0:T(8,128)S(1)} %collective-permute-done.4, f32[512,256]{1,0:T(8,128)S(1)} %collective-permute-done.3), kind=kLoop, calls=%fused_computation.6 | loop fusion | flops 786432 | bytes 3145728 | tf_op jit(solution)/shard_map/div | solution.py:116
  (5 shorter events, 0.0 us)
Async XLA Ops:
  6.5 11.9 %copy-start = (bf16[2,512,512]{2,1,0:T(8,128)(2,1)S(1)}, bf16[2,512,512]{2,1,0:T(8,128)(2,1)}, u32[]{:S(2)}) copy-start(bf16[2,512,512]{2,1,0:T(8,128)(2,1)} %param.5) | copy-start | bytes 3145732
  7.7 10.6 %collective-permute-start = (bf16[128,1024]{0,1:T(8,128)(2,1)S(1)}, bf16[128,1024]{0,1:T(8,128)(2,1)S(1)}, u32[]{:S(2)}, u32[]{:S(2)}) collective-permute-start(bf16[128,1024]{0,1:T(8,128)(2,1)S(1)} %copy.15), channel_id=1, source_target_pairs={{0,16},{16,0},{1,17},{17,1},{2,18},{18,2},{3,19},{19,3},{4,20},{20... | collective-permute-start | bytes 786440 | tf_op jit(solution)/shard_map/ppermute | solution.py:26
  13.8 9.3 %all-to-all-start = ((bf16[2,128,512]{2,1,0:T(8,128)(2,1)}), bf16[2,128,512]{2,1,0:T(8,128)(2,1)S(1)}, u32[]{:S(2)}, u32[]{:S(2)}) async-start(bf16[2,128,512]{2,1,0:T(8,128)(2,1)} %broadcast_in_dim.7), calls=%async_computation | async-start | bytes 524288 | tf_op jit(solution)/shard_map/all_to_all | solution.py:21
  18.2 71.0 %all-gather.2.cloned.1.call-start = ((), (), s32[]{:S(2)}) async-start(), calls=%async_computation.3 | async-start | bytes 4718592 | tf_op jit(solution)/shard_map/all_gather | solution.py:100
  24.0 34.4 %all-to-all-start.2 = ((bf16[8,128,256]{2,1,0:T(8,128)(2,1)}), bf16[8,128,256]{2,1,0:T(8,128)(2,1)S(1)}, u32[]{:S(2)}, u32[]{:S(2)}) async-start(bf16[8,128,256]{2,1,0:T(8,128)(2,1)} %shard_map.48), calls=%async_computation.2 | async-start | bytes 1048576 | tf_op jit(solution)/shard_map/all_to_all | solution.py:106
  58.4 18.4 %all-to-all-start.1 = ((bf16[8,128,256]{2,1,0:T(8,128)(2,1)}), bf16[8,128,256]{2,1,0:T(8,128)(2,1)S(1)}, u32[]{:S(2)}, u32[]{:S(2)}) async-start(bf16[8,128,256]{2,1,0:T(8,128)(2,1)} %shard_map.46), calls=%async_computation.1 | async-start | bytes 1048576 | tf_op jit(solution)/shard_map/all_to_all | solution.py:106
  61.9 27.3 %collective-permute-start.2 = (bf16[8,128,256]{2,1,0:T(8,128)(2,1)S(1)}, bf16[8,128,256]{2,1,0:T(8,128)(2,1)S(1)}, u32[]{:S(2)}, u32[]{:S(2)}) collective-permute-start(bf16[8,128,256]{2,1,0:T(8,128)(2,1)S(1)} %all-to-all-done.2.near_ref), channel_id=1, source_target_pairs={{0,256},{256,0},{1,257},{257,1},{2,258},{258,2},{3,259},{259,3},{4... | collective-permute-start | bytes 1572872 | tf_op jit(solution)/shard_map/ppermute | solution.py:26
  76.8 20.4 %collective-permute-start.1 = (bf16[8,128,256]{2,1,0:T(8,128)(2,1)S(1)}, bf16[8,128,256]{2,1,0:T(8,128)(2,1)S(1)}, u32[]{:S(2)}, u32[]{:S(2)}) collective-permute-start(bf16[8,128,256]{2,1,0:T(8,128)(2,1)S(1)} %all-to-all-done.1.near_ref), channel_id=1, source_target_pairs={{0,256},{256,0},{1,257},{257,1},{2,258},{258,2},{3,259},{259,3},{4... | collective-permute-start | bytes 1572872 | tf_op jit(solution)/shard_map/ppermute | solution.py:26
  89.2 2.2 %copy-start.1 = (bf16[8,2,1024,128]{3,2,1,0:T(8,128)(2,1)S(1)}, bf16[8,2,1024,128]{3,2,1,0:T(8,128)(2,1)}, u32[]{:S(2)}) copy-start(bf16[8,2,1024,128]{3,2,1,0:T(8,128)(2,1)} %all-gather.2.cloned.1.call-done.act_ref) | copy-start | bytes 12582916
  92.6 5.8 %collective-permute-start.3 = (f32[512,256]{1,0:T(8,128)S(1)}, f32[512,256]{1,0:T(8,128)S(1)}, u32[]{:S(2)}, u32[]{:S(2)}) collective-permute-start(f32[512,256]{1,0:T(8,128)S(1)} %get-tuple-element.9), channel_id=1, source_target_pairs={{0,1},{1,0},{2,3},{3,2},{4,5},{5,4},{6,7},{7,6},{8,9},{9,8},{10,11... | collective-permute-start | bytes 1572872 | tf_op jit(solution)/shard_map/ppermute | solution.py:26
  95.2 3.8 %collective-permute-start.4 = (f32[512,256]{1,0:T(8,128)S(1)}, f32[512,256]{1,0:T(8,128)S(1)}, u32[]{:S(2)}, u32[]{:S(2)}) collective-permute-start(f32[512,256]{1,0:T(8,128)S(1)} %get-tuple-element.10), channel_id=1, source_target_pairs={{0,1},{1,0},{2,3},{3,2},{4,5},{5,4},{6,7},{7,6},{8,9},{9,8},{10,11... | collective-permute-start | bytes 1572872 | tf_op jit(solution)/shard_map/ppermute | solution.py:26
Sparse Core Ops, SparseCore 0:
  21.1 68.0 all-gather.1

commit v17 on v14

--- a/solution.py
+++ b/solution.py
@@ -11,15 +11,66 @@
 XH, Z, XL, Y, C = 2, 8, 2, 8, 2
 
 
-def transpose_chips(x, sent):
+def vmem():
+    return pl.BlockSpec(memory_space=pltpu.VMEM)
+
+
+def squared_pair(gradients, basis):
+    def kernel(grad_ref, basis_ref, out_ref):
+        rot = jnp.dot(grad_ref[...], basis_ref[...], preferred_element_type=jnp.float32)
+        square = (rot * rot).astype(jnp.bfloat16)
+        out_ref[0] = square
+        out_ref[1] = square
+
+    rows, width = gradients.shape
+    return pl.pallas_call(
+        kernel,
+        in_specs=[vmem()] * 2,
+        out_specs=vmem(),
+        out_shape=jax.ShapeDtypeStruct((2, rows, width), jnp.bfloat16),
+        compiler_params=pltpu.CompilerParams(vmem_limit_bytes=16 * 1024 * 1024),
+        cost_estimate=pl.CostEstimate(
+            flops=2 * rows * width * width, bytes_accessed=2 * (width + 3 * rows) * width, transcendentals=0
+        ),
+    )(gradients, basis)
+
+
+def transposed_copies(pair, c):
     chips = XH * Z
     swaps = [[f * chips + m, m * chips + f] for f in range(chips) for m in range(f + 1, chips)]
     fixed = [f * chips + f for f in range(chips)]
     groups = swaps + [[fixed[i], fixed[i + 1]] for i in range(0, chips, 2)]
     f = lax.axis_index("xh") * Z + lax.axis_index("z")
     m = lax.axis_index("xl") * Y + lax.axis_index("y")
-    got = lax.all_to_all(sent, ("xh", "z", "xl", "y"), 0, 0, axis_index_groups=groups)
-    return jnp.where(f > m, got[0], jnp.where(f < m, got[1], x))
+    got = lax.all_to_all(pair, ("xh", "z", "xl", "y"), 0, 0, axis_index_groups=groups)
+    rows, cols = pair.shape[1], pair.shape[2] // 2
+
+    def kernel(where_ref, pair_ref, got_ref, other_ref, mine_ref):
+        def copy_from(ref, block):
+            for out_ref, half in ((other_ref, 1 - where_ref[1]), (mine_ref, where_ref[1])):
+                part = ref[block, :, pl.ds(pl.multiple_of(half * cols, cols), cols)]
+                out_ref[...] = jnp.broadcast_to(part[None], out_ref.shape)
+
+        @pl.when(where_ref[0] == 0)
+        def _():
+            copy_from(pair_ref, 0)
+
+        @pl.when(where_ref[0] > 0)
+        def _():
+            copy_from(got_ref, 0)
+
+        @pl.when(where_ref[0] < 0)
+        def _():
+            copy_from(got_ref, 1)
+
+    return pl.pallas_call(
+        kernel,
+        in_specs=[pl.BlockSpec(memory_space=pltpu.SMEM), vmem(), vmem()],
+        out_specs=[vmem()] * 2,
+        out_shape=[jax.ShapeDtypeStruct((Z, rows, cols), pair.dtype)] * 2,
+        compiler_params=pltpu.CompilerParams(vmem_limit_bytes=16 * 1024 * 1024),
+        cost_estimate=pl.CostEstimate(flops=0, bytes_accessed=4 * (Z + 2) * rows * cols, transcendentals=0),
+    )(jnp.stack([f - m, c]).astype(jnp.int32), pair, got)
 
 
 def swap(x, axis):
@@ -73,10 +124,7 @@
     rows, act_width = activations.shape
     xh, xl, c = (lax.axis_index(a) for a in ("xh", "xl", "c"))
 
-    grad_rot = jnp.dot(gradients, grad_basis, preferred_element_type=jnp.float32)
-    grad_sq = (grad_rot * grad_rot).astype(jnp.bfloat16)
-    grad_pair = jnp.broadcast_to(grad_sq, (2,) + grad_sq.shape)
-    own = transpose_chips(grad_sq, grad_pair)
+    grad_pair = squared_pair(gradients, grad_basis)
 
     def rotated(act):
         blocks = act.reshape(rows, act_width // BLOCK, BLOCK)
@@ -87,13 +135,9 @@
     act_pair = jnp.stack([rotated(activations), rotated(others)])
     act_all = lax.all_gather(act_pair, "y", axis=0)
 
-    cols = own.shape[1] // 2
-
-    def gathered(half):
-        mine = lax.dynamic_slice_in_dim(own, half * cols, cols, 1)
-        return lax.all_to_all(jnp.broadcast_to(mine, (Z,) + mine.shape), "z", 0, 0)
-
-    near_other, near_mine = gathered(1 - c), gathered(c)
+    copies_other, copies_mine = transposed_copies(grad_pair, c)
+    near_other = lax.all_to_all(copies_other, "z", 0, 0)
+    near_mine = lax.all_to_all(copies_mine, "z", 0, 0)
     far_other = swap(near_other, "xh")
     far_mine = swap(near_mine, "xh")
     swapped = (xh ^ xl)[None]

time: 107 us -> 107 us (level)
  Pallas kernels: 2.5 us -> 5.28 us
  waiting for transfers between devices: 14.6 us -> 12.5 us
  matrix products: 3.13 us -> 1.79 us
    pallas_call x0 -> x2, Pallas kernels: none -> 2.79 us  [the longest x1 1.85 us: transposed_copies(): pl.pallas_call(kernel, in_specs=[pl.BlockSpec(memory_space=pltpu.SMEM), v...]
    unnamed x4 -> x8, local copies, waits for them, and re-layouts: 2.19 us -> 4.13 us
    broadcast_in_dim x3 -> x0, local copies, waits for them, and re-layouts: 1.58 us -> none  [the longest x2 0.87 us: gathered(): return lax.all_to_all(jnp.broadcast_to(mine, (Z,) + mine.shape), 'z', 0, 0)]
    dot_general x1 -> x0, matrix products: 1.35 us -> none  [per_device(): jnp.dot(gradients, grad_basis, preferred_element_type=jnp.float32)]
    ppermute x5, waiting for transfers between devices: 1.72 us -> 0.61 us  [swap(): return lax.ppermute(x, axis, [(0, 1), (1, 0)])]
  transfers between devices with their start and end apart: 8 -> 8, of which waited for: 5 -> 4; matrix products, arithmetic and copies ran while one was open for 4% -> 1% of each run, Pallas kernels for 2% -> 5%
where the time goes in v17:
time: 107 us; the launch traced here: 106 us
  starting transfers between devices  35.2 us (33%)
  blocking collectives  31.9 us (30%)
  between operations  13.5 us (13%)
  waiting for transfers between devices  12.5 us (12%)
  Pallas kernels  5.28 us (5%)
  local copies, waits for them, and re-layouts  4.3 us (4%)
  other arithmetic  2.03 us (2%)
  matrix products  1.79 us (2%)
    all_to_all x1, blocking collectives, per_device(): near_other = lax.all_to_all(copies_other, 'z', 0, 0)  31.9 us
    ppermute x5, starting transfers between devices, swap(): return lax.ppermute(x, axis, [(0, 1), (1, 0)])  25.2 us
    all_to_all x1, waiting for transfers between devices, per_device(): near_mine = lax.all_to_all(copies_mine, 'z', 0, 0)  6.5 us
    all_to_all x1, starting transfers between devices, transposed_copies(): lax.all_to_all(pair, ('xh', 'z', 'xl', 'y'), 0, 0, axis_index_groups=groups)  6.15 us
    all_to_all x1, waiting for transfers between devices, transposed_copies(): lax.all_to_all(pair, ('xh', 'z', 'xl', 'y'), 0, 0, axis_index_groups=groups)  4.85 us
    unnamed x8, local copies, waits for them, and re-layouts  4.13 us
    all_to_all x1, starting transfers between devices, per_device(): near_mine = lax.all_to_all(copies_mine, 'z', 0, 0)  3.84 us
    pallas_call x2, Pallas kernels, product(): pl.pallas_call(kernel, in_specs=[pl.BlockSpec(memory_space=pltpu.SMEM), v...  2.5 us
  transfers between devices with their start and end apart: 8, of which 4 were waited for; matrix products, arithmetic and copies ran while one was open for 1% of the time, Pallas kernels for 5%

profile of v17, /device:TPU:1, one launch (start us, length us, event | category | flops | bytes accessed | tf_op | source)
XLA Modules:
  0.0 106.5 jit_solution(2818101308128797308)
XLA Ops:
  6.5 0.0 copy-start
  6.5 4.1 %collective-permute-start = (bf16[128,1024]{1,0:T(8,128)(2,1)}, bf16[128,1024]{1,0:T(8,128)(2,1)S(1)}, u32[]{:S(2)}, u32[]{:S(2)}) collective-permute-start(bf16[128,1024]{1,0:T(8,128)(2,1)} %param.4), channel_id=1, source_target_pairs={{0,16},{16,0},{1,17},{17,1},{2,18},{18,2},{3,19},{19,3},{4,20},{20... | collective-permute-start | bytes 786440 | tf_op jit(solution)/shard_map/ppermute | solution.py:77
  10.6 1.0 copy-done.2
  11.7 0.9 copy-done.3
  12.6 0.9 shard_map.46.pair_ref
  13.5 0.0 copy-done
  13.5 1.5 %fusion = bf16[2,512,128]{2,1,0:T(8,128)(2,1)S(1)} fusion(bf16[2,512,512]{2,1,0:T(8,128)(2,1)S(1)} %copy-done, bf16[16,2,8,512]{3,2,1,0:T(8,128)(2,1)} %bitcast.22), kind=kOutput, calls=%fused_computation.2 | convolution fusion | flops 134479872 | bytes 1572864 | tf_op jit(solution)/shard_map/tbk,bkj->bjt/dot_general | solution.py:131
  15.0 0.0 collective-permute-done
  15.0 0.3 fusion.2
  15.3 0.2 copy.15
  15.5 0.8 pad_maximum_fusion
  16.3 0.0 all-gather.3.cloned.1.call-update
  16.4 6.2 %all-to-all-start = ((bf16[2,128,512]{2,1,0:T(8,128)(2,1)}), bf16[2,128,512]{2,1,0:T(8,128)(2,1)S(1)}, u32[]{:S(2)}, u32[]{:S(2)}) async-start(bf16[2,128,512]{2,1,0:T(8,128)(2,1)} %shard_map.46.pair_ref), calls=%async_computation | async-start | bytes 524288 | tf_op jit(solution)/shard_map/all_to_all | solution.py:45
  22.5 0.1 pad_add_fusion.where_ref
  22.6 4.9 %all-to-all-done.got_ref = bf16[2,128,512]{2,1,0:T(8,128)(2,1)S(1)} async-done(((bf16[2,128,512]{2,1,0:T(8,128)(2,1)}), bf16[2,128,512]{2,1,0:T(8,128)(2,1)S(1)}, u32[]{:S(2)}, u32[]{:S(2)}) %all-to-all-start) | async-done | bytes 262176 | tf_op jit(solution)/shard_map/all_to_all | solution.py:45
  27.4 1.8 %shard_map.47 = (bf16[8,128,256]{2,1,0:T(8,128)(2,1)S(1)}, bf16[8,128,256]{2,1,0:T(8,128)(2,1)}) custom-call(s32[2]{0:T(128)S(1)} %pad_add_fusion.where_ref, bf16[2,128,512]{2,1,0:T(8,128)(2,1)} %shard_map.46.pair_ref, bf16[2,128,512]{2,1,0:T(8,128)(2,1)S(1)} %all-to-all-done.got_ref), custom_call_target="tpu_custom_call" | custom-call | bytes 1310720 | tf_op jit(solution)/shard_map/pallas_call | solution.py:66
  29.3 31.9 %all_to_all.15.near_ref = bf16[8,128,256]{2,1,0:T(8,128)(2,1)S(1)} all-to-all(bf16[8,128,256]{2,1,0:T(8,128)(2,1)S(1)} %get-tuple-element.14), channel_id=1, replica_groups=mesh['xh'=2,'z'=8,'xl'=2,'y'=8,'c'=2] {'z'}, dimensions={0} | all-to-all | bytes 1048576 | tf_op jit(solution)/shard_map/all_to_all | solution.py:139
  61.2 3.8 %all-to-all-start.1 = ((bf16[8,128,256]{2,1,0:T(8,128)(2,1)}), bf16[8,128,256]{2,1,0:T(8,128)(2,1)S(1)}, u32[]{:S(2)}, u32[]{:S(2)}) async-start(bf16[8,128,256]{2,1,0:T(8,128)(2,1)} %get-tuple-element.12), calls=%async_computation.1 | async-start | bytes 1048576 | tf_op jit(solution)/shard_map/all_to_all | solution.py:140
  65.0 5.5 %collective-permute-start.2 = (bf16[8,128,256]{2,1,0:T(8,128)(2,1)S(1)}, bf16[8,128,256]{2,1,0:T(8,128)(2,1)S(1)}, u32[]{:S(2)}, u32[]{:S(2)}) collective-permute-start(bf16[8,128,256]{2,1,0:T(8,128)(2,1)S(1)} %all_to_all.15.near_ref), channel_id=1, source_target_pairs={{0,256},{256,0},{1,257},{257,1},{2,258},{258,2},{3,259},{259,3},{4... | collective-permute-start | bytes 1572872 | tf_op jit(solution)/shard_map/ppermute | solution.py:77
  70.6 6.5 %all-to-all-done.1.near_ref = bf16[8,128,256]{2,1,0:T(8,128)(2,1)S(1)} async-done(((bf16[8,128,256]{2,1,0:T(8,128)(2,1)}), bf16[8,128,256]{2,1,0:T(8,128)(2,1)S(1)}, u32[]{:S(2)}, u32[]{:S(2)}) %all-to-all-start.1) | async-done | bytes 524320 | tf_op jit(solution)/shard_map/all_to_all | solution.py:140
  77.1 5.5 %collective-permute-start.1 = (bf16[8,128,256]{2,1,0:T(8,128)(2,1)S(1)}, bf16[8,128,256]{2,1,0:T(8,128)(2,1)S(1)}, u32[]{:S(2)}, u32[]{:S(2)}) collective-permute-start(bf16[8,128,256]{2,1,0:T(8,128)(2,1)S(1)} %all-to-all-done.1.near_ref), channel_id=1, source_target_pairs={{0,256},{256,0},{1,257},{257,1},{2,258},{258,2},{3,259},{259,3},{4... | collective-permute-start | bytes 1572872 | tf_op jit(solution)/shard_map/ppermute | solution.py:77
  82.6 0.5 all-gather.3.cloned.1.call-done
  83.1 0.0 collective-permute-done.2.far_ref
  83.2 2.2 %copy-done.1 = bf16[16,1024,128]{2,1,0:T(8,128)(2,1)S(1)} copy-done((bf16[16,1024,128]{2,1,0:T(8,128)(2,1)S(1)}, bf16[16,1024,128]{2,1,0:T(8,128)(2,1)}, u32[]{:S(2)}) %copy-start.1) | copy-done | bytes 4194328
  85.3 1.2 %shard_map.49 = (f32[512,256]{1,0:T(8,128)S(1)}, f32[512,256]{1,0:T(8,128)S(1)}) custom-call(s32[1]{0:T(128)} %bitcast.swapped_ref, bf16[8,2,1024,128]{3,2,1,0:T(8,128)(2,1)S(1)} %bitcast.18, bf16[8,128,256]{2,1,0:T(8,128)(2,1)S(1)} %all_to_all.15.near_ref, bf16[8,128,256]{2,1,0:T(8,128)(2,1)S(1)} %collective-permute-done.2.far_ref), custom_call_target="tpu_custom_call" | custom-call | flops 1073741824 | bytes 6291456 | tf_op jit(solution)/shard_map/pallas_call | solution.py:109
  86.6 8.1 %collective-permute-start.3 = (f32[512,256]{1,0:T(8,128)S(1)}, f32[512,256]{1,0:T(8,128)S(1)}, u32[]{:S(2)}, u32[]{:S(2)}) collective-permute-start(f32[512,256]{1,0:T(8,128)S(1)} %get-tuple-element.15), channel_id=1, source_target_pairs={{0,1},{1,0},{2,3},{3,2},{4,5},{5,4},{6,7},{7,6},{8,9},{9,8},{10,11... | collective-permute-start | bytes 1572872 | tf_op jit(solution)/shard_map/ppermute | solution.py:77
  94.7 1.9 %collective-permute-start.4 = (f32[512,256]{1,0:T(8,128)S(1)}, f32[512,256]{1,0:T(8,128)S(1)}, u32[]{:S(2)}, u32[]{:S(2)}) collective-permute-start(f32[512,256]{1,0:T(8,128)S(1)} %get-tuple-element.16), channel_id=1, source_target_pairs={{0,1},{1,0},{2,3},{3,2},{4,5},{5,4},{6,7},{7,6},{8,9},{9,8},{10,11... | collective-permute-start | bytes 1572872 | tf_op jit(solution)/shard_map/ppermute | solution.py:77
  96.7 0.0 collective-permute-done.1.far_ref
  96.7 1.3 %shard_map.48 = f32[1024,256]{1,0:T(8,128)S(1)} custom-call(s32[1]{0:T(128)} %bitcast.swapped_ref, bf16[8,2,1024,128]{3,2,1,0:T(8,128)(2,1)S(1)} %bitcast.19, bf16[8,128,256]{2,1,0:T(8,128)(2,1)S(1)} %all-to-all-done.1.near_ref, bf16[8,128,256]{2,1,0:T(8,128)(2,1)S(1)} %collective-permute-done.1.far_ref), custom_call_target="tpu_custom_call" | custom-call | flops 1073741824 | bytes 6291456 | tf_op jit(solution)/shard_map/pallas_call | solution.py:109
  97.9 0.0 collective-permute-done.3
  97.9 0.6 collective-permute-done.4
  98.5 1.1 %fusion.3 = f32[1024,256]{1,0:T(8,128)} fusion(f32[1024,256]{1,0:T(8,128)S(1)} %shard_map.48, f32[512,256]{1,0:T(8,128)S(1)} %collective-permute-done.4, f32[512,256]{1,0:T(8,128)S(1)} %collective-permute-done.3), kind=kLoop, calls=%fused_computation.6 | loop fusion | flops 786432 | bytes 3145728 | tf_op jit(solution)/shard_map/div | solution.py:148
  (4 shorter events, 0.0 us)
Async XLA Ops:
  6.5 7.0 %copy-start = (bf16[2,512,512]{2,1,0:T(8,128)(2,1)S(1)}, bf16[2,512,512]{2,1,0:T(8,128)(2,1)}, u32[]{:S(2)}) copy-start(bf16[2,512,512]{2,1,0:T(8,128)(2,1)} %param.5) | copy-start | bytes 3145732
  6.5 76.6 %all-gather.3.cloned.1.call-start = ((), (), s32[]{:S(2)}) async-start(), calls=%async_computation.3 | async-start | bytes 4718592 | tf_op jit(solution)/shard_map/all_gather | solution.py:136
  6.5 8.5 %collective-permute-start = (bf16[128,1024]{1,0:T(8,128)(2,1)}, bf16[128,1024]{1,0:T(8,128)(2,1)S(1)}, u32[]{:S(2)}, u32[]{:S(2)}) collective-permute-start(bf16[128,1024]{1,0:T(8,128)(2,1)} %param.4), channel_id=1, source_target_pairs={{0,16},{16,0},{1,17},{17,1},{2,18},{18,2},{3,19},{19,3},{4,20},{20... | collective-permute-start | bytes 786440 | tf_op jit(solution)/shard_map/ppermute | solution.py:77
  10.6 1.0 copy-start.2
  11.7 0.9 copy-start.3
  16.4 11.1 %all-to-all-start = ((bf16[2,128,512]{2,1,0:T(8,128)(2,1)}), bf16[2,128,512]{2,1,0:T(8,128)(2,1)S(1)}, u32[]{:S(2)}, u32[]{:S(2)}) async-start(bf16[2,128,512]{2,1,0:T(8,128)(2,1)} %shard_map.46.pair_ref), calls=%async_computation | async-start | bytes 524288 | tf_op jit(solution)/shard_map/all_to_all | solution.py:45
  61.2 15.9 %all-to-all-start.1 = ((bf16[8,128,256]{2,1,0:T(8,128)(2,1)}), bf16[8,128,256]{2,1,0:T(8,128)(2,1)S(1)}, u32[]{:S(2)}, u32[]{:S(2)}) async-start(bf16[8,128,256]{2,1,0:T(8,128)(2,1)} %get-tuple-element.12), calls=%async_computation.1 | async-start | bytes 1048576 | tf_op jit(solution)/shard_map/all_to_all | solution.py:140
  65.0 18.1 %collective-permute-start.2 = (bf16[8,128,256]{2,1,0:T(8,128)(2,1)S(1)}, bf16[8,128,256]{2,1,0:T(8,128)(2,1)S(1)}, u32[]{:S(2)}, u32[]{:S(2)}) collective-permute-start(bf16[8,128,256]{2,1,0:T(8,128)(2,1)S(1)} %all_to_all.15.near_ref), channel_id=1, source_target_pairs={{0,256},{256,0},{1,257},{257,1},{2,258},{258,2},{3,259},{259,3},{4... | collective-permute-start | bytes 1572872 | tf_op jit(solution)/shard_map/ppermute | solution.py:77
  77.1 19.6 %collective-permute-start.1 = (bf16[8,128,256]{2,1,0:T(8,128)(2,1)S(1)}, bf16[8,128,256]{2,1,0:T(8,128)(2,1)S(1)}, u32[]{:S(2)}, u32[]{:S(2)}) collective-permute-start(bf16[8,128,256]{2,1,0:T(8,128)(2,1)S(1)} %all-to-all-done.1.near_ref), channel_id=1, source_target_pairs={{0,256},{256,0},{1,257},{257,1},{2,258},{258,2},{3,259},{259,3},{4... | collective-permute-start | bytes 1572872 | tf_op jit(solution)/shard_map/ppermute | solution.py:77
  83.1 2.2 %copy-start.1 = (bf16[16,1024,128]{2,1,0:T(8,128)(2,1)S(1)}, bf16[16,1024,128]{2,1,0:T(8,128)(2,1)}, u32[]{:S(2)}) copy-start(bf16[16,1024,128]{2,1,0:T(8,128)(2,1)} %all-gather.3.cloned.1.call-done) | copy-start | bytes 12582916
  86.6 11.3 %collective-permute-start.3 = (f32[512,256]{1,0:T(8,128)S(1)}, f32[512,256]{1,0:T(8,128)S(1)}, u32[]{:S(2)}, u32[]{:S(2)}) collective-permute-start(f32[512,256]{1,0:T(8,128)S(1)} %get-tuple-element.15), channel_id=1, source_target_pairs={{0,1},{1,0},{2,3},{3,2},{4,5},{5,4},{6,7},{7,6},{8,9},{9,8},{10,11... | collective-permute-start | bytes 1572872 | tf_op jit(solution)/shard_map/ppermute | solution.py:77
  94.7 3.8 %collective-permute-start.4 = (f32[512,256]{1,0:T(8,128)S(1)}, f32[512,256]{1,0:T(8,128)S(1)}, u32[]{:S(2)}, u32[]{:S(2)}) collective-permute-start(f32[512,256]{1,0:T(8,128)S(1)} %get-tuple-element.16), channel_id=1, source_target_pairs={{0,1},{1,0},{2,3},{3,2},{4,5},{5,4},{6,7},{7,6},{8,9},{9,8},{10,11... | collective-permute-start | bytes 1572872 | tf_op jit(solution)/shard_map/ppermute | solution.py:77
Sparse Core Ops, SparseCore 0:
  16.5 66.6 all-gather.2

commit v18 on v14

--- a/solution.py
+++ b/solution.py
@@ -9,6 +9,30 @@
 BLOCK = 512
 TOKENS = 4096
 XH, Z, XL, Y, C = 2, 8, 2, 8, 2
+
+
+def vmem():
+    return pl.BlockSpec(memory_space=pltpu.VMEM)
+
+
+def squared_pair(gradients, basis):
+    def kernel(grad_ref, basis_ref, out_ref):
+        rot = jnp.dot(grad_ref[...], basis_ref[...], preferred_element_type=jnp.float32)
+        square = (rot * rot).astype(jnp.bfloat16)
+        out_ref[0] = square
+        out_ref[1] = square
+
+    rows, width = gradients.shape
+    return pl.pallas_call(
+        kernel,
+        in_specs=[vmem()] * 2,
+        out_specs=vmem(),
+        out_shape=jax.ShapeDtypeStruct((2, rows, width), jnp.bfloat16),
+        compiler_params=pltpu.CompilerParams(vmem_limit_bytes=16 * 1024 * 1024),
+        cost_estimate=pl.CostEstimate(
+            flops=2 * rows * width * width, bytes_accessed=2 * (width + 3 * rows) * width, transcendentals=0
+        ),
+    )(gradients, basis)
 
 
 def transpose_chips(x, sent):
@@ -73,10 +97,7 @@
     rows, act_width = activations.shape
     xh, xl, c = (lax.axis_index(a) for a in ("xh", "xl", "c"))
 
-    grad_rot = jnp.dot(gradients, grad_basis, preferred_element_type=jnp.float32)
-    grad_sq = (grad_rot * grad_rot).astype(jnp.bfloat16)
-    grad_pair = jnp.broadcast_to(grad_sq, (2,) + grad_sq.shape)
-    own = transpose_chips(grad_sq, grad_pair)
+    grad_pair = squared_pair(gradients, grad_basis)
 
     def rotated(act):
         blocks = act.reshape(rows, act_width // BLOCK, BLOCK)
@@ -87,6 +108,7 @@
     act_pair = jnp.stack([rotated(activations), rotated(others)])
     act_all = lax.all_gather(act_pair, "y", axis=0)
 
+    own = transpose_chips(grad_pair[0], grad_pair)
     cols = own.shape[1] // 2
 
     def gathered(half):

time: 107 us -> 107 us (level)
  waiting for transfers between devices: 14.6 us -> 12.6 us
  matrix products: 3.13 us -> 1.79 us
  local copies, waits for them, and re-layouts: 3.96 us -> 5.18 us
    unnamed x4 -> x8, local copies, waits for them, and re-layouts: 2.19 us -> 4.13 us
    dot_general x1 -> x0, matrix products: 1.35 us -> none  [per_device(): jnp.dot(gradients, grad_basis, preferred_element_type=jnp.float32)]
    ppermute x5, waiting for transfers between devices: 1.72 us -> 0.61 us  [swap(): return lax.ppermute(x, axis, [(0, 1), (1, 0)])]
  transfers between devices with their start and end apart: 8 -> 8, of which waited for: 5 -> 4; matrix products, arithmetic and copies ran while one was open for 4% -> 3% of each run, Pallas kernels for 2% -> 3%
where the time goes in v18:
time: 107 us; the launch traced here: 106 us
  starting transfers between devices  35.2 us (33%)
  blocking collectives  31.9 us (30%)
  between operations  13.5 us (13%)
  waiting for transfers between devices  12.6 us (12%)
  local copies, waits for them, and re-layouts  5.18 us (5%)
  Pallas kernels  3.44 us (3%)
  other arithmetic  2.88 us (3%)
  matrix products  1.79 us (2%)
    all_to_all x1, blocking collectives, gathered(): return lax.all_to_all(jnp.broadcast_to(mine, (Z,) + mine.shape), 'z', 0, 0)  31.9 us
    ppermute x5, starting transfers between devices, swap(): return lax.ppermute(x, axis, [(0, 1), (1, 0)])  25.2 us
    all_to_all x1, waiting for transfers between devices, gathered(): return lax.all_to_all(jnp.broadcast_to(mine, (Z,) + mine.shape), 'z', 0, 0)  6.51 us
    all_to_all x1, starting transfers between devices, transpose_chips(): lax.all_to_all(sent, ('xh', 'z', 'xl', 'y'), 0, 0, axis_index_groups=groups)  6.15 us
    all_to_all x1, waiting for transfers between devices, transpose_chips(): lax.all_to_all(sent, ('xh', 'z', 'xl', 'y'), 0, 0, axis_index_groups=groups)  4.93 us
    unnamed x8, local copies, waits for them, and re-layouts  4.13 us
    all_to_all x1, starting transfers between devices, gathered(): return lax.all_to_all(jnp.broadcast_to(mine, (Z,) + mine.shape), 'z', 0, 0)  3.84 us
    pallas_call x2, Pallas kernels, product(): pl.pallas_call(kernel, in_specs=[pl.BlockSpec(memory_space=pltpu.SMEM), v...  2.5 us
  transfers between devices with their start and end apart: 8, of which 4 were waited for; matrix products, arithmetic and copies ran while one was open for 3% of the time, Pallas kernels for 3%

profile of v18, /device:TPU:1, one launch (start us, length us, event | category | flops | bytes accessed | tf_op | source)
XLA Modules:
  0.0 106.5 jit_solution(11345518207642632459)
XLA Ops:
  6.5 0.0 copy-start
  6.5 4.1 %collective-permute-start = (bf16[128,1024]{1,0:T(8,128)(2,1)}, bf16[128,1024]{1,0:T(8,128)(2,1)S(1)}, u32[]{:S(2)}, u32[]{:S(2)}) collective-permute-start(bf16[128,1024]{1,0:T(8,128)(2,1)} %param.4), channel_id=1, source_target_pairs={{0,16},{16,0},{1,17},{17,1},{2,18},{18,2},{3,19},{19,3},{4,20},{20... | collective-permute-start | bytes 786440 | tf_op jit(solution)/shard_map/ppermute | solution.py:50
  10.6 1.0 copy-done.2
  11.7 0.9 copy-done.3
  12.6 0.9 shard_map.46
  13.5 0.0 copy-done
  13.5 1.5 %fusion = bf16[2,512,128]{2,1,0:T(8,128)(2,1)S(1)} fusion(bf16[2,512,512]{2,1,0:T(8,128)(2,1)S(1)} %copy-done, bf16[16,2,8,512]{3,2,1,0:T(8,128)(2,1)} %bitcast.24), kind=kOutput, calls=%fused_computation.2 | convolution fusion | flops 134479872 | bytes 1572864 | tf_op jit(solution)/shard_map/tbk,bkj->bjt/dot_general | solution.py:104
  15.0 0.0 collective-permute-done
  15.0 0.3 fusion.2
  15.3 0.2 copy.15
  15.5 0.8 pad_maximum_fusion
  16.3 0.0 all-gather.3.cloned.1.call-update
  16.4 6.2 %all-to-all-start = ((bf16[2,128,512]{2,1,0:T(8,128)(2,1)}), bf16[2,128,512]{2,1,0:T(8,128)(2,1)S(1)}, u32[]{:S(2)}, u32[]{:S(2)}) async-start(bf16[2,128,512]{2,1,0:T(8,128)(2,1)} %shard_map.46), calls=%async_computation | async-start | bytes 524288 | tf_op jit(solution)/shard_map/all_to_all | solution.py:45
  22.5 4.9 %all-to-all-done = bf16[2,128,512]{2,1,0:T(8,128)(2,1)S(1)} async-done(((bf16[2,128,512]{2,1,0:T(8,128)(2,1)}), bf16[2,128,512]{2,1,0:T(8,128)(2,1)S(1)}, u32[]{:S(2)}, u32[]{:S(2)}) %all-to-all-start) | async-done | bytes 262176 | tf_op jit(solution)/shard_map/all_to_all | solution.py:45
  27.4 0.9 fusion.8
  28.4 31.9 %all_to_all.15.near_ref = bf16[8,128,256]{2,1,0:T(8,128)(2,1)S(1)} all-to-all(bf16[8,128,256]{2,1,0:T(8,128)(2,1)S(1)} %broadcast_in_dim.11), channel_id=1, replica_groups=mesh['xh'=2,'z'=8,'xl'=2,'y'=8,'c'=2] {'z'}, dimensions={0} | all-to-all | bytes 1048576 | tf_op jit(solution)/shard_map/all_to_all | solution.py:116
  60.3 0.8 broadcast_in_dim.10
  61.2 3.8 %all-to-all-start.1 = ((bf16[8,128,256]{2,1,0:T(8,128)(2,1)}), bf16[8,128,256]{2,1,0:T(8,128)(2,1)S(1)}, u32[]{:S(2)}, u32[]{:S(2)}) async-start(bf16[8,128,256]{2,1,0:T(8,128)(2,1)} %broadcast_in_dim.10), calls=%async_computation.1 | async-start | bytes 1048576 | tf_op jit(solution)/shard_map/all_to_all | solution.py:116
  65.0 5.5 %collective-permute-start.2 = (bf16[8,128,256]{2,1,0:T(8,128)(2,1)S(1)}, bf16[8,128,256]{2,1,0:T(8,128)(2,1)S(1)}, u32[]{:S(2)}, u32[]{:S(2)}) collective-permute-start(bf16[8,128,256]{2,1,0:T(8,128)(2,1)S(1)} %all_to_all.15.near_ref), channel_id=1, source_target_pairs={{0,256},{256,0},{1,257},{257,1},{2,258},{258,2},{3,259},{259,3},{4... | collective-permute-start | bytes 1572872 | tf_op jit(solution)/shard_map/ppermute | solution.py:50
  70.5 6.5 %all-to-all-done.1.near_ref = bf16[8,128,256]{2,1,0:T(8,128)(2,1)S(1)} async-done(((bf16[8,128,256]{2,1,0:T(8,128)(2,1)}), bf16[8,128,256]{2,1,0:T(8,128)(2,1)S(1)}, u32[]{:S(2)}, u32[]{:S(2)}) %all-to-all-start.1) | async-done | bytes 524320 | tf_op jit(solution)/shard_map/all_to_all | solution.py:116
  77.1 5.5 %collective-permute-start.1 = (bf16[8,128,256]{2,1,0:T(8,128)(2,1)S(1)}, bf16[8,128,256]{2,1,0:T(8,128)(2,1)S(1)}, u32[]{:S(2)}, u32[]{:S(2)}) collective-permute-start(bf16[8,128,256]{2,1,0:T(8,128)(2,1)S(1)} %all-to-all-done.1.near_ref), channel_id=1, source_target_pairs={{0,256},{256,0},{1,257},{257,1},{2,258},{258,2},{3,259},{259,3},{4... | collective-permute-start | bytes 1572872 | tf_op jit(solution)/shard_map/ppermute | solution.py:50
  82.6 0.5 all-gather.3.cloned.1.call-done
  83.1 0.0 collective-permute-done.2.far_ref
  83.2 2.2 %copy-done.1 = bf16[16,1024,128]{2,1,0:T(8,128)(2,1)S(1)} copy-done((bf16[16,1024,128]{2,1,0:T(8,128)(2,1)S(1)}, bf16[16,1024,128]{2,1,0:T(8,128)(2,1)}, u32[]{:S(2)}) %copy-start.1) | copy-done | bytes 4194328
  85.3 1.2 %shard_map.48 = (f32[512,256]{1,0:T(8,128)S(1)}, f32[512,256]{1,0:T(8,128)S(1)}) custom-call(s32[1]{0:T(128)} %bitcast.swapped_ref, bf16[8,2,1024,128]{3,2,1,0:T(8,128)(2,1)S(1)} %bitcast.20, bf16[8,128,256]{2,1,0:T(8,128)(2,1)S(1)} %all_to_all.15.near_ref, bf16[8,128,256]{2,1,0:T(8,128)(2,1)S(1)} %collective-permute-done.2.far_ref), custom_call_target="tpu_custom_call" | custom-call | flops 1073741824 | bytes 6291456 | tf_op jit(solution)/shard_map/pallas_call | solution.py:82
  86.6 8.1 %collective-permute-start.3 = (f32[512,256]{1,0:T(8,128)S(1)}, f32[512,256]{1,0:T(8,128)S(1)}, u32[]{:S(2)}, u32[]{:S(2)}) collective-permute-start(f32[512,256]{1,0:T(8,128)S(1)} %get-tuple-element.11), channel_id=1, source_target_pairs={{0,1},{1,0},{2,3},{3,2},{4,5},{5,4},{6,7},{7,6},{8,9},{9,8},{10,11... | collective-permute-start | bytes 1572872 | tf_op jit(solution)/shard_map/ppermute | solution.py:50
  94.7 1.9 %collective-permute-start.4 = (f32[512,256]{1,0:T(8,128)S(1)}, f32[512,256]{1,0:T(8,128)S(1)}, u32[]{:S(2)}, u32[]{:S(2)}) collective-permute-start(f32[512,256]{1,0:T(8,128)S(1)} %get-tuple-element.12), channel_id=1, source_target_pairs={{0,1},{1,0},{2,3},{3,2},{4,5},{5,4},{6,7},{7,6},{8,9},{9,8},{10,11... | collective-permute-start | bytes 1572872 | tf_op jit(solution)/shard_map/ppermute | solution.py:50
  96.6 0.0 collective-permute-done.1.far_ref
  96.7 1.3 %shard_map.47 = f32[1024,256]{1,0:T(8,128)S(1)} custom-call(s32[1]{0:T(128)} %bitcast.swapped_ref, bf16[8,2,1024,128]{3,2,1,0:T(8,128)(2,1)S(1)} %bitcast.21, bf16[8,128,256]{2,1,0:T(8,128)(2,1)S(1)} %all-to-all-done.1.near_ref, bf16[8,128,256]{2,1,0:T(8,128)(2,1)S(1)} %collective-permute-done.1.far_ref), custom_call_target="tpu_custom_call" | custom-call | flops 1073741824 | bytes 6291456 | tf_op jit(solution)/shard_map/pallas_call | solution.py:82
  97.9 0.0 collective-permute-done.3
  97.9 0.6 collective-permute-done.4
  98.5 1.1 %fusion.3 = f32[1024,256]{1,0:T(8,128)} fusion(f32[1024,256]{1,0:T(8,128)S(1)} %shard_map.47, f32[512,256]{1,0:T(8,128)S(1)} %collective-permute-done.4, f32[512,256]{1,0:T(8,128)S(1)} %collective-permute-done.3), kind=kLoop, calls=%fused_computation.6 | loop fusion | flops 786432 | bytes 3145728 | tf_op jit(solution)/shard_map/div | solution.py:126
  (6 shorter events, 0.1 us)
Async XLA Ops:
  6.5 7.0 %copy-start = (bf16[2,512,512]{2,1,0:T(8,128)(2,1)S(1)}, bf16[2,512,512]{2,1,0:T(8,128)(2,1)}, u32[]{:S(2)}) copy-start(bf16[2,512,512]{2,1,0:T(8,128)(2,1)} %param.5) | copy-start | bytes 3145732
  6.5 76.6 %all-gather.3.cloned.1.call-start = ((), (), s32[]{:S(2)}) async-start(), calls=%async_computation.3 | async-start | bytes 4718592 | tf_op jit(solution)/shard_map/all_gather | solution.py:109
  6.5 8.5 %collective-permute-start = (bf16[128,1024]{1,0:T(8,128)(2,1)}, bf16[128,1024]{1,0:T(8,128)(2,1)S(1)}, u32[]{:S(2)}, u32[]{:S(2)}) collective-permute-start(bf16[128,1024]{1,0:T(8,128)(2,1)} %param.4), channel_id=1, source_target_pairs={{0,16},{16,0},{1,17},{17,1},{2,18},{18,2},{3,19},{19,3},{4,20},{20... | collective-permute-start | bytes 786440 | tf_op jit(solution)/shard_map/ppermute | solution.py:50
  10.6 1.0 copy-start.2
  11.7 0.9 copy-start.3
  16.4 11.1 %all-to-all-start = ((bf16[2,128,512]{2,1,0:T(8,128)(2,1)}), bf16[2,128,512]{2,1,0:T(8,128)(2,1)S(1)}, u32[]{:S(2)}, u32[]{:S(2)}) async-start(bf16[2,128,512]{2,1,0:T(8,128)(2,1)} %shard_map.46), calls=%async_computation | async-start | bytes 524288 | tf_op jit(solution)/shard_map/all_to_all | solution.py:45
  61.2 15.9 %all-to-all-start.1 = ((bf16[8,128,256]{2,1,0:T(8,128)(2,1)}), bf16[8,128,256]{2,1,0:T(8,128)(2,1)S(1)}, u32[]{:S(2)}, u32[]{:S(2)}) async-start(bf16[8,128,256]{2,1,0:T(8,128)(2,1)} %broadcast_in_dim.10), calls=%async_computation.1 | async-start | bytes 1048576 | tf_op jit(solution)/shard_map/all_to_all | solution.py:116
  65.0 18.2 %collective-permute-start.2 = (bf16[8,128,256]{2,1,0:T(8,128)(2,1)S(1)}, bf16[8,128,256]{2,1,0:T(8,128)(2,1)S(1)}, u32[]{:S(2)}, u32[]{:S(2)}) collective-permute-start(bf16[8,128,256]{2,1,0:T(8,128)(2,1)S(1)} %all_to_all.15.near_ref), channel_id=1, source_target_pairs={{0,256},{256,0},{1,257},{257,1},{2,258},{258,2},{3,259},{259,3},{4... | collective-permute-start | bytes 1572872 | tf_op jit(solution)/shard_map/ppermute | solution.py:50
  77.1 19.6 %collective-permute-start.1 = (bf16[8,128,256]{2,1,0:T(8,128)(2,1)S(1)}, bf16[8,128,256]{2,1,0:T(8,128)(2,1)S(1)}, u32[]{:S(2)}, u32[]{:S(2)}) collective-permute-start(bf16[8,128,256]{2,1,0:T(8,128)(2,1)S(1)} %all-to-all-done.1.near_ref), channel_id=1, source_target_pairs={{0,256},{256,0},{1,257},{257,1},{2,258},{258,2},{3,259},{259,3},{4... | collective-permute-start | bytes 1572872 | tf_op jit(solution)/shard_map/ppermute | solution.py:50
  83.1 2.2 %copy-start.1 = (bf16[16,1024,128]{2,1,0:T(8,128)(2,1)S(1)}, bf16[16,1024,128]{2,1,0:T(8,128)(2,1)}, u32[]{:S(2)}) copy-start(bf16[16,1024,128]{2,1,0:T(8,128)(2,1)} %all-gather.3.cloned.1.call-done) | copy-start | bytes 12582916
  86.6 11.3 %collective-permute-start.3 = (f32[512,256]{1,0:T(8,128)S(1)}, f32[512,256]{1,0:T(8,128)S(1)}, u32[]{:S(2)}, u32[]{:S(2)}) collective-permute-start(f32[512,256]{1,0:T(8,128)S(1)} %get-tuple-element.11), channel_id=1, source_target_pairs={{0,1},{1,0},{2,3},{3,2},{4,5},{5,4},{6,7},{7,6},{8,9},{9,8},{10,11... | collective-permute-start | bytes 1572872 | tf_op jit(solution)/shard_map/ppermute | solution.py:50
  94.7 3.8 %collective-permute-start.4 = (f32[512,256]{1,0:T(8,128)S(1)}, f32[512,256]{1,0:T(8,128)S(1)}, u32[]{:S(2)}, u32[]{:S(2)}) collective-permute-start(f32[512,256]{1,0:T(8,128)S(1)} %get-tuple-element.12), channel_id=1, source_target_pairs={{0,1},{1,0},{2,3},{3,2},{4,5},{5,4},{6,7},{7,6},{8,9},{9,8},{10,11... | collective-permute-start | bytes 1572872 | tf_op jit(solution)/shard_map/ppermute | solution.py:50
Sparse Core Ops, SparseCore 0:
  16.5 66.6 all-gather.2

commit v19 on v14

--- a/solution.py
+++ b/solution.py
@@ -26,12 +26,14 @@
     return lax.ppermute(x, axis, [(0, 1), (1, 0)])
 
 
-def product(swapped, act_all, near, far, parts):
+def product(swapped, act_all, near, far, got=()):
     _, _, width, rows = act_all.shape
     cols = near.shape[2]
     tile = width // 2
 
-    def kernel(swapped_ref, act_ref, near_ref, far_ref, *out_refs):
+    def kernel(swapped_ref, act_ref, near_ref, far_ref, *refs):
+        got_refs, out_refs = refs[: len(got)], refs[len(got) :]
+
         def go(blocks):
             for t in range(width // tile):
                 at = slice(t * tile, (t + 1) * tile)
@@ -41,8 +43,8 @@
                     grad = jnp.concatenate([blocks[pair][y] for y in range(Y)], axis=0)
                     part = jnp.dot(act, grad, preferred_element_type=jnp.float32)
                     total = part if total is None else total + part
-                if parts == 1:
-                    out_refs[0][at] = total
+                if got:
+                    out_refs[0][at] = (total + got_refs[t][...]) * (1.0 / TOKENS)
                 else:
                     out_refs[t][...] = total
 
@@ -55,9 +57,10 @@
             go((far_ref, near_ref))
 
     vmem = pl.BlockSpec(memory_space=pltpu.VMEM)
+    parts = 1 if got else 2
     return pl.pallas_call(
         kernel,
-        in_specs=[pl.BlockSpec(memory_space=pltpu.SMEM), vmem, vmem, vmem],
+        in_specs=[pl.BlockSpec(memory_space=pltpu.SMEM)] + [vmem] * (3 + len(got)),
         out_specs=[vmem] * parts,
         out_shape=[jax.ShapeDtypeStruct((width // parts, cols), jnp.float32)] * parts,
         compiler_params=pltpu.CompilerParams(vmem_limit_bytes=16 * 1024 * 1024),
@@ -66,7 +69,7 @@
             bytes_accessed=act_all.size * 2 + near.size * 4 + width * cols * 4,
             transcendentals=0,
         ),
-    )(swapped, act_all, near, far)
+    )(swapped, act_all, near, far, *got)
 
 
 def per_device(activations, act_basis, gradients, grad_basis):
@@ -98,10 +101,10 @@
     far_mine = swap(near_mine, "xh")
     swapped = (xh ^ xl)[None]
     act_all, _ = lax.optimization_barrier((act_all, near_mine))
-    other = product(swapped, act_all, near_other, far_other, 2)
+    other = product(swapped, act_all, near_other, far_other)
     got = [swap(part, "c") for part in other]
-    (mine,) = product(swapped, act_all, near_mine, far_mine, 1)
-    return (mine + jnp.concatenate(got)) / TOKENS
+    (moments,) = product(swapped, act_all, near_mine, far_mine, got)
+    return moments
 
 
 def solution(mesh):

time: 107 us -> 108 us (level)
  waiting for transfers between devices: 14.6 us -> 15.9 us
  other arithmetic: 1.97 us -> 0.87 us
    ppermute x5, waiting for transfers between devices: 1.72 us -> 2.97 us  [swap(): return lax.ppermute(x, axis, [(0, 1), (1, 0)])]
    div x1 -> x0, other arithmetic: 1.11 us -> none  [per_device(): return (mine + jnp.concatenate(got)) / TOKENS]
  transfers between devices with their start and end apart: 8 -> 8, of which waited for: 5 -> 5; matrix products, arithmetic and copies ran while one was open for 4% -> 3% of each run, Pallas kernels for 2% -> 1%
where the time goes in v19:
time: 108 us; the launch traced here: 107 us
  starting transfers between devices  34.7 us (32%)
  blocking collectives  31.9 us (30%)
  waiting for transfers between devices  15.9 us (15%)
  between operations  13.5 us (12%)
  local copies, waits for them, and re-layouts  3.96 us (4%)
  Pallas kernels  3.51 us (3%)
  matrix products  3.13 us (3%)
    all_to_all x1, blocking collectives, gathered(): return lax.all_to_all(jnp.broadcast_to(mine, (Z,) + mine.shape), 'z', 0, 0)  31.9 us
    ppermute x5, starting transfers between devices, swap(): return lax.ppermute(x, axis, [(0, 1), (1, 0)])  24.3 us
    all_to_all x1, starting transfers between devices, transpose_chips(): lax.all_to_all(sent, ('xh', 'z', 'xl', 'y'), 0, 0, axis_index_groups=groups)  6.58 us
    all_to_all x1, waiting for transfers between devices, gathered(): return lax.all_to_all(jnp.broadcast_to(mine, (Z,) + mine.shape), 'z', 0, 0)  6.51 us
    all_to_all x1, waiting for transfers between devices, transpose_chips(): lax.all_to_all(sent, ('xh', 'z', 'xl', 'y'), 0, 0, axis_index_groups=groups)  4.93 us
    all_to_all x1, starting transfers between devices, gathered(): return lax.all_to_all(jnp.broadcast_to(mine, (Z,) + mine.shape), 'z', 0, 0)  3.84 us
    pallas_call x2, Pallas kernels, product(): pl.pallas_call(kernel, in_specs=[pl.BlockSpec(memory_space=pltpu.SMEM)] +...  3.51 us
    ppermute x5, waiting for transfers between devices, swap(): return lax.ppermute(x, axis, [(0, 1), (1, 0)])  2.97 us
  transfers between devices with their start and end apart: 8, of which 5 were waited for; matrix products, arithmetic and copies ran while one was open for 3% of the time, Pallas kernels for 1%

profile of v19, /device:TPU:1, one launch (start us, length us, event | category | flops | bytes accessed | tf_op | source)
XLA Modules:
  0.0 107.4 jit_solution(1790565386609003935)
XLA Ops:
  6.5 0.0 copy-start
  6.5 0.0 all-gather.3.cloned.1.call-start
  6.5 4.1 %collective-permute-start = (bf16[128,1024]{1,0:T(8,128)(2,1)}, bf16[128,1024]{1,0:T(8,128)(2,1)S(1)}, u32[]{:S(2)}, u32[]{:S(2)}) collective-permute-start(bf16[128,1024]{1,0:T(8,128)(2,1)} %param.4), channel_id=1, source_target_pairs={{0,16},{16,0},{1,17},{17,1},{2,18},{18,2},{3,19},{19,3},{4,20},{20... | collective-permute-start | bytes 786440 | tf_op jit(solution)/shard_map/ppermute | solution.py:26
  10.6 1.3 %fusion.3 = bf16[128,512]{1,0:T(8,128)(2,1)S(1)} fusion(bf16[128,512]{1,0:T(8,128)(2,1)} %param.6, bf16[512,512]{1,0:T(8,128)(2,1)} %param.7), kind=kOutput, calls=%fused_computation.6 | convolution fusion | flops 67239936 | bytes 786432 | tf_op jit(solution)/shard_map/dot_general | solution.py:79
  12.0 0.0 copy-done
  12.0 1.5 %fusion = bf16[2,512,128]{2,1,0:T(8,128)(2,1)S(1)} fusion(bf16[2,512,512]{2,1,0:T(8,128)(2,1)S(1)} %copy-done, bf16[16,2,8,512]{3,2,1,0:T(8,128)(2,1)} %bitcast.32), kind=kOutput, calls=%fused_computation.2 | convolution fusion | flops 134479872 | bytes 1572864 | tf_op jit(solution)/shard_map/tbk,bkj->bjt/dot_general | solution.py:86
  13.5 1.1 %collective-permute-done = bf16[128,1024]{1,0:T(8,128)(2,1)S(1)} collective-permute-done((bf16[128,1024]{1,0:T(8,128)(2,1)}, bf16[128,1024]{1,0:T(8,128)(2,1)S(1)}, u32[]{:S(2)}, u32[]{:S(2)}) %collective-permute-start) | collective-permute-done | bytes 262176 | tf_op jit(solution)/shard_map/ppermute | solution.py:26
  14.6 0.7 broadcast_in_dim.13
  15.3 0.3 fusion.2
  15.6 0.2 copy.15
  15.8 0.8 pad_maximum_fusion
  16.6 0.0 all-gather.3.cloned.1.call-update
  16.7 6.6 %all-to-all-start = ((bf16[2,128,512]{2,1,0:T(8,128)(2,1)}), bf16[2,128,512]{2,1,0:T(8,128)(2,1)S(1)}, u32[]{:S(2)}, u32[]{:S(2)}) async-start(bf16[2,128,512]{2,1,0:T(8,128)(2,1)} %broadcast_in_dim.13), calls=%async_computation | async-start | bytes 524288 | tf_op jit(solution)/shard_map/all_to_all | solution.py:21
  23.2 4.9 %all-to-all-done = bf16[2,128,512]{2,1,0:T(8,128)(2,1)S(1)} async-done(((bf16[2,128,512]{2,1,0:T(8,128)(2,1)}), bf16[2,128,512]{2,1,0:T(8,128)(2,1)S(1)}, u32[]{:S(2)}, u32[]{:S(2)}) %all-to-all-start) | async-done | bytes 262176 | tf_op jit(solution)/shard_map/all_to_all | solution.py:21
  28.3 31.9 %all_to_all.15.near_ref = bf16[8,128,256]{2,1,0:T(8,128)(2,1)S(1)} all-to-all(bf16[8,128,256]{2,1,0:T(8,128)(2,1)S(1)} %broadcast_in_dim.15), channel_id=1, replica_groups=mesh['xh'=2,'z'=8,'xl'=2,'y'=8,'c'=2] {'z'}, dimensions={0} | all-to-all | bytes 1048576 | tf_op jit(solution)/shard_map/all_to_all | solution.py:97
  60.1 0.8 broadcast_in_dim.14
  61.0 3.8 %all-to-all-start.1 = ((bf16[8,128,256]{2,1,0:T(8,128)(2,1)}), bf16[8,128,256]{2,1,0:T(8,128)(2,1)S(1)}, u32[]{:S(2)}, u32[]{:S(2)}) async-start(bf16[8,128,256]{2,1,0:T(8,128)(2,1)} %broadcast_in_dim.14), calls=%async_computation.1 | async-start | bytes 1048576 | tf_op jit(solution)/shard_map/all_to_all | solution.py:97
  64.8 5.5 %collective-permute-start.2 = (bf16[8,128,256]{2,1,0:T(8,128)(2,1)S(1)}, bf16[8,128,256]{2,1,0:T(8,128)(2,1)S(1)}, u32[]{:S(2)}, u32[]{:S(2)}) collective-permute-start(bf16[8,128,256]{2,1,0:T(8,128)(2,1)S(1)} %all_to_all.15.near_ref), channel_id=1, source_target_pairs={{0,256},{256,0},{1,257},{257,1},{2,258},{258,2},{3,259},{259,3},{4... | collective-permute-start | bytes 1572872 | tf_op jit(solution)/shard_map/ppermute | solution.py:26
  70.4 6.5 %all-to-all-done.1.near_ref = bf16[8,128,256]{2,1,0:T(8,128)(2,1)S(1)} async-done(((bf16[8,128,256]{2,1,0:T(8,128)(2,1)}), bf16[8,128,256]{2,1,0:T(8,128)(2,1)S(1)}, u32[]{:S(2)}, u32[]{:S(2)}) %all-to-all-start.1) | async-done | bytes 524320 | tf_op jit(solution)/shard_map/all_to_all | solution.py:97
  76.9 5.5 %collective-permute-start.1 = (bf16[8,128,256]{2,1,0:T(8,128)(2,1)S(1)}, bf16[8,128,256]{2,1,0:T(8,128)(2,1)S(1)}, u32[]{:S(2)}, u32[]{:S(2)}) collective-permute-start(bf16[8,128,256]{2,1,0:T(8,128)(2,1)S(1)} %all-to-all-done.1.near_ref), channel_id=1, source_target_pairs={{0,256},{256,0},{1,257},{257,1},{2,258},{258,2},{3,259},{259,3},{4... | collective-permute-start | bytes 1572872 | tf_op jit(solution)/shard_map/ppermute | solution.py:26
  82.4 1.5 %all-gather.3.cloned.1.call-done = bf16[16,1024,128]{2,1,0:T(8,128)(2,1)} async-done(((bf16[2,1024,128]{2,1,0:T(8,128)(2,1)}), bf16[16,1024,128]{2,1,0:T(8,128)(2,1)}) %all-gather.3.cloned.1.call-update) | async-done | bytes 4194320 | tf_op jit(solution)/shard_map/all_gather | solution.py:91
  83.9 0.0 collective-permute-done.2.far_ref
  83.9 0.0 copy-start.1
  83.9 2.2 %copy-done.1 = bf16[16,1024,128]{2,1,0:T(8,128)(2,1)S(1)} copy-done((bf16[16,1024,128]{2,1,0:T(8,128)(2,1)S(1)}, bf16[16,1024,128]{2,1,0:T(8,128)(2,1)}, u32[]{:S(2)}) %copy-start.1) | copy-done | bytes 4194328
  86.1 1.2 %shard_map.46 = (f32[512,256]{1,0:T(8,128)S(1)}, f32[512,256]{1,0:T(8,128)S(1)}) custom-call(s32[1]{0:T(128)} %bitcast.swapped_ref, bf16[8,2,1024,128]{3,2,1,0:T(8,128)(2,1)S(1)} %bitcast.28, bf16[8,128,256]{2,1,0:T(8,128)(2,1)S(1)} %all_to_all.15.near_ref, bf16[8,128,256]{2,1,0:T(8,128)(2,1)S(1)} %collective-permute-done.2.far_ref), custom_call_target="tpu_custom_call" | custom-call | flops 1073741824 | bytes 6291456 | tf_op jit(solution)/shard_map/pallas_call | solution.py:61
  87.3 7.2 %collective-permute-start.3 = (f32[512,256]{1,0:T(8,128)S(1)}, f32[512,256]{1,0:T(8,128)S(1)}, u32[]{:S(2)}, u32[]{:S(2)}) collective-permute-start(f32[512,256]{1,0:T(8,128)S(1)} %get-tuple-element.11), channel_id=1, source_target_pairs={{0,1},{1,0},{2,3},{3,2},{4,5},{5,4},{6,7},{7,6},{8,9},{9,8},{10,11... | collective-permute-start | bytes 1572872 | tf_op jit(solution)/shard_map/ppermute | solution.py:26
  94.5 1.9 %collective-permute-start.4 = (f32[512,256]{1,0:T(8,128)S(1)}, f32[512,256]{1,0:T(8,128)S(1)}, u32[]{:S(2)}, u32[]{:S(2)}) collective-permute-start(f32[512,256]{1,0:T(8,128)S(1)} %get-tuple-element.12), channel_id=1, source_target_pairs={{0,1},{1,0},{2,3},{3,2},{4,5},{5,4},{6,7},{7,6},{8,9},{9,8},{10,11... | collective-permute-start | bytes 1572872 | tf_op jit(solution)/shard_map/ppermute | solution.py:26
  96.4 0.0 collective-permute-done.1.far_ref
  96.4 0.0 collective-permute-done.3.refs_0_
  96.5 1.9 %collective-permute-done.4.refs_1_ = f32[512,256]{1,0:T(8,128)S(1)} collective-permute-done((f32[512,256]{1,0:T(8,128)S(1)}, f32[512,256]{1,0:T(8,128)S(1)}, u32[]{:S(2)}, u32[]{:S(2)}) %collective-permute-start.4) | collective-permute-done | bytes 524320 | tf_op jit(solution)/shard_map/ppermute | solution.py:26
  98.3 2.3 %shard_map.47 = f32[1024,256]{1,0:T(8,128)} custom-call(s32[1]{0:T(128)} %bitcast.swapped_ref, bf16[8,2,1024,128]{3,2,1,0:T(8,128)(2,1)S(1)} %bitcast.29, bf16[8,128,256]{2,1,0:T(8,128)(2,1)S(1)} %all-to-all-done.1.near_ref, bf16[8,128,256]{2,1,0:T(8,128)(2,1)S(1)} %collective-permute-done.1.far_ref, f32[512,256]{1,0:T(8,128)S(1)} %collective-permute-done.3.refs_0_, ...), custom_call_target="tpu_custom_call" | custom-call | flops 1073741824 | bytes 6291456 | tf_op jit(solution)/shard_map/pallas_call | solution.py:61
  (3 shorter events, 0.1 us)
Async XLA Ops:
  6.5 5.4 %copy-start = (bf16[2,512,512]{2,1,0:T(8,128)(2,1)S(1)}, bf16[2,512,512]{2,1,0:T(8,128)(2,1)}, u32[]{:S(2)}) copy-start(bf16[2,512,512]{2,1,0:T(8,128)(2,1)} %param.5) | copy-start | bytes 3145732
  6.5 77.3 %all-gather.3.cloned.1.call-start = ((), (), s32[]{:S(2)}) async-start(), calls=%async_computation.3 | async-start | bytes 4718592 | tf_op jit(solution)/shard_map/all_gather | solution.py:91
  6.5 8.0 %collective-permute-start = (bf16[128,1024]{1,0:T(8,128)(2,1)}, bf16[128,1024]{1,0:T(8,128)(2,1)S(1)}, u32[]{:S(2)}, u32[]{:S(2)}) collective-permute-start(bf16[128,1024]{1,0:T(8,128)(2,1)} %param.4), channel_id=1, source_target_pairs={{0,16},{16,0},{1,17},{17,1},{2,18},{18,2},{3,19},{19,3},{4,20},{20... | collective-permute-start | bytes 786440 | tf_op jit(solution)/shard_map/ppermute | solution.py:26
  16.7 11.5 %all-to-all-start = ((bf16[2,128,512]{2,1,0:T(8,128)(2,1)}), bf16[2,128,512]{2,1,0:T(8,128)(2,1)S(1)}, u32[]{:S(2)}, u32[]{:S(2)}) async-start(bf16[2,128,512]{2,1,0:T(8,128)(2,1)} %broadcast_in_dim.13), calls=%async_computation | async-start | bytes 524288 | tf_op jit(solution)/shard_map/all_to_all | solution.py:21
  61.0 15.9 %all-to-all-start.1 = ((bf16[8,128,256]{2,1,0:T(8,128)(2,1)}), bf16[8,128,256]{2,1,0:T(8,128)(2,1)S(1)}, u32[]{:S(2)}, u32[]{:S(2)}) async-start(bf16[8,128,256]{2,1,0:T(8,128)(2,1)} %broadcast_in_dim.14), calls=%async_computation.1 | async-start | bytes 1048576 | tf_op jit(solution)/shard_map/all_to_all | solution.py:97
  64.8 19.1 %collective-permute-start.2 = (bf16[8,128,256]{2,1,0:T(8,128)(2,1)S(1)}, bf16[8,128,256]{2,1,0:T(8,128)(2,1)S(1)}, u32[]{:S(2)}, u32[]{:S(2)}) collective-permute-start(bf16[8,128,256]{2,1,0:T(8,128)(2,1)S(1)} %all_to_all.15.near_ref), channel_id=1, source_target_pairs={{0,256},{256,0},{1,257},{257,1},{2,258},{258,2},{3,259},{259,3},{4... | collective-permute-start | bytes 1572872 | tf_op jit(solution)/shard_map/ppermute | solution.py:26
  76.9 19.6 %collective-permute-start.1 = (bf16[8,128,256]{2,1,0:T(8,128)(2,1)S(1)}, bf16[8,128,256]{2,1,0:T(8,128)(2,1)S(1)}, u32[]{:S(2)}, u32[]{:S(2)}) collective-permute-start(bf16[8,128,256]{2,1,0:T(8,128)(2,1)S(1)} %all-to-all-done.1.near_ref), channel_id=1, source_target_pairs={{0,256},{256,0},{1,257},{257,1},{2,258},{258,2},{3,259},{259,3},{4... | collective-permute-start | bytes 1572872 | tf_op jit(solution)/shard_map/ppermute | solution.py:26
  83.9 2.2 %copy-start.1 = (bf16[16,1024,128]{2,1,0:T(8,128)(2,1)S(1)}, bf16[16,1024,128]{2,1,0:T(8,128)(2,1)}, u32[]{:S(2)}) copy-start(bf16[16,1024,128]{2,1,0:T(8,128)(2,1)} %all-gather.3.cloned.1.call-done) | copy-start | bytes 12582916
  87.3 9.1 %collective-permute-start.3 = (f32[512,256]{1,0:T(8,128)S(1)}, f32[512,256]{1,0:T(8,128)S(1)}, u32[]{:S(2)}, u32[]{:S(2)}) collective-permute-start(f32[512,256]{1,0:T(8,128)S(1)} %get-tuple-element.11), channel_id=1, source_target_pairs={{0,1},{1,0},{2,3},{3,2},{4,5},{5,4},{6,7},{7,6},{8,9},{9,8},{10,11... | collective-permute-start | bytes 1572872 | tf_op jit(solution)/shard_map/ppermute | solution.py:26
  94.5 3.8 %collective-permute-start.4 = (f32[512,256]{1,0:T(8,128)S(1)}, f32[512,256]{1,0:T(8,128)S(1)}, u32[]{:S(2)}, u32[]{:S(2)}) collective-permute-start(f32[512,256]{1,0:T(8,128)S(1)} %get-tuple-element.12), channel_id=1, source_target_pairs={{0,1},{1,0},{2,3},{3,2},{4,5},{5,4},{6,7},{7,6},{8,9},{9,8},{10,11... | collective-permute-start | bytes 1572872 | tf_op jit(solution)/shard_map/ppermute | solution.py:26
Sparse Core Ops, SparseCore 0:
  16.8 67.0 all-gather.2
